TPU v7x, 256 devices: a whole 4x4x8 slice. The times are simulated.
256 devices in a mesh: blk: 8 (over x_lo, y), grp: 32 (over x_hi, z, core).
Axes of the slice: x: 4 (x_hi: 2, x_lo: 2; x = x_hi * 2 + x_lo), y: 4, z: 8, core: 2. Of those that a mesh axis runs over, the one named last changes fastest.
Arguments:
- picture_vectors_prenorm: float32 [4096, 1152], P(('blk', 'grp')), may hold values from -2 to 2, as said below
- caption_vectors_prenorm: float32 [4096, 1152], P(('blk', 'grp')), may hold values from -2 to 2, as said below
- matched_caption_ids: int32 [4096], P(('blk', 'grp')), may hold values from 0 to 4095, each once
- sharpness_coefficient: float32 [1], replicated, may hold values from 4 to 12
- additive_offset_term: float32 [1], replicated, may hold values from -6 to -2
- heads_mixed_concluding: bfloat16 [98304, 1536], P(('blk', 'grp')), may hold values from -6 to 6
- dense_result_adjoint: bfloat16 [98304, 1536], P(('blk', 'grp')), may hold values from -6 to 6
- dense_mapping_matrix: bfloat16 [1536, 1536], P('grp'), may hold values from -0.15625 to 0.15625
Outputs:
- image_grad: float32 [4096, 1152], P(('blk', 'grp'))
- text_grad: float32 [4096, 1152], P(('blk', 'grp'))
- attn_grad: bfloat16 [98304, 1536], P(('blk', 'grp'))
- weight_grad: float32 [1536, 1536], P('grp')
Inputs may be any that keep to these rules, and one draw needn't show every extreme that they name: `matched_caption_ids`: each text index appears once. `picture_vectors_prenorm`: raw embedding entries. `caption_vectors_prenorm`: raw embedding entries.
All inputs are finite; a program needn't handle non-finite values.
Results may differ from a plain program's by a relative error of at most 0.0053.
Values may be sent and summed in bfloat16 or wider, within the bound.
No kernel may reach another device: no remote copies, remote signals or barrier semaphores. Data moves between devices by JAX's collectives and lax.ppermute only.
A program may use at most 128 MiB of HBM per device.

v0:
```python
import math

import jax
import jax.numpy as jnp
from jax import lax
from jax.sharding import PartitionSpec as P

stability_floor = 1e-06


def as_sent(x):

    def short(part):
        return part.astype(jnp.bfloat16) if part.dtype == jnp.float32 else part

    return jax.tree.map(short, x)


def passed_along(x, axis, by):
    peers = lax.axis_size(axis)
    return lax.ppermute(x, axis, [(i, (i + by) % peers) for i in range(peers)])


def unit_rows(raw):
    row_scale = lax.rsqrt(jnp.sum(raw * raw, axis=1, keepdims=True) + stability_floor)
    return (raw * row_scale, row_scale)


def back_through_norm(normed, row_scale, row_grad):
    along_unit = jnp.sum(normed * row_grad, axis=1, keepdims=True)
    return (row_grad - normed * along_unit) * row_scale


def weighted_sum(query_half, key_half, labels, sigmoid_multiplier, bias_value):
    inner_dots = lax.dot_general(
        query_half, key_half, (((1,), (1,)), ((), ())), preferred_element_type=jnp.float32
    )
    logits = sigmoid_multiplier * inner_dots + bias_value
    pair_weights = (sigmoid_multiplier * (jax.nn.sigmoid(logits) - labels)).astype(jnp.bfloat16)
    return jnp.dot(pair_weights, key_half, preferred_element_type=jnp.float32)


def pass_on(held_rows, direction):
    return jax.tree.map(
        lambda part, own: part.astype(own.dtype),
        passed_along(as_sent(held_rows), "blk", direction),
        held_rows,
    )


def per_device(
    picture_vectors_prenorm,
    caption_vectors_prenorm,
    matched_caption_ids,
    sharpness_coefficient,
    additive_offset_term,
    heads_mixed_concluding,
    dense_result_adjoint,
    dense_mapping_matrix,
):
    image_units, image_scale = unit_rows(picture_vectors_prenorm)
    text_units, text_scale = unit_rows(caption_vectors_prenorm)
    image_half = image_units.astype(jnp.bfloat16)
    text_half = text_units.astype(jnp.bfloat16)
    sigmoid_multiplier = sharpness_coefficient[0]
    bias_value = additive_offset_term[0]
    own_rows = image_half.shape[0]
    own_first = (lax.axis_index("blk") * lax.axis_size("grp") + lax.axis_index("grp")) * own_rows
    text_index = own_first + lax.broadcasted_iota(jnp.int32, (own_rows, 1), 0)
    grads = (jnp.zeros(image_units.shape, jnp.float32), jnp.zeros(text_units.shape, jnp.float32))
    image_block, text_block, owner_ids = (
        lax.all_gather(image_half, "grp", axis=0, tiled=True),
        lax.all_gather(text_half, "grp", axis=0, tiled=True),
        lax.all_gather(matched_caption_ids, "grp", axis=0, tiled=True),
    )
    group_rows = image_block.shape[0]
    cycle_size = lax.axis_size("blk")
    cycle_place = lax.axis_index("blk")
    streams = [(1, 0, (image_block, text_block, owner_ids))]
    for cycle_step in range(cycle_size):
        next_streams = []
        for direction, offset, held_rows in streams:
            anchor = jnp.remainder(cycle_place - direction * cycle_step, cycle_size)
            absorb_text_block = held_rows[1]
            columns = (
                anchor * group_rows
                + offset
                + lax.broadcasted_iota(jnp.int32, (1, absorb_text_block.shape[0]), 1)
            )
            image_labels = (matched_caption_ids[:, None] == columns).astype(jnp.float32)
            text_labels = (text_index == held_rows[2][None, :]).astype(jnp.float32)
            image_part = weighted_sum(
                image_half, absorb_text_block, image_labels, sigmoid_multiplier, bias_value
            )
            text_part = weighted_sum(
                text_half, held_rows[0], text_labels, sigmoid_multiplier, bias_value
            )
            grads = (grads[0] + image_part, grads[1] + text_part)
            if cycle_step + 1 < cycle_size:
                held_rows = pass_on(held_rows, direction)
            next_streams.append((direction, offset, held_rows))
        streams = next_streams
    image_grad = back_through_norm(image_units, image_scale, grads[0])
    text_grad = back_through_norm(text_units, text_scale, grads[1])
    attn_grad = lax.dot_general(
        dense_result_adjoint,
        lax.all_gather(dense_mapping_matrix, "grp", axis=0, tiled=True),
        (((1,), (1,)), ((), ())),
        preferred_element_type=jnp.float32,
    ).astype(jnp.bfloat16)
    weight_share = lax.psum_scatter(
        lax.dot_general(
            heads_mixed_concluding,
            dense_result_adjoint,
            (((0,), (0,)), ((), ())),
            preferred_element_type=jnp.float32,
        ),
        "grp",
        scatter_dimension=0,
        tiled=True,
    )
    weight_total = lax.psum(weight_share, "blk")
    token_count = heads_mixed_concluding.shape[0] * lax.axis_size("blk") * lax.axis_size("grp")
    weight_grad = weight_total * (1.0 / math.sqrt(token_count))
    return (image_grad, text_grad, attn_grad, weight_grad)


def solution(mesh):
    placed = (
        P(("blk", "grp"), None),
        P(("blk", "grp"), None),
        P(("blk", "grp")),
        P(),
        P(),
        P(("blk", "grp"), None),
        P(("blk", "grp"), None),
        P("grp", None),
    )
    return jax.shard_map(
        per_device,
        mesh=mesh,
        in_specs=placed,
        out_specs=(
            P(("blk", "grp"), None),
            P(("blk", "grp"), None),
            P(("blk", "grp"), None),
            P("grp", None),
        ),
        check_vma=False,
    )
```

profile of v0, /device:TPU:2, one launch (start us, length us, event | category | flops | bytes accessed | tf_op | source)
XLA Modules:
  0.0 646.9 jit_solution(5559939389831891325)
XLA Ops:
  7.2 1.1 multiply_reduce_fusion.3
  8.3 1.6 multiply_convert_fusion.1
  10.0 1.0 multiply_reduce_fusion.2
  11.0 1.6 multiply_convert_fusion
  13.4 6.4 fusion.258
  19.9 70.8 %all-gather.6.cloned.1.call-done = bf16[512,1152]{1,0:T(8,128)(2,1)} async-done(((bf16[16,1152]{1,0:T(8,128)(2,1)}), bf16[512,1152]{1,0:T(8,128)(2,1)}) %all-gather.6.cloned.1.call-update) | async-done | bytes 1179664 | tf_op jit(solution)/shard_map/all_gather | solution.py:72
  90.7 1.5 collective-permute-start.7
  92.2 76.4 %all-gather.4.cloned.1.call-done = bf16[512,1152]{1,0:T(8,128)(2,1)} async-done(((bf16[16,1152]{1,0:T(8,128)(2,1)}), bf16[512,1152]{1,0:T(8,128)(2,1)}) %all-gather.4.cloned.1.call-update) | async-done | bytes 1179664 | tf_op jit(solution)/shard_map/all_gather | solution.py:73
  168.5 1.5 collective-permute-start
  170.0 1.5 collective-permute-start.9
  171.5 29.7 %collective-permute-done = bf16[512,1152]{1,0:T(8,128)(2,1)S(1)} collective-permute-done((bf16[512,1152]{1,0:T(8,128)(2,1)}, bf16[512,1152]{1,0:T(8,128)(2,1)S(1)}, u32[]{:S(2)}, u32[]{:S(2)}) %collective-permute-start) | collective-permute-done | bytes 1179680 | tf_op jit(solution)/shard_map/ppermute | solution.py:21
  201.2 29.7 %collective-permute-done.9 = bf16[512,1152]{1,0:T(8,128)(2,1)S(1)} collective-permute-done((bf16[512,1152]{1,0:T(8,128)(2,1)S(1)}, bf16[512,1152]{1,0:T(8,128)(2,1)S(1)}, u32[]{:S(2)}, u32[]{:S(2)}) %collective-permute-start.9) | collective-permute-done | bytes 1179680 | tf_op jit(solution)/shard_map/ppermute | solution.py:21
  231.0 33.6 %collective-permute-done.1 = bf16[512,1152]{1,0:T(8,128)(2,1)} collective-permute-done((bf16[512,1152]{1,0:T(8,128)(2,1)S(1)}, bf16[512,1152]{1,0:T(8,128)(2,1)}, u32[]{:S(2)}, u32[]{:S(2)}) %collective-permute-start.1) | collective-permute-done | bytes 1179680 | tf_op jit(solution)/shard_map/ppermute | solution.py:21
  266.0 15.8 %all-reduce = s32[512]{0:T(512)} all-reduce(s32[512]{0:T(512)S(1)} %dynamic-update-slice), channel_id=1, replica_groups=mesh['blk'=8,'grp'=32] {'grp'}, use_global_device_ids=true, to_apply=%add | all-reduce | flops 512 | bytes 4096
  282.5 7.3 %collective-permute-done.11 = bf16[512,1152]{1,0:T(8,128)(2,1)} collective-permute-done((bf16[512,1152]{1,0:T(8,128)(2,1)S(1)}, bf16[512,1152]{1,0:T(8,128)(2,1)}, u32[]{:S(2)}, u32[]{:S(2)}) %collective-permute-start.11) | collective-permute-done | bytes 1179680 | tf_op jit(solution)/shard_map/ppermute | solution.py:21
  290.4 24.1 %collective-permute-done.2 = bf16[512,1152]{1,0:T(8,128)(2,1)} collective-permute-done((bf16[512,1152]{1,0:T(8,128)(2,1)}, bf16[512,1152]{1,0:T(8,128)(2,1)}, u32[]{:S(2)}, u32[]{:S(2)}) %collective-permute-start.2) | collective-permute-done | bytes 1179680 | tf_op jit(solution)/shard_map/ppermute | solution.py:21
  314.5 3.5 collective-permute-start.3
  318.0 0.8 collective-permute-done.8
  319.4 63.2 %collective-permute-done.10 = s32[512]{0:T(512)} collective-permute-done((s32[512]{0:T(512)S(1)}, s32[512]{0:T(512)}, u32[]{:S(2)}, u32[]{:S(2)}) %collective-permute-start.10) | collective-permute-done | bytes 2080 | tf_op jit(solution)/shard_map/ppermute | solution.py:21
  383.2 5.4 collective-permute-done.12
  389.3 5.4 collective-permute-done.14
  395.3 5.4 collective-permute-done.16
  402.0 4.7 collective-permute-done.18
  406.7 3.1 fusion.129
  409.8 2.1 fusion.128
  411.9 2.3 convolution_add_fusion.6
  414.2 2.3 convolution_add_fusion.13
  416.5 1.6 convolution_add_fusion.5
  418.2 3.0 convolution_add_fusion.12
  421.1 22.9 %collective-permute-done.15 = bf16[512,1152]{1,0:T(8,128)(2,1)} collective-permute-done((bf16[512,1152]{1,0:T(8,128)(2,1)}, bf16[512,1152]{1,0:T(8,128)(2,1)}, u32[]{:S(2)}, u32[]{:S(2)}) %collective-permute-start.15) | collective-permute-done | bytes 1179680 | tf_op jit(solution)/shard_map/ppermute | solution.py:21
  444.0 2.9 convolution_add_fusion.4
  447.0 22.3 %collective-permute-done.4 = bf16[512,1152]{1,0:T(8,128)(2,1)} collective-permute-done((bf16[512,1152]{1,0:T(8,128)(2,1)}, bf16[512,1152]{1,0:T(8,128)(2,1)}, u32[]{:S(2)}, u32[]{:S(2)}) %collective-permute-start.4) | collective-permute-done | bytes 1179680 | tf_op jit(solution)/shard_map/ppermute | solution.py:21
  469.3 3.0 convolution_add_fusion.11
  472.3 3.0 convolution_add_fusion.3
  475.3 3.0 convolution_add_fusion.10
  478.3 3.0 convolution_add_fusion.2
  481.3 13.2 %collective-permute-done.17 = bf16[512,1152]{1,0:T(8,128)(2,1)S(1)} collective-permute-done((bf16[512,1152]{1,0:T(8,128)(2,1)}, bf16[512,1152]{1,0:T(8,128)(2,1)S(1)}, u32[]{:S(2)}, u32[]{:S(2)}) %collective-permute-start.17) | collective-permute-done | bytes 1179680 | tf_op jit(solution)/shard_map/ppermute | solution.py:21
  494.5 3.0 convolution_add_fusion.9
  497.4 22.3 %collective-permute-done.5 = bf16[512,1152]{1,0:T(8,128)(2,1)S(1)} collective-permute-done((bf16[512,1152]{1,0:T(8,128)(2,1)}, bf16[512,1152]{1,0:T(8,128)(2,1)S(1)}, u32[]{:S(2)}, u32[]{:S(2)}) %collective-permute-start.5) | collective-permute-done | bytes 1179680 | tf_op jit(solution)/shard_map/ppermute | solution.py:21
  519.8 5.4 convolution_convert_fusion
  525.1 2.2 convolution_add_fusion.1
  527.4 2.2 convolution_add_fusion.8
  529.6 15.6 %collective-permute-done.19 = bf16[512,1152]{1,0:T(8,128)(2,1)} collective-permute-done((bf16[512,1152]{1,0:T(8,128)(2,1)S(1)}, bf16[512,1152]{1,0:T(8,128)(2,1)}, u32[]{:S(2)}, u32[]{:S(2)}) %collective-permute-start.19) | collective-permute-done | bytes 1179680 | tf_op jit(solution)/shard_map/ppermute | solution.py:21
  545.2 2.5 multiply_reduce_fusion
  547.7 14.5 %collective-permute-done.6 = bf16[512,1152]{1,0:T(8,128)(2,1)} collective-permute-done((bf16[512,1152]{1,0:T(8,128)(2,1)S(1)}, bf16[512,1152]{1,0:T(8,128)(2,1)}, u32[]{:S(2)}, u32[]{:S(2)}) %collective-permute-start.6) | collective-permute-done | bytes 1179680 | tf_op jit(solution)/shard_map/ppermute | solution.py:21
  562.2 2.4 multiply_reduce_fusion.1
  566.1 72.6 %all-reduce.3.cloned.1.call-done = f32[48,1536]{1,0:T(8,128)} async-done(((f32[48,1536]{1,0:T(8,128)}), f32[48,1536]{1,0:T(8,128)}) %all-reduce.3.cloned.1.call-update) | async-done | bytes 294928 | tf_op jit(solution)/shard_map/psum | solution.py:122
  638.7 1.7 broadcast_multiply_fusion
  (97 shorter events, 6.9 us)
Async XLA Ops:
  7.2 6.2 copy-start
  7.2 83.5 %all-gather.6.cloned.1.call-start = ((), (), s32[]{:S(2)}) async-start(), calls=%async_computation.2 | async-start | bytes 1216512 | tf_op jit(solution)/shard_map/all_gather | solution.py:72
  8.3 11.5 %copy-start.18 = (f32[16]{0:T(128)}, f32[16]{0:T(128)S(1)}, u32[]{:S(2)}) copy-start(f32[16]{0:T(128)S(1)} %add_rsqrt_fusion.1) | copy-start | bytes 196
  9.9 158.6 %all-gather.4.cloned.1.call-start = ((), (), s32[]{:S(2)}) async-start(), calls=%async_computation.1 | async-start | bytes 1216512 | tf_op jit(solution)/shard_map/all_gather | solution.py:73
  11.0 8.8 %copy-start.20 = (f32[16]{0:T(128)}, f32[16]{0:T(128)S(1)}, u32[]{:S(2)}) copy-start(f32[16]{0:T(128)S(1)} %add_rsqrt_fusion) | copy-start | bytes 196
  12.6 507.2 %all-gather.8.cloned.1.call-start = ((), (), s32[]{:S(2)}) async-start(), calls=%async_computation.3 | async-start | bytes 4866048 | tf_op jit(solution)/shard_map/all_gather | solution.py:107
  13.3 552.1 %reduce-scatter.2.cloned.1.call-start = ((), (), s32[]{:S(2)}) async-start(), calls=%async_computation.4 | async-start | bytes 9732096 | tf_op jit(solution)/shard_map/reduce_scatter | solution.py:111
  19.8 244.7 %copy-start.23 = (u32[256]{0:T(256)S(1)}, u32[256]{0:T(256)}, u32[]{:S(2)}) copy-start(u32[256]{0:T(256)} %constant.93) | copy-start | bytes 3076
  19.8 246.0 %copy-start.13 = (s32[16]{0:T(128)S(1)}, s32[16]{0:T(128)}, u32[]{:S(2)}) copy-start(s32[16]{0:T(128)} %param.10) | copy-start | bytes 196
  19.9 618.8 %all-reduce.3.cloned.1.call-start = ((), (), s32[]{:S(2)}) async-start(), calls=%async_computation.5 | async-start | bytes 589824 | tf_op jit(solution)/shard_map/psum | solution.py:122
  90.7 79.3 %collective-permute-start.7 = (bf16[512,1152]{1,0:T(8,128)(2,1)}, bf16[512,1152]{1,0:T(8,128)(2,1)S(1)}, u32[]{:S(2)}, u32[]{:S(2)}) collective-permute-start(bf16[512,1152]{1,0:T(8,128)(2,1)} %all-gather.6.cloned.1.call-done), channel_id=1, source_target_pairs={{0,32},{32,64},{64,96},{96,128},{128,160},{160,192},{192,224},{224... | collective-permute-start | bytes 3538952 | tf_op jit(solution)/shard_map/ppermute | solution.py:21
  168.5 32.7 %collective-permute-start = (bf16[512,1152]{1,0:T(8,128)(2,1)}, bf16[512,1152]{1,0:T(8,128)(2,1)S(1)}, u32[]{:S(2)}, u32[]{:S(2)}) collective-permute-start(bf16[512,1152]{1,0:T(8,128)(2,1)} %all-gather.4.cloned.1.call-done), channel_id=1, source_target_pairs={{0,32},{32,64},{64,96},{96,128},{128,160},{160,192},{192,224},{224... | collective-permute-start | bytes 3538952 | tf_op jit(solution)/shard_map/ppermute | solution.py:21
  170.0 60.9 %collective-permute-start.9 = (bf16[512,1152]{1,0:T(8,128)(2,1)S(1)}, bf16[512,1152]{1,0:T(8,128)(2,1)S(1)}, u32[]{:S(2)}, u32[]{:S(2)}) collective-permute-start(bf16[512,1152]{1,0:T(8,128)(2,1)S(1)} %collective-permute-done.7), channel_id=1, source_target_pairs={{0,32},{32,64},{64,96},{96,128},{128,160},{160,192},{192,224},{224... | collective-permute-start | bytes 3538952 | tf_op jit(solution)/shard_map/ppermute | solution.py:21
  201.2 29.7 %copy-start.2 = (bf16[512,1152]{1,0:T(8,128)(2,1)}, bf16[512,1152]{1,0:T(8,128)(2,1)S(1)}, u32[]{:S(2)}) copy-start(bf16[512,1152]{1,0:T(8,128)(2,1)S(1)} %collective-permute-done) | copy-start | bytes 3538948
  201.2 63.3 %collective-permute-start.1 = (bf16[512,1152]{1,0:T(8,128)(2,1)S(1)}, bf16[512,1152]{1,0:T(8,128)(2,1)}, u32[]{:S(2)}, u32[]{:S(2)}) collective-permute-start(bf16[512,1152]{1,0:T(8,128)(2,1)S(1)} %collective-permute-done), channel_id=1, source_target_pairs={{0,32},{32,64},{64,96},{96,128},{128,160},{160,192},{192,224},{224... | collective-permute-start | bytes 3538952 | tf_op jit(solution)/shard_map/ppermute | solution.py:21
  231.0 175.8 %copy-start.4 = (bf16[512,1152]{1,0:T(8,128)(2,1)}, bf16[512,1152]{1,0:T(8,128)(2,1)S(1)}, u32[]{:S(2)}) copy-start(bf16[512,1152]{1,0:T(8,128)(2,1)S(1)} %collective-permute-done.9) | copy-start | bytes 3538948
  231.0 58.9 %collective-permute-start.11 = (bf16[512,1152]{1,0:T(8,128)(2,1)S(1)}, bf16[512,1152]{1,0:T(8,128)(2,1)}, u32[]{:S(2)}, u32[]{:S(2)}) collective-permute-start(bf16[512,1152]{1,0:T(8,128)(2,1)S(1)} %collective-permute-done.9), channel_id=1, source_target_pairs={{0,32},{32,64},{64,96},{96,128},{128,160},{160,192},{192,224},{224... | collective-permute-start | bytes 3538952 | tf_op jit(solution)/shard_map/ppermute | solution.py:21
  264.5 49.9 %collective-permute-start.2 = (bf16[512,1152]{1,0:T(8,128)(2,1)}, bf16[512,1152]{1,0:T(8,128)(2,1)}, u32[]{:S(2)}, u32[]{:S(2)}) collective-permute-start(bf16[512,1152]{1,0:T(8,128)(2,1)} %collective-permute-done.1), channel_id=1, source_target_pairs={{0,32},{32,64},{64,96},{96,128},{128,160},{160,192},{192,224},{224... | collective-permute-start | bytes 3538952 | tf_op jit(solution)/shard_map/ppermute | solution.py:21
  281.9 36.9 %collective-permute-start.8 = (s32[512]{0:T(512)}, s32[512]{0:T(512)S(1)}, u32[]{:S(2)}, u32[]{:S(2)}) collective-permute-start(s32[512]{0:T(512)} %all-reduce), channel_id=1, source_target_pairs={{0,32},{32,64},{64,96},{96,128},{128,160},{160,192},{192,224},{224... | collective-permute-start | bytes 6152 | tf_op jit(solution)/shard_map/ppermute | solution.py:21
  289.8 120.0 %collective-permute-start.13 = (bf16[512,1152]{1,0:T(8,128)(2,1)}, bf16[512,1152]{1,0:T(8,128)(2,1)}, u32[]{:S(2)}, u32[]{:S(2)}) collective-permute-start(bf16[512,1152]{1,0:T(8,128)(2,1)} %collective-permute-done.11), channel_id=1, source_target_pairs={{0,32},{32,64},{64,96},{96,128},{128,160},{160,192},{192,224},{224... | collective-permute-start | bytes 3538952 | tf_op jit(solution)/shard_map/ppermute | solution.py:21
  314.5 97.4 %collective-permute-start.3 = (bf16[512,1152]{1,0:T(8,128)(2,1)}, bf16[512,1152]{1,0:T(8,128)(2,1)}, u32[]{:S(2)}, u32[]{:S(2)}) collective-permute-start(bf16[512,1152]{1,0:T(8,128)(2,1)} %collective-permute-done.2), channel_id=1, source_target_pairs={{0,32},{32,64},{64,96},{96,128},{128,160},{160,192},{192,224},{224... | collective-permute-start | bytes 3538952 | tf_op jit(solution)/shard_map/ppermute | solution.py:21
  318.8 81.9 %copy-start.22 = (s32[512]{0:T(512)}, s32[512]{0:T(512)S(1)}, u32[]{:S(2)}) copy-start(s32[512]{0:T(512)S(1)} %collective-permute-done.8) | copy-start | bytes 6148
  318.8 63.8 %collective-permute-start.10 = (s32[512]{0:T(512)S(1)}, s32[512]{0:T(512)}, u32[]{:S(2)}, u32[]{:S(2)}) collective-permute-start(s32[512]{0:T(512)S(1)} %collective-permute-done.8), channel_id=1, source_target_pairs={{0,32},{32,64},{64,96},{96,128},{128,160},{160,192},{192,224},{224... | collective-permute-start | bytes 6152 | tf_op jit(solution)/shard_map/ppermute | solution.py:21
  382.6 6.0 collective-permute-start.12
  388.7 6.0 collective-permute-start.14
  394.7 6.0 collective-permute-start.16
  400.7 6.0 collective-permute-start.18
  406.7 122.9 %collective-permute-start.20 = (s32[512]{0:T(512)}, s32[512]{0:T(512)}, u32[]{:S(2)}, u32[]{:S(2)}) collective-permute-start(s32[512]{0:T(512)} %collective-permute-done.18), channel_id=1, source_target_pairs={{0,32},{32,64},{64,96},{96,128},{128,160},{160,192},{192,224},{224... | collective-permute-start | bytes 6152 | tf_op jit(solution)/shard_map/ppermute | solution.py:21
  406.7 3.1 copy-start.1
  409.8 34.2 %collective-permute-start.15 = (bf16[512,1152]{1,0:T(8,128)(2,1)}, bf16[512,1152]{1,0:T(8,128)(2,1)}, u32[]{:S(2)}, u32[]{:S(2)}) collective-permute-start(bf16[512,1152]{1,0:T(8,128)(2,1)} %collective-permute-done.13), channel_id=1, source_target_pairs={{0,32},{32,64},{64,96},{96,128},{128,160},{160,192},{192,224},{224... | collective-permute-start | bytes 3538952 | tf_op jit(solution)/shard_map/ppermute | solution.py:21
  411.9 57.4 %collective-permute-start.4 = (bf16[512,1152]{1,0:T(8,128)(2,1)}, bf16[512,1152]{1,0:T(8,128)(2,1)}, u32[]{:S(2)}, u32[]{:S(2)}) collective-permute-start(bf16[512,1152]{1,0:T(8,128)(2,1)} %collective-permute-done.3), channel_id=1, source_target_pairs={{0,32},{32,64},{64,96},{96,128},{128,160},{160,192},{192,224},{224... | collective-permute-start | bytes 3538952 | tf_op jit(solution)/shard_map/ppermute | solution.py:21
  411.9 2.3 copy-start.3
  414.2 2.3 copy-start.5
  418.2 25.9 %copy-start.8 = (bf16[16,1152]{1,0:T(8,128)(2,1)S(1)}, bf16[16,1152]{1,0:T(8,128)(2,1)}, u32[]{:S(2)}) copy-start(bf16[16,1152]{1,0:T(8,128)(2,1)} %multiply_convert_fusion) | copy-start | bytes 110596
  444.0 50.5 %collective-permute-start.17 = (bf16[512,1152]{1,0:T(8,128)(2,1)}, bf16[512,1152]{1,0:T(8,128)(2,1)S(1)}, u32[]{:S(2)}, u32[]{:S(2)}) collective-permute-start(bf16[512,1152]{1,0:T(8,128)(2,1)} %collective-permute-done.15), channel_id=1, source_target_pairs={{0,32},{32,64},{64,96},{96,128},{128,160},{160,192},{192,224},{224... | collective-permute-start | bytes 3538952 | tf_op jit(solution)/shard_map/ppermute | solution.py:21
  469.3 50.5 %collective-permute-start.5 = (bf16[512,1152]{1,0:T(8,128)(2,1)}, bf16[512,1152]{1,0:T(8,128)(2,1)S(1)}, u32[]{:S(2)}, u32[]{:S(2)}) collective-permute-start(bf16[512,1152]{1,0:T(8,128)(2,1)} %collective-permute-done.4), channel_id=1, source_target_pairs={{0,32},{32,64},{64,96},{96,128},{128,160},{160,192},{192,224},{224... | collective-permute-start | bytes 3538952 | tf_op jit(solution)/shard_map/ppermute | solution.py:21
  472.3 3.0 copy-start.14
  478.3 16.2 %copy-start.15 = (s32[512]{0:T(512)S(1)}, s32[512]{0:T(512)}, u32[]{:S(2)}) copy-start(s32[512]{0:T(512)} %iota_add_fusion.2) | copy-start | bytes 6148
  494.5 50.7 %collective-permute-start.19 = (bf16[512,1152]{1,0:T(8,128)(2,1)S(1)}, bf16[512,1152]{1,0:T(8,128)(2,1)}, u32[]{:S(2)}, u32[]{:S(2)}) collective-permute-start(bf16[512,1152]{1,0:T(8,128)(2,1)S(1)} %collective-permute-done.17), channel_id=1, source_target_pairs={{0,32},{32,64},{64,96},{96,128},{128,160},{160,192},{192,224},{224... | collective-permute-start | bytes 3538952 | tf_op jit(solution)/shard_map/ppermute | solution.py:21
  519.8 42.4 %collective-permute-start.6 = (bf16[512,1152]{1,0:T(8,128)(2,1)S(1)}, bf16[512,1152]{1,0:T(8,128)(2,1)}, u32[]{:S(2)}, u32[]{:S(2)}) collective-permute-start(bf16[512,1152]{1,0:T(8,128)(2,1)S(1)} %collective-permute-done.5), channel_id=1, source_target_pairs={{0,32},{32,64},{64,96},{96,128},{128,160},{160,192},{192,224},{224... | collective-permute-start | bytes 3538952 | tf_op jit(solution)/shard_map/ppermute | solution.py:21
  525.1 2.2 copy-start.16
  527.4 17.8 %copy-start.21 = (f32[16]{0:T(128)S(1)}, f32[16]{0:T(128)}, u32[]{:S(2)}) copy-start(f32[16]{0:T(128)} %copy-done.20) | copy-start | bytes 196
  545.1 17.0 %copy-start.7 = (bf16[16,1152]{1,0:T(8,128)(2,1)S(1)}, bf16[16,1152]{1,0:T(8,128)(2,1)}, u32[]{:S(2)}) copy-start(bf16[16,1152]{1,0:T(8,128)(2,1)} %multiply_convert_fusion.1) | copy-start | bytes 110596
  545.2 17.0 %copy-start.10 = (f32[16,1152]{1,0:T(8,128)S(1)}, f32[16,1152]{1,0:T(8,128)}, u32[]{:S(2)}) copy-start(f32[16,1152]{1,0:T(8,128)} %param.8) | copy-start | bytes 221188
  545.2 17.0 %copy-start.11 = (f32[16,1152]{1,0:T(8,128)S(1)}, f32[16,1152]{1,0:T(8,128)}, u32[]{:S(2)}) copy-start(f32[16,1152]{1,0:T(8,128)} %convolution_add_fusion.8) | copy-start | bytes 221188
  545.2 17.0 %copy-start.17 = (s32[512]{0:T(512)S(1)}, s32[512]{0:T(512)}, u32[]{:S(2)}) copy-start(s32[512]{0:T(512)} %iota_add_fusion) | copy-start | bytes 6148
  545.2 17.0 %copy-start.19 = (f32[16]{0:T(128)S(1)}, f32[16]{0:T(128)}, u32[]{:S(2)}) copy-start(f32[16]{0:T(128)} %copy-done.18) | copy-start | bytes 196
  562.2 2.5 copy-start.9
  (2 other events, 3.2 us)
Sparse Core Ops, SparseCore 0:
  10.7 79.9 all-gather.5
  93.9 74.5 all-gather.3
  171.3 85.4 all-gather.7
  261.1 181.1 reduce-scatter.1
  565.6 73.1 all-reduce.2
where the time goes:
time: 650 us; the launch traced here: 647 us
  waiting for transfers between devices  541 us (83%)
  matrix products  53.3 us (8%)
  between operations  15.9 us (2%)
  blocking collectives  15.8 us (2%)
  other arithmetic  11.9 us (2%)
  starting transfers between devices  8.22 us (1%)
    ppermute x21, waiting for transfers between devices, passed_along(): return lax.ppermute(x, axis, [(i, (i + by) % peers) for i in range(peers)])  320 us
    all_gather x1, waiting for transfers between devices, per_device(): lax.all_gather(text_half, 'grp', axis=0, tiled=True)  76.4 us
    psum x1, waiting for transfers between devices, per_device(): weight_total = lax.psum(weight_share, 'blk')  72.6 us
    all_gather x1, waiting for transfers between devices, per_device(): lax.all_gather(image_half, 'grp', axis=0, tiled=True)  70.8 us
    dot_general x16, matrix products, weighted_sum(): return jnp.dot(pair_weights, key_half, preferred_element_type=jnp.float32)  41.5 us
    unnamed x1, blocking collectives  15.8 us
  transfers between devices with their start and end apart: 26, of which 20 were waited for; matrix products, arithmetic and copies ran while one was open for 10% of the time, Pallas kernels for 0%

commit v1 on v0

v1 whole, which is shorter than its diff:
```python
import math

import jax
import jax.numpy as jnp
from jax import lax
from jax.sharding import Mesh, PartitionSpec as P

stability_floor = 1e-06

AXES = ("xl", "y", "xh", "z", "c")
SIZES = (2, 4, 2, 8, 2)
PLANE = ("y", "xh", "xl")


def unit_rows(raw):
    row_scale = lax.rsqrt(jnp.sum(raw * raw, axis=1, keepdims=True) + stability_floor)
    return (raw * row_scale, row_scale)


def back_through_norm(normed, row_scale, row_grad):
    along_unit = jnp.sum(normed * row_grad, axis=1, keepdims=True)
    return (row_grad - normed * along_unit) * row_scale


def swap_cores(x):
    return lax.ppermute(x, "c", [(0, 1), (1, 0)])


def exchange(x, axes):
    return lax.all_to_all(x, axes, 0, 0, tiled=True)


def to_everyone(x, count):
    return jnp.broadcast_to(x[None], (count,) + x.shape)


def fold(x):
    lead, rows = x.shape[:-2], x.shape[-2]
    return jnp.swapaxes(x.reshape(lead + (rows, 3, 384)), -3, -2).reshape(lead + (3 * rows, 384))


def unfold(x):
    lead, rows = x.shape[:-2], x.shape[-2] // 3
    return jnp.swapaxes(x.reshape(lead + (3, rows, 384)), -3, -2).reshape(lead + (rows, 1152))


def per_device(
    picture_vectors_prenorm,
    caption_vectors_prenorm,
    matched_caption_ids,
    sharpness_coefficient,
    additive_offset_term,
    heads_mixed_concluding,
    dense_result_adjoint,
    dense_mapping_matrix,
):
    f32, bf16 = jnp.float32, jnp.bfloat16
    xl, y, xh, c = (lax.axis_index(name) for name in ("xl", "y", "xh", "c"))
    other_tokens = swap_cores(heads_mixed_concluding)
    other_adjoint = swap_cores(dense_result_adjoint)

    image_units, image_scale = unit_rows(picture_vectors_prenorm)
    text_units, text_scale = unit_rows(caption_vectors_prenorm)
    image_half = image_units.astype(bf16)
    text_half = text_units.astype(bf16)

    own_piece = lax.dynamic_slice(dense_mapping_matrix, (xl * 24, y * 384), (24, 384))
    sent = jnp.concatenate([text_half, unfold(own_piece)], axis=0)
    along_z = exchange(to_everyone(sent, 8), "z")
    text_here = along_z[:, :16].reshape(128, 1152)
    mapping_piece = fold(along_z[:, 16:]).reshape(192, 384)
    text_block = jnp.concatenate([text_here, swap_cores(text_here)], axis=0)

    def own_columns(tokens):
        blocks = tokens.T.reshape(16, 2, 48, 384)
        return lax.dynamic_index_in_dim(blocks, c, 1, keepdims=False).reshape(768, 384)

    weight_share = jnp.dot(
        jnp.concatenate([own_columns(heads_mixed_concluding), own_columns(other_tokens)], axis=1),
        jnp.concatenate([dense_result_adjoint, other_adjoint], axis=0),
        preferred_element_type=f32,
    ).astype(bf16)
    weight_share = weight_share.reshape(2, 8, 2, 24, 4, 384).transpose(4, 0, 2, 1, 3, 5)
    weight_share = weight_share.reshape(16, 192, 384)
    id_parts = jnp.stack([matched_caption_ids // 64, matched_caption_ids % 64]).astype(bf16)
    id_rows = jnp.pad(id_parts, ((0, 6), (0, 368)))
    image_sent = jnp.concatenate([fold(image_half), id_rows], axis=0)
    in_plane = exchange(
        jnp.concatenate([weight_share, to_everyone(image_sent, 16)], axis=1), PLANE
    )
    weight_plane = jnp.sum(in_plane[:, :192].astype(f32), axis=0)
    image_block = unfold(in_plane[:, 192:240]).reshape(256, 1152)
    ids = in_plane[:, 240:242, :16].astype(jnp.int32)
    ids = (ids[:, 0] * 64 + ids[:, 1]).reshape(256, 1)

    sharpness = sharpness_coefficient[0]
    offset = additive_offset_term[0]
    plane_first = ((xl * 4 + y) * 2 + xh) * 256
    row = lax.broadcasted_iota(jnp.int32, (1, 256), 1)
    core = jnp.where(row < 128, c, 1 - c)
    row = row % 128
    text_index = plane_first + ((row // 16) * 2 + core) * 16 + row % 16
    dots = lax.dot_general(
        image_block, text_block, (((1,), (1,)), ((), ())), preferred_element_type=f32
    )
    labels = (ids == text_index).astype(f32)
    pair_weights = (sharpness * (jax.nn.sigmoid(sharpness * dots + offset) - labels)).astype(bf16)
    image_part = jnp.dot(pair_weights, text_block, preferred_element_type=f32).astype(bf16)
    text_part = lax.dot_general(
        pair_weights, image_block, (((0,), (0,)), ((), ())), preferred_element_type=f32
    )
    text_part = text_part[:128] + swap_cores(text_part[128:].astype(bf16)).astype(f32)

    back = jnp.concatenate(
        [
            text_part.astype(bf16).reshape(8, 16, 1152),
            unfold(weight_plane.astype(bf16).reshape(8, 24, 384)),
        ],
        axis=1,
    )
    back = jnp.sum(exchange(back, "z").astype(f32), axis=0)
    text_grad = back_through_norm(text_units, text_scale, back[:16])
    weight_piece = fold(back[16:]) * (1.0 / math.sqrt(98304))
    pieces = exchange(to_everyone(weight_piece, 8), ("xl", "y"))
    weight_grad = pieces.reshape(2, 4, 24, 384).transpose(0, 2, 1, 3).reshape(48, 1536)

    back = jnp.concatenate(
        [fold(image_part.reshape(16, 16, 1152)), to_everyone(mapping_piece, 16)], axis=1
    )
    back = exchange(back, PLANE)
    image_grad = back_through_norm(
        image_units, image_scale, unfold(jnp.sum(back[:, :48].astype(f32), axis=0))
    )
    rows = back[:, 48:].reshape(4, 2, 2, 8, 24, 384).transpose(1, 3, 2, 4, 0, 5)
    rows = rows.reshape(16, 48, 1536)
    other_rows = swap_cores(rows)
    mapping = jnp.stack(
        [jnp.where(c == 0, rows, other_rows), jnp.where(c == 0, other_rows, rows)], axis=1
    ).reshape(1536, 1536)
    attn_grad = lax.dot_general(
        dense_result_adjoint, mapping, (((1,), (1,)), ((), ())), preferred_element_type=f32
    ).astype(bf16)
    return (image_grad, text_grad, attn_grad, weight_grad)


def solution(mesh):
    chips = Mesh(mesh.devices.reshape(SIZES), AXES)
    everywhere = P(AXES, None)
    by_group = P(("xh", "z", "c"), None)
    return jax.shard_map(
        per_device,
        mesh=chips,
        in_specs=(
            everywhere,
            everywhere,
            P(AXES),
            P(),
            P(),
            everywhere,
            everywhere,
            by_group,
        ),
        out_specs=(everywhere, everywhere, everywhere, by_group),
        check_vma=False,
    )
```

time: 650 us -> 186 us (0.29)
  waiting for transfers between devices: 541 us -> 91.7 us
  matrix products: 53.3 us -> 12.7 us
  starting transfers between devices: 8.22 us -> 40.7 us
  local copies, waits for them, and re-layouts: 0.93 us -> 25.1 us
  blocking collectives: 15.8 us -> 0 us
  between operations: 15.9 us -> 2.29 us
    ppermute x21 -> x5, waiting for transfers between devices: 320 us -> 4.05 us  [swap_cores(): return lax.ppermute(x, 'c', [(0, 1), (1, 0)])]
    all_gather x3 -> x0, waiting for transfers between devices: 147 us -> none  [the longest x1 76.4 us: per_device(): lax.all_gather(text_half, 'grp', axis=0, tiled=True)]
    all_to_all x0 -> x5, waiting for transfers between devices: none -> 87.7 us  [exchange(): return lax.all_to_all(x, axes, 0, 0, tiled=True)]
    psum x1 -> x0, waiting for transfers between devices: 72.6 us -> none  [per_device(): weight_total = lax.psum(weight_share, 'blk')]
    dot_general x18 -> x5, matrix products: 53.3 us -> 12.7 us  [the longest x1 4.67 us: per_device(): jnp.dot(jnp.concatenate([own_columns(heads_mixed_concluding), own_columns...]
    all_to_all x0 -> x5, starting transfers between devices: none -> 40 us  [exchange(): return lax.all_to_all(x, axes, 0, 0, tiled=True)]
    unnamed x1 -> x0, blocking collectives: 15.8 us -> none
    ppermute x21 -> x5, starting transfers between devices: 8.02 us -> 0.67 us  [swap_cores(): return lax.ppermute(x, 'c', [(0, 1), (1, 0)])]
  transfers between devices with their start and end apart: 26 -> 10, of which waited for: 20 -> 6; matrix products, arithmetic and copies ran while one was open for 10% -> 16% of each run, Pallas kernels for 0% -> 0%
where the time goes in v1:
time: 186 us; the launch traced here: 185 us
  waiting for transfers between devices  91.7 us (49%)
  starting transfers between devices  40.7 us (22%)
  local copies, waits for them, and re-layouts  25.1 us (13%)
  other arithmetic  12.9 us (7%)
  matrix products  12.7 us (7%)
  between operations  2.29 us (1%)
    all_to_all x5, waiting for transfers between devices, exchange(): return lax.all_to_all(x, axes, 0, 0, tiled=True)  87.7 us
    all_to_all x5, starting transfers between devices, exchange(): return lax.all_to_all(x, axes, 0, 0, tiled=True)  40 us
    unnamed x24, local copies, waits for them, and re-layouts  5.73 us
    dot_general x1, matrix products, per_device(): jnp.dot(jnp.concatenate([own_columns(heads_mixed_concluding), own_columns...  4.67 us
    reshape x2, local copies, waits for them, and re-layouts, per_device(): weight_share.reshape(2, 8, 2, 24, 4, 384).transpose(4, 0, 2, 1, 3, 5)  4.56 us
    ppermute x5, waiting for transfers between devices, swap_cores(): return lax.ppermute(x, 'c', [(0, 1), (1, 0)])  4.05 us
  transfers between devices with their start and end apart: 10, of which 6 were waited for; matrix products, arithmetic and copies ran while one was open for 16% of the time, Pallas kernels for 0%

profile of v1, /device:TPU:2, one launch (start us, length us, event | category | flops | bytes accessed | tf_op | source)
XLA Modules:
  0.0 185.3 jit_solution(5036233762075617647)
XLA Ops:
  0.7 1.1 multiply_reduce_fusion.2
  1.8 1.0 multiply_convert_fusion
  2.7 0.7 dynamic_slice.12
  3.5 0.8 broadcast_in_dim.19
  4.3 8.5 %all-to-all-start.1 = ((bf16[8,24,1152]{2,1,0:T(8,128)(2,1)}), bf16[8,24,1152]{2,1,0:T(8,128)(2,1)S(1)}, u32[]{:S(2)}, u32[]{:S(2)}) async-start(bf16[8,24,1152]{2,1,0:T(8,128)(2,1)} %broadcast_in_dim.19), calls=%async_computation.1 | async-start | bytes 884736 | tf_op jit(solution)/shard_map/all_to_all | solution.py:30
  12.8 0.7 copy.22
  13.5 0.6 collective-permute-start
  14.5 2.8 %collective-permute-done = bf16[384,1536]{0,1:T(8,128)(2,1)S(1)} collective-permute-done((bf16[384,1536]{0,1:T(8,128)(2,1)S(1)}, bf16[384,1536]{0,1:T(8,128)(2,1)S(1)}, u32[]{:S(2)}, u32[]{:S(2)}) %collective-permute-start) | collective-permute-done | bytes 1179680 | tf_op jit(solution)/shard_map/ppermute | solution.py:26
  17.3 1.0 copy-done.6
  18.3 1.1 constant_dynamic-slice_fusion
  19.4 4.7 %convolution_convert_fusion = bf16[768,1536]{1,0:T(8,128)(2,1)} fusion(bf16[384,1536]{1,0:T(8,128)(2,1)} %collective-permute-done.1, bf16[384,1536]{1,0:T(8,128)(2,1)S(1)} %copy-done.7, bf16[768,384]{1,0:T(8,128)(2,1)S(1)} %bitcast.95, bf16[768,384]{1,0:T(8,128)(2,1)S(1)} %bitcast.94), kind=kOutput, calls=%fused_computation.1 | convolution fusion | flops 1820196864 | bytes 5898240 | tf_op jit(solution)/shard_map/dot_general | solution.py:78
  24.1 4.1 %reshape.206 = bf16[2,8,2,24,4,384]{5,4,3,2,1,0:T(4,128)(2,1)S(1)} reshape(bf16[768,1536]{1,0:T(8,128)(2,1)} %convolution_convert_fusion) | data formatting | bytes 4718592 | tf_op jit(solution)/shard_map/reshape | solution.py:83
  28.3 0.4 copy.24
  28.8 1.9 %pad_maximum_fusion.1 = bf16[16,248,384]{2,1,0:T(8,128)(2,1)} fusion(bf16[16,56,384]{2,1,0:T(8,128)(2,1)S(1)} %broadcast_in_dim.18, bf16[16,192,384]{2,1,0:T(8,128)(2,1)S(1)} %bitcast.78), kind=kLoop, calls=%fused_computation.2 | loop fusion | flops 6094848 | bytes 6094848 | tf_op jit(solution)/shard_map/concatenate | solution.py:89
  30.7 7.5 %all-to-all-start = ((bf16[16,248,384]{2,1,0:T(8,128)(2,1)}), bf16[16,248,384]{2,1,0:T(8,128)(2,1)S(1)}, u32[]{:S(2)}, u32[]{:S(2)}) async-start(bf16[16,248,384]{2,1,0:T(8,128)(2,1)} %pad_maximum_fusion.1), calls=%async_computation | async-start | bytes 6094848 | tf_op jit(solution)/shard_map/all_to_all | solution.py:30
  39.5 0.7 slice.54
  40.2 40.7 %all-to-all-done = bf16[16,248,384]{2,1,0:T(8,128)(2,1)S(1)} async-done(((bf16[16,248,384]{2,1,0:T(8,128)(2,1)}), bf16[16,248,384]{2,1,0:T(8,128)(2,1)S(1)}, u32[]{:S(2)}, u32[]{:S(2)}) %all-to-all-start) | async-done | bytes 3047456 | tf_op jit(solution)/shard_map/all_to_all | solution.py:30
  81.0 0.4 copy.26
  81.4 0.9 copy.34
  82.5 1.6 fusion.14
  84.1 2.3 %convolution_convert_fusion.2 = bf16[256,1152]{1,0:T(8,128)(2,1)} fusion(bf16[256,256]{1,0:T(8,128)(2,1)S(1)} %fusion.14, bf16[128,1152]{1,0:T(8,128)(2,1)} %collective-permute-done.2, bf16[128,1152]{1,0:T(8,128)(2,1)} %bitcast.18), kind=kOutput, calls=%fused_computation.6 | convolution fusion | flops 152469504 | bytes 1310720 | tf_op jit(solution)/shard_map/dot_general | solution.py:108
  86.4 1.9 %reshape_reshape.10 = bf16[16,16,3,384]{3,2,1,0:T(4,128)(2,1)} reshape(bf16[256,1152]{1,0:T(8,128)(2,1)} %convolution_convert_fusion.2) | data formatting | bytes 1179648 | tf_op jit(solution)/shard_map/reshape;reshape | solution.py:39
  88.3 1.2 copy.27
  89.8 1.9 %pad_maximum_fusion.2 = bf16[16,240,384]{2,1,0:T(8,128)(2,1)} fusion(bf16[16,192,384]{2,1,0:T(8,128)(2,1)S(1)} %broadcast_in_dim.42, bf16[16,48,384]{2,1,0:T(8,128)(2,1)S(1)} %bitcast.83), kind=kLoop, calls=%fused_computation.3 | loop fusion | flops 5898240 | bytes 5898240 | tf_op jit(solution)/shard_map/concatenate | solution.py:127
  91.8 8.5 %all-to-all-start.2 = ((bf16[16,240,384]{2,1,0:T(8,128)(2,1)}), bf16[16,240,384]{2,1,0:T(8,128)(2,1)}, u32[]{:S(2)}, u32[]{:S(2)}) async-start(bf16[16,240,384]{2,1,0:T(8,128)(2,1)} %pad_maximum_fusion.2), calls=%async_computation.2 | async-start | bytes 5898240 | tf_op jit(solution)/shard_map/all_to_all | solution.py:30
  100.2 1.4 fusion.32
  101.8 0.3 slice_reduce_fusion
  102.1 1.2 collective-permute-done.3
  103.4 0.8 pad_maximum_fusion.4
  104.2 33.6 %all-to-all-done.2 = bf16[16,240,384]{2,1,0:T(8,128)(2,1)} async-done(((bf16[16,240,384]{2,1,0:T(8,128)(2,1)}), bf16[16,240,384]{2,1,0:T(8,128)(2,1)}, u32[]{:S(2)}, u32[]{:S(2)}) %all-to-all-start.2) | async-done | bytes 2949152 | tf_op jit(solution)/shard_map/all_to_all | solution.py:30
  137.8 7.2 %all-to-all-start.3 = ((bf16[8,24,1152]{2,1,0:T(8,128)(2,1)}), bf16[8,24,1152]{2,1,0:T(8,128)(2,1)S(1)}, u32[]{:S(2)}, u32[]{:S(2)}) async-start(bf16[8,24,1152]{2,1,0:T(8,128)(2,1)} %pad_maximum_fusion.4), calls=%async_computation.3 | async-start | bytes 884736 | tf_op jit(solution)/shard_map/all_to_all | solution.py:30
  144.9 1.9 %slice.64 = bf16[16,192,384]{2,1,0:T(8,128)(2,1)S(1)} slice(bf16[16,240,384]{2,1,0:T(8,128)(2,1)} %all-to-all-done.2), slice={[0:16], [48:240], [0:384]} | slice | bytes 4718592 | tf_op jit(solution)/shard_map/slice | solution.py:134
  146.9 1.8 copy.29
  148.7 2.3 %reshape.221 = bf16[16,48,1536]{2,1,0:T(8,128)(2,1)} reshape(bf16[2,8,2,24,4,384]{5,4,3,2,1,0:T(4,128)(2,1)S(1)} %copy.29) | data formatting | bytes 4718592 | tf_op jit(solution)/shard_map/reshape | solution.py:135
  151.1 8.3 %all-to-all-done.3 = bf16[8,24,1152]{2,1,0:T(8,128)(2,1)S(1)} async-done(((bf16[8,24,1152]{2,1,0:T(8,128)(2,1)}), bf16[8,24,1152]{2,1,0:T(8,128)(2,1)S(1)}, u32[]{:S(2)}, u32[]{:S(2)}) %all-to-all-start.3) | async-done | bytes 442400 | tf_op jit(solution)/shard_map/all_to_all | solution.py:30
  159.4 0.7 broadcast_in_dim.43
  160.1 8.4 %all-to-all-start.4 = ((f32[8,24,384]{2,1,0:T(8,128)}), f32[8,24,384]{2,1,0:T(8,128)S(1)}, u32[]{:S(2)}, u32[]{:S(2)}) async-start(f32[8,24,384]{2,1,0:T(8,128)} %broadcast_in_dim.43), calls=%async_computation.4 | async-start | bytes 589824 | tf_op jit(solution)/shard_map/all_to_all | solution.py:30
  168.7 0.7 subtract_multiply_fusion
  169.4 5.1 %all-to-all-done.4 = f32[8,24,384]{2,1,0:T(8,128)S(1)} async-done(((f32[8,24,384]{2,1,0:T(8,128)}), f32[8,24,384]{2,1,0:T(8,128)S(1)}, u32[]{:S(2)}, u32[]{:S(2)}) %all-to-all-start.4) | async-done | bytes 294944 | tf_op jit(solution)/shard_map/all_to_all | solution.py:30
  174.6 0.7 copy.35
  175.4 1.2 convert_reduce_fusion
  176.7 0.7 subtract_multiply_fusion.1
  177.5 2.0 %select_bitcast_fusion.1 = (bf16[16,1,48,1536]{3,2,0,1:T(8,128)(2,1)S(1)}, bf16[16,1,48,1536]{3,2,0,1:T(8,128)(2,1)S(1)}) fusion(bf16[16,48,1536]{2,1,0:T(8,128)(2,1)S(1)} %copy-done, bf16[16,48,1536]{2,1,0:T(8,128)(2,1)} %collective-permute-done.4, pred[]{:T(512)S(6)} %eq.25), kind=kLoop, calls=%fused_computation.12 | loop fusion | flops 2359296 | bytes 9437185 | tf_op jit(solution)/shard_map/stack | solution.py:137
  179.4 0.4 pad_maximum_fusion
  179.9 0.4 copy.30
  180.3 0.8 copy-done.8
  181.2 2.7 %fusion = bf16[384,1536]{0,1:T(8,128)(2,1)S(1)} fusion(bf16[1536,1536]{1,0:T(8,128)(2,1)S(1)} %bitcast.79, bf16[384,1536]{1,0:T(8,128)(2,1)S(1)} %copy-done.8), kind=kOutput, calls=%fused_computation.5 | convolution fusion | flops 1812529152 | bytes 7077888 | tf_op jit(solution)/shard_map/dot_general | solution.py:140
  183.8 1.5 copy.32
  (54 shorter events, 1.7 us)
Async XLA Ops:
  0.6 12.1 %copy-start.5 = (bf16[384,1536]{1,0:T(8,128)(2,1)S(1)}, bf16[384,1536]{1,0:T(8,128)(2,1)}, u32[]{:S(2)}) copy-start(bf16[384,1536]{1,0:T(8,128)(2,1)} %param.13) | copy-start | bytes 3538948
  0.6 13.4 %copy-start.3 = (f32[16,1152]{1,0:T(8,128)S(1)}, f32[16,1152]{1,0:T(8,128)}, u32[]{:S(2)}) copy-start(f32[16,1152]{1,0:T(8,128)} %param.8) | copy-start | bytes 221188
  0.7 13.7 %copy-start.9 = (s32[16]{0:T(128)S(1)}, s32[16]{0:T(128)}, u32[]{:S(2)}) copy-start(s32[16]{0:T(128)} %param.10) | copy-start | bytes 196
  4.3 26.4 %all-to-all-start.1 = ((bf16[8,24,1152]{2,1,0:T(8,128)(2,1)}), bf16[8,24,1152]{2,1,0:T(8,128)(2,1)S(1)}, u32[]{:S(2)}, u32[]{:S(2)}) async-start(bf16[8,24,1152]{2,1,0:T(8,128)(2,1)} %broadcast_in_dim.19), calls=%async_computation.1 | async-start | bytes 884736 | tf_op jit(solution)/shard_map/all_to_all | solution.py:30
  12.7 6.7 %collective-permute-start.1 = (bf16[384,1536]{1,0:T(8,128)(2,1)}, bf16[384,1536]{1,0:T(8,128)(2,1)}, u32[]{:S(2)}, u32[]{:S(2)}) collective-permute-start(bf16[384,1536]{1,0:T(8,128)(2,1)} %param.14), channel_id=1, source_target_pairs={{0,1},{1,0},{2,3},{3,2},{4,5},{5,4},{6,7},{7,6},{8,9},{9,8},{10,11... | collective-permute-start | bytes 3538952 | tf_op jit(solution)/shard_map/ppermute | solution.py:26
  13.5 3.8 %collective-permute-start = (bf16[384,1536]{0,1:T(8,128)(2,1)S(1)}, bf16[384,1536]{0,1:T(8,128)(2,1)S(1)}, u32[]{:S(2)}, u32[]{:S(2)}) collective-permute-start(bf16[384,1536]{0,1:T(8,128)(2,1)S(1)} %copy.22), channel_id=1, source_target_pairs={{0,1},{1,0},{2,3},{3,2},{4,5},{5,4},{6,7},{7,6},{8,9},{9,8},{10,11... | collective-permute-start | bytes 3538952 | tf_op jit(solution)/shard_map/ppermute | solution.py:26
  14.4 5.0 %copy-start.7 = (bf16[384,1536]{1,0:T(8,128)(2,1)S(1)}, bf16[384,1536]{1,0:T(8,128)(2,1)}, u32[]{:S(2)}) copy-start(bf16[384,1536]{1,0:T(8,128)(2,1)} %param.14) | copy-start | bytes 3538948
  17.3 1.0 copy-start.6
  30.7 9.5 %copy-start.1 = (bf16[8,24,1152]{2,1,0:T(8,128)(2,1)}, bf16[8,24,1152]{2,1,0:T(8,128)(2,1)S(1)}, u32[]{:S(2)}) copy-start(bf16[8,24,1152]{2,1,0:T(8,128)(2,1)S(1)} %all-to-all-done.1) | copy-start | bytes 1327108
  30.7 50.3 %all-to-all-start = ((bf16[16,248,384]{2,1,0:T(8,128)(2,1)}), bf16[16,248,384]{2,1,0:T(8,128)(2,1)S(1)}, u32[]{:S(2)}, u32[]{:S(2)}) async-start(bf16[16,248,384]{2,1,0:T(8,128)(2,1)} %pad_maximum_fusion.1), calls=%async_computation | async-start | bytes 6094848 | tf_op jit(solution)/shard_map/all_to_all | solution.py:30
  40.2 42.2 %collective-permute-start.2 = (bf16[128,1152]{1,0:T(8,128)(2,1)}, bf16[128,1152]{1,0:T(8,128)(2,1)}, u32[]{:S(2)}, u32[]{:S(2)}) collective-permute-start(bf16[128,1152]{1,0:T(8,128)(2,1)} %bitcast.18), channel_id=1, source_target_pairs={{0,1},{1,0},{2,3},{3,2},{4,5},{5,4},{6,7},{7,6},{8,9},{9,8},{10,11... | collective-permute-start | bytes 884744 | tf_op jit(solution)/shard_map/ppermute | solution.py:26
  84.1 5.4 %slice-start = ((bf16[8,24,1152]{2,1,0:T(8,128)(2,1)}), bf16[8,8,1152]{2,1,0:T(8,128)(2,1)S(1)}, s32[]{:S(2)}) async-start(bf16[8,24,1152]{2,1,0:T(8,128)(2,1)} %copy-done.1), calls=%async_computation.5 | async-start | bytes 294912 | tf_op jit(solution)/shard_map/slice | solution.py:71
  91.8 46.0 %all-to-all-start.2 = ((bf16[16,240,384]{2,1,0:T(8,128)(2,1)}), bf16[16,240,384]{2,1,0:T(8,128)(2,1)}, u32[]{:S(2)}, u32[]{:S(2)}) async-start(bf16[16,240,384]{2,1,0:T(8,128)(2,1)} %pad_maximum_fusion.2), calls=%async_computation.2 | async-start | bytes 5898240 | tf_op jit(solution)/shard_map/all_to_all | solution.py:30
  101.7 1.7 collective-permute-start.3
  137.8 21.5 %all-to-all-start.3 = ((bf16[8,24,1152]{2,1,0:T(8,128)(2,1)}), bf16[8,24,1152]{2,1,0:T(8,128)(2,1)S(1)}, u32[]{:S(2)}, u32[]{:S(2)}) async-start(bf16[8,24,1152]{2,1,0:T(8,128)(2,1)} %pad_maximum_fusion.4), calls=%async_computation.3 | async-start | bytes 884736 | tf_op jit(solution)/shard_map/all_to_all | solution.py:30
  148.7 19.9 %copy-start.2 = (f32[16,1152]{1,0:T(8,128)S(1)}, f32[16,1152]{1,0:T(8,128)}, u32[]{:S(2)}) copy-start(f32[16,1152]{1,0:T(8,128)} %param.9) | copy-start | bytes 221188
  151.0 25.5 %copy-start.4 = (f32[16,1152]{1,0:T(8,128)S(1)}, f32[16,1152]{1,0:T(8,128)}, u32[]{:S(2)}) copy-start(f32[16,1152]{1,0:T(8,128)} %param.8) | copy-start | bytes 221188
  151.0 26.4 %copy-start = (bf16[16,48,1536]{2,1,0:T(8,128)(2,1)S(1)}, bf16[16,48,1536]{2,1,0:T(8,128)(2,1)}, u32[]{:S(2)}) copy-start(bf16[16,48,1536]{2,1,0:T(8,128)(2,1)} %reshape.221) | copy-start | bytes 7077892
  151.0 26.4 %collective-permute-start.4 = (bf16[16,48,1536]{2,1,0:T(8,128)(2,1)}, bf16[16,48,1536]{2,1,0:T(8,128)(2,1)}, u32[]{:S(2)}, u32[]{:S(2)}) collective-permute-start(bf16[16,48,1536]{2,1,0:T(8,128)(2,1)} %reshape.221), channel_id=1, source_target_pairs={{0,1},{1,0},{2,3},{3,2},{4,5},{5,4},{6,7},{7,6},{8,9},{9,8},{10,11... | collective-permute-start | bytes 7077896 | tf_op jit(solution)/shard_map/ppermute | solution.py:26
  160.1 14.4 %all-to-all-start.4 = ((f32[8,24,384]{2,1,0:T(8,128)}), f32[8,24,384]{2,1,0:T(8,128)S(1)}, u32[]{:S(2)}, u32[]{:S(2)}) async-start(f32[8,24,384]{2,1,0:T(8,128)} %broadcast_in_dim.43), calls=%async_computation.4 | async-start | bytes 589824 | tf_op jit(solution)/shard_map/all_to_all | solution.py:30
  179.9 1.3 copy-start.8

commit v2 on v1

v2 whole, which is shorter than its diff:
```python
import math

import jax
import jax.numpy as jnp
from jax import lax
from jax.sharding import Mesh, PartitionSpec as P

stability_floor = 1e-06

AXES = ("xl", "y", "xh", "z", "c")
SIZES = (2, 4, 2, 8, 2)
ROW = (("xl", "xh"), (0, 2, 1, 3))
COLUMN = ("y", (0, 1, 2, 3))


def unit_rows(raw):
    row_scale = lax.rsqrt(jnp.sum(raw * raw, axis=1, keepdims=True) + stability_floor)
    return (raw * row_scale, row_scale)


def back_through_norm(normed, row_scale, row_grad):
    along_unit = jnp.sum(normed * row_grad, axis=1, keepdims=True)
    return (row_grad - normed * along_unit) * row_scale


def swap_cores(x):
    return lax.ppermute(x, "c", [(0, 1), (1, 0)])


def turn(x, ring, by):
    axes, at = ring
    return lax.ppermute(x, axes, [(at[i], at[(i + by) % 4]) for i in range(4)])


def swap_halves(x):
    axes, at = ROW
    return lax.ppermute(x, axes, [(at[i], at[3 - i]) for i in range(4)])


def exchange(x, axes):
    return lax.all_to_all(x, axes, 0, 0, tiled=True)


def to_everyone(x, count):
    return jnp.broadcast_to(x[None], (count,) + x.shape)


def fold(x):
    lead, rows = x.shape[:-2], x.shape[-2]
    return jnp.swapaxes(x.reshape(lead + (rows, 3, 384)), -3, -2).reshape(lead + (3 * rows, 384))


def unfold(x):
    lead, rows = x.shape[:-2], x.shape[-2] // 3
    return jnp.swapaxes(x.reshape(lead + (3, rows, 384)), -3, -2).reshape(lead + (rows, 1152))


def gathered(x, ring):
    return [x] + [turn(x, ring, k) for k in (1, 2, 3)]


def summed_back(parts, ring):
    total = parts[0].astype(jnp.float32)
    for k in (1, 2, 3):
        total = total + turn(parts[k], ring, -k).astype(jnp.float32)
    return total


def per_device(
    picture_vectors_prenorm,
    caption_vectors_prenorm,
    matched_caption_ids,
    sharpness_coefficient,
    additive_offset_term,
    heads_mixed_concluding,
    dense_result_adjoint,
    dense_mapping_matrix,
):
    f32, bf16 = jnp.float32, jnp.bfloat16
    xl, y, xh, c = (lax.axis_index(name) for name in ("xl", "y", "xh", "c"))

    def columns_of(core):
        blocks = heads_mixed_concluding.T.reshape(16, 2, 48, 384)
        return lax.dynamic_index_in_dim(blocks, core, 1, keepdims=False).reshape(768, 384)

    other_adjoint = swap_cores(dense_result_adjoint)
    other_tokens = swap_cores(columns_of(1 - c))

    image_units, image_scale = unit_rows(picture_vectors_prenorm)
    text_units, text_scale = unit_rows(caption_vectors_prenorm)
    image_half = image_units.astype(bf16)
    text_half = text_units.astype(bf16)

    own_piece = lax.dynamic_slice(dense_mapping_matrix, (0, y * 384), (48, 384))
    sent = jnp.concatenate([fold(text_half), own_piece], axis=0)
    along_z = exchange(to_everyone(sent, 8), "z")
    text_here = unfold(along_z[:, :48]).reshape(128, 1152)
    mapping_piece = along_z[:, 48:]
    text_block = jnp.concatenate([text_here, swap_cores(text_here)], axis=0)

    id_parts = jnp.stack([matched_caption_ids // 64, matched_caption_ids % 64]).astype(bf16)
    id_rows = jnp.pad(id_parts, ((0, 6), (0, 1152 - 16)))
    image_sent = jnp.concatenate([image_half, id_rows], axis=0)
    column = jnp.stack(gathered(image_sent, COLUMN))
    image_sent = jnp.concatenate(gathered(column, ROW))
    image_block = image_sent[:, :16].reshape(256, 1152)
    ids = image_sent[:, 16:18, :16].astype(jnp.int32)
    ids = (ids[:, 0] * 64 + ids[:, 1]).reshape(256, 1)

    weight_share = jnp.dot(
        jnp.concatenate([columns_of(c), other_tokens], axis=1),
        jnp.concatenate([dense_result_adjoint, other_adjoint], axis=0),
        preferred_element_type=f32,
    ).astype(bf16)
    weight_share = weight_share.reshape(2, 8, 48, 1536)

    def column_block(share, k):
        return lax.dynamic_slice_in_dim(share, ((y + 4 - k) % 4) * 384, 384, axis=-1)

    def half_of(share, which):
        return lax.dynamic_index_in_dim(share, which, 0, keepdims=False)

    first = summed_back([column_block(weight_share[:, :4], k) for k in range(4)], COLUMN)
    first = half_of(first, xh) + swap_halves(half_of(first, 1 - xh).astype(bf16)).astype(f32)
    second = weight_share[:, 4:]
    second = half_of(second, xh).astype(f32) + swap_halves(half_of(second, 1 - xh)).astype(f32)
    second = second.astype(bf16)
    second = summed_back([column_block(second, k) for k in range(4)], COLUMN)
    weight_plane = jnp.concatenate([first, second], axis=0).astype(bf16)

    sharpness = sharpness_coefficient[0]
    offset = additive_offset_term[0]
    plane_first = ((xl * 4 + y) * 2 + xh) * 256
    row = lax.broadcasted_iota(jnp.int32, (1, 256), 1)
    core = jnp.where(row < 128, c, 1 - c)
    row = row % 128
    text_index = plane_first + ((row // 16) * 2 + core) * 16 + row % 16
    dots = lax.dot_general(
        image_block, text_block, (((1,), (1,)), ((), ())), preferred_element_type=f32
    )
    labels = (ids == text_index).astype(f32)
    pair_weights = (sharpness * (jax.nn.sigmoid(sharpness * dots + offset) - labels)).astype(bf16)
    image_part = jnp.dot(pair_weights, text_block, preferred_element_type=f32).astype(bf16)
    text_part = lax.dot_general(
        pair_weights, image_block, (((0,), (0,)), ((), ())), preferred_element_type=f32
    )
    text_part = text_part[:128] + swap_cores(text_part[128:].astype(bf16)).astype(f32)

    image_part = image_part.reshape(4, 64, 1152)
    image_part = summed_back([image_part[k] for k in range(4)], ROW).astype(bf16)
    image_part = image_part.reshape(4, 16, 1152)
    image_part = summed_back([image_part[k] for k in range(4)], COLUMN)
    image_grad = back_through_norm(image_units, image_scale, image_part)

    back = jnp.concatenate([fold(text_part.astype(bf16).reshape(8, 16, 1152)), weight_plane], 1)
    back = jnp.sum(exchange(back, "z").astype(f32), axis=0)
    text_grad = back_through_norm(text_units, text_scale, unfold(back[:48]))
    weight_piece = back[48:] * (1.0 / math.sqrt(98304))
    pieces = exchange(to_everyone(weight_piece.astype(bf16), 8), ("xl", "y"))
    weight_grad = jnp.sum(pieces.reshape(2, 4, 48, 384).astype(f32), axis=0)
    weight_grad = weight_grad.transpose(1, 0, 2).reshape(48, 1536)

    def both_halves(x):
        other = swap_halves(x)
        low = xh == 0
        return jnp.stack([jnp.where(low, x, other), jnp.where(low, other, x)])

    first = jnp.concatenate(gathered(both_halves(mapping_piece[:4]), COLUMN), axis=-1)
    second = jnp.concatenate(gathered(mapping_piece[4:], COLUMN), axis=-1)
    second = both_halves(second)

    def both_cores(x):
        other = swap_cores(x)
        low = c == 0
        return jnp.stack([jnp.where(low, x, other), jnp.where(low, other, x)], axis=2)

    mapping = jnp.concatenate([both_cores(first), both_cores(second)], axis=1).reshape(1536, 1536)
    adjoint = jnp.concatenate([column_block(dense_result_adjoint, k) for k in range(4)], axis=1)
    attn_grad = lax.dot_general(
        adjoint, mapping, (((1,), (1,)), ((), ())), preferred_element_type=f32
    ).astype(bf16)
    return (image_grad, text_grad, attn_grad, weight_grad)


def solution(mesh):
    chips = Mesh(mesh.devices.reshape(SIZES), AXES)
    everywhere = P(AXES, None)
    by_group = P(("xh", "z", "c"), None)
    return jax.shard_map(
        per_device,
        mesh=chips,
        in_specs=(
            everywhere,
            everywhere,
            P(AXES),
            P(),
            P(),
            everywhere,
            everywhere,
            by_group,
        ),
        out_specs=(everywhere, everywhere, everywhere, by_group),
        check_vma=False,
    )
```

time: 186 us -> 150 us (0.81)
  waiting for transfers between devices: 91.7 us -> 38.7 us
  starting transfers between devices: 40.7 us -> 70.6 us
  local copies, waits for them, and re-layouts: 25.1 us -> 9.89 us
  other arithmetic: 12.9 us -> 19.4 us
  matrix products: 12.7 us -> 8 us
    all_to_all x5 -> x3, waiting for transfers between devices: 87.7 us -> 10.5 us  [exchange(): return lax.all_to_all(x, axes, 0, 0, tiled=True)]
    ppermute x0 -> x28, starting transfers between devices: none -> 47.5 us  [the longest x24 42.6 us: turn(): return lax.ppermute(x, axes, [(at[i], at[(i + by) % 4]) for i in range(4)])]
    ppermute x0 -> x28, waiting for transfers between devices: none -> 28.2 us  [the longest x24 22 us: turn(): return lax.ppermute(x, axes, [(at[i], at[(i + by) % 4]) for i in range(4)])]
    all_to_all x5 -> x3, starting transfers between devices: 40 us -> 22.3 us  [exchange(): return lax.all_to_all(x, axes, 0, 0, tiled=True)]
    reshape x3 -> x1, local copies, waits for them, and re-layouts: 6.9 us -> 0.74 us  [per_device(): weight_grad = weight_grad.transpose(1, 0, 2).reshape(48, 1536)]
    another operation x2 -> x10, other arithmetic: 2.41 us -> 7.86 us  [the longest x2 4.33 us: both_cores(): jnp.stack([jnp.where(low, x, other), jnp.where(low, other, x)], axis=2)]
    ppermute x5 -> x6, waiting for transfers between devices: 4.05 us -> 0.02 us  [swap_cores(): return lax.ppermute(x, 'c', [(0, 1), (1, 0)])]
    unnamed x24 -> x52, local copies, waits for them, and re-layouts: 5.73 us -> 2.16 us
  transfers between devices with their start and end apart: 10 -> 37, of which waited for: 6 -> 16; matrix products, arithmetic and copies ran while one was open for 16% -> 22% of each run, Pallas kernels for 0% -> 0%
where the time goes in v2:
time: 150 us; the launch traced here: 149 us
  starting transfers between devices  70.6 us (47%)
  waiting for transfers between devices  38.7 us (26%)
  other arithmetic  19.4 us (13%)
  local copies, waits for them, and re-layouts  9.89 us (7%)
  matrix products  8 us (5%)
  between operations  2.56 us (2%)
    ppermute x24, starting transfers between devices, turn(): return lax.ppermute(x, axes, [(at[i], at[(i + by) % 4]) for i in range(4)])  42.6 us
    all_to_all x3, starting transfers between devices, exchange(): return lax.all_to_all(x, axes, 0, 0, tiled=True)  22.3 us
    ppermute x24, waiting for transfers between devices, turn(): return lax.ppermute(x, axes, [(at[i], at[(i + by) % 4]) for i in range(4)])  22 us
    all_to_all x3, waiting for transfers between devices, exchange(): return lax.all_to_all(x, axes, 0, 0, tiled=True)  10.5 us
    ppermute x4, waiting for transfers between devices, swap_halves(): return lax.ppermute(x, axes, [(at[i], at[3 - i]) for i in range(4)])  6.11 us
    ppermute x4, starting transfers between devices, swap_halves(): return lax.ppermute(x, axes, [(at[i], at[3 - i]) for i in range(4)])  4.89 us
    another operation x2, other arithmetic, both_cores(): jnp.stack([jnp.where(low, x, other), jnp.where(low, other, x)], axis=2)  4.33 us
    dot_general x1, matrix products, per_device(): jnp.dot(jnp.concatenate([columns_of(c), other_tokens], axis=1), jnp.conca...  3.79 us
  transfers between devices with their start and end apart: 37, of which 16 were waited for; matrix products, arithmetic and copies ran while one was open for 22% of the time, Pallas kernels for 0%

profile of v2, /device:TPU:2, one launch (start us, length us, event | category | flops | bytes accessed | tf_op | source)
XLA Modules:
  0.0 149.1 jit_solution(5043625439502647)
XLA Ops:
  0.6 1.0 multiply_reduce_fusion.3
  3.4 1.7 %collective-permute-start = (bf16[24,1152]{1,0:T(8,128)(2,1)S(1)}, bf16[24,1152]{1,0:T(8,128)(2,1)S(1)}, u32[]{:S(2)}, u32[]{:S(2)}) collective-permute-start(bf16[24,1152]{1,0:T(8,128)(2,1)S(1)} %get-tuple-element.36), channel_id=1, source_target_pairs={{0,32},{32,64},{64,96},{96,0},{1,33},{33,65},{65,97},{97,1},{2,34}... | collective-permute-start | bytes 165896 | tf_op jit(solution)/shard_map/ppermute | solution.py:32
  5.0 2.9 %collective-permute-start.1 = (bf16[24,1152]{1,0:T(8,128)(2,1)S(1)}, bf16[24,1152]{1,0:T(8,128)(2,1)S(1)}, u32[]{:S(2)}, u32[]{:S(2)}) collective-permute-start(bf16[24,1152]{1,0:T(8,128)(2,1)S(1)} %get-tuple-element.36), channel_id=1, source_target_pairs={{0,64},{32,96},{64,0},{96,32},{1,65},{33,97},{65,1},{97,33},{2,66}... | collective-permute-start | bytes 165896 | tf_op jit(solution)/shard_map/ppermute | solution.py:32
  7.9 1.3 collective-permute-start.2
  9.3 1.0 multiply_reduce_fusion.2
  10.3 1.1 multiply_convert_fusion
  12.3 8.5 %all-to-all-start = ((bf16[8,96,384]{2,1,0:T(8,128)(2,1)}), bf16[8,96,384]{2,1,0:T(8,128)(2,1)S(1)}, u32[]{:S(2)}, u32[]{:S(2)}) async-start(bf16[8,96,384]{2,1,0:T(8,128)(2,1)} %broadcast_in_dim.12), calls=%async_computation | async-start | bytes 1179648 | tf_op jit(solution)/shard_map/all_to_all | solution.py:41
  21.5 1.2 constant_dynamic-slice_fusion.11
  23.2 2.3 %constant_dynamic-slice_fusion.3 = (bf16[384,384]{1,0:T(8,128)(2,1)}, bf16[384,384]{1,0:T(8,128)(2,1)}, bf16[384,384]{1,0:T(8,128)(2,1)}, bf16[384,384]{1,0:T(8,128)(2,1)}) fusion(bf16[384,1536]{1,0:T(8,128)(2,1)} %param.14, s32[]{:T(128)S(6)} %select_n.181, s32[]{:T(128)S(6)} %select_n.183, s32[]{:T(128)S(6)} %select_n.187, s32[]{:T(128)S(6)} %select_n.185), kind=kLoop, calls=%fused_computation.93 | loop fusion | bytes 2359312 | tf_op jit(solution)/shard_map/dynamic_slice | solution.py:118
  26.9 1.6 %collective-permute-start.3 = (bf16[4,24,1152]{2,1,0:T(8,128)(2,1)S(1)}, bf16[4,24,1152]{2,1,0:T(8,128)(2,1)S(1)}, u32[]{:S(2)}, u32[]{:S(2)}) collective-permute-start(bf16[4,24,1152]{2,1,0:T(8,128)(2,1)S(1)} %pad_maximum_fusion.5), channel_id=1, source_target_pairs={{0,128},{128,16},{16,144},{144,0},{1,129},{129,17},{17,145},{145,1... | collective-permute-start | bytes 663560 | tf_op jit(solution)/shard_map/ppermute | solution.py:32
  28.5 1.1 collective-permute-start.4
  29.6 2.2 %collective-permute-start.5 = (bf16[4,24,1152]{2,1,0:T(8,128)(2,1)S(1)}, bf16[4,24,1152]{2,1,0:T(8,128)(2,1)S(1)}, u32[]{:S(2)}, u32[]{:S(2)}) collective-permute-start(bf16[4,24,1152]{2,1,0:T(8,128)(2,1)S(1)} %pad_maximum_fusion.5), channel_id=1, source_target_pairs={{0,144},{128,0},{16,128},{144,16},{1,145},{129,1},{17,129},{145,17... | collective-permute-start | bytes 663560 | tf_op jit(solution)/shard_map/ppermute | solution.py:32
  31.8 3.5 %collective-permute-done.3 = bf16[4,24,1152]{2,1,0:T(8,128)(2,1)S(1)} collective-permute-done((bf16[4,24,1152]{2,1,0:T(8,128)(2,1)S(1)}, bf16[4,24,1152]{2,1,0:T(8,128)(2,1)S(1)}, u32[]{:S(2)}, u32[]{:S(2)}) %collective-permute-start.3) | collective-permute-done | bytes 221216 | tf_op jit(solution)/shard_map/ppermute | solution.py:32
  35.3 3.0 %collective-permute-done.4 = bf16[4,24,1152]{2,1,0:T(8,128)(2,1)S(1)} collective-permute-done((bf16[4,24,1152]{2,1,0:T(8,128)(2,1)S(1)}, bf16[4,24,1152]{2,1,0:T(8,128)(2,1)S(1)}, u32[]{:S(2)}, u32[]{:S(2)}) %collective-permute-start.4) | collective-permute-done | bytes 221216 | tf_op jit(solution)/shard_map/ppermute | solution.py:32
  38.3 2.9 %collective-permute-done.5 = bf16[4,24,1152]{2,1,0:T(8,128)(2,1)S(1)} collective-permute-done((bf16[4,24,1152]{2,1,0:T(8,128)(2,1)S(1)}, bf16[4,24,1152]{2,1,0:T(8,128)(2,1)S(1)}, u32[]{:S(2)}, u32[]{:S(2)}) %collective-permute-start.5) | collective-permute-done | bytes 221216 | tf_op jit(solution)/shard_map/ppermute | solution.py:32
  41.8 1.4 collective-permute-start.24
  43.2 4.9 %collective-permute-done.24 = bf16[4,48,384]{2,1,0:T(8,128)(2,1)S(1)} collective-permute-done((bf16[4,48,384]{2,1,0:T(8,128)(2,1)S(1)}, bf16[4,48,384]{2,1,0:T(8,128)(2,1)S(1)}, u32[]{:S(2)}, u32[]{:S(2)}) %collective-permute-start.24) | collective-permute-done | bytes 147488 | tf_op jit(solution)/shard_map/ppermute | solution.py:37
  48.3 2.7 %collective-permute-start.30 = (bf16[4,48,384]{2,1,0:T(8,128)(2,1)S(1)}, bf16[4,48,384]{2,1,0:T(8,128)(2,1)S(1)}, u32[]{:S(2)}, u32[]{:S(2)}) collective-permute-start(bf16[4,48,384]{2,1,0:T(8,128)(2,1)S(1)} %get-tuple-element.23), channel_id=1, source_target_pairs={{0,64},{32,96},{64,0},{96,32},{1,65},{33,97},{65,1},{97,33},{2,66}... | collective-permute-start | bytes 442376 | tf_op jit(solution)/shard_map/ppermute | solution.py:32
  51.1 3.2 %collective-permute-start.27 = (bf16[2,4,48,384]{3,2,1,0:T(8,128)(2,1)S(1)}, bf16[2,4,48,384]{3,2,1,0:T(8,128)(2,1)S(1)}, u32[]{:S(2)}, u32[]{:S(2)}) collective-permute-start(bf16[2,4,48,384]{3,2,1,0:T(8,128)(2,1)S(1)} %pad_maximum_fusion.4), channel_id=1, source_target_pairs={{0,96},{32,0},{64,32},{96,64},{1,97},{33,1},{65,33},{97,65},{2,98}... | collective-permute-start | bytes 884744 | tf_op jit(solution)/shard_map/ppermute | solution.py:32
  54.4 3.8 %convolution_convert_fusion = bf16[768,1536]{1,0:T(8,128)(2,1)S(1)} fusion(bf16[384,1536]{1,0:T(8,128)(2,1)} %collective-permute-done.15, bf16[384,1536]{1,0:T(8,128)(2,1)} %param.14, bf16[768,384]{1,0:T(8,128)(2,1)} %collective-permute-done.14, bf16[768,384]{1,0:T(8,128)(2,1)S(1)} %bitcast.95), kind=kOutput, calls=%fused_computation.1 | convolution fusion | flops 1820196864 | bytes 5898240 | tf_op jit(solution)/shard_map/dot_general | solution.py:110
  61.5 1.4 collective-permute-start.9
  62.8 2.7 %collective-permute-start.8 = (bf16[64,1152]{1,0:T(8,128)(2,1)S(1)}, bf16[64,1152]{1,0:T(8,128)(2,1)S(1)}, u32[]{:S(2)}, u32[]{:S(2)}) collective-permute-start(bf16[64,1152]{1,0:T(8,128)(2,1)S(1)} %get-tuple-element.29), channel_id=1, source_target_pairs={{0,16},{128,144},{16,0},{144,128},{1,17},{129,145},{17,1},{145,129... | collective-permute-start | bytes 442376 | tf_op jit(solution)/shard_map/ppermute | solution.py:32
  65.5 1.6 %collective-permute-start.7 = (bf16[64,1152]{1,0:T(8,128)(2,1)S(1)}, bf16[64,1152]{1,0:T(8,128)(2,1)S(1)}, u32[]{:S(2)}, u32[]{:S(2)}) collective-permute-start(bf16[64,1152]{1,0:T(8,128)(2,1)S(1)} %get-tuple-element.27), channel_id=1, source_target_pairs={{0,144},{128,0},{16,128},{144,16},{1,145},{129,1},{17,129},{145,17... | collective-permute-start | bytes 442376 | tf_op jit(solution)/shard_map/ppermute | solution.py:32
  67.6 1.5 %collective-permute-start.25 = (bf16[2,4,48,384]{3,2,1,0:T(8,128)(2,1)S(1)}, bf16[2,4,48,384]{3,2,1,0:T(8,128)(2,1)S(1)}, u32[]{:S(2)}, u32[]{:S(2)}) collective-permute-start(bf16[2,4,48,384]{3,2,1,0:T(8,128)(2,1)S(1)} %pad_maximum_fusion.4), channel_id=1, source_target_pairs={{0,32},{32,64},{64,96},{96,0},{1,33},{33,65},{65,97},{97,1},{2,34}... | collective-permute-start | bytes 884744 | tf_op jit(solution)/shard_map/ppermute | solution.py:32
  69.1 1.0 collective-permute-done.8
  70.1 1.1 collective-permute-start.18
  71.6 3.1 %collective-permute-start.17 = (bf16[2,4,48,384]{3,2,1,0:T(8,128)(2,1)S(1)}, bf16[2,4,48,384]{3,2,1,0:T(8,128)(2,1)S(1)}, u32[]{:S(2)}, u32[]{:S(2)}) collective-permute-start(bf16[2,4,48,384]{3,2,1,0:T(8,128)(2,1)S(1)} %get-tuple-element.18), channel_id=1, source_target_pairs={{0,64},{32,96},{64,0},{96,32},{1,65},{33,97},{65,1},{97,33},{2,66}... | collective-permute-start | bytes 884744 | tf_op jit(solution)/shard_map/ppermute | solution.py:32
  74.7 1.2 collective-permute-start.16
  75.9 2.1 %collective-permute-start.20 = (bf16[4,48,1536]{2,1,0:T(8,128)(2,1)}, bf16[4,48,1536]{2,1,0:T(8,128)(2,1)}, u32[]{:S(2)}, u32[]{:S(2)}) collective-permute-start(bf16[4,48,1536]{2,1,0:T(8,128)(2,1)} %dynamic-slice_bitcast_fusion), channel_id=1, source_target_pairs={{0,144},{128,16},{16,128},{144,0},{1,145},{129,17},{17,129},{145,1... | collective-permute-start | bytes 1769480 | tf_op jit(solution)/shard_map/ppermute | solution.py:37
  79.3 1.2 pad_maximum_fusion.1
  80.5 5.1 %collective-permute-done.18 = bf16[2,4,48,384]{3,2,1,0:T(8,128)(2,1)S(1)} collective-permute-done((bf16[2,4,48,384]{3,2,1,0:T(8,128)(2,1)S(1)}, bf16[2,4,48,384]{3,2,1,0:T(8,128)(2,1)S(1)}, u32[]{:S(2)}, u32[]{:S(2)}) %collective-permute-start.18) | collective-permute-done | bytes 294944 | tf_op jit(solution)/shard_map/ppermute | solution.py:32
  85.6 2.8 %collective-permute-start.12 = (bf16[16,1152]{1,0:T(8,128)(2,1)S(1)}, bf16[16,1152]{1,0:T(8,128)(2,1)S(1)}, u32[]{:S(2)}, u32[]{:S(2)}) collective-permute-start(bf16[16,1152]{1,0:T(8,128)(2,1)S(1)} %get-tuple-element.33), channel_id=1, source_target_pairs={{0,32},{32,64},{64,96},{96,0},{1,33},{33,65},{65,97},{97,1},{2,34}... | collective-permute-start | bytes 110600 | tf_op jit(solution)/shard_map/ppermute | solution.py:32
  88.7 2.1 %collective-permute-start.11 = (bf16[16,1152]{1,0:T(8,128)(2,1)S(1)}, bf16[16,1152]{1,0:T(8,128)(2,1)S(1)}, u32[]{:S(2)}, u32[]{:S(2)}) collective-permute-start(bf16[16,1152]{1,0:T(8,128)(2,1)S(1)} %get-tuple-element.34), channel_id=1, source_target_pairs={{0,64},{32,96},{64,0},{96,32},{1,65},{33,97},{65,1},{97,33},{2,66}... | collective-permute-start | bytes 110600 | tf_op jit(solution)/shard_map/ppermute | solution.py:32
  90.8 2.6 %collective-permute-start.10 = (bf16[16,1152]{1,0:T(8,128)(2,1)S(1)}, bf16[16,1152]{1,0:T(8,128)(2,1)S(1)}, u32[]{:S(2)}, u32[]{:S(2)}) collective-permute-start(bf16[16,1152]{1,0:T(8,128)(2,1)S(1)} %get-tuple-element.32), channel_id=1, source_target_pairs={{0,96},{32,0},{64,32},{96,64},{1,97},{33,1},{65,33},{97,65},{2,98}... | collective-permute-start | bytes 110600 | tf_op jit(solution)/shard_map/ppermute | solution.py:32
  97.1 1.2 fusion.13
  98.4 1.2 collective-permute-start.23
  99.6 3.8 %collective-permute-start.22 = (bf16[4,48,384]{2,1,0:T(8,128)(2,1)S(1)}, bf16[4,48,384]{2,1,0:T(8,128)(2,1)S(1)}, u32[]{:S(2)}, u32[]{:S(2)}) collective-permute-start(bf16[4,48,384]{2,1,0:T(8,128)(2,1)S(1)} %get-tuple-element.26), channel_id=1, source_target_pairs={{0,64},{32,96},{64,0},{96,32},{1,65},{33,97},{65,1},{97,33},{2,66}... | collective-permute-start | bytes 442376 | tf_op jit(solution)/shard_map/ppermute | solution.py:32
  103.4 1.2 collective-permute-done.19
  106.7 1.8 %collective-permute-done.22 = bf16[4,48,384]{2,1,0:T(8,128)(2,1)S(1)} collective-permute-done((bf16[4,48,384]{2,1,0:T(8,128)(2,1)S(1)}, bf16[4,48,384]{2,1,0:T(8,128)(2,1)S(1)}, u32[]{:S(2)}, u32[]{:S(2)}) %collective-permute-start.22) | collective-permute-done | bytes 147488 | tf_op jit(solution)/shard_map/ppermute | solution.py:32
  108.4 1.3 collective-permute-done.21
  110.7 7.2 %all-to-all-start.1 = ((bf16[8,96,384]{2,1,0:T(8,128)(2,1)}), bf16[8,96,384]{2,1,0:T(8,128)(2,1)S(1)}, u32[]{:S(2)}, u32[]{:S(2)}) async-start(bf16[8,96,384]{2,1,0:T(8,128)(2,1)} %maximum_maximum_fusion.1), calls=%async_computation.1 | async-start | bytes 1179648 | tf_op jit(solution)/shard_map/all_to_all | solution.py:41
  118.0 1.3 select_bitcast_fusion.5
  119.3 1.1 pad_maximum_fusion.2
  120.7 2.8 %select_bitcast_fusion.3 = (bf16[2,4,1,48,1536]{4,3,1,0,2:T(8,128)(2,1)S(1)}, bf16[2,4,1,48,1536]{4,3,1,0,2:T(8,128)(2,1)}) fusion(bf16[2,4,48,1536]{3,2,1,0:T(8,128)(2,1)} %collective-permute-done.28, pred[]{:T(512)S(6)} %eq.42, bf16[2,4,48,384]{3,2,1,0:T(8,128)(2,1)S(1)} %copy-done.3, bf16[2,4,48,384]{3,2,1,0:T(8,128)(2,1)S(1)} %copy-done.5, ...), kind=kLoop, calls=%fused_computation.25 | loop fusion | flops 7077888 | bytes 4718593 | tf_op jit(solution)/shard_map/stack | solution.py:175
  123.5 10.5 %all-to-all-done.1 = bf16[8,96,384]{2,1,0:T(8,128)(2,1)S(1)} async-done(((bf16[8,96,384]{2,1,0:T(8,128)(2,1)}), bf16[8,96,384]{2,1,0:T(8,128)(2,1)S(1)}, u32[]{:S(2)}, u32[]{:S(2)}) %all-to-all-start.1) | async-done | bytes 589856 | tf_op jit(solution)/shard_map/all_to_all | solution.py:41
  134.9 6.6 %all-to-all-start.2 = ((bf16[8,48,384]{2,1,0:T(8,128)(2,1)}), bf16[8,48,384]{2,1,0:T(8,128)(2,1)S(1)}, u32[]{:S(2)}, u32[]{:S(2)}) async-start(bf16[8,48,384]{2,1,0:T(8,128)(2,1)} %broadcast_in_dim.15), calls=%async_computation.2 | async-start | bytes 589824 | tf_op jit(solution)/shard_map/all_to_all | solution.py:41
  142.4 1.5 %select_bitcast_fusion.1 = (bf16[2,4,1,48,1536]{4,3,2,1,0:T(8,128)(2,1)S(1)}, bf16[2,4,1,48,1536]{4,3,2,1,0:T(8,128)(2,1)S(1)}) fusion(bf16[2,4,48,1536]{3,2,1,0:T(8,128)(2,1)} %collective-permute-done.33, pred[]{:T(512)S(6)} %eq.42, bf16[1,4,48,1536]{3,2,1,0:T(8,128)(2,1)S(1)} %get-tuple-element.15, bf16[1,4,48,1536]{3,2,1,0:T(8,128)(2,1)S(1)} %get-tuple-element.14), kind=kLoop, calls=%fused_computation.23 | loop fusion | flops 1769472 | bytes 4718593 | tf_op jit(solution)/shard_map/stack | solution.py:175
  145.3 3.1 %convolution_convert_fusion.1 = bf16[384,1536]{1,0:T(8,128)(2,1)} fusion(bf16[1536,1536]{1,0:T(8,128)(2,1)S(1)} %bitcast.80, bf16[384,384]{1,0:T(8,128)(2,1)S(1)} %copy-done.20, bf16[384,384]{1,0:T(8,128)(2,1)S(1)} %copy-done.21, bf16[384,384]{1,0:T(8,128)(2,1)S(1)} %copy-done.19, bf16[384,384]{1,0:T(8,128)(2,1)S(1)} %copy-done.18), kind=kOutput, calls=%fused_computation.2 | convolution fusion | flops 1817247744 | bytes 7077888 | tf_op jit(solution)/shard_map/dot_general | solution.py:179
  (147 shorter events, 21.3 us)
Async XLA Ops:
  0.6 10.8 %copy-start = (bf16[48,1536]{1,0:T(8,128)(2,1)S(1)}, bf16[48,1536]{1,0:T(8,128)(2,1)}, u32[]{:S(2)}) copy-start(bf16[48,1536]{1,0:T(8,128)(2,1)} %param.15) | copy-start | bytes 442372
  3.4 23.5 %collective-permute-start = (bf16[24,1152]{1,0:T(8,128)(2,1)S(1)}, bf16[24,1152]{1,0:T(8,128)(2,1)S(1)}, u32[]{:S(2)}, u32[]{:S(2)}) collective-permute-start(bf16[24,1152]{1,0:T(8,128)(2,1)S(1)} %get-tuple-element.36), channel_id=1, source_target_pairs={{0,32},{32,64},{64,96},{96,0},{1,33},{33,65},{65,97},{97,1},{2,34}... | collective-permute-start | bytes 165896 | tf_op jit(solution)/shard_map/ppermute | solution.py:32
  5.0 21.8 %collective-permute-start.1 = (bf16[24,1152]{1,0:T(8,128)(2,1)S(1)}, bf16[24,1152]{1,0:T(8,128)(2,1)S(1)}, u32[]{:S(2)}, u32[]{:S(2)}) collective-permute-start(bf16[24,1152]{1,0:T(8,128)(2,1)S(1)} %get-tuple-element.36), channel_id=1, source_target_pairs={{0,64},{32,96},{64,0},{96,32},{1,65},{33,97},{65,1},{97,33},{2,66}... | collective-permute-start | bytes 165896 | tf_op jit(solution)/shard_map/ppermute | solution.py:32
  7.9 18.9 %collective-permute-start.2 = (bf16[24,1152]{1,0:T(8,128)(2,1)S(1)}, bf16[24,1152]{1,0:T(8,128)(2,1)S(1)}, u32[]{:S(2)}, u32[]{:S(2)}) collective-permute-start(bf16[24,1152]{1,0:T(8,128)(2,1)S(1)} %get-tuple-element.36), channel_id=1, source_target_pairs={{0,96},{32,0},{64,32},{96,64},{1,97},{33,1},{65,33},{97,65},{2,98}... | collective-permute-start | bytes 165896 | tf_op jit(solution)/shard_map/ppermute | solution.py:32
  10.3 10.5 %copy-start.9 = (bf16[384,1536]{1,0:T(8,128)(2,1)S(1)}, bf16[384,1536]{1,0:T(8,128)(2,1)}, u32[]{:S(2)}) copy-start(bf16[384,1536]{1,0:T(8,128)(2,1)} %param.13) | copy-start | bytes 3538948
  12.3 29.1 %all-to-all-start = ((bf16[8,96,384]{2,1,0:T(8,128)(2,1)}), bf16[8,96,384]{2,1,0:T(8,128)(2,1)S(1)}, u32[]{:S(2)}, u32[]{:S(2)}) async-start(bf16[8,96,384]{2,1,0:T(8,128)(2,1)} %broadcast_in_dim.12), calls=%async_computation | async-start | bytes 1179648 | tf_op jit(solution)/shard_map/all_to_all | solution.py:41
  20.8 30.4 %collective-permute-start.15 = (bf16[384,1536]{1,0:T(8,128)(2,1)}, bf16[384,1536]{1,0:T(8,128)(2,1)}, u32[]{:S(2)}, u32[]{:S(2)}) collective-permute-start(bf16[384,1536]{1,0:T(8,128)(2,1)} %param.14), channel_id=1, source_target_pairs={{0,1},{1,0},{2,3},{3,2},{4,5},{5,4},{6,7},{7,6},{8,9},{9,8},{10,11... | collective-permute-start | bytes 3538952 | tf_op jit(solution)/shard_map/ppermute | solution.py:27
  22.7 28.3 %collective-permute-start.14 = (bf16[768,384]{1,0:T(8,128)(2,1)}, bf16[768,384]{1,0:T(8,128)(2,1)}, u32[]{:S(2)}, u32[]{:S(2)}) collective-permute-start(bf16[768,384]{1,0:T(8,128)(2,1)} %bitcast.19), channel_id=1, source_target_pairs={{0,1},{1,0},{2,3},{3,2},{4,5},{5,4},{6,7},{7,6},{8,9},{9,8},{10,11... | collective-permute-start | bytes 1769480 | tf_op jit(solution)/shard_map/ppermute | solution.py:27
  26.9 8.4 %collective-permute-start.3 = (bf16[4,24,1152]{2,1,0:T(8,128)(2,1)S(1)}, bf16[4,24,1152]{2,1,0:T(8,128)(2,1)S(1)}, u32[]{:S(2)}, u32[]{:S(2)}) collective-permute-start(bf16[4,24,1152]{2,1,0:T(8,128)(2,1)S(1)} %pad_maximum_fusion.5), channel_id=1, source_target_pairs={{0,128},{128,16},{16,144},{144,0},{1,129},{129,17},{17,145},{145,1... | collective-permute-start | bytes 663560 | tf_op jit(solution)/shard_map/ppermute | solution.py:32
  28.5 9.8 %collective-permute-start.4 = (bf16[4,24,1152]{2,1,0:T(8,128)(2,1)S(1)}, bf16[4,24,1152]{2,1,0:T(8,128)(2,1)S(1)}, u32[]{:S(2)}, u32[]{:S(2)}) collective-permute-start(bf16[4,24,1152]{2,1,0:T(8,128)(2,1)S(1)} %pad_maximum_fusion.5), channel_id=1, source_target_pairs={{0,16},{128,144},{16,0},{144,128},{1,17},{129,145},{17,1},{145,129... | collective-permute-start | bytes 663560 | tf_op jit(solution)/shard_map/ppermute | solution.py:32
  29.6 11.6 %collective-permute-start.5 = (bf16[4,24,1152]{2,1,0:T(8,128)(2,1)S(1)}, bf16[4,24,1152]{2,1,0:T(8,128)(2,1)S(1)}, u32[]{:S(2)}, u32[]{:S(2)}) collective-permute-start(bf16[4,24,1152]{2,1,0:T(8,128)(2,1)S(1)} %pad_maximum_fusion.5), channel_id=1, source_target_pairs={{0,144},{128,0},{16,128},{144,16},{1,145},{129,1},{17,129},{145,17... | collective-permute-start | bytes 663560 | tf_op jit(solution)/shard_map/ppermute | solution.py:32
  41.7 12.7 %copy-start.17 = (bf16[16,1,48,384]{3,2,1,0:T(8,128)(2,1)S(1)}, bf16[16,1,48,384]{3,2,1,0:T(8,128)(2,1)}, u32[]{:S(2)}) copy-start(bf16[16,1,48,384]{3,2,1,0:T(8,128)(2,1)} %get-tuple-element.19) | copy-start | bytes 1769476
  41.7 18.9 %collective-permute-start.6 = (bf16[128,1152]{1,0:T(8,128)(2,1)S(1)}, bf16[128,1152]{1,0:T(8,128)(2,1)S(1)}, u32[]{:S(2)}, u32[]{:S(2)}) collective-permute-start(bf16[128,1152]{1,0:T(8,128)(2,1)S(1)} %bitcast.89), channel_id=1, source_target_pairs={{0,1},{1,0},{2,3},{3,2},{4,5},{5,4},{6,7},{7,6},{8,9},{9,8},{10,11... | collective-permute-start | bytes 884744 | tf_op jit(solution)/shard_map/ppermute | solution.py:27
  41.8 6.3 %collective-permute-start.24 = (bf16[4,48,384]{2,1,0:T(8,128)(2,1)S(1)}, bf16[4,48,384]{2,1,0:T(8,128)(2,1)S(1)}, u32[]{:S(2)}, u32[]{:S(2)}) collective-permute-start(bf16[4,48,384]{2,1,0:T(8,128)(2,1)S(1)} %slice.117), channel_id=1, source_target_pairs={{0,144},{128,16},{16,128},{144,0},{1,145},{129,17},{17,129},{145,1... | collective-permute-start | bytes 442376 | tf_op jit(solution)/shard_map/ppermute | solution.py:37
  48.2 11.2 %collective-permute-start.31 = (bf16[4,48,384]{2,1,0:T(8,128)(2,1)S(1)}, bf16[4,48,384]{2,1,0:T(8,128)(2,1)S(1)}, u32[]{:S(2)}, u32[]{:S(2)}) collective-permute-start(bf16[4,48,384]{2,1,0:T(8,128)(2,1)S(1)} %get-tuple-element.23), channel_id=1, source_target_pairs={{0,96},{32,0},{64,32},{96,64},{1,97},{33,1},{65,33},{97,65},{2,98}... | collective-permute-start | bytes 442376 | tf_op jit(solution)/shard_map/ppermute | solution.py:32
  48.3 11.4 %collective-permute-start.30 = (bf16[4,48,384]{2,1,0:T(8,128)(2,1)S(1)}, bf16[4,48,384]{2,1,0:T(8,128)(2,1)S(1)}, u32[]{:S(2)}, u32[]{:S(2)}) collective-permute-start(bf16[4,48,384]{2,1,0:T(8,128)(2,1)S(1)} %get-tuple-element.23), channel_id=1, source_target_pairs={{0,64},{32,96},{64,0},{96,32},{1,65},{33,97},{65,1},{97,33},{2,66}... | collective-permute-start | bytes 442376 | tf_op jit(solution)/shard_map/ppermute | solution.py:32
  51.0 8.6 %collective-permute-start.29 = (bf16[4,48,384]{2,1,0:T(8,128)(2,1)S(1)}, bf16[4,48,384]{2,1,0:T(8,128)(2,1)S(1)}, u32[]{:S(2)}, u32[]{:S(2)}) collective-permute-start(bf16[4,48,384]{2,1,0:T(8,128)(2,1)S(1)} %get-tuple-element.23), channel_id=1, source_target_pairs={{0,32},{32,64},{64,96},{96,0},{1,33},{33,65},{65,97},{97,1},{2,34}... | collective-permute-start | bytes 442376 | tf_op jit(solution)/shard_map/ppermute | solution.py:32
  51.1 23.6 %collective-permute-start.27 = (bf16[2,4,48,384]{3,2,1,0:T(8,128)(2,1)S(1)}, bf16[2,4,48,384]{3,2,1,0:T(8,128)(2,1)S(1)}, u32[]{:S(2)}, u32[]{:S(2)}) collective-permute-start(bf16[2,4,48,384]{3,2,1,0:T(8,128)(2,1)S(1)} %pad_maximum_fusion.4), channel_id=1, source_target_pairs={{0,96},{32,0},{64,32},{96,64},{1,97},{33,1},{65,33},{97,65},{2,98}... | collective-permute-start | bytes 884744 | tf_op jit(solution)/shard_map/ppermute | solution.py:32
  59.4 16.6 %collective-permute-start.26 = (bf16[2,4,48,384]{3,2,1,0:T(8,128)(2,1)S(1)}, bf16[2,4,48,384]{3,2,1,0:T(8,128)(2,1)S(1)}, u32[]{:S(2)}, u32[]{:S(2)}) collective-permute-start(bf16[2,4,48,384]{3,2,1,0:T(8,128)(2,1)S(1)} %pad_maximum_fusion.4), channel_id=1, source_target_pairs={{0,64},{32,96},{64,0},{96,32},{1,65},{33,97},{65,1},{97,33},{2,66}... | collective-permute-start | bytes 884744 | tf_op jit(solution)/shard_map/ppermute | solution.py:32
  61.5 6.1 %collective-permute-start.9 = (bf16[64,1152]{1,0:T(8,128)(2,1)S(1)}, bf16[64,1152]{1,0:T(8,128)(2,1)S(1)}, u32[]{:S(2)}, u32[]{:S(2)}) collective-permute-start(bf16[64,1152]{1,0:T(8,128)(2,1)S(1)} %get-tuple-element.28), channel_id=1, source_target_pairs={{0,128},{128,16},{16,144},{144,0},{1,129},{129,17},{17,145},{145,1... | collective-permute-start | bytes 442376 | tf_op jit(solution)/shard_map/ppermute | solution.py:32
  62.8 7.3 %collective-permute-start.8 = (bf16[64,1152]{1,0:T(8,128)(2,1)S(1)}, bf16[64,1152]{1,0:T(8,128)(2,1)S(1)}, u32[]{:S(2)}, u32[]{:S(2)}) collective-permute-start(bf16[64,1152]{1,0:T(8,128)(2,1)S(1)} %get-tuple-element.29), channel_id=1, source_target_pairs={{0,16},{128,144},{16,0},{144,128},{1,17},{129,145},{17,1},{145,129... | collective-permute-start | bytes 442376 | tf_op jit(solution)/shard_map/ppermute | solution.py:32
  65.5 6.0 %collective-permute-start.7 = (bf16[64,1152]{1,0:T(8,128)(2,1)S(1)}, bf16[64,1152]{1,0:T(8,128)(2,1)S(1)}, u32[]{:S(2)}, u32[]{:S(2)}) collective-permute-start(bf16[64,1152]{1,0:T(8,128)(2,1)S(1)} %get-tuple-element.27), channel_id=1, source_target_pairs={{0,144},{128,0},{16,128},{144,16},{1,145},{129,1},{17,129},{145,17... | collective-permute-start | bytes 442376 | tf_op jit(solution)/shard_map/ppermute | solution.py:32
  67.6 11.1 %collective-permute-start.25 = (bf16[2,4,48,384]{3,2,1,0:T(8,128)(2,1)S(1)}, bf16[2,4,48,384]{3,2,1,0:T(8,128)(2,1)S(1)}, u32[]{:S(2)}, u32[]{:S(2)}) collective-permute-start(bf16[2,4,48,384]{3,2,1,0:T(8,128)(2,1)S(1)} %pad_maximum_fusion.4), channel_id=1, source_target_pairs={{0,32},{32,64},{64,96},{96,0},{1,33},{33,65},{65,97},{97,1},{2,34}... | collective-permute-start | bytes 884744 | tf_op jit(solution)/shard_map/ppermute | solution.py:32
  70.1 15.5 %collective-permute-start.18 = (bf16[2,4,48,384]{3,2,1,0:T(8,128)(2,1)S(1)}, bf16[2,4,48,384]{3,2,1,0:T(8,128)(2,1)S(1)}, u32[]{:S(2)}, u32[]{:S(2)}) collective-permute-start(bf16[2,4,48,384]{3,2,1,0:T(8,128)(2,1)S(1)} %get-tuple-element.17), channel_id=1, source_target_pairs={{0,32},{32,64},{64,96},{96,0},{1,33},{33,65},{65,97},{97,1},{2,34}... | collective-permute-start | bytes 884744 | tf_op jit(solution)/shard_map/ppermute | solution.py:32
  71.6 17.1 %collective-permute-start.17 = (bf16[2,4,48,384]{3,2,1,0:T(8,128)(2,1)S(1)}, bf16[2,4,48,384]{3,2,1,0:T(8,128)(2,1)S(1)}, u32[]{:S(2)}, u32[]{:S(2)}) collective-permute-start(bf16[2,4,48,384]{3,2,1,0:T(8,128)(2,1)S(1)} %get-tuple-element.18), channel_id=1, source_target_pairs={{0,64},{32,96},{64,0},{96,32},{1,65},{33,97},{65,1},{97,33},{2,66}... | collective-permute-start | bytes 884744 | tf_op jit(solution)/shard_map/ppermute | solution.py:32
  74.7 5.8 %copy-start.2 = (bf16[2,4,48,384]{3,2,1,0:T(8,128)(2,1)}, bf16[2,4,48,384]{3,2,1,0:T(8,128)(2,1)S(1)}, u32[]{:S(2)}) copy-start(bf16[2,4,48,384]{3,2,1,0:T(8,128)(2,1)S(1)} %collective-permute-done.27) | copy-start | bytes 884740
  74.7 16.1 %collective-permute-start.16 = (bf16[2,4,48,384]{3,2,1,0:T(8,128)(2,1)S(1)}, bf16[2,4,48,384]{3,2,1,0:T(8,128)(2,1)S(1)}, u32[]{:S(2)}, u32[]{:S(2)}) collective-permute-start(bf16[2,4,48,384]{3,2,1,0:T(8,128)(2,1)S(1)} %get-tuple-element.16), channel_id=1, source_target_pairs={{0,96},{32,0},{64,32},{96,64},{1,97},{33,1},{65,33},{97,65},{2,98}... | collective-permute-start | bytes 884744 | tf_op jit(solution)/shard_map/ppermute | solution.py:32
  75.9 4.5 %copy-start.4 = (bf16[2,4,48,384]{3,2,1,0:T(8,128)(2,1)}, bf16[2,4,48,384]{3,2,1,0:T(8,128)(2,1)S(1)}, u32[]{:S(2)}) copy-start(bf16[2,4,48,384]{3,2,1,0:T(8,128)(2,1)S(1)} %collective-permute-done.26) | copy-start | bytes 884740
  75.9 21.1 %collective-permute-start.20 = (bf16[4,48,1536]{2,1,0:T(8,128)(2,1)}, bf16[4,48,1536]{2,1,0:T(8,128)(2,1)}, u32[]{:S(2)}, u32[]{:S(2)}) collective-permute-start(bf16[4,48,1536]{2,1,0:T(8,128)(2,1)} %dynamic-slice_bitcast_fusion), channel_id=1, source_target_pairs={{0,144},{128,16},{16,128},{144,0},{1,145},{129,17},{17,129},{145,1... | collective-permute-start | bytes 1769480 | tf_op jit(solution)/shard_map/ppermute | solution.py:37
  78.7 1.7 %copy-start.6 = (bf16[2,4,48,384]{3,2,1,0:T(8,128)(2,1)}, bf16[2,4,48,384]{3,2,1,0:T(8,128)(2,1)S(1)}, u32[]{:S(2)}) copy-start(bf16[2,4,48,384]{3,2,1,0:T(8,128)(2,1)S(1)} %collective-permute-done.25) | copy-start | bytes 884740
  78.7 39.2 %collective-permute-start.32 = (bf16[4,48,1536]{2,1,0:T(8,128)(2,1)}, bf16[4,48,1536]{2,1,0:T(8,128)(2,1)}, u32[]{:S(2)}, u32[]{:S(2)}) collective-permute-start(bf16[4,48,1536]{2,1,0:T(8,128)(2,1)} %pad_maximum_fusion.3), channel_id=1, source_target_pairs={{0,144},{128,16},{16,128},{144,0},{1,145},{129,17},{17,129},{145,1... | collective-permute-start | bytes 1769480 | tf_op jit(solution)/shard_map/ppermute | solution.py:37
  80.5 15.5 %copy-start.10 = (f32[16,1152]{1,0:T(8,128)S(1)}, f32[16,1152]{1,0:T(8,128)}, u32[]{:S(2)}) copy-start(f32[16,1152]{1,0:T(8,128)} %param.8) | copy-start | bytes 221188
  85.6 8.1 %collective-permute-start.12 = (bf16[16,1152]{1,0:T(8,128)(2,1)S(1)}, bf16[16,1152]{1,0:T(8,128)(2,1)S(1)}, u32[]{:S(2)}, u32[]{:S(2)}) collective-permute-start(bf16[16,1152]{1,0:T(8,128)(2,1)S(1)} %get-tuple-element.33), channel_id=1, source_target_pairs={{0,32},{32,64},{64,96},{96,0},{1,33},{33,65},{65,97},{97,1},{2,34}... | collective-permute-start | bytes 110600 | tf_op jit(solution)/shard_map/ppermute | solution.py:32
  88.7 5.5 %collective-permute-start.11 = (bf16[16,1152]{1,0:T(8,128)(2,1)S(1)}, bf16[16,1152]{1,0:T(8,128)(2,1)S(1)}, u32[]{:S(2)}, u32[]{:S(2)}) collective-permute-start(bf16[16,1152]{1,0:T(8,128)(2,1)S(1)} %get-tuple-element.34), channel_id=1, source_target_pairs={{0,64},{32,96},{64,0},{96,32},{1,65},{33,97},{65,1},{97,33},{2,66}... | collective-permute-start | bytes 110600 | tf_op jit(solution)/shard_map/ppermute | solution.py:32
  90.8 4.3 %collective-permute-start.10 = (bf16[16,1152]{1,0:T(8,128)(2,1)S(1)}, bf16[16,1152]{1,0:T(8,128)(2,1)S(1)}, u32[]{:S(2)}, u32[]{:S(2)}) collective-permute-start(bf16[16,1152]{1,0:T(8,128)(2,1)S(1)} %get-tuple-element.32), channel_id=1, source_target_pairs={{0,96},{32,0},{64,32},{96,64},{1,97},{33,1},{65,33},{97,65},{2,98}... | collective-permute-start | bytes 110600 | tf_op jit(solution)/shard_map/ppermute | solution.py:32
  93.7 3.2 %collective-permute-start.13 = (bf16[128,1152]{1,0:T(8,128)(2,1)S(1)}, bf16[128,1152]{1,0:T(8,128)(2,1)S(1)}, u32[]{:S(2)}, u32[]{:S(2)}) collective-permute-start(bf16[128,1152]{1,0:T(8,128)(2,1)S(1)} %slice.142), channel_id=1, source_target_pairs={{0,1},{1,0},{2,3},{3,2},{4,5},{5,4},{6,7},{7,6},{8,9},{9,8},{10,11... | collective-permute-start | bytes 884744 | tf_op jit(solution)/shard_map/ppermute | solution.py:27
  94.2 26.2 %collective-permute-start.28 = (bf16[2,4,48,1536]{3,2,1,0:T(8,128)(2,1)}, bf16[2,4,48,1536]{3,2,1,0:T(8,128)(2,1)}, u32[]{:S(2)}, u32[]{:S(2)}) collective-permute-start(bf16[2,4,48,1536]{3,2,1,0:T(8,128)(2,1)} %pad_maximum_fusion.1), channel_id=1, source_target_pairs={{0,1},{1,0},{2,3},{3,2},{4,5},{5,4},{6,7},{7,6},{8,9},{9,8},{10,11... | collective-permute-start | bytes 3538952 | tf_op jit(solution)/shard_map/ppermute | solution.py:27
  95.1 9.5 %collective-permute-start.19 = (bf16[4,48,384]{2,1,0:T(8,128)(2,1)S(1)}, bf16[4,48,384]{2,1,0:T(8,128)(2,1)}, u32[]{:S(2)}, u32[]{:S(2)}) collective-permute-start(bf16[4,48,384]{2,1,0:T(8,128)(2,1)S(1)} %fusion.24), channel_id=1, source_target_pairs={{0,144},{128,16},{16,128},{144,0},{1,145},{129,17},{17,129},{145,1... | collective-permute-start | bytes 442376 | tf_op jit(solution)/shard_map/ppermute | solution.py:37
  98.4 8.3 %collective-permute-start.23 = (bf16[4,48,384]{2,1,0:T(8,128)(2,1)S(1)}, bf16[4,48,384]{2,1,0:T(8,128)(2,1)S(1)}, u32[]{:S(2)}, u32[]{:S(2)}) collective-permute-start(bf16[4,48,384]{2,1,0:T(8,128)(2,1)S(1)} %get-tuple-element.25), channel_id=1, source_target_pairs={{0,32},{32,64},{64,96},{96,0},{1,33},{33,65},{65,97},{97,1},{2,34}... | collective-permute-start | bytes 442376 | tf_op jit(solution)/shard_map/ppermute | solution.py:32
  99.6 8.8 %collective-permute-start.22 = (bf16[4,48,384]{2,1,0:T(8,128)(2,1)S(1)}, bf16[4,48,384]{2,1,0:T(8,128)(2,1)S(1)}, u32[]{:S(2)}, u32[]{:S(2)}) collective-permute-start(bf16[4,48,384]{2,1,0:T(8,128)(2,1)S(1)} %get-tuple-element.26), channel_id=1, source_target_pairs={{0,64},{32,96},{64,0},{96,32},{1,65},{33,97},{65,1},{97,33},{2,66}... | collective-permute-start | bytes 442376 | tf_op jit(solution)/shard_map/ppermute | solution.py:32
  104.6 5.1 %collective-permute-start.21 = (bf16[4,48,384]{2,1,0:T(8,128)(2,1)S(1)}, bf16[4,48,384]{2,1,0:T(8,128)(2,1)S(1)}, u32[]{:S(2)}, u32[]{:S(2)}) collective-permute-start(bf16[4,48,384]{2,1,0:T(8,128)(2,1)S(1)} %get-tuple-element.24), channel_id=1, source_target_pairs={{0,96},{32,0},{64,32},{96,64},{1,97},{33,1},{65,33},{97,65},{2,98}... | collective-permute-start | bytes 442376 | tf_op jit(solution)/shard_map/ppermute | solution.py:32
  109.8 8.1 %copy-start.12 = (bf16[4,48,384]{2,1,0:T(8,128)(2,1)S(1)}, bf16[4,48,384]{2,1,0:T(8,128)(2,1)}, u32[]{:S(2)}) copy-start(bf16[4,48,384]{2,1,0:T(8,128)(2,1)} %copy-done.11) | copy-start | bytes 442372
  109.8 8.1 %copy-start.14 = (bf16[4,48,384]{2,1,0:T(8,128)(2,1)S(1)}, bf16[4,48,384]{2,1,0:T(8,128)(2,1)}, u32[]{:S(2)}) copy-start(bf16[4,48,384]{2,1,0:T(8,128)(2,1)} %copy-done.13) | copy-start | bytes 442372
  109.8 8.1 %copy-start.16 = (bf16[4,48,384]{2,1,0:T(8,128)(2,1)S(1)}, bf16[4,48,384]{2,1,0:T(8,128)(2,1)}, u32[]{:S(2)}) copy-start(bf16[4,48,384]{2,1,0:T(8,128)(2,1)} %copy-done.15) | copy-start | bytes 442372
  110.7 23.3 %all-to-all-start.1 = ((bf16[8,96,384]{2,1,0:T(8,128)(2,1)}), bf16[8,96,384]{2,1,0:T(8,128)(2,1)S(1)}, u32[]{:S(2)}, u32[]{:S(2)}) async-start(bf16[8,96,384]{2,1,0:T(8,128)(2,1)} %maximum_maximum_fusion.1), calls=%async_computation.1 | async-start | bytes 1179648 | tf_op jit(solution)/shard_map/all_to_all | solution.py:41
  120.4 22.0 %collective-permute-start.33 = (bf16[2,4,48,1536]{3,2,1,0:T(8,128)(2,1)}, bf16[2,4,48,1536]{3,2,1,0:T(8,128)(2,1)}, u32[]{:S(2)}, u32[]{:S(2)}) collective-permute-start(bf16[2,4,48,1536]{3,2,1,0:T(8,128)(2,1)} %pad_maximum_fusion.2), channel_id=1, source_target_pairs={{0,1},{1,0},{2,3},{3,2},{4,5},{5,4},{6,7},{7,6},{8,9},{9,8},{10,11... | collective-permute-start | bytes 3538952 | tf_op jit(solution)/shard_map/ppermute | solution.py:27
  123.5 18.0 %copy-start.8 = (f32[16,1152]{1,0:T(8,128)S(1)}, f32[16,1152]{1,0:T(8,128)}, u32[]{:S(2)}) copy-start(f32[16,1152]{1,0:T(8,128)} %param.9) | copy-start | bytes 221188
  134.9 13.5 %all-to-all-start.2 = ((bf16[8,48,384]{2,1,0:T(8,128)(2,1)}), bf16[8,48,384]{2,1,0:T(8,128)(2,1)S(1)}, u32[]{:S(2)}, u32[]{:S(2)}) async-start(bf16[8,48,384]{2,1,0:T(8,128)(2,1)} %broadcast_in_dim.15), calls=%async_computation.2 | async-start | bytes 589824 | tf_op jit(solution)/shard_map/all_to_all | solution.py:41
  (11 other events, 12.9 us)

commit v3 on v1

v3 whole, which is shorter than its diff:
```python
import math

import jax
import jax.numpy as jnp
from jax import lax
from jax.experimental import pallas as pl
from jax.experimental.pallas import tpu as pltpu
from jax.sharding import Mesh, PartitionSpec as P

stability_floor = 1e-06
f32, bf16 = jnp.float32, jnp.bfloat16

AXES = ("xl", "y", "xh", "z", "c")
SIZES = (2, 4, 2, 8, 2)
ROW = (("xl", "xh"), (0, 2, 1, 3))
COLUMN = ("y", (0, 1, 2, 3))
CUT = 144
BACK = (((1,), (1,)), ((), ()))


def swap_cores(x):
    return lax.ppermute(x, "c", [(0, 1), (1, 0)])


def turn(x, ring, by):
    axes, at = ring
    return lax.ppermute(x, axes, [(at[i], at[(i + by) % 4]) for i in range(4)])


def swap_halves(x):
    axes, at = ROW
    return lax.ppermute(x, axes, [(at[i], at[3 - i]) for i in range(4)])


def swap_pairs(x):
    return lax.ppermute(x, "xl", [(0, 1), (1, 0)])


def swap_far(x):
    return lax.ppermute(x, "xh", [(0, 1), (1, 0)])


def exchange(x, axes):
    return lax.all_to_all(x, axes, 0, 0, tiled=True)


def after(x, *earlier):
    return lax.optimization_barrier((x, *earlier))[0]


def fold(x):
    return jnp.concatenate([x[:, i * 384 : (i + 1) * 384] for i in range(3)], axis=0)


def unfold(x):
    return jnp.concatenate([x[i * 16 : (i + 1) * 16] for i in range(3)], axis=1)


def unit_rows(raw):
    row_scale = lax.rsqrt(jnp.sum(raw * raw, axis=1, keepdims=True) + stability_floor)
    return raw * row_scale, row_scale


def back_through_norm(raw, row_grad):
    normed, row_scale = unit_rows(raw)
    along_unit = jnp.sum(normed * row_grad, axis=1, keepdims=True)
    return (row_grad - normed * along_unit) * row_scale


def call(kernel, outs, place, *operands, scratch=(), flops=0, spaces=()):
    moved = sum(math.prod(o.shape) * o.dtype.itemsize for o in (*outs, *operands))
    spaces = tuple(spaces) + (pltpu.VMEM,) * (len(operands) - len(spaces))
    return pl.pallas_call(
        kernel,
        out_shape=tuple(outs),
        in_specs=[pl.BlockSpec(memory_space=space) for space in (pltpu.SMEM, *spaces)],
        out_specs=tuple(pl.BlockSpec(memory_space=pltpu.VMEM) for _ in outs),
        scratch_shapes=scratch,
        compiler_params=pltpu.CompilerParams(vmem_limit_bytes=16 * 2**20),
        cost_estimate=pl.CostEstimate(flops=flops, bytes_accessed=moved, transcendentals=0),
    )(place, *operands)


def shape(*dims, dtype=bf16):
    return jax.ShapeDtypeStruct(dims, dtype)


def text_kernel(place, cap, rows, z_out):
    text = fold(unit_rows(cap[...])[0].astype(bf16))
    for k in range(8):
        z_out[k, :48, :] = text
        for j in range(4):
            z_out[k, 48 + j * 48 : 96 + j * 48, :] = rows[:, j * 384 : j * 384 + 384]


def weight_kernel(place, ids, pic, tokens, other_tokens, adj, other_adj, *rest):
    a0, a1, a2, a3, b_own, b_out, image, turned, own, other = rest
    y, low, c = place[0], place[2] == 0, place[3]
    line = lax.broadcasted_iota(jnp.int32, (16, 384), 0)
    number = jnp.zeros((16, 384), jnp.int32)
    for i in range(16):
        number = jnp.where(line == i, ids[i], number)
    lane = lax.broadcasted_iota(jnp.int32, (16, 384), 1)
    split = jnp.where(lane == 0, number >> 6, jnp.where(lane == 1, number & 63, 0))
    image[48:, :] = split.astype(f32).astype(bf16)
    image[:48, :] = fold(unit_rows(pic[...])[0].astype(bf16))
    for source, target in ((tokens, own), (other_tokens, other)):
        turned[...] = source[...].T
        for chip in range(16):
            here = pl.ds(pl.multiple_of(chip * 96 + c * 48, 16), 48)
            target[chip * 48 : chip * 48 + 48, :] = turned[here, :]
    for k, out in enumerate((a0, a1, a2, a3)):
        at = pl.ds(pl.multiple_of(((y - k) & 3) * 384, 384), 384)
        acc = jnp.dot(own[...], adj[:, at], preferred_element_type=f32)
        acc = acc + jnp.dot(other[...], other_adj[:, at], preferred_element_type=f32)
        acc = acc.astype(bf16)
        out[:CUT, :] = acc[:CUT]
        out[CUT : 2 * CUT, :] = acc[384 : 384 + CUT]
        b_own[:, at] = jnp.where(low, acc[CUT:384], acc[384 + CUT :])
        b_out[:, at] = jnp.where(low, acc[384 + CUT :], acc[CUT:384])
        if k:
            out[2 * CUT :, :] = image[...]


def first_sum_kernel(
    place, a0, a1, a2, a3, b_own, b_in, image, a_own, near, b0, b1, b2, b3, total
):
    y, xh = place[0], place[2]
    total[...] = a0[...].astype(f32)
    for part in (a1, a2, a3):
        total[...] += part[: 2 * CUT, :].astype(f32)
    a_own[...] = total[pl.ds(pl.multiple_of(xh * CUT, 16), CUT), :]
    near[:CUT, :] = total[pl.ds(pl.multiple_of((1 - xh) * CUT, 16), CUT), :].astype(bf16)
    for k, out in enumerate((b0, b1, b2, b3)):
        at = pl.ds(pl.multiple_of(((y - k) & 3) * 384, 384), 384)
        both = b_own[:, at].astype(f32) + b_in[:, at].astype(f32)
        out[...] = both.astype(out.dtype)
    near[CUT : CUT + 64, :] = image[...]
    for k, part in enumerate((a1, a2, a3)):
        near[CUT + 64 + 64 * k : CUT + 128 + 64 * k, :] = part[2 * CUT :, :]


def second_sum_kernel(place, a_own, near_in, b0, b1, b2, b3, out):
    out[:CUT, :] = (a_own[...] + near_in[:CUT, :].astype(f32)).astype(bf16)
    total = b0[...]
    for part in (b1, b2, b3):
        total = total + part[...].astype(f32)
    out[CUT:, :] = total.astype(bf16)


def tile_kernel(
    place, knobs, i0, i1, i2, i3, text, other_text, g0, g1, g2, g3, t_own, t_out, images, texts, ids
):
    y, xl, xh, c = place[0], place[1], place[2], place[3]
    for k, part in enumerate((i0, i1, i2, i3)):
        first = part.shape[0] - 256
        for j in range(4):
            at = k * 64 + j * 16
            here = first + j * 64
            images[at : at + 16, :] = unfold(part[here : here + 48, :])
            split = part[here + 48 : here + 64, :128].astype(f32)
            ids[at : at + 16, :] = (split[:, 0:1] * 64.0 + split[:, 1:2]).astype(jnp.int32)
    for k in range(8):
        texts[k * 16 : k * 16 + 16, :] = unfold(text[k, :48, :])
        texts[128 + k * 16 : 144 + k * 16, :] = unfold(other_text[k, :, :])
    sharpness, offset = knobs[0, 0], knobs[0, 1]
    col = lax.broadcasted_iota(jnp.int32, (256, 256), 1)
    core = jnp.where(col < 128, c, 1 - c)
    first = ((xl * 4 + y) * 2 + xh) * 256
    index = first + (((col & 127) >> 4) * 2 + core) * 16 + (col & 15)
    dots = lax.dot_general(images[...], texts[...], BACK, preferred_element_type=f32)
    labels = (ids[...] == index).astype(f32)
    weights = sharpness * (jax.nn.sigmoid(sharpness * dots + offset) - labels)
    half = weights.astype(bf16)
    for k, out in enumerate((g0, g1, g2, g3)):
        part = jnp.dot(half[k * 64 : k * 64 + 64], texts[...], preferred_element_type=f32)
        for j in range(4):
            out[j * 48 : j * 48 + 48, :] = fold(part[j * 16 : j * 16 + 16]).astype(out.dtype)
    half = weights.T.astype(bf16)
    t_own[...] = jnp.dot(half[:128], images[...], preferred_element_type=f32)
    t_out[...] = jnp.dot(half[128:], images[...], preferred_element_type=f32).astype(bf16)


def send_back_kernel(place, t_own, t_in, weight, out):
    total = (t_own[...] + t_in[...].astype(f32)).astype(bf16)
    for k in range(8):
        out[k, :48, :] = fold(total[k * 16 : k * 16 + 16])
        out[k, 48:, :] = weight[k * 48 : k * 48 + 48, :]


def text_end_kernel(place, back, cap, grad, pieces):
    total = back[0].astype(f32)
    for k in range(1, 8):
        total = total + back[k].astype(f32)
    grad[...] = back_through_norm(cap[...], unfold(total[:48]))
    piece = total[48:] * (1.0 / math.sqrt(98304))
    for k in range(8):
        pieces[k] = piece


def image_middle_kernel(place, g0, g1, g2, g3, h0, h1, h2, h3):
    total = g0[...]
    for part in (g1, g2, g3):
        total = total + part[...].astype(f32)
    for k, out in enumerate((h0, h1, h2, h3)):
        out[...] = total[k * 48 : k * 48 + 48].astype(out.dtype)


def image_end_kernel(place, h0, h1, h2, h3, pic, grad):
    total = h0[...]
    for part in (h1, h2, h3):
        total = total + part[...].astype(f32)
    grad[...] = back_through_norm(pic[...], unfold(total))


def weight_end_kernel(place, pieces, grad):
    for k in range(4):
        grad[:, k * 384 : k * 384 + 384] = pieces[k] + pieces[4 + k]


def project_kernel(place, adj, w, other_w, *rest):
    out, rows = rest[-2:]
    c = place[3]
    for z in range(8):
        for k in range(4):
            at = slice(k * 384, k * 384 + 384)
            rows[z * 2 + c, :, at] = w[z, k * 48 : k * 48 + 48, :]
            rows[z * 2 + 1 - c, :, at] = other_w[z, k * 48 : k * 48 + 48, :]
    for k in range(2):
        part = rows[k * 8 : k * 8 + 8].reshape(384, 1536)
        out[:, k * 384 : k * 384 + 384] = lax.dot_general(
            adj[...], part, BACK, preferred_element_type=f32
        ).astype(bf16)


def project(place, half, adj, w, other_w, before=None):
    whole = pl.BlockSpec(memory_space=pltpu.VMEM)
    operands = [adj, w, other_w] + ([] if before is None else [before])
    in_specs = [whole] * 3 + ([] if before is None else [pl.BlockSpec(memory_space=pl.ANY)])
    return pl.pallas_call(
        project_kernel,
        grid_spec=pltpu.PrefetchScalarGridSpec(
            num_scalar_prefetch=1,
            grid=(1,),
            in_specs=in_specs,
            out_specs=pl.BlockSpec((384, 768), lambda i, place: (0, place[half])),
            scratch_shapes=[pltpu.VMEM((16, 48, 1536), bf16)],
        ),
        out_shape=shape(384, 1536),
        input_output_aliases={} if before is None else {4: 0},
        compiler_params=pltpu.CompilerParams(vmem_limit_bytes=16 * 2**20),
        cost_estimate=pl.CostEstimate(
            flops=2 * 384 * 768 * 1536, bytes_accessed=6 * 2**20, transcendentals=0
        ),
    )(place, *operands)


def per_device(
    picture_vectors_prenorm,
    caption_vectors_prenorm,
    matched_caption_ids,
    sharpness_coefficient,
    additive_offset_term,
    heads_mixed_concluding,
    dense_result_adjoint,
    dense_mapping_matrix,
):
    y, xl, xh, c = (lax.axis_index(name) for name in ("y", "xl", "xh", "c"))
    place = jnp.stack([y, xl, xh, c, 1 - xh]).astype(jnp.int32)
    other_adjoint = swap_cores(dense_result_adjoint)
    other_tokens = swap_cores(heads_mixed_concluding)

    (along_z,) = call(
        text_kernel, (shape(8, 240, 384),), place, caption_vectors_prenorm, dense_mapping_matrix
    )
    along_z = exchange(along_z, "z")

    *a, b_own, b_out, image = call(
        weight_kernel,
        (
            shape(2 * CUT, 384),
            *[shape(2 * CUT + 64, 384)] * 3,
            shape(384 - CUT, 1536),
            shape(384 - CUT, 1536),
            shape(64, 384),
        ),
        place,
        matched_caption_ids,
        picture_vectors_prenorm,
        heads_mixed_concluding,
        other_tokens,
        dense_result_adjoint,
        other_adjoint,
        scratch=[
            pltpu.VMEM((1536, 384), bf16),
            pltpu.VMEM((768, 384), bf16),
            pltpu.VMEM((768, 384), bf16),
        ],
        spaces=(pltpu.SMEM,),
        flops=4 * 768 * 384 * 1536,
    )
    b_in = swap_halves(b_out)
    a_in = [turn(a[k], COLUMN, -k) for k in (1, 2, 3)]
    a_own, near, *b = call(
        first_sum_kernel,
        (
            shape(CUT, 384, dtype=f32),
            shape(CUT + 256, 384),
            shape(384 - CUT, 384, dtype=f32),
            *[shape(384 - CUT, 384)] * 3,
        ),
        place,
        a[0],
        *a_in,
        b_own,
        b_in,
        image,
        scratch=[pltpu.VMEM((2 * CUT, 384), f32)],
    )
    near_in = swap_halves(near)
    b = [b[0]] + [turn(b[k], COLUMN, -k) for k in (1, 2, 3)]
    column = near[CUT:]
    images = [column, near_in, swap_pairs(column), swap_far(column)]
    (weight_plane,) = call(second_sum_kernel, (shape(384, 384),), place, a_own, near_in, *b)
    images = [after(image, weight_plane) for image in images]

    along_z = after(along_z, near)
    other_text = swap_cores(along_z[:, :48])
    knobs = jnp.concatenate([sharpness_coefficient, additive_offset_term]).reshape(1, 2)
    *g, t_own, t_out = call(
        tile_kernel,
        (
            shape(192, 384, dtype=f32),
            *[shape(192, 384)] * 3,
            shape(128, 1152, dtype=f32),
            shape(128, 1152),
        ),
        place,
        knobs,
        *images,
        along_z,
        other_text,
        scratch=[
            pltpu.VMEM((256, 1152), bf16),
            pltpu.VMEM((256, 1152), bf16),
            pltpu.VMEM((256, 1), jnp.int32),
        ],
        flops=6 * 256 * 256 * 1152,
    )

    rows = after(along_z[:, 48:], *images[1:])
    far_rows = swap_halves(rows)
    core_rows = swap_cores(rows)

    t_in = swap_cores(t_out)
    (back,) = call(send_back_kernel, (shape(8, 96, 384),), place, t_own, t_in, weight_plane)
    g = [after(part, back) for part in g]
    back = exchange(back, "z")
    g = [g[0], swap_halves(g[1]), swap_pairs(g[2]), swap_far(g[3])]
    far_rows = after(far_rows, *g)
    h = call(
        image_middle_kernel, (shape(48, 384, dtype=f32), *[shape(48, 384)] * 3), place, *g
    )
    attn_grad = project(place, 2, dense_result_adjoint, rows, core_rows)
    back = after(back, attn_grad)
    text_grad, pieces = call(
        text_end_kernel,
        (shape(16, 1152, dtype=f32), shape(8, 48, 384, dtype=f32)),
        place,
        back,
        caption_vectors_prenorm,
    )
    pieces = exchange(pieces, ("xl", "y"))
    h = [h[0]] + [turn(h[k], COLUMN, k) for k in (1, 2, 3)]
    (image_grad,) = call(
        image_end_kernel, (shape(16, 1152, dtype=f32),), place, *h, picture_vectors_prenorm
    )
    attn_grad = project(
        place, 4, dense_result_adjoint, far_rows, swap_cores(far_rows), attn_grad
    )
    pieces = after(pieces, attn_grad, image_grad)
    (weight_grad,) = call(weight_end_kernel, (shape(48, 1536, dtype=f32),), place, pieces)
    return (image_grad, text_grad, attn_grad, weight_grad)


def solution(mesh):
    chips = Mesh(mesh.devices.reshape(SIZES), AXES)
    everywhere = P(AXES, None)
    by_group = P(("xh", "z", "c"), None)
    return jax.shard_map(
        per_device,
        mesh=chips,
        in_specs=(
            everywhere,
            everywhere,
            P(AXES),
            P(),
            P(),
            everywhere,
            everywhere,
            by_group,
        ),
        out_specs=(everywhere, everywhere, everywhere, by_group),
        check_vma=False,
    )
```

time: 186 us -> 130 us (0.70)
  waiting for transfers between devices: 91.7 us -> 44.8 us
  Pallas kernels: 0 us -> 24.4 us
  local copies, waits for them, and re-layouts: 25.1 us -> 7.57 us
  other arithmetic: 12.9 us -> 0.08 us
  matrix products: 12.7 us -> 0 us
  starting transfers between devices: 40.7 us -> 49.7 us
    all_to_all x5 -> x3, waiting for transfers between devices: 87.7 us -> 0.01 us  [exchange(): return lax.all_to_all(x, axes, 0, 0, tiled=True)]
    ppermute x0 -> x17, waiting for transfers between devices: none -> 39.5 us  [the longest x9 28.4 us: turn(): return lax.ppermute(x, axes, [(at[i], at[(i + by) % 4]) for i in range(4)])]
    ppermute x0 -> x17, starting transfers between devices: none -> 26.5 us  [the longest x9 13.8 us: turn(): return lax.ppermute(x, axes, [(at[i], at[(i + by) % 4]) for i in range(4)])]
    pallas_call x0 -> x12, Pallas kernels: none -> 24.4 us  [the longest x10 15.6 us: call(): pl.pallas_call(kernel, out_shape=tuple(outs), in_specs=[pl.BlockSpec(memo...]
    all_to_all x5 -> x3, starting transfers between devices: 40 us -> 22 us  [exchange(): return lax.all_to_all(x, axes, 0, 0, tiled=True)]
    dot_general x5 -> x0, matrix products: 12.7 us -> none  [the longest x1 4.67 us: per_device(): jnp.dot(jnp.concatenate([own_columns(heads_mixed_concluding), own_columns...]
    reshape x6 -> x0, local copies, waits for them, and re-layouts: 7.29 us -> none  [the longest x2 4.56 us: per_device(): weight_share.reshape(2, 8, 2, 24, 4, 384).transpose(4, 0, 2, 1, 3, 5)]
    concatenate x5 -> x0, other arithmetic: 4.69 us -> none  [the longest x1 1.94 us: per_device(): jnp.concatenate([weight_share, to_everyone(image_sent, 16)], axis=1)]
  transfers between devices with their start and end apart: 10 -> 26, of which waited for: 6 -> 11; matrix products, arithmetic and copies ran while one was open for 16% -> 0% of each run, Pallas kernels for 0% -> 17%
where the time goes in v3:
time: 130 us; the launch traced here: 129 us
  starting transfers between devices  49.7 us (38%)
  waiting for transfers between devices  44.8 us (34%)
  Pallas kernels  24.4 us (19%)
  local copies, waits for them, and re-layouts  7.57 us (6%)
  between operations  2.12 us (2%)
    ppermute x9, waiting for transfers between devices, turn(): return lax.ppermute(x, axes, [(at[i], at[(i + by) % 4]) for i in range(4)])  28.4 us
    all_to_all x3, starting transfers between devices, exchange(): return lax.all_to_all(x, axes, 0, 0, tiled=True)  22 us
    pallas_call x10, Pallas kernels, call(): pl.pallas_call(kernel, out_shape=tuple(outs), in_specs=[pl.BlockSpec(memo...  15.6 us
    ppermute x9, starting transfers between devices, turn(): return lax.ppermute(x, axes, [(at[i], at[(i + by) % 4]) for i in range(4)])  13.8 us
    ppermute x4, waiting for transfers between devices, swap_halves(): return lax.ppermute(x, axes, [(at[i], at[3 - i]) for i in range(4)])  11.1 us
    pallas_call x2, Pallas kernels, project(): pl.pallas_call(project_kernel, grid_spec=pltpu.PrefetchScalarGridSpec(num...  8.82 us
    unnamed x42, local copies, waits for them, and re-layouts  7.31 us
    ppermute x2, starting transfers between devices, swap_pairs(): return lax.ppermute(x, 'xl', [(0, 1), (1, 0)])  5.97 us
  transfers between devices with their start and end apart: 26, of which 11 were waited for; matrix products, arithmetic and copies ran while one was open for 0% of the time, Pallas kernels for 17%

profile of v3, /device:TPU:2, one launch (start us, length us, event | category | flops | bytes accessed | tf_op | source)
XLA Modules:
  0.0 128.6 jit_solution(10565642731872908894)
XLA Ops:
  0.7 0.9 copy-done.3
  1.6 0.9 copy-done.11
  2.5 1.8 %shard_map.114 = bf16[8,240,384]{2,1,0:T(8,128)(2,1)} custom-call(s32[5]{0:T(128)S(1)} %stack.23.place, f32[16,1152]{1,0:T(8,128)S(1)} %copy-done.3, bf16[48,1536]{1,0:T(8,128)(2,1)S(1)} %copy-done.11), custom_call_target="tpu_custom_call" | custom-call | bytes 1695744 | tf_op jit(solution)/shard_map/pallas_call | solution.py:73
  4.3 8.6 %all-to-all-start = ((bf16[8,240,384]{2,1,0:T(8,128)(2,1)}), bf16[8,240,384]{2,1,0:T(8,128)(2,1)S(1)}, u32[]{:S(2)}, u32[]{:S(2)}) async-start(bf16[8,240,384]{2,1,0:T(8,128)(2,1)} %shard_map.114), calls=%async_computation | async-start | bytes 2949120 | tf_op jit(solution)/shard_map/all_to_all | solution.py:44
  13.4 3.2 %collective-permute-done.other_tokens = bf16[384,1536]{1,0:T(8,128)(2,1)S(1)} collective-permute-done((bf16[384,1536]{1,0:T(8,128)(2,1)}, bf16[384,1536]{1,0:T(8,128)(2,1)S(1)}, u32[]{:S(2)}, u32[]{:S(2)}) %collective-permute-start) | collective-permute-done | bytes 1179680 | tf_op jit(solution)/shard_map/ppermute | solution.py:22
  16.6 0.9 collective-permute-done.1.other_adj
  17.5 1.3 copy-done.17
  18.8 4.3 %shard_map.111 = (bf16[288,384]{1,0:T(8,128)(2,1)S(1)}, bf16[352,384]{1,0:T(8,128)(2,1)S(1)}, bf16[352,384]{1,0:T(8,128)(2,1)S(1)}, bf16[352,384]{1,0:T(8,128)(2...) custom-call(s32[5]{0:T(128)S(1)} %stack.23.place, ...), custom_call_target="tpu_custom_call" | custom-call | flops 1811939328 | bytes 7348288 | tf_op jit(solution)/shard_map/pallas_call | solution.py:73
  23.0 1.6 %collective-permute-start.5 = (bf16[240,1536]{1,0:T(8,128)(2,1)S(1)}, bf16[240,1536]{1,0:T(8,128)(2,1)S(1)}, u32[]{:S(2)}, u32[]{:S(2)}) collective-permute-start(bf16[240,1536]{1,0:T(8,128)(2,1)S(1)} %get-tuple-element.47), channel_id=1, source_target_pairs={{0,144},{128,16},{16,128},{144,0},{1,145},{129,17},{17,129},{145,1... | collective-permute-start | bytes 2211848 | tf_op jit(solution)/shard_map/ppermute | solution.py:32
  24.6 3.0 %collective-permute-start.2 = (bf16[352,384]{1,0:T(8,128)(2,1)S(1)}, bf16[352,384]{1,0:T(8,128)(2,1)S(1)}, u32[]{:S(2)}, u32[]{:S(2)}) collective-permute-start(bf16[352,384]{1,0:T(8,128)(2,1)S(1)} %get-tuple-element.43), channel_id=1, source_target_pairs={{0,96},{32,0},{64,32},{96,64},{1,97},{33,1},{65,33},{97,65},{2,98}... | collective-permute-start | bytes 811016 | tf_op jit(solution)/shard_map/ppermute | solution.py:27
  27.6 0.6 collective-permute-start.3
  28.3 1.0 collective-permute-start.4
  29.2 9.9 %collective-permute-done.2.a1 = bf16[352,384]{1,0:T(8,128)(2,1)S(1)} collective-permute-done((bf16[352,384]{1,0:T(8,128)(2,1)S(1)}, bf16[352,384]{1,0:T(8,128)(2,1)S(1)}, u32[]{:S(2)}, u32[]{:S(2)}) %collective-permute-start.2) | collective-permute-done | bytes 270368 | tf_op jit(solution)/shard_map/ppermute | solution.py:27
  39.2 3.7 %collective-permute-done.4.a3 = bf16[352,384]{1,0:T(8,128)(2,1)S(1)} collective-permute-done((bf16[352,384]{1,0:T(8,128)(2,1)S(1)}, bf16[352,384]{1,0:T(8,128)(2,1)S(1)}, u32[]{:S(2)}, u32[]{:S(2)}) %collective-permute-start.4) | collective-permute-done | bytes 270368 | tf_op jit(solution)/shard_map/ppermute | solution.py:27
  42.9 1.0 shard_map.112
  43.9 1.9 %collective-permute-start.7 = (bf16[240,384]{1,0:T(8,128)(2,1)S(1)}, bf16[240,384]{1,0:T(8,128)(2,1)S(1)}, u32[]{:S(2)}, u32[]{:S(2)}) collective-permute-start(bf16[240,384]{1,0:T(8,128)(2,1)S(1)} %get-tuple-element.52), channel_id=1, source_target_pairs={{0,96},{32,0},{64,32},{96,64},{1,97},{33,1},{65,33},{97,65},{2,98}... | collective-permute-start | bytes 552968 | tf_op jit(solution)/shard_map/ppermute | solution.py:27
  45.7 1.5 %collective-permute-start.6 = (bf16[400,384]{1,0:T(8,128)(2,1)S(1)}, bf16[400,384]{1,0:T(8,128)(2,1)S(1)}, u32[]{:S(2)}, u32[]{:S(2)}) collective-permute-start(bf16[400,384]{1,0:T(8,128)(2,1)S(1)} %get-tuple-element.49), channel_id=1, source_target_pairs={{0,144},{128,16},{16,128},{144,0},{1,145},{129,17},{17,129},{145,1... | collective-permute-start | bytes 921608 | tf_op jit(solution)/shard_map/ppermute | solution.py:32
  47.2 3.1 %collective-permute-start.10 = (bf16[256,384]{1,0:T(8,128)(2,1)S(1)}, bf16[256,384]{1,0:T(8,128)(2,1)S(1)}, u32[]{:S(2)}, u32[]{:S(2)}) collective-permute-start(bf16[256,384]{1,0:T(8,128)(2,1)S(1)} %slice.9.i0), channel_id=1, source_target_pairs={{0,128},{128,0},{1,129},{129,1},{2,130},{130,2},{3,131},{131,3},{4... | collective-permute-start | bytes 589832 | tf_op jit(solution)/shard_map/ppermute | solution.py:36
  50.3 0.6 collective-permute-start.8
  51.0 1.0 collective-permute-start.9
  51.9 6.9 %collective-permute-done.8.b2 = bf16[240,384]{1,0:T(8,128)(2,1)S(1)} collective-permute-done((bf16[240,384]{1,0:T(8,128)(2,1)S(1)}, bf16[240,384]{1,0:T(8,128)(2,1)S(1)}, u32[]{:S(2)}, u32[]{:S(2)}) %collective-permute-start.8) | collective-permute-done | bytes 184352 | tf_op jit(solution)/shard_map/ppermute | solution.py:27
  58.9 1.9 %collective-permute-done.9.b3 = bf16[240,384]{1,0:T(8,128)(2,1)S(1)} collective-permute-done((bf16[240,384]{1,0:T(8,128)(2,1)S(1)}, bf16[240,384]{1,0:T(8,128)(2,1)S(1)}, u32[]{:S(2)}, u32[]{:S(2)}) %collective-permute-start.9) | collective-permute-done | bytes 184352 | tf_op jit(solution)/shard_map/ppermute | solution.py:27
  60.8 0.7 shard_map.113.weight
  61.5 0.7 copy-done.7
  62.2 0.7 copy-done.9
  63.0 1.6 %collective-permute-start.21 = (bf16[8,192,384]{2,1,0:T(8,128)(2,1)S(1)}, bf16[8,192,384]{2,1,0:T(8,128)(2,1)}, u32[]{:S(2)}, u32[]{:S(2)}) collective-permute-start(bf16[8,192,384]{2,1,0:T(8,128)(2,1)S(1)} %slice.11.w), channel_id=1, source_target_pairs={{0,144},{128,16},{16,128},{144,0},{1,145},{129,17},{17,129},{145,1... | collective-permute-start | bytes 3538952 | tf_op jit(solution)/shard_map/ppermute | solution.py:32
  66.3 2.4 %shard_map.115 = (f32[192,384]{1,0:T(8,128)S(1)}, bf16[192,384]{1,0:T(8,128)(2,1)}, bf16[192,384]{1,0:T(8,128)(2,1)}, bf16[192,384]{1,0:T(8,128)(2,1)S(1)}, f32[...) custom-call(s32[5]{0:T(128)S(1)} %stack.23.place, f32[1,2]{1,0:T(1,128)S(1)} %maximum_bitcast_fusion.knobs, ...), custom_call_target="tpu_custom_call" | custom-call | flops 452984832 | bytes 4288520 | tf_op jit(solution)/shard_map/pallas_call | solution.py:73
  68.8 0.7 copy-done.5
  69.5 0.7 copy-done.18
  70.7 1.1 collective-permute-done.13.t_in
  71.7 0.6 shard_map.116
  72.4 0.8 copy-done.2
  73.2 7.3 %all-to-all-start.1 = ((bf16[8,96,384]{2,1,0:T(8,128)(2,1)}), bf16[8,96,384]{2,1,0:T(8,128)(2,1)S(1)}, u32[]{:S(2)}, u32[]{:S(2)}) async-start(bf16[8,96,384]{2,1,0:T(8,128)(2,1)} %copy-done.2), calls=%async_computation.1 | async-start | bytes 1179648 | tf_op jit(solution)/shard_map/all_to_all | solution.py:44
  81.0 2.9 %collective-permute-start.15 = (bf16[192,384]{1,0:T(8,128)(2,1)}, bf16[192,384]{1,0:T(8,128)(2,1)S(1)}, u32[]{:S(2)}, u32[]{:S(2)}) collective-permute-start(bf16[192,384]{1,0:T(8,128)(2,1)} %get-tuple-element.67), channel_id=1, source_target_pairs={{0,128},{128,0},{1,129},{129,1},{2,130},{130,2},{3,131},{131,3},{4... | collective-permute-start | bytes 442376 | tf_op jit(solution)/shard_map/ppermute | solution.py:36
  83.9 1.6 %collective-permute-start.16 = (bf16[192,384]{1,0:T(8,128)(2,1)S(1)}, bf16[192,384]{1,0:T(8,128)(2,1)S(1)}, u32[]{:S(2)}, u32[]{:S(2)}) collective-permute-start(bf16[192,384]{1,0:T(8,128)(2,1)S(1)} %copy-done.19), channel_id=1, source_target_pairs={{0,16},{16,0},{1,17},{17,1},{2,18},{18,2},{3,19},{19,3},{4,20},{20... | collective-permute-start | bytes 442376 | tf_op jit(solution)/shard_map/ppermute | solution.py:40
  85.5 11.1 %collective-permute-done.14.g1 = bf16[192,384]{1,0:T(8,128)(2,1)S(1)} collective-permute-done((bf16[192,384]{1,0:T(8,128)(2,1)}, bf16[192,384]{1,0:T(8,128)(2,1)S(1)}, u32[]{:S(2)}, u32[]{:S(2)}) %collective-permute-start.14) | collective-permute-done | bytes 147488 | tf_op jit(solution)/shard_map/ppermute | solution.py:32
  96.6 0.7 copy-done.12
  97.4 4.2 %shard_map.119.rest_0_ = bf16[384,1536]{1,0:T(8,128)(2,1)} custom-call(s32[5]{0:T(128)S(1)} %stack.23.place, bf16[384,1536]{1,0:T(8,128)(2,1)S(1)} %copy-done.1, bf16[8,192,384]{2,1,0:T(8,128)(2,1)S(1)} %slice.11.w, bf16[8,192,384]{2,1,0:T(8,128)(2,1)} %collective-permute-done.20.other_w), custom_call_target="tpu_custom_call" | custom-call | flops 905969664 | bytes 6291456 | tf_op jit(solution)/shard_map/pallas_call | solution.py:240
  101.6 1.5 %shard_map.120 = (f32[16,1152]{1,0:T(8,128)}, f32[8,48,384]{2,1,0:T(8,128)}) custom-call(s32[5]{0:T(128)S(1)} %stack.23.place, bf16[8,96,384]{2,1,0:T(8,128)(2,1)S(1)} %all-to-all-done.1.back, f32[16,1152]{1,0:T(8,128)S(1)} %copy-done.4), custom_call_target="tpu_custom_call" | custom-call | bytes 1327104 | tf_op jit(solution)/shard_map/pallas_call | solution.py:73
  103.2 6.0 %all-to-all-start.2 = ((f32[8,48,384]{2,1,0:T(8,128)}), f32[8,48,384]{2,1,0:T(8,128)S(1)}, u32[]{:S(2)}, u32[]{:S(2)}) async-start(f32[8,48,384]{2,1,0:T(8,128)} %get-tuple-element.78), calls=%async_computation.2 | async-start | bytes 1179648 | tf_op jit(solution)/shard_map/all_to_all | solution.py:44
  109.9 1.5 %collective-permute-start.17 = (bf16[48,384]{1,0:T(8,128)(2,1)S(1)}, bf16[48,384]{1,0:T(8,128)(2,1)S(1)}, u32[]{:S(2)}, u32[]{:S(2)}) collective-permute-start(bf16[48,384]{1,0:T(8,128)(2,1)S(1)} %get-tuple-element.71), channel_id=1, source_target_pairs={{0,32},{32,64},{64,96},{96,0},{1,33},{33,65},{65,97},{97,1},{2,34}... | collective-permute-start | bytes 110600 | tf_op jit(solution)/shard_map/ppermute | solution.py:27
  111.4 2.7 %collective-permute-start.18 = (bf16[48,384]{1,0:T(8,128)(2,1)S(1)}, bf16[48,384]{1,0:T(8,128)(2,1)S(1)}, u32[]{:S(2)}, u32[]{:S(2)}) collective-permute-start(bf16[48,384]{1,0:T(8,128)(2,1)S(1)} %get-tuple-element.72), channel_id=1, source_target_pairs={{0,64},{32,96},{64,0},{96,32},{1,65},{33,97},{65,1},{97,33},{2,66}... | collective-permute-start | bytes 110600 | tf_op jit(solution)/shard_map/ppermute | solution.py:27
  114.1 1.5 %collective-permute-start.19 = (bf16[48,384]{1,0:T(8,128)(2,1)S(1)}, bf16[48,384]{1,0:T(8,128)(2,1)S(1)}, u32[]{:S(2)}, u32[]{:S(2)}) collective-permute-start(bf16[48,384]{1,0:T(8,128)(2,1)S(1)} %get-tuple-element.73), channel_id=1, source_target_pairs={{0,96},{32,0},{64,32},{96,64},{1,97},{33,1},{65,33},{97,65},{2,98}... | collective-permute-start | bytes 110600 | tf_op jit(solution)/shard_map/ppermute | solution.py:27
  115.5 4.8 %collective-permute-done.17.h1 = bf16[48,384]{1,0:T(8,128)(2,1)S(1)} collective-permute-done((bf16[48,384]{1,0:T(8,128)(2,1)S(1)}, bf16[48,384]{1,0:T(8,128)(2,1)S(1)}, u32[]{:S(2)}, u32[]{:S(2)}) %collective-permute-start.17) | collective-permute-done | bytes 36896 | tf_op jit(solution)/shard_map/ppermute | solution.py:27
  120.4 1.0 collective-permute-done.18.h2
  121.4 1.4 %shard_map.118 = f32[16,1152]{1,0:T(8,128)} custom-call(s32[5]{0:T(128)S(1)} %stack.23.place, f32[48,384]{1,0:T(8,128)S(1)} %get-tuple-element.70.h0, bf16[48,384]{1,0:T(8,128)(2,1)S(1)} %collective-permute-done.17.h1, bf16[48,384]{1,0:T(8,128)(2,1)S(1)} %collective-permute-done.18.h2, bf16[48,384]{1,0:T(8,128)(2,1)S(1)} %collective-permute-done.19.h3, ...), custom_call_target="tpu_custom_call" | custom-call | bytes 331776 | tf_op jit(solution)/shard_map/pallas_call | solution.py:73
  122.8 4.6 %shard_map.121 = bf16[384,1536]{1,0:T(8,128)(2,1)} custom-call(s32[5]{0:T(128)S(1)} %stack.23.place, bf16[384,1536]{1,0:T(8,128)(2,1)S(1)} %copy-done.1, bf16[8,192,384]{2,1,0:T(8,128)(2,1)} %collective-permute-done.21.w, bf16[8,192,384]{2,1,0:T(8,128)(2,1)} %collective-permute-done.22.other_w, ...), custom_call_target="tpu_custom_call", output_to_operand_aliasing={{}: (4, {})} | custom-call | flops 905969664 | bytes 6291456 | tf_op jit(solution)/shard_map/pallas_call | solution.py:240
  127.3 1.3 shard_map.122
  (63 shorter events, 2.9 us)
Async XLA Ops:
  0.7 0.9 copy-start.3
  1.6 0.9 copy-start.11
  4.3 8.6 %copy-start = (bf16[384,1536]{1,0:T(8,128)(2,1)S(1)}, bf16[384,1536]{1,0:T(8,128)(2,1)}, u32[]{:S(2)}) copy-start(bf16[384,1536]{1,0:T(8,128)(2,1)} %adj.5) | copy-start | bytes 3538948
  4.3 13.1 %copy-start.16 = (f32[16,1152]{1,0:T(8,128)S(1)}, f32[16,1152]{1,0:T(8,128)}, u32[]{:S(2)}) copy-start(f32[16,1152]{1,0:T(8,128)} %pic.3) | copy-start | bytes 221188
  4.3 13.1 %copy-start.20 = (s32[16]{0:T(128)S(1)}, s32[16]{0:T(128)}, u32[]{:S(2)}) copy-start(s32[16]{0:T(128)} %ids.1) | copy-start | bytes 196
  4.3 58.5 %all-to-all-start = ((bf16[8,240,384]{2,1,0:T(8,128)(2,1)}), bf16[8,240,384]{2,1,0:T(8,128)(2,1)S(1)}, u32[]{:S(2)}, u32[]{:S(2)}) async-start(bf16[8,240,384]{2,1,0:T(8,128)(2,1)} %shard_map.114), calls=%async_computation | async-start | bytes 2949120 | tf_op jit(solution)/shard_map/all_to_all | solution.py:44
  12.9 3.7 %collective-permute-start = (bf16[384,1536]{1,0:T(8,128)(2,1)}, bf16[384,1536]{1,0:T(8,128)(2,1)S(1)}, u32[]{:S(2)}, u32[]{:S(2)}) collective-permute-start(bf16[384,1536]{1,0:T(8,128)(2,1)} %tokens.1), channel_id=1, source_target_pairs={{0,1},{1,0},{2,3},{3,2},{4,5},{5,4},{6,7},{7,6},{8,9},{9,8},{10,11... | collective-permute-start | bytes 3538952 | tf_op jit(solution)/shard_map/ppermute | solution.py:22
  13.0 4.5 %collective-permute-start.1 = (bf16[384,1536]{1,0:T(8,128)(2,1)S(1)}, bf16[384,1536]{1,0:T(8,128)(2,1)S(1)}, u32[]{:S(2)}, u32[]{:S(2)}) collective-permute-start(bf16[384,1536]{1,0:T(8,128)(2,1)S(1)} %copy-done), channel_id=1, source_target_pairs={{0,1},{1,0},{2,3},{3,2},{4,5},{5,4},{6,7},{7,6},{8,9},{9,8},{10,11... | collective-permute-start | bytes 3538952 | tf_op jit(solution)/shard_map/ppermute | solution.py:22
  17.5 1.3 copy-start.17
  23.0 19.8 %collective-permute-start.5 = (bf16[240,1536]{1,0:T(8,128)(2,1)S(1)}, bf16[240,1536]{1,0:T(8,128)(2,1)S(1)}, u32[]{:S(2)}, u32[]{:S(2)}) collective-permute-start(bf16[240,1536]{1,0:T(8,128)(2,1)S(1)} %get-tuple-element.47), channel_id=1, source_target_pairs={{0,144},{128,16},{16,128},{144,0},{1,145},{129,17},{17,129},{145,1... | collective-permute-start | bytes 2211848 | tf_op jit(solution)/shard_map/ppermute | solution.py:32
  24.6 14.6 %collective-permute-start.2 = (bf16[352,384]{1,0:T(8,128)(2,1)S(1)}, bf16[352,384]{1,0:T(8,128)(2,1)S(1)}, u32[]{:S(2)}, u32[]{:S(2)}) collective-permute-start(bf16[352,384]{1,0:T(8,128)(2,1)S(1)} %get-tuple-element.43), channel_id=1, source_target_pairs={{0,96},{32,0},{64,32},{96,64},{1,97},{33,1},{65,33},{97,65},{2,98}... | collective-permute-start | bytes 811016 | tf_op jit(solution)/shard_map/ppermute | solution.py:27
  27.6 11.6 %collective-permute-start.3 = (bf16[352,384]{1,0:T(8,128)(2,1)S(1)}, bf16[352,384]{1,0:T(8,128)(2,1)S(1)}, u32[]{:S(2)}, u32[]{:S(2)}) collective-permute-start(bf16[352,384]{1,0:T(8,128)(2,1)S(1)} %get-tuple-element.44), channel_id=1, source_target_pairs={{0,64},{32,96},{64,0},{96,32},{1,65},{33,97},{65,1},{97,33},{2,66}... | collective-permute-start | bytes 811016 | tf_op jit(solution)/shard_map/ppermute | solution.py:27
  28.3 14.6 %collective-permute-start.4 = (bf16[352,384]{1,0:T(8,128)(2,1)S(1)}, bf16[352,384]{1,0:T(8,128)(2,1)S(1)}, u32[]{:S(2)}, u32[]{:S(2)}) collective-permute-start(bf16[352,384]{1,0:T(8,128)(2,1)S(1)} %get-tuple-element.45), channel_id=1, source_target_pairs={{0,32},{32,64},{64,96},{96,0},{1,33},{33,65},{65,97},{97,1},{2,34}... | collective-permute-start | bytes 811016 | tf_op jit(solution)/shard_map/ppermute | solution.py:27
  43.9 7.1 %collective-permute-start.7 = (bf16[240,384]{1,0:T(8,128)(2,1)S(1)}, bf16[240,384]{1,0:T(8,128)(2,1)S(1)}, u32[]{:S(2)}, u32[]{:S(2)}) collective-permute-start(bf16[240,384]{1,0:T(8,128)(2,1)S(1)} %get-tuple-element.52), channel_id=1, source_target_pairs={{0,96},{32,0},{64,32},{96,64},{1,97},{33,1},{65,33},{97,65},{2,98}... | collective-permute-start | bytes 552968 | tf_op jit(solution)/shard_map/ppermute | solution.py:27
  45.7 15.1 %collective-permute-start.6 = (bf16[400,384]{1,0:T(8,128)(2,1)S(1)}, bf16[400,384]{1,0:T(8,128)(2,1)S(1)}, u32[]{:S(2)}, u32[]{:S(2)}) collective-permute-start(bf16[400,384]{1,0:T(8,128)(2,1)S(1)} %get-tuple-element.49), channel_id=1, source_target_pairs={{0,144},{128,16},{16,128},{144,0},{1,145},{129,17},{17,129},{145,1... | collective-permute-start | bytes 921608 | tf_op jit(solution)/shard_map/ppermute | solution.py:32
  47.2 14.2 %collective-permute-start.10 = (bf16[256,384]{1,0:T(8,128)(2,1)S(1)}, bf16[256,384]{1,0:T(8,128)(2,1)S(1)}, u32[]{:S(2)}, u32[]{:S(2)}) collective-permute-start(bf16[256,384]{1,0:T(8,128)(2,1)S(1)} %slice.9.i0), channel_id=1, source_target_pairs={{0,128},{128,0},{1,129},{129,1},{2,130},{130,2},{3,131},{131,3},{4... | collective-permute-start | bytes 589832 | tf_op jit(solution)/shard_map/ppermute | solution.py:36
  50.3 11.8 %collective-permute-start.11 = (bf16[256,384]{1,0:T(8,128)(2,1)S(1)}, bf16[256,384]{1,0:T(8,128)(2,1)S(1)}, u32[]{:S(2)}, u32[]{:S(2)}) collective-permute-start(bf16[256,384]{1,0:T(8,128)(2,1)S(1)} %slice.9.i0), channel_id=1, source_target_pairs={{0,16},{16,0},{1,17},{17,1},{2,18},{18,2},{3,19},{19,3},{4,20},{20... | collective-permute-start | bytes 589832 | tf_op jit(solution)/shard_map/ppermute | solution.py:40
  50.3 8.5 %collective-permute-start.8 = (bf16[240,384]{1,0:T(8,128)(2,1)S(1)}, bf16[240,384]{1,0:T(8,128)(2,1)S(1)}, u32[]{:S(2)}, u32[]{:S(2)}) collective-permute-start(bf16[240,384]{1,0:T(8,128)(2,1)S(1)} %get-tuple-element.53), channel_id=1, source_target_pairs={{0,64},{32,96},{64,0},{96,32},{1,65},{33,97},{65,1},{97,33},{2,66}... | collective-permute-start | bytes 552968 | tf_op jit(solution)/shard_map/ppermute | solution.py:27
  51.0 9.8 %collective-permute-start.9 = (bf16[240,384]{1,0:T(8,128)(2,1)S(1)}, bf16[240,384]{1,0:T(8,128)(2,1)S(1)}, u32[]{:S(2)}, u32[]{:S(2)}) collective-permute-start(bf16[240,384]{1,0:T(8,128)(2,1)S(1)} %get-tuple-element.54), channel_id=1, source_target_pairs={{0,32},{32,64},{64,96},{96,0},{1,33},{33,65},{65,97},{97,1},{2,34}... | collective-permute-start | bytes 552968 | tf_op jit(solution)/shard_map/ppermute | solution.py:27
  61.5 0.7 copy-start.7
  62.2 0.7 copy-start.9
  62.8 3.5 %copy-start.8 = (bf16[256,384]{1,0:T(8,128)(2,1)S(1)}, bf16[256,384]{1,0:T(8,128)(2,1)}, u32[]{:S(2)}) copy-start(bf16[256,384]{1,0:T(8,128)(2,1)} %copy-done.7) | copy-start | bytes 589828
  62.8 3.5 %copy-start.10 = (bf16[256,384]{1,0:T(8,128)(2,1)S(1)}, bf16[256,384]{1,0:T(8,128)(2,1)}, u32[]{:S(2)}) copy-start(bf16[256,384]{1,0:T(8,128)(2,1)} %copy-done.9) | copy-start | bytes 589828
  63.0 34.3 %collective-permute-start.21 = (bf16[8,192,384]{2,1,0:T(8,128)(2,1)S(1)}, bf16[8,192,384]{2,1,0:T(8,128)(2,1)}, u32[]{:S(2)}, u32[]{:S(2)}) collective-permute-start(bf16[8,192,384]{2,1,0:T(8,128)(2,1)S(1)} %slice.11.w), channel_id=1, source_target_pairs={{0,144},{128,16},{16,128},{144,0},{1,145},{129,17},{17,129},{145,1... | collective-permute-start | bytes 3538952 | tf_op jit(solution)/shard_map/ppermute | solution.py:32
  64.7 1.7 %collective-permute-start.12 = (bf16[8,48,384]{2,1,0:T(8,128)(2,1)S(1)}, bf16[8,48,384]{2,1,0:T(8,128)(2,1)S(1)}, u32[]{:S(2)}, u32[]{:S(2)}) collective-permute-start(bf16[8,48,384]{2,1,0:T(8,128)(2,1)S(1)} %slice.10), channel_id=1, source_target_pairs={{0,1},{1,0},{2,3},{3,2},{4,5},{5,4},{6,7},{7,6},{8,9},{9,8},{10,11... | collective-permute-start | bytes 884744 | tf_op jit(solution)/shard_map/ppermute | solution.py:22
  68.8 0.7 copy-start.5
  69.5 0.7 copy-start.18
  70.2 1.6 %collective-permute-start.13 = (bf16[128,1152]{1,0:T(8,128)(2,1)S(1)}, bf16[128,1152]{1,0:T(8,128)(2,1)S(1)}, u32[]{:S(2)}, u32[]{:S(2)}) collective-permute-start(bf16[128,1152]{1,0:T(8,128)(2,1)S(1)} %get-tuple-element.62), channel_id=1, source_target_pairs={{0,1},{1,0},{2,3},{3,2},{4,5},{5,4},{6,7},{7,6},{8,9},{9,8},{10,11... | collective-permute-start | bytes 884744 | tf_op jit(solution)/shard_map/ppermute | solution.py:22
  70.5 26.9 %collective-permute-start.20 = (bf16[8,192,384]{2,1,0:T(8,128)(2,1)S(1)}, bf16[8,192,384]{2,1,0:T(8,128)(2,1)}, u32[]{:S(2)}, u32[]{:S(2)}) collective-permute-start(bf16[8,192,384]{2,1,0:T(8,128)(2,1)S(1)} %slice.11.w), channel_id=1, source_target_pairs={{0,1},{1,0},{2,3},{3,2},{4,5},{5,4},{6,7},{7,6},{8,9},{9,8},{10,11... | collective-permute-start | bytes 3538952 | tf_op jit(solution)/shard_map/ppermute | solution.py:22
  71.7 25.6 %copy-start.1 = (bf16[384,1536]{1,0:T(8,128)(2,1)S(1)}, bf16[384,1536]{1,0:T(8,128)(2,1)}, u32[]{:S(2)}) copy-start(bf16[384,1536]{1,0:T(8,128)(2,1)} %adj.5) | copy-start | bytes 3538948
  72.4 0.8 copy-start.2
  73.2 10.7 %copy-start.19 = (bf16[192,384]{1,0:T(8,128)(2,1)S(1)}, bf16[192,384]{1,0:T(8,128)(2,1)}, u32[]{:S(2)}) copy-start(bf16[192,384]{1,0:T(8,128)(2,1)} %copy-done.18) | copy-start | bytes 442372
  73.2 28.4 %all-to-all-start.1 = ((bf16[8,96,384]{2,1,0:T(8,128)(2,1)}), bf16[8,96,384]{2,1,0:T(8,128)(2,1)S(1)}, u32[]{:S(2)}, u32[]{:S(2)}) async-start(bf16[8,96,384]{2,1,0:T(8,128)(2,1)} %copy-done.2), calls=%async_computation.1 | async-start | bytes 1179648 | tf_op jit(solution)/shard_map/all_to_all | solution.py:44
  80.5 16.0 %collective-permute-start.14 = (bf16[192,384]{1,0:T(8,128)(2,1)}, bf16[192,384]{1,0:T(8,128)(2,1)S(1)}, u32[]{:S(2)}, u32[]{:S(2)}) collective-permute-start(bf16[192,384]{1,0:T(8,128)(2,1)} %get-tuple-element.65), channel_id=1, source_target_pairs={{0,144},{128,16},{16,128},{144,0},{1,145},{129,17},{17,129},{145,1... | collective-permute-start | bytes 442376 | tf_op jit(solution)/shard_map/ppermute | solution.py:32
  81.0 15.6 %collective-permute-start.15 = (bf16[192,384]{1,0:T(8,128)(2,1)}, bf16[192,384]{1,0:T(8,128)(2,1)S(1)}, u32[]{:S(2)}, u32[]{:S(2)}) collective-permute-start(bf16[192,384]{1,0:T(8,128)(2,1)} %get-tuple-element.67), channel_id=1, source_target_pairs={{0,128},{128,0},{1,129},{129,1},{2,130},{130,2},{3,131},{131,3},{4... | collective-permute-start | bytes 442376 | tf_op jit(solution)/shard_map/ppermute | solution.py:36
  83.9 13.4 %collective-permute-start.16 = (bf16[192,384]{1,0:T(8,128)(2,1)S(1)}, bf16[192,384]{1,0:T(8,128)(2,1)S(1)}, u32[]{:S(2)}, u32[]{:S(2)}) collective-permute-start(bf16[192,384]{1,0:T(8,128)(2,1)S(1)} %copy-done.19), channel_id=1, source_target_pairs={{0,16},{16,0},{1,17},{17,1},{2,18},{18,2},{3,19},{19,3},{4,20},{20... | collective-permute-start | bytes 442376 | tf_op jit(solution)/shard_map/ppermute | solution.py:40
  85.4 16.2 %copy-start.4 = (f32[16,1152]{1,0:T(8,128)S(1)}, f32[16,1152]{1,0:T(8,128)}, u32[]{:S(2)}) copy-start(f32[16,1152]{1,0:T(8,128)} %cap.3) | copy-start | bytes 221188
  96.6 0.7 copy-start.12
  97.2 4.4 %copy-start.14 = (bf16[192,384]{1,0:T(8,128)(2,1)}, bf16[192,384]{1,0:T(8,128)(2,1)S(1)}, u32[]{:S(2)}) copy-start(bf16[192,384]{1,0:T(8,128)(2,1)S(1)} %collective-permute-done.16.g3) | copy-start | bytes 442372
  97.2 25.5 %collective-permute-start.22 = (bf16[8,192,384]{2,1,0:T(8,128)(2,1)}, bf16[8,192,384]{2,1,0:T(8,128)(2,1)}, u32[]{:S(2)}, u32[]{:S(2)}) collective-permute-start(bf16[8,192,384]{2,1,0:T(8,128)(2,1)} %collective-permute-done.21.w), channel_id=1, source_target_pairs={{0,1},{1,0},{2,3},{3,2},{4,5},{5,4},{6,7},{7,6},{8,9},{9,8},{10,11... | collective-permute-start | bytes 3538952 | tf_op jit(solution)/shard_map/ppermute | solution.py:22
  101.6 7.6 %copy-start.6 = (f32[192,384]{1,0:T(8,128)S(1)}, f32[192,384]{1,0:T(8,128)}, u32[]{:S(2)}) copy-start(f32[192,384]{1,0:T(8,128)} %copy-done.5) | copy-start | bytes 884740
  101.6 7.6 %copy-start.13 = (bf16[192,384]{1,0:T(8,128)(2,1)S(1)}, bf16[192,384]{1,0:T(8,128)(2,1)}, u32[]{:S(2)}) copy-start(bf16[192,384]{1,0:T(8,128)(2,1)} %copy-done.12) | copy-start | bytes 442372
  101.6 7.6 %copy-start.15 = (bf16[192,384]{1,0:T(8,128)(2,1)S(1)}, bf16[192,384]{1,0:T(8,128)(2,1)}, u32[]{:S(2)}) copy-start(bf16[192,384]{1,0:T(8,128)(2,1)} %copy-done.14) | copy-start | bytes 442372
  103.2 24.2 %all-to-all-start.2 = ((f32[8,48,384]{2,1,0:T(8,128)}), f32[8,48,384]{2,1,0:T(8,128)S(1)}, u32[]{:S(2)}, u32[]{:S(2)}) async-start(f32[8,48,384]{2,1,0:T(8,128)} %get-tuple-element.78), calls=%async_computation.2 | async-start | bytes 1179648 | tf_op jit(solution)/shard_map/all_to_all | solution.py:44
  109.9 10.5 %collective-permute-start.17 = (bf16[48,384]{1,0:T(8,128)(2,1)S(1)}, bf16[48,384]{1,0:T(8,128)(2,1)S(1)}, u32[]{:S(2)}, u32[]{:S(2)}) collective-permute-start(bf16[48,384]{1,0:T(8,128)(2,1)S(1)} %get-tuple-element.71), channel_id=1, source_target_pairs={{0,32},{32,64},{64,96},{96,0},{1,33},{33,65},{65,97},{97,1},{2,34}... | collective-permute-start | bytes 110600 | tf_op jit(solution)/shard_map/ppermute | solution.py:27
  111.4 10.0 %collective-permute-start.18 = (bf16[48,384]{1,0:T(8,128)(2,1)S(1)}, bf16[48,384]{1,0:T(8,128)(2,1)S(1)}, u32[]{:S(2)}, u32[]{:S(2)}) collective-permute-start(bf16[48,384]{1,0:T(8,128)(2,1)S(1)} %get-tuple-element.72), channel_id=1, source_target_pairs={{0,64},{32,96},{64,0},{96,32},{1,65},{33,97},{65,1},{97,33},{2,66}... | collective-permute-start | bytes 110600 | tf_op jit(solution)/shard_map/ppermute | solution.py:27
  114.1 7.3 %collective-permute-start.19 = (bf16[48,384]{1,0:T(8,128)(2,1)S(1)}, bf16[48,384]{1,0:T(8,128)(2,1)S(1)}, u32[]{:S(2)}, u32[]{:S(2)}) collective-permute-start(bf16[48,384]{1,0:T(8,128)(2,1)S(1)} %get-tuple-element.73), channel_id=1, source_target_pairs={{0,96},{32,0},{64,32},{96,64},{1,97},{33,1},{65,33},{97,65},{2,98}... | collective-permute-start | bytes 110600 | tf_op jit(solution)/shard_map/ppermute | solution.py:27

commit v4 on v3

--- a/solution.py
+++ b/solution.py
@@ -14,7 +14,7 @@
 SIZES = (2, 4, 2, 8, 2)
 ROW = (("xl", "xh"), (0, 2, 1, 3))
 COLUMN = ("y", (0, 1, 2, 3))
-CUT = 144
+CUT = 192
 BACK = (((1,), (1,)), ((), ()))
 
 
@@ -87,10 +87,11 @@
 
 def text_kernel(place, cap, rows, z_out):
     text = fold(unit_rows(cap[...])[0].astype(bf16))
+    piece = rows[:, pl.ds(pl.multiple_of(place[1] * 768, 384), 768)]
     for k in range(8):
         z_out[k, :48, :] = text
-        for j in range(4):
-            z_out[k, 48 + j * 48 : 96 + j * 48, :] = rows[:, j * 384 : j * 384 + 384]
+        z_out[k, 48:96, :] = piece[:, :384]
+        z_out[k, 96:, :] = piece[:, 384:]
 
 
 def weight_kernel(place, ids, pic, tokens, other_tokens, adj, other_adj, *rest):
@@ -123,8 +124,9 @@
 
 
 def first_sum_kernel(
-    place, a0, a1, a2, a3, b_own, b_in, image, a_own, near, b0, b1, b2, b3, total
+    place, a0, a1, a2, a3, b_own, b_in, image, a_own, near, column, *rest
 ):
+    b0, b1, b2, b3, total = rest
     y, xh = place[0], place[2]
     total[...] = a0[...].astype(f32)
     for part in (a1, a2, a3):
@@ -135,22 +137,22 @@
         at = pl.ds(pl.multiple_of(((y - k) & 3) * 384, 384), 384)
         both = b_own[:, at].astype(f32) + b_in[:, at].astype(f32)
         out[...] = both.astype(out.dtype)
-    near[CUT : CUT + 64, :] = image[...]
-    for k, part in enumerate((a1, a2, a3)):
-        near[CUT + 64 + 64 * k : CUT + 128 + 64 * k, :] = part[2 * CUT :, :]
-
-
-def second_sum_kernel(place, a_own, near_in, b0, b1, b2, b3, out):
-    out[:CUT, :] = (a_own[...] + near_in[:CUT, :].astype(f32)).astype(bf16)
+    for target, first in ((near, CUT), (column, 0)):
+        target[first : first + 64, :] = image[...]
+        for k, part in enumerate((a1, a2, a3)):
+            at = first + 64 + 64 * k
+            target[at : at + 64, :] = part[2 * CUT :, :]
+
+
+def tile_kernel(place, sharp, bias, i0, i1, i2, i3, other_text, along_z, a_own, *rest):
+    b0, b1, b2, b3, rows, weight, g0, g1, g2, g3, t_own, t_out, images, texts, ids = rest
+    for k in range(8):
+        rows[k] = along_z[k, 48:, :]
+    weight[:CUT, :] = (a_own[...] + i1[:CUT, :].astype(f32)).astype(bf16)
     total = b0[...]
     for part in (b1, b2, b3):
         total = total + part[...].astype(f32)
-    out[CUT:, :] = total.astype(bf16)
-
-
-def tile_kernel(
-    place, knobs, i0, i1, i2, i3, text, other_text, g0, g1, g2, g3, t_own, t_out, images, texts, ids
-):
+    weight[CUT:, :] = total.astype(bf16)
     y, xl, xh, c = place[0], place[1], place[2], place[3]
     for k, part in enumerate((i0, i1, i2, i3)):
         first = part.shape[0] - 256
@@ -161,9 +163,9 @@
             split = part[here + 48 : here + 64, :128].astype(f32)
             ids[at : at + 16, :] = (split[:, 0:1] * 64.0 + split[:, 1:2]).astype(jnp.int32)
     for k in range(8):
-        texts[k * 16 : k * 16 + 16, :] = unfold(text[k, :48, :])
+        texts[k * 16 : k * 16 + 16, :] = unfold(along_z[k, :48, :])
         texts[128 + k * 16 : 144 + k * 16, :] = unfold(other_text[k, :, :])
-    sharpness, offset = knobs[0, 0], knobs[0, 1]
+    sharpness, offset = sharp[0], bias[0]
     col = lax.broadcasted_iota(jnp.int32, (256, 256), 1)
     core = jnp.where(col < 128, c, 1 - c)
     first = ((xl * 4 + y) * 2 + xh) * 256
@@ -172,10 +174,10 @@
     labels = (ids[...] == index).astype(f32)
     weights = sharpness * (jax.nn.sigmoid(sharpness * dots + offset) - labels)
     half = weights.astype(bf16)
-    for k, out in enumerate((g0, g1, g2, g3)):
+    for k in range(4):
         part = jnp.dot(half[k * 64 : k * 64 + 64], texts[...], preferred_element_type=f32)
-        for j in range(4):
-            out[j * 48 : j * 48 + 48, :] = fold(part[j * 16 : j * 16 + 16]).astype(out.dtype)
+        for j, out in enumerate((g0, g1, g2, g3)):
+            out[k * 48 : k * 48 + 48, :] = fold(part[j * 16 : j * 16 + 16]).astype(out.dtype)
     half = weights.T.astype(bf16)
     t_own[...] = jnp.dot(half[:128], images[...], preferred_element_type=f32)
     t_out[...] = jnp.dot(half[128:], images[...], preferred_element_type=f32).astype(bf16)
@@ -188,7 +190,7 @@
         out[k, 48:, :] = weight[k * 48 : k * 48 + 48, :]
 
 
-def text_end_kernel(place, back, cap, grad, pieces):
+def middle_kernel(place, back, cap, g0, g1, g2, g3, grad, pieces, h0, h1, h2, h3):
     total = back[0].astype(f32)
     for k in range(1, 8):
         total = total + back[k].astype(f32)
@@ -196,9 +198,6 @@
     piece = total[48:] * (1.0 / math.sqrt(98304))
     for k in range(8):
         pieces[k] = piece
-
-
-def image_middle_kernel(place, g0, g1, g2, g3, h0, h1, h2, h3):
     total = g0[...]
     for part in (g1, g2, g3):
         total = total + part[...].astype(f32)
@@ -206,26 +205,23 @@
         out[...] = total[k * 48 : k * 48 + 48].astype(out.dtype)
 
 
-def image_end_kernel(place, h0, h1, h2, h3, pic, grad):
+def end_kernel(place, h0, h1, h2, h3, pic, pieces, image_grad, weight_grad):
     total = h0[...]
     for part in (h1, h2, h3):
         total = total + part[...].astype(f32)
-    grad[...] = back_through_norm(pic[...], unfold(total))
-
-
-def weight_end_kernel(place, pieces, grad):
+    image_grad[...] = back_through_norm(pic[...], unfold(total))
     for k in range(4):
-        grad[:, k * 384 : k * 384 + 384] = pieces[k] + pieces[4 + k]
-
-
-def project_kernel(place, adj, w, other_w, *rest):
+        weight_grad[:, k * 384 : k * 384 + 384] = pieces[k] + pieces[4 + k]
+
+
+def project_kernel(place, adj, w, w_pair, other, other_pair, *rest):
     out, rows = rest[-2:]
-    c = place[3]
-    for z in range(8):
-        for k in range(4):
-            at = slice(k * 384, k * 384 + 384)
-            rows[z * 2 + c, :, at] = w[z, k * 48 : k * 48 + 48, :]
-            rows[z * 2 + 1 - c, :, at] = other_w[z, k * 48 : k * 48 + 48, :]
+    xl, c = place[1], place[3]
+    for core, side, part in ((c, xl, w), (c, 1 - xl, w_pair), (1 - c, xl, other), (1 - c, 1 - xl, other_pair)):
+        for k in range(2):
+            at = pl.ds(pl.multiple_of(side * 768 + k * 384, 384), 384)
+            for z in range(8):
+                rows[z * 2 + core, :, at] = part[z, k * 48 : k * 48 + 48, :]
     for k in range(2):
         part = rows[k * 8 : k * 8 + 8].reshape(384, 1536)
         out[:, k * 384 : k * 384 + 384] = lax.dot_general(
@@ -233,10 +229,10 @@
         ).astype(bf16)
 
 
-def project(place, half, adj, w, other_w, before=None):
+def project(place, half, adj, parts, before=None):
     whole = pl.BlockSpec(memory_space=pltpu.VMEM)
-    operands = [adj, w, other_w] + ([] if before is None else [before])
-    in_specs = [whole] * 3 + ([] if before is None else [pl.BlockSpec(memory_space=pl.ANY)])
+    operands = [adj, *parts] + ([] if before is None else [before])
+    in_specs = [whole] * 5 + ([] if before is None else [pl.BlockSpec(memory_space=pl.ANY)])
     return pl.pallas_call(
         project_kernel,
         grid_spec=pltpu.PrefetchScalarGridSpec(
@@ -247,7 +243,7 @@
             scratch_shapes=[pltpu.VMEM((16, 48, 1536), bf16)],
         ),
         out_shape=shape(384, 1536),
-        input_output_aliases={} if before is None else {4: 0},
+        input_output_aliases={} if before is None else {6: 0},
         compiler_params=pltpu.CompilerParams(vmem_limit_bytes=16 * 2**20),
         cost_estimate=pl.CostEstimate(
             flops=2 * 384 * 768 * 1536, bytes_accessed=6 * 2**20, transcendentals=0
@@ -271,9 +267,9 @@
     other_tokens = swap_cores(heads_mixed_concluding)
 
     (along_z,) = call(
-        text_kernel, (shape(8, 240, 384),), place, caption_vectors_prenorm, dense_mapping_matrix
-    )
-    along_z = exchange(along_z, "z")
+        text_kernel, (shape(8, 144, 384),), place, caption_vectors_prenorm, dense_mapping_matrix
+    )
+    along_z = exchange(after(along_z, other_tokens, other_adjoint), "z")
 
     *a, b_own, b_out, image = call(
         weight_kernel,
@@ -301,11 +297,12 @@
     )
     b_in = swap_halves(b_out)
     a_in = [turn(a[k], COLUMN, -k) for k in (1, 2, 3)]
-    a_own, near, *b = call(
+    a_own, near, column, *b = call(
         first_sum_kernel,
         (
             shape(CUT, 384, dtype=f32),
             shape(CUT + 256, 384),
+            shape(256, 384),
             shape(384 - CUT, 384, dtype=f32),
             *[shape(384 - CUT, 384)] * 3,
         ),
@@ -319,67 +316,82 @@
     )
     near_in = swap_halves(near)
     b = [b[0]] + [turn(b[k], COLUMN, -k) for k in (1, 2, 3)]
-    column = near[CUT:]
-    images = [column, near_in, swap_pairs(column), swap_far(column)]
-    (weight_plane,) = call(second_sum_kernel, (shape(384, 384),), place, a_own, near_in, *b)
-    images = [after(image, weight_plane) for image in images]
-
+    pair_in, far_in = swap_pairs(column), swap_far(column)
     along_z = after(along_z, near)
     other_text = swap_cores(along_z[:, :48])
-    knobs = jnp.concatenate([sharpness_coefficient, additive_offset_term]).reshape(1, 2)
-    *g, t_own, t_out = call(
+    here, weight_plane, *g, t_own, t_out = call(
         tile_kernel,
         (
+            shape(8, 96, 384),
+            shape(384, 384),
             shape(192, 384, dtype=f32),
             *[shape(192, 384)] * 3,
             shape(128, 1152, dtype=f32),
             shape(128, 1152),
         ),
         place,
-        knobs,
-        *images,
+        sharpness_coefficient,
+        additive_offset_term,
+        column,
+        near_in,
+        pair_in,
+        far_in,
+        other_text,
         along_z,
-        other_text,
+        a_own,
+        *b,
         scratch=[
             pltpu.VMEM((256, 1152), bf16),
             pltpu.VMEM((256, 1152), bf16),
             pltpu.VMEM((256, 1), jnp.int32),
         ],
+        spaces=(pltpu.SMEM, pltpu.SMEM),
         flops=6 * 256 * 256 * 1152,
     )
 
-    rows = after(along_z[:, 48:], *images[1:])
-    far_rows = swap_halves(rows)
-    core_rows = swap_cores(rows)
+    pair = swap_pairs(here)
+    there = swap_halves(here)
+    there_pair = swap_pairs(there)
 
     t_in = swap_cores(t_out)
     (back,) = call(send_back_kernel, (shape(8, 96, 384),), place, t_own, t_in, weight_plane)
-    g = [after(part, back) for part in g]
+    other, other_pair = swap_cores(here), swap_cores(pair)
     back = exchange(back, "z")
-    g = [g[0], swap_halves(g[1]), swap_pairs(g[2]), swap_far(g[3])]
-    far_rows = after(far_rows, *g)
-    h = call(
-        image_middle_kernel, (shape(48, 384, dtype=f32), *[shape(48, 384)] * 3), place, *g
-    )
-    attn_grad = project(place, 2, dense_result_adjoint, rows, core_rows)
-    back = after(back, attn_grad)
-    text_grad, pieces = call(
-        text_end_kernel,
-        (shape(16, 1152, dtype=f32), shape(8, 48, 384, dtype=f32)),
-        place,
-        back,
+    attn_grad = project(
+        place, 2, dense_result_adjoint, (here, pair, other, other_pair)
+    )
+
+    g = [g[0]] + [turn(g[k], COLUMN, k) for k in (1, 2, 3)]
+    text_grad, pieces, *h = call(
+        middle_kernel,
+        (
+            shape(16, 1152, dtype=f32),
+            shape(8, 48, 384, dtype=f32),
+            shape(48, 384, dtype=f32),
+            *[shape(48, 384)] * 3,
+        ),
+        place,
+        after(back, attn_grad),
         caption_vectors_prenorm,
+        *g,
     )
     pieces = exchange(pieces, ("xl", "y"))
-    h = [h[0]] + [turn(h[k], COLUMN, k) for k in (1, 2, 3)]
-    (image_grad,) = call(
-        image_end_kernel, (shape(16, 1152, dtype=f32),), place, *h, picture_vectors_prenorm
-    )
+    h = [h[0], swap_halves(h[1]), swap_pairs(h[2]), swap_far(h[3])]
     attn_grad = project(
-        place, 4, dense_result_adjoint, far_rows, swap_cores(far_rows), attn_grad
-    )
-    pieces = after(pieces, attn_grad, image_grad)
-    (weight_grad,) = call(weight_end_kernel, (shape(48, 1536, dtype=f32),), place, pieces)
+        place,
+        4,
+        dense_result_adjoint,
+        (there_pair, there, swap_cores(after(there_pair, h[0])), swap_cores(after(there, h[0]))),
+        attn_grad,
+    )
+    image_grad, weight_grad = call(
+        end_kernel,
+        (shape(16, 1152, dtype=f32), shape(48, 1536, dtype=f32)),
+        place,
+        *h,
+        picture_vectors_prenorm,
+        after(pieces, attn_grad),
+    )
     return (image_grad, text_grad, attn_grad, weight_grad)
 
 

time: 130 us -> 116 us (0.89)
  waiting for transfers between devices: 44.8 us -> 35.3 us
  starting transfers between devices: 49.7 us -> 46.6 us
    ppermute x4, waiting for transfers between devices: 11.1 us -> 0.67 us  [swap_halves(): return lax.ppermute(x, axes, [(at[i], at[3 - i]) for i in range(4)])]
    ppermute x2 -> x4, waiting for transfers between devices: 0.01 us -> 5.06 us  [swap_pairs(): return lax.ppermute(x, 'xl', [(0, 1), (1, 0)])]
    ppermute x9, waiting for transfers between devices: 28.4 us -> 23.3 us  [turn(): return lax.ppermute(x, axes, [(at[i], at[(i + by) % 4]) for i in range(4)])]
    all_to_all x3, waiting for transfers between devices: 0.01 us -> 4.86 us  [exchange(): return lax.all_to_all(x, axes, 0, 0, tiled=True)]
    ppermute x6 -> x8, waiting for transfers between devices: 5.3 us -> 0.92 us  [swap_cores(): return lax.ppermute(x, 'c', [(0, 1), (1, 0)])]
    ppermute x9, starting transfers between devices: 13.8 us -> 9.94 us  [turn(): return lax.ppermute(x, axes, [(at[i], at[(i + by) % 4]) for i in range(4)])]
    ppermute x2, starting transfers between devices: 1.6 us -> 3.95 us  [swap_far(): return lax.ppermute(x, 'xh', [(0, 1), (1, 0)])]
    all_to_all x3, starting transfers between devices: 22 us -> 19.8 us  [exchange(): return lax.all_to_all(x, axes, 0, 0, tiled=True)]
  transfers between devices with their start and end apart: 26 -> 30, of which waited for: 11 -> 10; matrix products, arithmetic and copies ran while one was open for 0% -> 0% of each run, Pallas kernels for 17% -> 18%
where the time goes in v4:
time: 116 us; the launch traced here: 115 us
  starting transfers between devices  46.6 us (40%)
  waiting for transfers between devices  35.3 us (30%)
  Pallas kernels  24.6 us (21%)
  local copies, waits for them, and re-layouts  6.38 us (6%)
  between operations  2.09 us (2%)
    ppermute x9, waiting for transfers between devices, turn(): return lax.ppermute(x, axes, [(at[i], at[(i + by) % 4]) for i in range(4)])  23.3 us
    all_to_all x3, starting transfers between devices, exchange(): return lax.all_to_all(x, axes, 0, 0, tiled=True)  19.8 us
    pallas_call x7, Pallas kernels, call(): pl.pallas_call(kernel, out_shape=tuple(outs), in_specs=[pl.BlockSpec(memo...  16.3 us
    ppermute x9, starting transfers between devices, turn(): return lax.ppermute(x, axes, [(at[i], at[(i + by) % 4]) for i in range(4)])  9.94 us
    pallas_call x2, Pallas kernels, project(): pl.pallas_call(project_kernel, grid_spec=pltpu.PrefetchScalarGridSpec(num...  8.39 us
    ppermute x4, starting transfers between devices, swap_pairs(): return lax.ppermute(x, 'xl', [(0, 1), (1, 0)])  7.75 us
    unnamed x36, local copies, waits for them, and re-layouts  6.26 us
    ppermute x4, waiting for transfers between devices, swap_pairs(): return lax.ppermute(x, 'xl', [(0, 1), (1, 0)])  5.06 us
  transfers between devices with their start and end apart: 30, of which 10 were waited for; matrix products, arithmetic and copies ran while one was open for 0% of the time, Pallas kernels for 18%

profile of v4, /device:TPU:2, one launch (start us, length us, event | category | flops | bytes accessed | tf_op | source)
XLA Modules:
  0.0 115.0 jit_solution(8257887146060190038)
XLA Ops:
  0.7 0.5 collective-permute-start.1
  1.3 0.9 copy-done.1
  2.2 0.9 copy-done.7
  3.1 1.6 %shard_map.113 = bf16[8,144,384]{2,1,0:T(8,128)(2,1)} custom-call(s32[5]{0:T(128)S(1)} %stack.23.place, f32[16,1152]{1,0:T(8,128)S(1)} %copy-done.1, bf16[48,1536]{1,0:T(8,128)(2,1)S(1)} %copy-done.7), custom_call_target="tpu_custom_call" | custom-call | bytes 1105920 | tf_op jit(solution)/shard_map/pallas_call | solution.py:73
  4.7 0.9 collective-permute-done.1.other_adj
  5.6 8.5 %all-to-all-start = ((bf16[8,144,384]{2,1,0:T(8,128)(2,1)}), bf16[8,144,384]{2,1,0:T(8,128)(2,1)S(1)}, u32[]{:S(2)}, u32[]{:S(2)}) async-start(bf16[8,144,384]{2,1,0:T(8,128)(2,1)} %shard_map.113), calls=%async_computation | async-start | bytes 1769472 | tf_op jit(solution)/shard_map/all_to_all | solution.py:44
  14.1 5.4 %shard_map.111 = (bf16[384,384]{1,0:T(8,128)(2,1)S(1)}, bf16[448,384]{1,0:T(8,128)(2,1)S(1)}, bf16[448,384]{1,0:T(8,128)(2,1)S(1)}, bf16[448,384]{1,0:T(8,128)(2...) custom-call(s32[5]{0:T(128)S(1)} %stack.23.place, ...), custom_call_target="tpu_custom_call" | custom-call | flops 1811939328 | bytes 7348288 | tf_op jit(solution)/shard_map/pallas_call | solution.py:73
  19.5 1.6 %collective-permute-start.5 = (bf16[192,1536]{1,0:T(8,128)(2,1)S(1)}, bf16[192,1536]{1,0:T(8,128)(2,1)S(1)}, u32[]{:S(2)}, u32[]{:S(2)}) collective-permute-start(bf16[192,1536]{1,0:T(8,128)(2,1)S(1)} %get-tuple-element.45), channel_id=1, source_target_pairs={{0,144},{128,16},{16,128},{144,0},{1,145},{129,17},{17,129},{145,1... | collective-permute-start | bytes 1769480 | tf_op jit(solution)/shard_map/ppermute | solution.py:32
  21.0 3.0 %collective-permute-start.2 = (bf16[448,384]{1,0:T(8,128)(2,1)S(1)}, bf16[448,384]{1,0:T(8,128)(2,1)S(1)}, u32[]{:S(2)}, u32[]{:S(2)}) collective-permute-start(bf16[448,384]{1,0:T(8,128)(2,1)S(1)} %get-tuple-element.41), channel_id=1, source_target_pairs={{0,96},{32,0},{64,32},{96,64},{1,97},{33,1},{65,33},{97,65},{2,98}... | collective-permute-start | bytes 1032200 | tf_op jit(solution)/shard_map/ppermute | solution.py:27
  24.1 0.6 collective-permute-start.3
  24.7 1.0 collective-permute-start.4
  25.7 12.8 %collective-permute-done.2.a1 = bf16[448,384]{1,0:T(8,128)(2,1)S(1)} collective-permute-done((bf16[448,384]{1,0:T(8,128)(2,1)S(1)}, bf16[448,384]{1,0:T(8,128)(2,1)S(1)}, u32[]{:S(2)}, u32[]{:S(2)}) %collective-permute-start.2) | collective-permute-done | bytes 344096 | tf_op jit(solution)/shard_map/ppermute | solution.py:27
  38.5 3.7 %collective-permute-done.4.a3 = bf16[448,384]{1,0:T(8,128)(2,1)S(1)} collective-permute-done((bf16[448,384]{1,0:T(8,128)(2,1)S(1)}, bf16[448,384]{1,0:T(8,128)(2,1)S(1)}, u32[]{:S(2)}, u32[]{:S(2)}) %collective-permute-start.4) | collective-permute-done | bytes 344096 | tf_op jit(solution)/shard_map/ppermute | solution.py:27
  42.2 1.7 %shard_map.112 = (f32[192,384]{1,0:T(8,128)S(1)}, bf16[448,384]{1,0:T(8,128)(2,1)}, bf16[256,384]{1,0:T(8,128)(2,1)S(1)}, f32[192,384]{1,0:T(8,128)S(1)}, bf16[1...) custom-call(s32[5]{0:T(128)S(1)} %stack.23.place, ...), custom_call_target="tpu_custom_call" | custom-call | bytes 4128768 | tf_op jit(solution)/shard_map/pallas_call | solution.py:73
  43.9 0.7 copy-done.16
  44.6 0.6 collective-permute-start.10
  45.2 0.5 collective-permute-start.6
  45.7 0.6 collective-permute-start.11
  46.5 3.4 %collective-permute-start.8 = (bf16[256,384]{1,0:T(8,128)(2,1)S(1)}, bf16[256,384]{1,0:T(8,128)(2,1)S(1)}, u32[]{:S(2)}, u32[]{:S(2)}) collective-permute-start(bf16[256,384]{1,0:T(8,128)(2,1)S(1)} %get-tuple-element.47.i0), channel_id=1, source_target_pairs={{0,16},{16,0},{1,17},{17,1},{2,18},{18,2},{3,19},{19,3},{4,20},{20... | collective-permute-start | bytes 589832 | tf_op jit(solution)/shard_map/ppermute | solution.py:40
  49.9 1.6 %collective-permute-done.10.rest_1_ = bf16[192,384]{1,0:T(8,128)(2,1)S(1)} collective-permute-done((bf16[192,384]{1,0:T(8,128)(2,1)}, bf16[192,384]{1,0:T(8,128)(2,1)S(1)}, u32[]{:S(2)}, u32[]{:S(2)}) %collective-permute-start.10) | collective-permute-done | bytes 147488 | tf_op jit(solution)/shard_map/ppermute | solution.py:27
  51.5 0.7 copy-done.3
  52.1 1.8 %collective-permute-start.7 = (bf16[256,384]{1,0:T(8,128)(2,1)S(1)}, bf16[256,384]{1,0:T(8,128)(2,1)S(1)}, u32[]{:S(2)}, u32[]{:S(2)}) collective-permute-start(bf16[256,384]{1,0:T(8,128)(2,1)S(1)} %get-tuple-element.47.i0), channel_id=1, source_target_pairs={{0,128},{128,0},{1,129},{129,1},{2,130},{130,2},{3,131},{131,3},{4... | collective-permute-start | bytes 589832 | tf_op jit(solution)/shard_map/ppermute | solution.py:36
  53.9 0.7 copy-done.5
  56.0 5.2 %collective-permute-done.12.rest_3_ = bf16[192,384]{1,0:T(8,128)(2,1)S(1)} collective-permute-done((bf16[192,384]{1,0:T(8,128)(2,1)}, bf16[192,384]{1,0:T(8,128)(2,1)S(1)}, u32[]{:S(2)}, u32[]{:S(2)}) %collective-permute-start.12) | collective-permute-done | bytes 147488 | tf_op jit(solution)/shard_map/ppermute | solution.py:27
  61.2 0.9 copy-done.4
  62.1 0.9 copy-done.6
  63.0 2.8 %shard_map.114 = (bf16[8,96,384]{2,1,0:T(8,128)(2,1)}, bf16[384,384]{1,0:T(8,128)(2,1)S(1)}, f32[192,384]{1,0:T(8,128)S(1)}, bf16[192,384]{1,0:T(8,128)(2,1)S(1)...) custom-call(s32[5]{0:T(128)S(1)} %stack.23.place, ...), custom_call_target="tpu_custom_call" | custom-call | flops 452984832 | bytes 5652488 | tf_op jit(solution)/shard_map/pallas_call | solution.py:73
  65.8 1.1 collective-permute-start.14
  66.9 1.5 %collective-permute-start.23 = (bf16[8,96,384]{2,1,0:T(8,128)(2,1)}, bf16[8,96,384]{2,1,0:T(8,128)(2,1)S(1)}, u32[]{:S(2)}, u32[]{:S(2)}) collective-permute-start(bf16[8,96,384]{2,1,0:T(8,128)(2,1)} %get-tuple-element.59.w), channel_id=1, source_target_pairs={{0,144},{128,16},{16,128},{144,0},{1,145},{129,17},{17,129},{145,1... | collective-permute-start | bytes 1769480 | tf_op jit(solution)/shard_map/ppermute | solution.py:32
  68.4 1.5 %shard_map.115 = bf16[8,96,384]{2,1,0:T(8,128)(2,1)} custom-call(s32[5]{0:T(128)S(1)} %stack.23.place, f32[128,1152]{1,0:T(8,128)S(1)} %get-tuple-element.56.t_own, bf16[128,1152]{1,0:T(8,128)(2,1)S(1)} %collective-permute-done.13.t_in, bf16[384,384]{1,0:T(8,128)(2,1)S(1)} %get-tuple-element.58.weight), custom_call_target="tpu_custom_call" | custom-call | bytes 1769472 | tf_op jit(solution)/shard_map/pallas_call | solution.py:73
  69.9 6.9 %all-to-all-start.1 = ((bf16[8,96,384]{2,1,0:T(8,128)(2,1)}), bf16[8,96,384]{2,1,0:T(8,128)(2,1)S(1)}, u32[]{:S(2)}, u32[]{:S(2)}) async-start(bf16[8,96,384]{2,1,0:T(8,128)(2,1)} %shard_map.115), calls=%async_computation.1 | async-start | bytes 1179648 | tf_op jit(solution)/shard_map/all_to_all | solution.py:44
  76.8 5.1 %collective-permute-done.14.w_pair = bf16[8,96,384]{2,1,0:T(8,128)(2,1)} collective-permute-done((bf16[8,96,384]{2,1,0:T(8,128)(2,1)}, bf16[8,96,384]{2,1,0:T(8,128)(2,1)}, u32[]{:S(2)}, u32[]{:S(2)}) %collective-permute-start.14) | collective-permute-done | bytes 589856 | tf_op jit(solution)/shard_map/ppermute | solution.py:36
  81.9 0.7 collective-permute-done.23.w_pair
  82.5 2.2 %collective-permute-start.24 = (bf16[8,96,384]{2,1,0:T(8,128)(2,1)S(1)}, bf16[8,96,384]{2,1,0:T(8,128)(2,1)S(1)}, u32[]{:S(2)}, u32[]{:S(2)}) collective-permute-start(bf16[8,96,384]{2,1,0:T(8,128)(2,1)S(1)} %collective-permute-done.23.w_pair), channel_id=1, source_target_pairs={{0,128},{128,0},{1,129},{129,1},{2,130},{130,2},{3,131},{131,3},{4... | collective-permute-start | bytes 1769480 | tf_op jit(solution)/shard_map/ppermute | solution.py:36
  84.7 0.8 collective-permute-start.17
  85.5 2.6 %collective-permute-start.18 = (bf16[192,384]{1,0:T(8,128)(2,1)}, bf16[192,384]{1,0:T(8,128)(2,1)}, u32[]{:S(2)}, u32[]{:S(2)}) collective-permute-start(bf16[192,384]{1,0:T(8,128)(2,1)} %copy-done.14), channel_id=1, source_target_pairs={{0,64},{32,96},{64,0},{96,32},{1,65},{33,97},{65,1},{97,33},{2,66}... | collective-permute-start | bytes 442376 | tf_op jit(solution)/shard_map/ppermute | solution.py:27
  88.1 0.6 collective-permute-start.19
  88.7 4.2 %shard_map.116.rest_0_ = bf16[384,1536]{1,0:T(8,128)(2,1)} custom-call(s32[5]{0:T(128)S(1)} %stack.23.place, bf16[384,1536]{1,0:T(8,128)(2,1)S(1)} %copy-done, bf16[8,96,384]{2,1,0:T(8,128)(2,1)} %get-tuple-element.59.w, bf16[8,96,384]{2,1,0:T(8,128)(2,1)} %collective-permute-done.14.w_pair, bf16[8,96,384]{2,1,0:T(8,128)(2,1)S(1)} %collective-permute-done.15.other, ...), custom_call_target="tpu_custom_call" | custom-call | flops 905969664 | bytes 6291456 | tf_op jit(solution)/shard_map/pallas_call | solution.py:236
  92.9 2.8 %all-to-all-done.1.back = bf16[8,96,384]{2,1,0:T(8,128)(2,1)S(1)} async-done(((bf16[8,96,384]{2,1,0:T(8,128)(2,1)}), bf16[8,96,384]{2,1,0:T(8,128)(2,1)S(1)}, u32[]{:S(2)}, u32[]{:S(2)}) %all-to-all-start.1) | async-done | bytes 589856 | tf_op jit(solution)/shard_map/all_to_all | solution.py:44
  95.8 2.0 %shard_map.117 = (f32[16,1152]{1,0:T(8,128)}, f32[8,48,384]{2,1,0:T(8,128)}, f32[48,384]{1,0:T(8,128)S(1)}, bf16[48,384]{1,0:T(8,128)(2,1)}, bf16[48,384]{1,0:T(8,128)(2,1)}, /*index=5*/bf16[48,384]{1,0:T(8,128)(2,1)S(1)}) custom-call(s32[5]{0:T(128)S(1)} %stack.23.place, bf16[8,96,384]{2,1,0:T(8,128)(2,1)S(1)} %all-to-all-done.1.back, ...), custom_call_target="tpu_custom_call" | custom-call | bytes 2248704 | tf_op jit(solution)/shard_map/pallas_call | solution.py:73
  97.8 0.6 copy-done.10
  98.4 0.5 collective-permute-start.26
  98.9 4.4 %all-to-all-start.2 = ((f32[8,48,384]{2,1,0:T(8,128)}), f32[8,48,384]{2,1,0:T(8,128)S(1)}, u32[]{:S(2)}, u32[]{:S(2)}) async-start(f32[8,48,384]{2,1,0:T(8,128)} %get-tuple-element.69), calls=%async_computation.2 | async-start | bytes 1179648 | tf_op jit(solution)/shard_map/all_to_all | solution.py:44
  103.7 2.6 %collective-permute-start.21 = (bf16[48,384]{1,0:T(8,128)(2,1)}, bf16[48,384]{1,0:T(8,128)(2,1)S(1)}, u32[]{:S(2)}, u32[]{:S(2)}) collective-permute-start(bf16[48,384]{1,0:T(8,128)(2,1)} %get-tuple-element.67), channel_id=1, source_target_pairs={{0,128},{128,0},{1,129},{129,1},{2,130},{130,2},{3,131},{131,3},{4... | collective-permute-start | bytes 110600 | tf_op jit(solution)/shard_map/ppermute | solution.py:36
  106.3 0.5 collective-permute-start.22
  106.8 4.2 %shard_map.118 = bf16[384,1536]{1,0:T(8,128)(2,1)} custom-call(s32[5]{0:T(128)S(1)} %stack.23.place, bf16[384,1536]{1,0:T(8,128)(2,1)S(1)} %copy-done, bf16[8,96,384]{2,1,0:T(8,128)(2,1)S(1)} %collective-permute-done.24.w, bf16[8,96,384]{2,1,0:T(8,128)(2,1)S(1)} %collective-permute-done.23.w_pair, ...), custom_call_target="tpu_custom_call", output_to_operand_aliasing={{}: (6, {})} | custom-call | flops 905969664 | bytes 6291456 | tf_op jit(solution)/shard_map/pallas_call | solution.py:236
  111.0 2.0 %all-to-all-done.2.pieces = f32[8,48,384]{2,1,0:T(8,128)S(1)} async-done(((f32[8,48,384]{2,1,0:T(8,128)}), f32[8,48,384]{2,1,0:T(8,128)S(1)}, u32[]{:S(2)}, u32[]{:S(2)}) %all-to-all-start.2) | async-done | bytes 589856 | tf_op jit(solution)/shard_map/all_to_all | solution.py:44
  113.6 1.4 %shard_map.119 = (f32[16,1152]{1,0:T(8,128)}, f32[48,1536]{1,0:T(8,128)}) custom-call(s32[5]{0:T(128)S(1)} %stack.23.place, f32[48,384]{1,0:T(8,128)S(1)} %copy-done.11, bf16[48,384]{1,0:T(8,128)(2,1)S(1)} %collective-permute-done.20.h1, bf16[48,384]{1,0:T(8,128)(2,1)S(1)} %collective-permute-done.21.h2, bf16[48,384]{1,0:T(8,128)(2,1)S(1)} %collective-permute-done.22.h3, ...), custom_call_target="tpu_custom_call" | custom-call | bytes 1216512 | tf_op jit(solution)/shard_map/pallas_call | solution.py:73
  (59 shorter events, 1.3 us)
Async XLA Ops:
  0.6 4.1 %collective-permute-start = (bf16[384,1536]{1,0:T(8,128)(2,1)}, bf16[384,1536]{1,0:T(8,128)(2,1)}, u32[]{:S(2)}, u32[]{:S(2)}) collective-permute-start(bf16[384,1536]{1,0:T(8,128)(2,1)} %tokens.1), channel_id=1, source_target_pairs={{0,1},{1,0},{2,3},{3,2},{4,5},{5,4},{6,7},{7,6},{8,9},{9,8},{10,11... | collective-permute-start | bytes 3538952 | tf_op jit(solution)/shard_map/ppermute | solution.py:22
  0.7 4.9 %collective-permute-start.1 = (bf16[384,1536]{1,0:T(8,128)(2,1)}, bf16[384,1536]{1,0:T(8,128)(2,1)}, u32[]{:S(2)}, u32[]{:S(2)}) collective-permute-start(bf16[384,1536]{1,0:T(8,128)(2,1)} %adj.5), channel_id=1, source_target_pairs={{0,1},{1,0},{2,3},{3,2},{4,5},{5,4},{6,7},{7,6},{8,9},{9,8},{10,11... | collective-permute-start | bytes 3538952 | tf_op jit(solution)/shard_map/ppermute | solution.py:22
  1.3 0.9 copy-start.1
  2.2 0.9 copy-start.7
  3.1 11.0 %copy-start = (bf16[384,1536]{1,0:T(8,128)(2,1)S(1)}, bf16[384,1536]{1,0:T(8,128)(2,1)}, u32[]{:S(2)}) copy-start(bf16[384,1536]{1,0:T(8,128)(2,1)} %adj.5) | copy-start | bytes 3538948
  3.1 11.0 %copy-start.8 = (f32[16,1152]{1,0:T(8,128)S(1)}, f32[16,1152]{1,0:T(8,128)}, u32[]{:S(2)}) copy-start(f32[16,1152]{1,0:T(8,128)} %pic.3) | copy-start | bytes 221188
  3.1 11.0 %copy-start.12 = (bf16[384,1536]{1,0:T(8,128)(2,1)S(1)}, bf16[384,1536]{1,0:T(8,128)(2,1)}, u32[]{:S(2)}) copy-start(bf16[384,1536]{1,0:T(8,128)(2,1)} %tokens.1) | copy-start | bytes 3538948
  3.1 11.0 %copy-start.17 = (s32[16]{0:T(128)S(1)}, s32[16]{0:T(128)}, u32[]{:S(2)}) copy-start(s32[16]{0:T(128)} %ids.1) | copy-start | bytes 196
  5.6 40.7 %all-to-all-start = ((bf16[8,144,384]{2,1,0:T(8,128)(2,1)}), bf16[8,144,384]{2,1,0:T(8,128)(2,1)S(1)}, u32[]{:S(2)}, u32[]{:S(2)}) async-start(bf16[8,144,384]{2,1,0:T(8,128)(2,1)} %shard_map.113), calls=%async_computation | async-start | bytes 1769472 | tf_op jit(solution)/shard_map/all_to_all | solution.py:44
  19.5 22.8 %collective-permute-start.5 = (bf16[192,1536]{1,0:T(8,128)(2,1)S(1)}, bf16[192,1536]{1,0:T(8,128)(2,1)S(1)}, u32[]{:S(2)}, u32[]{:S(2)}) collective-permute-start(bf16[192,1536]{1,0:T(8,128)(2,1)S(1)} %get-tuple-element.45), channel_id=1, source_target_pairs={{0,144},{128,16},{16,128},{144,0},{1,145},{129,17},{17,129},{145,1... | collective-permute-start | bytes 1769480 | tf_op jit(solution)/shard_map/ppermute | solution.py:32
  21.0 17.5 %collective-permute-start.2 = (bf16[448,384]{1,0:T(8,128)(2,1)S(1)}, bf16[448,384]{1,0:T(8,128)(2,1)S(1)}, u32[]{:S(2)}, u32[]{:S(2)}) collective-permute-start(bf16[448,384]{1,0:T(8,128)(2,1)S(1)} %get-tuple-element.41), channel_id=1, source_target_pairs={{0,96},{32,0},{64,32},{96,64},{1,97},{33,1},{65,33},{97,65},{2,98}... | collective-permute-start | bytes 1032200 | tf_op jit(solution)/shard_map/ppermute | solution.py:27
  24.1 14.4 %collective-permute-start.3 = (bf16[448,384]{1,0:T(8,128)(2,1)S(1)}, bf16[448,384]{1,0:T(8,128)(2,1)S(1)}, u32[]{:S(2)}, u32[]{:S(2)}) collective-permute-start(bf16[448,384]{1,0:T(8,128)(2,1)S(1)} %get-tuple-element.42), channel_id=1, source_target_pairs={{0,64},{32,96},{64,0},{96,32},{1,65},{33,97},{65,1},{97,33},{2,66}... | collective-permute-start | bytes 1032200 | tf_op jit(solution)/shard_map/ppermute | solution.py:27
  24.7 17.5 %collective-permute-start.4 = (bf16[448,384]{1,0:T(8,128)(2,1)S(1)}, bf16[448,384]{1,0:T(8,128)(2,1)S(1)}, u32[]{:S(2)}, u32[]{:S(2)}) collective-permute-start(bf16[448,384]{1,0:T(8,128)(2,1)S(1)} %get-tuple-element.43), channel_id=1, source_target_pairs={{0,32},{32,64},{64,96},{96,0},{1,33},{33,65},{65,97},{97,1},{2,34}... | collective-permute-start | bytes 1032200 | tf_op jit(solution)/shard_map/ppermute | solution.py:27
  43.9 0.7 copy-start.16
  44.6 6.9 %collective-permute-start.10 = (bf16[192,384]{1,0:T(8,128)(2,1)}, bf16[192,384]{1,0:T(8,128)(2,1)S(1)}, u32[]{:S(2)}, u32[]{:S(2)}) collective-permute-start(bf16[192,384]{1,0:T(8,128)(2,1)} %get-tuple-element.53), channel_id=1, source_target_pairs={{0,96},{32,0},{64,32},{96,64},{1,97},{33,1},{65,33},{97,65},{2,98}... | collective-permute-start | bytes 442376 | tf_op jit(solution)/shard_map/ppermute | solution.py:27
  45.2 16.0 %collective-permute-start.6 = (bf16[448,384]{1,0:T(8,128)(2,1)}, bf16[448,384]{1,0:T(8,128)(2,1)S(1)}, u32[]{:S(2)}, u32[]{:S(2)}) collective-permute-start(bf16[448,384]{1,0:T(8,128)(2,1)} %get-tuple-element.48), channel_id=1, source_target_pairs={{0,144},{128,16},{16,128},{144,0},{1,145},{129,17},{17,129},{145,1... | collective-permute-start | bytes 1032200 | tf_op jit(solution)/shard_map/ppermute | solution.py:32
  45.7 8.2 %collective-permute-start.11 = (bf16[192,384]{1,0:T(8,128)(2,1)}, bf16[192,384]{1,0:T(8,128)(2,1)S(1)}, u32[]{:S(2)}, u32[]{:S(2)}) collective-permute-start(bf16[192,384]{1,0:T(8,128)(2,1)} %get-tuple-element.54), channel_id=1, source_target_pairs={{0,64},{32,96},{64,0},{96,32},{1,65},{33,97},{65,1},{97,33},{2,66}... | collective-permute-start | bytes 442376 | tf_op jit(solution)/shard_map/ppermute | solution.py:27
  46.4 14.8 %collective-permute-start.9 = (bf16[8,48,384]{2,1,0:T(8,128)(2,1)S(1)}, bf16[8,48,384]{2,1,0:T(8,128)(2,1)S(1)}, u32[]{:S(2)}, u32[]{:S(2)}) collective-permute-start(bf16[8,48,384]{2,1,0:T(8,128)(2,1)S(1)} %slice.3), channel_id=1, source_target_pairs={{0,1},{1,0},{2,3},{3,2},{4,5},{5,4},{6,7},{7,6},{8,9},{9,8},{10,11... | collective-permute-start | bytes 884744 | tf_op jit(solution)/shard_map/ppermute | solution.py:22
  46.5 14.7 %collective-permute-start.8 = (bf16[256,384]{1,0:T(8,128)(2,1)S(1)}, bf16[256,384]{1,0:T(8,128)(2,1)S(1)}, u32[]{:S(2)}, u32[]{:S(2)}) collective-permute-start(bf16[256,384]{1,0:T(8,128)(2,1)S(1)} %get-tuple-element.47.i0), channel_id=1, source_target_pairs={{0,16},{16,0},{1,17},{17,1},{2,18},{18,2},{3,19},{19,3},{4,20},{20... | collective-permute-start | bytes 589832 | tf_op jit(solution)/shard_map/ppermute | solution.py:40
  51.5 0.7 copy-start.3
  52.1 9.0 %collective-permute-start.7 = (bf16[256,384]{1,0:T(8,128)(2,1)S(1)}, bf16[256,384]{1,0:T(8,128)(2,1)S(1)}, u32[]{:S(2)}, u32[]{:S(2)}) collective-permute-start(bf16[256,384]{1,0:T(8,128)(2,1)S(1)} %get-tuple-element.47.i0), channel_id=1, source_target_pairs={{0,128},{128,0},{1,129},{129,1},{2,130},{130,2},{3,131},{131,3},{4... | collective-permute-start | bytes 589832 | tf_op jit(solution)/shard_map/ppermute | solution.py:36
  53.9 0.7 copy-start.5
  54.6 6.6 %collective-permute-start.12 = (bf16[192,384]{1,0:T(8,128)(2,1)}, bf16[192,384]{1,0:T(8,128)(2,1)S(1)}, u32[]{:S(2)}, u32[]{:S(2)}) collective-permute-start(bf16[192,384]{1,0:T(8,128)(2,1)} %copy-done.16), channel_id=1, source_target_pairs={{0,32},{32,64},{64,96},{96,0},{1,33},{33,65},{65,97},{97,1},{2,34}... | collective-permute-start | bytes 442376 | tf_op jit(solution)/shard_map/ppermute | solution.py:27
  61.2 0.9 copy-start.4
  62.1 0.9 copy-start.6
  65.8 2.6 %copy-start.13 = (bf16[192,384]{1,0:T(8,128)(2,1)}, bf16[192,384]{1,0:T(8,128)(2,1)S(1)}, u32[]{:S(2)}) copy-start(bf16[192,384]{1,0:T(8,128)(2,1)S(1)} %get-tuple-element.64) | copy-start | bytes 442372
  65.8 2.6 %copy-start.14 = (bf16[192,384]{1,0:T(8,128)(2,1)}, bf16[192,384]{1,0:T(8,128)(2,1)S(1)}, u32[]{:S(2)}) copy-start(bf16[192,384]{1,0:T(8,128)(2,1)S(1)} %get-tuple-element.63) | copy-start | bytes 442372
  65.8 2.6 %copy-start.15 = (bf16[192,384]{1,0:T(8,128)(2,1)}, bf16[192,384]{1,0:T(8,128)(2,1)S(1)}, u32[]{:S(2)}) copy-start(bf16[192,384]{1,0:T(8,128)(2,1)S(1)} %get-tuple-element.62) | copy-start | bytes 442372
  65.8 2.6 %collective-permute-start.13 = (bf16[128,1152]{1,0:T(8,128)(2,1)S(1)}, bf16[128,1152]{1,0:T(8,128)(2,1)S(1)}, u32[]{:S(2)}, u32[]{:S(2)}) collective-permute-start(bf16[128,1152]{1,0:T(8,128)(2,1)S(1)} %get-tuple-element.57), channel_id=1, source_target_pairs={{0,1},{1,0},{2,3},{3,2},{4,5},{5,4},{6,7},{7,6},{8,9},{9,8},{10,11... | collective-permute-start | bytes 884744 | tf_op jit(solution)/shard_map/ppermute | solution.py:22
  65.8 16.1 %collective-permute-start.14 = (bf16[8,96,384]{2,1,0:T(8,128)(2,1)}, bf16[8,96,384]{2,1,0:T(8,128)(2,1)}, u32[]{:S(2)}, u32[]{:S(2)}) collective-permute-start(bf16[8,96,384]{2,1,0:T(8,128)(2,1)} %get-tuple-element.59.w), channel_id=1, source_target_pairs={{0,128},{128,0},{1,129},{129,1},{2,130},{130,2},{3,131},{131,3},{4... | collective-permute-start | bytes 1769480 | tf_op jit(solution)/shard_map/ppermute | solution.py:36
  66.9 15.6 %collective-permute-start.23 = (bf16[8,96,384]{2,1,0:T(8,128)(2,1)}, bf16[8,96,384]{2,1,0:T(8,128)(2,1)S(1)}, u32[]{:S(2)}, u32[]{:S(2)}) collective-permute-start(bf16[8,96,384]{2,1,0:T(8,128)(2,1)} %get-tuple-element.59.w), channel_id=1, source_target_pairs={{0,144},{128,16},{16,128},{144,0},{1,145},{129,17},{17,129},{145,1... | collective-permute-start | bytes 1769480 | tf_op jit(solution)/shard_map/ppermute | solution.py:32
  69.9 25.9 %all-to-all-start.1 = ((bf16[8,96,384]{2,1,0:T(8,128)(2,1)}), bf16[8,96,384]{2,1,0:T(8,128)(2,1)S(1)}, u32[]{:S(2)}, u32[]{:S(2)}) async-start(bf16[8,96,384]{2,1,0:T(8,128)(2,1)} %shard_map.115), calls=%async_computation.1 | async-start | bytes 1179648 | tf_op jit(solution)/shard_map/all_to_all | solution.py:44
  76.8 11.3 %collective-permute-start.15 = (bf16[8,96,384]{2,1,0:T(8,128)(2,1)}, bf16[8,96,384]{2,1,0:T(8,128)(2,1)S(1)}, u32[]{:S(2)}, u32[]{:S(2)}) collective-permute-start(bf16[8,96,384]{2,1,0:T(8,128)(2,1)} %get-tuple-element.59.w), channel_id=1, source_target_pairs={{0,1},{1,0},{2,3},{3,2},{4,5},{5,4},{6,7},{7,6},{8,9},{9,8},{10,11... | collective-permute-start | bytes 1769480 | tf_op jit(solution)/shard_map/ppermute | solution.py:22
  81.9 6.8 %collective-permute-start.16 = (bf16[8,96,384]{2,1,0:T(8,128)(2,1)}, bf16[8,96,384]{2,1,0:T(8,128)(2,1)S(1)}, u32[]{:S(2)}, u32[]{:S(2)}) collective-permute-start(bf16[8,96,384]{2,1,0:T(8,128)(2,1)} %collective-permute-done.14.w_pair), channel_id=1, source_target_pairs={{0,1},{1,0},{2,3},{3,2},{4,5},{5,4},{6,7},{7,6},{8,9},{9,8},{10,11... | collective-permute-start | bytes 1769480 | tf_op jit(solution)/shard_map/ppermute | solution.py:22
  82.5 15.9 %collective-permute-start.24 = (bf16[8,96,384]{2,1,0:T(8,128)(2,1)S(1)}, bf16[8,96,384]{2,1,0:T(8,128)(2,1)S(1)}, u32[]{:S(2)}, u32[]{:S(2)}) collective-permute-start(bf16[8,96,384]{2,1,0:T(8,128)(2,1)S(1)} %collective-permute-done.23.w_pair), channel_id=1, source_target_pairs={{0,128},{128,0},{1,129},{129,1},{2,130},{130,2},{3,131},{131,3},{4... | collective-permute-start | bytes 1769480 | tf_op jit(solution)/shard_map/ppermute | solution.py:36
  84.7 11.0 %collective-permute-start.17 = (bf16[192,384]{1,0:T(8,128)(2,1)}, bf16[192,384]{1,0:T(8,128)(2,1)S(1)}, u32[]{:S(2)}, u32[]{:S(2)}) collective-permute-start(bf16[192,384]{1,0:T(8,128)(2,1)} %copy-done.15), channel_id=1, source_target_pairs={{0,32},{32,64},{64,96},{96,0},{1,33},{33,65},{65,97},{97,1},{2,34}... | collective-permute-start | bytes 442376 | tf_op jit(solution)/shard_map/ppermute | solution.py:27
  85.5 10.3 %collective-permute-start.18 = (bf16[192,384]{1,0:T(8,128)(2,1)}, bf16[192,384]{1,0:T(8,128)(2,1)}, u32[]{:S(2)}, u32[]{:S(2)}) collective-permute-start(bf16[192,384]{1,0:T(8,128)(2,1)} %copy-done.14), channel_id=1, source_target_pairs={{0,64},{32,96},{64,0},{96,32},{1,65},{33,97},{65,1},{97,33},{2,66}... | collective-permute-start | bytes 442376 | tf_op jit(solution)/shard_map/ppermute | solution.py:27
  88.1 7.7 %copy-start.2 = (f32[16,1152]{1,0:T(8,128)S(1)}, f32[16,1152]{1,0:T(8,128)}, u32[]{:S(2)}) copy-start(f32[16,1152]{1,0:T(8,128)} %cap.3) | copy-start | bytes 221188
  88.1 7.7 %collective-permute-start.19 = (bf16[192,384]{1,0:T(8,128)(2,1)}, bf16[192,384]{1,0:T(8,128)(2,1)}, u32[]{:S(2)}, u32[]{:S(2)}) collective-permute-start(bf16[192,384]{1,0:T(8,128)(2,1)} %copy-done.13), channel_id=1, source_target_pairs={{0,96},{32,0},{64,32},{96,64},{1,97},{33,1},{65,33},{97,65},{2,98}... | collective-permute-start | bytes 442376 | tf_op jit(solution)/shard_map/ppermute | solution.py:27
  97.8 0.6 copy-start.10
  98.4 8.4 %collective-permute-start.25 = (bf16[8,96,384]{2,1,0:T(8,128)(2,1)S(1)}, bf16[8,96,384]{2,1,0:T(8,128)(2,1)}, u32[]{:S(2)}, u32[]{:S(2)}) collective-permute-start(bf16[8,96,384]{2,1,0:T(8,128)(2,1)S(1)} %collective-permute-done.24.w), channel_id=1, source_target_pairs={{0,1},{1,0},{2,3},{3,2},{4,5},{5,4},{6,7},{7,6},{8,9},{9,8},{10,11... | collective-permute-start | bytes 1769480 | tf_op jit(solution)/shard_map/ppermute | solution.py:22
  98.4 8.4 %collective-permute-start.26 = (bf16[8,96,384]{2,1,0:T(8,128)(2,1)S(1)}, bf16[8,96,384]{2,1,0:T(8,128)(2,1)}, u32[]{:S(2)}, u32[]{:S(2)}) collective-permute-start(bf16[8,96,384]{2,1,0:T(8,128)(2,1)S(1)} %collective-permute-done.23.w_pair), channel_id=1, source_target_pairs={{0,1},{1,0},{2,3},{3,2},{4,5},{5,4},{6,7},{7,6},{8,9},{9,8},{10,11... | collective-permute-start | bytes 1769480 | tf_op jit(solution)/shard_map/ppermute | solution.py:22
  98.9 14.1 %all-to-all-start.2 = ((f32[8,48,384]{2,1,0:T(8,128)}), f32[8,48,384]{2,1,0:T(8,128)S(1)}, u32[]{:S(2)}, u32[]{:S(2)}) async-start(f32[8,48,384]{2,1,0:T(8,128)} %get-tuple-element.69), calls=%async_computation.2 | async-start | bytes 1179648 | tf_op jit(solution)/shard_map/all_to_all | solution.py:44
  103.3 9.7 %collective-permute-start.20 = (bf16[48,384]{1,0:T(8,128)(2,1)}, bf16[48,384]{1,0:T(8,128)(2,1)S(1)}, u32[]{:S(2)}, u32[]{:S(2)}) collective-permute-start(bf16[48,384]{1,0:T(8,128)(2,1)} %get-tuple-element.66), channel_id=1, source_target_pairs={{0,144},{128,16},{16,128},{144,0},{1,145},{129,17},{17,129},{145,1... | collective-permute-start | bytes 110600 | tf_op jit(solution)/shard_map/ppermute | solution.py:32
  103.7 9.4 %collective-permute-start.21 = (bf16[48,384]{1,0:T(8,128)(2,1)}, bf16[48,384]{1,0:T(8,128)(2,1)S(1)}, u32[]{:S(2)}, u32[]{:S(2)}) collective-permute-start(bf16[48,384]{1,0:T(8,128)(2,1)} %get-tuple-element.67), channel_id=1, source_target_pairs={{0,128},{128,0},{1,129},{129,1},{2,130},{130,2},{3,131},{131,3},{4... | collective-permute-start | bytes 110600 | tf_op jit(solution)/shard_map/ppermute | solution.py:36
  106.3 7.2 %copy-start.9 = (f32[16,1152]{1,0:T(8,128)S(1)}, f32[16,1152]{1,0:T(8,128)}, u32[]{:S(2)}) copy-start(f32[16,1152]{1,0:T(8,128)} %pic.3) | copy-start | bytes 221188
  106.3 7.2 %copy-start.11 = (f32[48,384]{1,0:T(8,128)S(1)}, f32[48,384]{1,0:T(8,128)}, u32[]{:S(2)}) copy-start(f32[48,384]{1,0:T(8,128)} %copy-done.10) | copy-start | bytes 221188
  106.3 7.2 %collective-permute-start.22 = (bf16[48,384]{1,0:T(8,128)(2,1)S(1)}, bf16[48,384]{1,0:T(8,128)(2,1)S(1)}, u32[]{:S(2)}, u32[]{:S(2)}) collective-permute-start(bf16[48,384]{1,0:T(8,128)(2,1)S(1)} %get-tuple-element.68), channel_id=1, source_target_pairs={{0,16},{16,0},{1,17},{17,1},{2,18},{18,2},{3,19},{19,3},{4,20},{20... | collective-permute-start | bytes 110600 | tf_op jit(solution)/shard_map/ppermute | solution.py:40

commit v5 on v4

--- a/solution.py
+++ b/solution.py
@@ -95,7 +95,7 @@
 
 
 def weight_kernel(place, ids, pic, tokens, other_tokens, adj, other_adj, *rest):
-    a0, a1, a2, a3, b_own, b_out, image, turned, own, other = rest
+    a0, a1, a2, a3, b_own, b_out, image, turned, both, block = rest
     y, low, c = place[0], place[2] == 0, place[3]
     line = lax.broadcasted_iota(jnp.int32, (16, 384), 0)
     number = jnp.zeros((16, 384), jnp.int32)
@@ -105,16 +105,16 @@
     split = jnp.where(lane == 0, number >> 6, jnp.where(lane == 1, number & 63, 0))
     image[48:, :] = split.astype(f32).astype(bf16)
     image[:48, :] = fold(unit_rows(pic[...])[0].astype(bf16))
-    for source, target in ((tokens, own), (other_tokens, other)):
+    for source, first in ((tokens, 0), (other_tokens, 384)):
         turned[...] = source[...].T
         for chip in range(16):
             here = pl.ds(pl.multiple_of(chip * 96 + c * 48, 16), 48)
-            target[chip * 48 : chip * 48 + 48, :] = turned[here, :]
+            both[chip * 48 : chip * 48 + 48, first : first + 384] = turned[here, :]
     for k, out in enumerate((a0, a1, a2, a3)):
         at = pl.ds(pl.multiple_of(((y - k) & 3) * 384, 384), 384)
-        acc = jnp.dot(own[...], adj[:, at], preferred_element_type=f32)
-        acc = acc + jnp.dot(other[...], other_adj[:, at], preferred_element_type=f32)
-        acc = acc.astype(bf16)
+        block[:384, :] = adj[:, at]
+        block[384:, :] = other_adj[:, at]
+        acc = jnp.dot(both[...], block[...], preferred_element_type=f32).astype(bf16)
         out[:CUT, :] = acc[:CUT]
         out[CUT : 2 * CUT, :] = acc[384 : 384 + CUT]
         b_own[:, at] = jnp.where(low, acc[CUT:384], acc[384 + CUT :])
@@ -128,11 +128,13 @@
 ):
     b0, b1, b2, b3, total = rest
     y, xh = place[0], place[2]
-    total[...] = a0[...].astype(f32)
-    for part in (a1, a2, a3):
-        total[...] += part[: 2 * CUT, :].astype(f32)
-    a_own[...] = total[pl.ds(pl.multiple_of(xh * CUT, 16), CUT), :]
-    near[:CUT, :] = total[pl.ds(pl.multiple_of((1 - xh) * CUT, 16), CUT), :].astype(bf16)
+    del total
+    for first, out in ((xh, a_own), (1 - xh, near)):
+        here = pl.ds(pl.multiple_of(first * CUT, 16), CUT)
+        half = a0[here, :].astype(f32)
+        for part in (a1, a2, a3):
+            half = half + part[here, :].astype(f32)
+        out[:CUT, :] = half.astype(out.dtype)
     for k, out in enumerate((b0, b1, b2, b3)):
         at = pl.ds(pl.multiple_of(((y - k) & 3) * 384, 384), 384)
         both = b_own[:, at].astype(f32) + b_in[:, at].astype(f32)
@@ -195,7 +197,7 @@
     for k in range(1, 8):
         total = total + back[k].astype(f32)
     grad[...] = back_through_norm(cap[...], unfold(total[:48]))
-    piece = total[48:] * (1.0 / math.sqrt(98304))
+    piece = total[48:].astype(bf16)
     for k in range(8):
         pieces[k] = piece
     total = g0[...]
@@ -211,7 +213,8 @@
         total = total + part[...].astype(f32)
     image_grad[...] = back_through_norm(pic[...], unfold(total))
     for k in range(4):
-        weight_grad[:, k * 384 : k * 384 + 384] = pieces[k] + pieces[4 + k]
+        piece = pieces[k].astype(f32) + pieces[4 + k].astype(f32)
+        weight_grad[:, k * 384 : k * 384 + 384] = piece * (1.0 / math.sqrt(98304))
 
 
 def project_kernel(place, adj, w, w_pair, other, other_pair, *rest):
@@ -269,7 +272,7 @@
     (along_z,) = call(
         text_kernel, (shape(8, 144, 384),), place, caption_vectors_prenorm, dense_mapping_matrix
     )
-    along_z = exchange(after(along_z, other_tokens, other_adjoint), "z")
+    along_z = exchange(after(along_z, other_tokens), "z")
 
     *a, b_own, b_out, image = call(
         weight_kernel,
@@ -289,7 +292,7 @@
         other_adjoint,
         scratch=[
             pltpu.VMEM((1536, 384), bf16),
-            pltpu.VMEM((768, 384), bf16),
+            pltpu.VMEM((768, 768), bf16),
             pltpu.VMEM((768, 384), bf16),
         ],
         spaces=(pltpu.SMEM,),
@@ -366,7 +369,7 @@
         middle_kernel,
         (
             shape(16, 1152, dtype=f32),
-            shape(8, 48, 384, dtype=f32),
+            shape(8, 48, 384),
             shape(48, 384, dtype=f32),
             *[shape(48, 384)] * 3,
         ),

time: 116 us -> 114 us (0.983)
  waiting for transfers between devices: 35.3 us -> 33.3 us
  local copies, waits for them, and re-layouts: 6.38 us -> 7.57 us
    ppermute x2, starting transfers between devices: 3.95 us -> 1.24 us  [swap_far(): return lax.ppermute(x, 'xh', [(0, 1), (1, 0)])]
    all_to_all x3, waiting for transfers between devices: 4.86 us -> 2.27 us  [exchange(): return lax.all_to_all(x, axes, 0, 0, tiled=True)]
    ppermute x9, starting transfers between devices: 9.94 us -> 12.2 us  [turn(): return lax.ppermute(x, axes, [(at[i], at[(i + by) % 4]) for i in range(4)])]
    unnamed x36 -> x38, local copies, waits for them, and re-layouts: 6.26 us -> 7.46 us
  transfers between devices with their start and end apart: 30 -> 30, of which waited for: 10 -> 8; matrix products, arithmetic and copies ran while one was open for 0% -> 0% of each run, Pallas kernels for 18% -> 17%
where the time goes in v5:
time: 114 us; the launch traced here: 113 us
  starting transfers between devices  46.8 us (41%)
  waiting for transfers between devices  33.3 us (29%)
  Pallas kernels  23.6 us (21%)
  local copies, waits for them, and re-layouts  7.57 us (7%)
  between operations  2.1 us (2%)
    ppermute x9, waiting for transfers between devices, turn(): return lax.ppermute(x, axes, [(at[i], at[(i + by) % 4]) for i in range(4)])  24.1 us
    all_to_all x3, starting transfers between devices, exchange(): return lax.all_to_all(x, axes, 0, 0, tiled=True)  20.3 us
    pallas_call x7, Pallas kernels, call(): pl.pallas_call(kernel, out_shape=tuple(outs), in_specs=[pl.BlockSpec(memo...  15.4 us
    ppermute x9, starting transfers between devices, turn(): return lax.ppermute(x, axes, [(at[i], at[(i + by) % 4]) for i in range(4)])  12.2 us
    pallas_call x2, Pallas kernels, project(): pl.pallas_call(project_kernel, grid_spec=pltpu.PrefetchScalarGridSpec(num...  8.21 us
    ppermute x4, starting transfers between devices, swap_pairs(): return lax.ppermute(x, 'xl', [(0, 1), (1, 0)])  7.83 us
    unnamed x38, local copies, waits for them, and re-layouts  7.46 us
    ppermute x4, waiting for transfers between devices, swap_pairs(): return lax.ppermute(x, 'xl', [(0, 1), (1, 0)])  4.38 us
  transfers between devices with their start and end apart: 30, of which 8 were waited for; matrix products, arithmetic and copies ran while one was open for 0% of the time, Pallas kernels for 17%

profile of v5, /device:TPU:2, one launch (start us, length us, event | category | flops | bytes accessed | tf_op | source)
XLA Modules:
  0.0 113.4 jit_solution(5779226684937056440)
XLA Ops:
  0.7 0.5 collective-permute-start.1
  1.3 0.9 copy-done.1
  2.2 0.9 copy-done.7
  3.1 1.6 %shard_map.113 = bf16[8,144,384]{2,1,0:T(8,128)(2,1)} custom-call(s32[5]{0:T(128)S(1)} %stack.23.place, f32[16,1152]{1,0:T(8,128)S(1)} %copy-done.1, bf16[48,1536]{1,0:T(8,128)(2,1)S(1)} %copy-done.7), custom_call_target="tpu_custom_call" | custom-call | bytes 1105920 | tf_op jit(solution)/shard_map/pallas_call | solution.py:73
  4.7 8.5 %all-to-all-start = ((bf16[8,144,384]{2,1,0:T(8,128)(2,1)}), bf16[8,144,384]{2,1,0:T(8,128)(2,1)S(1)}, u32[]{:S(2)}, u32[]{:S(2)}) async-start(bf16[8,144,384]{2,1,0:T(8,128)(2,1)} %shard_map.113), calls=%async_computation | async-start | bytes 1769472 | tf_op jit(solution)/shard_map/all_to_all | solution.py:44
  13.2 4.8 %shard_map.111 = (bf16[384,384]{1,0:T(8,128)(2,1)S(1)}, bf16[448,384]{1,0:T(8,128)(2,1)S(1)}, bf16[448,384]{1,0:T(8,128)(2,1)S(1)}, bf16[448,384]{1,0:T(8,128)(2...) custom-call(s32[5]{0:T(128)S(1)} %stack.23.place, ...), custom_call_target="tpu_custom_call" | custom-call | flops 1811939328 | bytes 7348288 | tf_op jit(solution)/shard_map/pallas_call | solution.py:73
  18.0 1.6 %collective-permute-start.5 = (bf16[192,1536]{1,0:T(8,128)(2,1)S(1)}, bf16[192,1536]{1,0:T(8,128)(2,1)S(1)}, u32[]{:S(2)}, u32[]{:S(2)}) collective-permute-start(bf16[192,1536]{1,0:T(8,128)(2,1)S(1)} %get-tuple-element.45), channel_id=1, source_target_pairs={{0,144},{128,16},{16,128},{144,0},{1,145},{129,17},{17,129},{145,1... | collective-permute-start | bytes 1769480 | tf_op jit(solution)/shard_map/ppermute | solution.py:32
  19.6 3.0 %collective-permute-start.2 = (bf16[448,384]{1,0:T(8,128)(2,1)S(1)}, bf16[448,384]{1,0:T(8,128)(2,1)S(1)}, u32[]{:S(2)}, u32[]{:S(2)}) collective-permute-start(bf16[448,384]{1,0:T(8,128)(2,1)S(1)} %get-tuple-element.41), channel_id=1, source_target_pairs={{0,96},{32,0},{64,32},{96,64},{1,97},{33,1},{65,33},{97,65},{2,98}... | collective-permute-start | bytes 1032200 | tf_op jit(solution)/shard_map/ppermute | solution.py:27
  22.6 0.6 collective-permute-start.3
  23.3 1.0 collective-permute-start.4
  24.3 12.8 %collective-permute-done.2.a1 = bf16[448,384]{1,0:T(8,128)(2,1)S(1)} collective-permute-done((bf16[448,384]{1,0:T(8,128)(2,1)S(1)}, bf16[448,384]{1,0:T(8,128)(2,1)S(1)}, u32[]{:S(2)}, u32[]{:S(2)}) %collective-permute-start.2) | collective-permute-done | bytes 344096 | tf_op jit(solution)/shard_map/ppermute | solution.py:27
  37.1 3.7 %collective-permute-done.4.a3 = bf16[448,384]{1,0:T(8,128)(2,1)S(1)} collective-permute-done((bf16[448,384]{1,0:T(8,128)(2,1)S(1)}, bf16[448,384]{1,0:T(8,128)(2,1)S(1)}, u32[]{:S(2)}, u32[]{:S(2)}) %collective-permute-start.4) | collective-permute-done | bytes 344096 | tf_op jit(solution)/shard_map/ppermute | solution.py:27
  40.8 1.5 %shard_map.112 = (f32[192,384]{1,0:T(8,128)S(1)}, bf16[448,384]{1,0:T(8,128)(2,1)}, bf16[256,384]{1,0:T(8,128)(2,1)S(1)}, f32[192,384]{1,0:T(8,128)S(1)}, bf16[1...) custom-call(s32[5]{0:T(128)S(1)} %stack.23.place, ...), custom_call_target="tpu_custom_call" | custom-call | bytes 4128768 | tf_op jit(solution)/shard_map/pallas_call | solution.py:73
  42.2 0.7 copy-done.14
  42.9 0.6 collective-permute-start.10
  43.5 0.5 collective-permute-start.6
  44.0 0.6 collective-permute-start.11
  44.8 1.8 %collective-permute-start.7 = (bf16[256,384]{1,0:T(8,128)(2,1)S(1)}, bf16[256,384]{1,0:T(8,128)(2,1)S(1)}, u32[]{:S(2)}, u32[]{:S(2)}) collective-permute-start(bf16[256,384]{1,0:T(8,128)(2,1)S(1)} %get-tuple-element.47.i0), channel_id=1, source_target_pairs={{0,128},{128,0},{1,129},{129,1},{2,130},{130,2},{3,131},{131,3},{4... | collective-permute-start | bytes 589832 | tf_op jit(solution)/shard_map/ppermute | solution.py:36
  46.6 3.2 %collective-permute-done.10.rest_1_ = bf16[192,384]{1,0:T(8,128)(2,1)S(1)} collective-permute-done((bf16[192,384]{1,0:T(8,128)(2,1)}, bf16[192,384]{1,0:T(8,128)(2,1)S(1)}, u32[]{:S(2)}, u32[]{:S(2)}) %collective-permute-start.10) | collective-permute-done | bytes 147488 | tf_op jit(solution)/shard_map/ppermute | solution.py:27
  49.8 0.7 copy-done.3
  50.5 0.8 collective-permute-start.8
  51.3 0.7 copy-done.5
  51.9 1.1 collective-permute-start.12
  54.3 4.4 %collective-permute-done.12.rest_3_ = bf16[192,384]{1,0:T(8,128)(2,1)S(1)} collective-permute-done((bf16[192,384]{1,0:T(8,128)(2,1)}, bf16[192,384]{1,0:T(8,128)(2,1)S(1)}, u32[]{:S(2)}, u32[]{:S(2)}) %collective-permute-start.12) | collective-permute-done | bytes 147488 | tf_op jit(solution)/shard_map/ppermute | solution.py:27
  58.8 0.9 copy-done.4
  59.7 0.9 copy-done.6
  60.6 2.8 %shard_map.114 = (bf16[8,96,384]{2,1,0:T(8,128)(2,1)}, bf16[384,384]{1,0:T(8,128)(2,1)S(1)}, f32[192,384]{1,0:T(8,128)S(1)}, bf16[192,384]{1,0:T(8,128)(2,1)S(1)...) custom-call(s32[5]{0:T(128)S(1)} %stack.23.place, ...), custom_call_target="tpu_custom_call" | custom-call | flops 452984832 | bytes 5652488 | tf_op jit(solution)/shard_map/pallas_call | solution.py:73
  63.4 1.9 %collective-permute-start.14 = (bf16[8,96,384]{2,1,0:T(8,128)(2,1)}, bf16[8,96,384]{2,1,0:T(8,128)(2,1)}, u32[]{:S(2)}, u32[]{:S(2)}) collective-permute-start(bf16[8,96,384]{2,1,0:T(8,128)(2,1)} %get-tuple-element.59.w), channel_id=1, source_target_pairs={{0,128},{128,0},{1,129},{129,1},{2,130},{130,2},{3,131},{131,3},{4... | collective-permute-start | bytes 1769480 | tf_op jit(solution)/shard_map/ppermute | solution.py:36
  65.3 1.5 %collective-permute-start.23 = (bf16[8,96,384]{2,1,0:T(8,128)(2,1)}, bf16[8,96,384]{2,1,0:T(8,128)(2,1)S(1)}, u32[]{:S(2)}, u32[]{:S(2)}) collective-permute-start(bf16[8,96,384]{2,1,0:T(8,128)(2,1)} %get-tuple-element.59.w), channel_id=1, source_target_pairs={{0,144},{128,16},{16,128},{144,0},{1,145},{129,17},{17,129},{145,1... | collective-permute-start | bytes 1769480 | tf_op jit(solution)/shard_map/ppermute | solution.py:32
  66.8 1.4 %shard_map.115 = bf16[8,96,384]{2,1,0:T(8,128)(2,1)} custom-call(s32[5]{0:T(128)S(1)} %stack.23.place, f32[128,1152]{1,0:T(8,128)S(1)} %get-tuple-element.56.t_own, bf16[128,1152]{1,0:T(8,128)(2,1)S(1)} %collective-permute-done.13.t_in, bf16[384,384]{1,0:T(8,128)(2,1)S(1)} %get-tuple-element.58.weight), custom_call_target="tpu_custom_call" | custom-call | bytes 1769472 | tf_op jit(solution)/shard_map/pallas_call | solution.py:73
  68.2 6.9 %all-to-all-start.1 = ((bf16[8,96,384]{2,1,0:T(8,128)(2,1)}), bf16[8,96,384]{2,1,0:T(8,128)(2,1)S(1)}, u32[]{:S(2)}, u32[]{:S(2)}) async-start(bf16[8,96,384]{2,1,0:T(8,128)(2,1)} %shard_map.115), calls=%async_computation.1 | async-start | bytes 1179648 | tf_op jit(solution)/shard_map/all_to_all | solution.py:44
  75.2 4.4 %collective-permute-done.14.w_pair = bf16[8,96,384]{2,1,0:T(8,128)(2,1)} collective-permute-done((bf16[8,96,384]{2,1,0:T(8,128)(2,1)}, bf16[8,96,384]{2,1,0:T(8,128)(2,1)}, u32[]{:S(2)}, u32[]{:S(2)}) %collective-permute-start.14) | collective-permute-done | bytes 589856 | tf_op jit(solution)/shard_map/ppermute | solution.py:36
  79.5 1.4 %collective-permute-done.23.w_pair = bf16[8,96,384]{2,1,0:T(8,128)(2,1)S(1)} collective-permute-done((bf16[8,96,384]{2,1,0:T(8,128)(2,1)}, bf16[8,96,384]{2,1,0:T(8,128)(2,1)S(1)}, u32[]{:S(2)}, u32[]{:S(2)}) %collective-permute-start.23) | collective-permute-done | bytes 589856 | tf_op jit(solution)/shard_map/ppermute | solution.py:32
  80.9 1.5 %collective-permute-start.24 = (bf16[8,96,384]{2,1,0:T(8,128)(2,1)S(1)}, bf16[8,96,384]{2,1,0:T(8,128)(2,1)S(1)}, u32[]{:S(2)}, u32[]{:S(2)}) collective-permute-start(bf16[8,96,384]{2,1,0:T(8,128)(2,1)S(1)} %collective-permute-done.23.w_pair), channel_id=1, source_target_pairs={{0,128},{128,0},{1,129},{129,1},{2,130},{130,2},{3,131},{131,3},{4... | collective-permute-start | bytes 1769480 | tf_op jit(solution)/shard_map/ppermute | solution.py:36
  82.4 1.5 %collective-permute-start.17 = (bf16[192,384]{1,0:T(8,128)(2,1)}, bf16[192,384]{1,0:T(8,128)(2,1)S(1)}, u32[]{:S(2)}, u32[]{:S(2)}) collective-permute-start(bf16[192,384]{1,0:T(8,128)(2,1)} %copy-done.13), channel_id=1, source_target_pairs={{0,32},{32,64},{64,96},{96,0},{1,33},{33,65},{65,97},{97,1},{2,34}... | collective-permute-start | bytes 442376 | tf_op jit(solution)/shard_map/ppermute | solution.py:27
  83.9 3.1 %collective-permute-start.18 = (bf16[192,384]{1,0:T(8,128)(2,1)}, bf16[192,384]{1,0:T(8,128)(2,1)}, u32[]{:S(2)}, u32[]{:S(2)}) collective-permute-start(bf16[192,384]{1,0:T(8,128)(2,1)} %copy-done.12), channel_id=1, source_target_pairs={{0,64},{32,96},{64,0},{96,32},{1,65},{33,97},{65,1},{97,33},{2,66}... | collective-permute-start | bytes 442376 | tf_op jit(solution)/shard_map/ppermute | solution.py:27
  87.0 0.6 collective-permute-start.19
  87.6 4.2 %shard_map.116.rest_0_ = bf16[384,1536]{1,0:T(8,128)(2,1)} custom-call(s32[5]{0:T(128)S(1)} %stack.23.place, bf16[384,1536]{1,0:T(8,128)(2,1)S(1)} %copy-done, bf16[8,96,384]{2,1,0:T(8,128)(2,1)} %get-tuple-element.59.w, bf16[8,96,384]{2,1,0:T(8,128)(2,1)} %collective-permute-done.14.w_pair, bf16[8,96,384]{2,1,0:T(8,128)(2,1)S(1)} %collective-permute-done.15.other, ...), custom_call_target="tpu_custom_call" | custom-call | flops 905969664 | bytes 6291456 | tf_op jit(solution)/shard_map/pallas_call | solution.py:239
  91.8 2.3 %all-to-all-done.1.back = bf16[8,96,384]{2,1,0:T(8,128)(2,1)S(1)} async-done(((bf16[8,96,384]{2,1,0:T(8,128)(2,1)}), bf16[8,96,384]{2,1,0:T(8,128)(2,1)S(1)}, u32[]{:S(2)}, u32[]{:S(2)}) %all-to-all-start.1) | async-done | bytes 589856 | tf_op jit(solution)/shard_map/all_to_all | solution.py:44
  94.1 1.9 %shard_map.117 = (f32[16,1152]{1,0:T(8,128)}, bf16[8,48,384]{2,1,0:T(8,128)(2,1)}, f32[48,384]{1,0:T(8,128)S(1)}, bf16[48,384]{1,0:T(8,128)(2,1)S(1)}, bf16[48,3...) custom-call(s32[5]{0:T(128)S(1)} %stack.23.place, bf16[8,96,384]{2,1,0:T(8,128)(2,1)S(1)} %all-to-all-done.1.back, ...), custom_call_target="tpu_custom_call" | custom-call | bytes 1953792 | tf_op jit(solution)/shard_map/pallas_call | solution.py:73
  96.0 0.6 copy-done.15
  96.6 0.6 copy-done.16
  97.2 0.6 copy-done.17
  98.4 4.9 %all-to-all-start.2 = ((bf16[8,48,384]{2,1,0:T(8,128)(2,1)}), bf16[8,48,384]{2,1,0:T(8,128)(2,1)S(1)}, u32[]{:S(2)}, u32[]{:S(2)}) async-start(bf16[8,48,384]{2,1,0:T(8,128)(2,1)} %get-tuple-element.69), calls=%async_computation.2 | async-start | bytes 589824 | tf_op jit(solution)/shard_map/all_to_all | solution.py:44
  103.7 2.6 %collective-permute-start.21 = (bf16[48,384]{1,0:T(8,128)(2,1)}, bf16[48,384]{1,0:T(8,128)(2,1)S(1)}, u32[]{:S(2)}, u32[]{:S(2)}) collective-permute-start(bf16[48,384]{1,0:T(8,128)(2,1)} %copy-done.16), channel_id=1, source_target_pairs={{0,128},{128,0},{1,129},{129,1},{2,130},{130,2},{3,131},{131,3},{4... | collective-permute-start | bytes 110600 | tf_op jit(solution)/shard_map/ppermute | solution.py:36
  106.8 4.0 %shard_map.118 = bf16[384,1536]{1,0:T(8,128)(2,1)} custom-call(s32[5]{0:T(128)S(1)} %stack.23.place, bf16[384,1536]{1,0:T(8,128)(2,1)S(1)} %copy-done, bf16[8,96,384]{2,1,0:T(8,128)(2,1)S(1)} %collective-permute-done.24.w, bf16[8,96,384]{2,1,0:T(8,128)(2,1)S(1)} %collective-permute-done.23.w_pair, ...), custom_call_target="tpu_custom_call", output_to_operand_aliasing={{}: (6, {})} | custom-call | flops 905969664 | bytes 6291456 | tf_op jit(solution)/shard_map/pallas_call | solution.py:239
  110.8 1.2 %collective-permute-done.22.h3 = bf16[48,384]{1,0:T(8,128)(2,1)S(1)} collective-permute-done((bf16[48,384]{1,0:T(8,128)(2,1)}, bf16[48,384]{1,0:T(8,128)(2,1)S(1)}, u32[]{:S(2)}, u32[]{:S(2)}) %collective-permute-start.22) | collective-permute-done | bytes 36896 | tf_op jit(solution)/shard_map/ppermute | solution.py:40
  112.0 1.4 %shard_map.119 = (f32[16,1152]{1,0:T(8,128)}, f32[48,1536]{1,0:T(8,128)}) custom-call(s32[5]{0:T(128)S(1)} %stack.23.place, f32[48,384]{1,0:T(8,128)S(1)} %get-tuple-element.65.h0, bf16[48,384]{1,0:T(8,128)(2,1)S(1)} %collective-permute-done.20.h1, bf16[48,384]{1,0:T(8,128)(2,1)S(1)} %collective-permute-done.21.h2, ...), custom_call_target="tpu_custom_call" | custom-call | bytes 921600 | tf_op jit(solution)/shard_map/pallas_call | solution.py:73
  (61 shorter events, 1.8 us)
Async XLA Ops:
  0.6 4.1 %collective-permute-start = (bf16[384,1536]{1,0:T(8,128)(2,1)}, bf16[384,1536]{1,0:T(8,128)(2,1)}, u32[]{:S(2)}, u32[]{:S(2)}) collective-permute-start(bf16[384,1536]{1,0:T(8,128)(2,1)} %tokens.1), channel_id=1, source_target_pairs={{0,1},{1,0},{2,3},{3,2},{4,5},{5,4},{6,7},{7,6},{8,9},{9,8},{10,11... | collective-permute-start | bytes 3538952 | tf_op jit(solution)/shard_map/ppermute | solution.py:22
  0.7 12.4 %collective-permute-start.1 = (bf16[384,1536]{1,0:T(8,128)(2,1)}, bf16[384,1536]{1,0:T(8,128)(2,1)}, u32[]{:S(2)}, u32[]{:S(2)}) collective-permute-start(bf16[384,1536]{1,0:T(8,128)(2,1)} %adj.5), channel_id=1, source_target_pairs={{0,1},{1,0},{2,3},{3,2},{4,5},{5,4},{6,7},{7,6},{8,9},{9,8},{10,11... | collective-permute-start | bytes 3538952 | tf_op jit(solution)/shard_map/ppermute | solution.py:22
  1.3 0.9 copy-start.1
  2.2 0.9 copy-start.7
  3.1 10.1 %copy-start = (bf16[384,1536]{1,0:T(8,128)(2,1)S(1)}, bf16[384,1536]{1,0:T(8,128)(2,1)}, u32[]{:S(2)}) copy-start(bf16[384,1536]{1,0:T(8,128)(2,1)} %adj.5) | copy-start | bytes 3538948
  3.1 10.1 %copy-start.8 = (f32[16,1152]{1,0:T(8,128)S(1)}, f32[16,1152]{1,0:T(8,128)}, u32[]{:S(2)}) copy-start(f32[16,1152]{1,0:T(8,128)} %pic.3) | copy-start | bytes 221188
  3.1 10.1 %copy-start.10 = (bf16[384,1536]{1,0:T(8,128)(2,1)S(1)}, bf16[384,1536]{1,0:T(8,128)(2,1)}, u32[]{:S(2)}) copy-start(bf16[384,1536]{1,0:T(8,128)(2,1)} %tokens.1) | copy-start | bytes 3538948
  3.1 10.1 %copy-start.18 = (s32[16]{0:T(128)S(1)}, s32[16]{0:T(128)}, u32[]{:S(2)}) copy-start(s32[16]{0:T(128)} %ids.1) | copy-start | bytes 196
  4.7 40.0 %all-to-all-start = ((bf16[8,144,384]{2,1,0:T(8,128)(2,1)}), bf16[8,144,384]{2,1,0:T(8,128)(2,1)S(1)}, u32[]{:S(2)}, u32[]{:S(2)}) async-start(bf16[8,144,384]{2,1,0:T(8,128)(2,1)} %shard_map.113), calls=%async_computation | async-start | bytes 1769472 | tf_op jit(solution)/shard_map/all_to_all | solution.py:44
  18.0 22.7 %collective-permute-start.5 = (bf16[192,1536]{1,0:T(8,128)(2,1)S(1)}, bf16[192,1536]{1,0:T(8,128)(2,1)S(1)}, u32[]{:S(2)}, u32[]{:S(2)}) collective-permute-start(bf16[192,1536]{1,0:T(8,128)(2,1)S(1)} %get-tuple-element.45), channel_id=1, source_target_pairs={{0,144},{128,16},{16,128},{144,0},{1,145},{129,17},{17,129},{145,1... | collective-permute-start | bytes 1769480 | tf_op jit(solution)/shard_map/ppermute | solution.py:32
  19.6 17.4 %collective-permute-start.2 = (bf16[448,384]{1,0:T(8,128)(2,1)S(1)}, bf16[448,384]{1,0:T(8,128)(2,1)S(1)}, u32[]{:S(2)}, u32[]{:S(2)}) collective-permute-start(bf16[448,384]{1,0:T(8,128)(2,1)S(1)} %get-tuple-element.41), channel_id=1, source_target_pairs={{0,96},{32,0},{64,32},{96,64},{1,97},{33,1},{65,33},{97,65},{2,98}... | collective-permute-start | bytes 1032200 | tf_op jit(solution)/shard_map/ppermute | solution.py:27
  22.6 14.4 %collective-permute-start.3 = (bf16[448,384]{1,0:T(8,128)(2,1)S(1)}, bf16[448,384]{1,0:T(8,128)(2,1)S(1)}, u32[]{:S(2)}, u32[]{:S(2)}) collective-permute-start(bf16[448,384]{1,0:T(8,128)(2,1)S(1)} %get-tuple-element.42), channel_id=1, source_target_pairs={{0,64},{32,96},{64,0},{96,32},{1,65},{33,97},{65,1},{97,33},{2,66}... | collective-permute-start | bytes 1032200 | tf_op jit(solution)/shard_map/ppermute | solution.py:27
  23.3 17.5 %collective-permute-start.4 = (bf16[448,384]{1,0:T(8,128)(2,1)S(1)}, bf16[448,384]{1,0:T(8,128)(2,1)S(1)}, u32[]{:S(2)}, u32[]{:S(2)}) collective-permute-start(bf16[448,384]{1,0:T(8,128)(2,1)S(1)} %get-tuple-element.43), channel_id=1, source_target_pairs={{0,32},{32,64},{64,96},{96,0},{1,33},{33,65},{65,97},{97,1},{2,34}... | collective-permute-start | bytes 1032200 | tf_op jit(solution)/shard_map/ppermute | solution.py:27
  42.2 0.7 copy-start.14
  42.9 6.9 %collective-permute-start.10 = (bf16[192,384]{1,0:T(8,128)(2,1)}, bf16[192,384]{1,0:T(8,128)(2,1)S(1)}, u32[]{:S(2)}, u32[]{:S(2)}) collective-permute-start(bf16[192,384]{1,0:T(8,128)(2,1)} %get-tuple-element.53), channel_id=1, source_target_pairs={{0,96},{32,0},{64,32},{96,64},{1,97},{33,1},{65,33},{97,65},{2,98}... | collective-permute-start | bytes 442376 | tf_op jit(solution)/shard_map/ppermute | solution.py:27
  43.5 15.3 %collective-permute-start.6 = (bf16[448,384]{1,0:T(8,128)(2,1)}, bf16[448,384]{1,0:T(8,128)(2,1)S(1)}, u32[]{:S(2)}, u32[]{:S(2)}) collective-permute-start(bf16[448,384]{1,0:T(8,128)(2,1)} %get-tuple-element.48), channel_id=1, source_target_pairs={{0,144},{128,16},{16,128},{144,0},{1,145},{129,17},{17,129},{145,1... | collective-permute-start | bytes 1032200 | tf_op jit(solution)/shard_map/ppermute | solution.py:32
  44.0 7.2 %collective-permute-start.11 = (bf16[192,384]{1,0:T(8,128)(2,1)}, bf16[192,384]{1,0:T(8,128)(2,1)S(1)}, u32[]{:S(2)}, u32[]{:S(2)}) collective-permute-start(bf16[192,384]{1,0:T(8,128)(2,1)} %get-tuple-element.54), channel_id=1, source_target_pairs={{0,64},{32,96},{64,0},{96,32},{1,65},{33,97},{65,1},{97,33},{2,66}... | collective-permute-start | bytes 442376 | tf_op jit(solution)/shard_map/ppermute | solution.py:27
  44.7 14.1 %collective-permute-start.9 = (bf16[8,48,384]{2,1,0:T(8,128)(2,1)S(1)}, bf16[8,48,384]{2,1,0:T(8,128)(2,1)S(1)}, u32[]{:S(2)}, u32[]{:S(2)}) collective-permute-start(bf16[8,48,384]{2,1,0:T(8,128)(2,1)S(1)} %slice.3), channel_id=1, source_target_pairs={{0,1},{1,0},{2,3},{3,2},{4,5},{5,4},{6,7},{7,6},{8,9},{9,8},{10,11... | collective-permute-start | bytes 884744 | tf_op jit(solution)/shard_map/ppermute | solution.py:22
  44.8 14.0 %collective-permute-start.7 = (bf16[256,384]{1,0:T(8,128)(2,1)S(1)}, bf16[256,384]{1,0:T(8,128)(2,1)S(1)}, u32[]{:S(2)}, u32[]{:S(2)}) collective-permute-start(bf16[256,384]{1,0:T(8,128)(2,1)S(1)} %get-tuple-element.47.i0), channel_id=1, source_target_pairs={{0,128},{128,0},{1,129},{129,1},{2,130},{130,2},{3,131},{131,3},{4... | collective-permute-start | bytes 589832 | tf_op jit(solution)/shard_map/ppermute | solution.py:36
  49.8 0.7 copy-start.3
  50.5 8.3 %collective-permute-start.8 = (bf16[256,384]{1,0:T(8,128)(2,1)S(1)}, bf16[256,384]{1,0:T(8,128)(2,1)S(1)}, u32[]{:S(2)}, u32[]{:S(2)}) collective-permute-start(bf16[256,384]{1,0:T(8,128)(2,1)S(1)} %get-tuple-element.47.i0), channel_id=1, source_target_pairs={{0,16},{16,0},{1,17},{17,1},{2,18},{18,2},{3,19},{19,3},{4,20},{20... | collective-permute-start | bytes 589832 | tf_op jit(solution)/shard_map/ppermute | solution.py:40
  51.2 0.7 copy-start.5
  51.9 6.8 %collective-permute-start.12 = (bf16[192,384]{1,0:T(8,128)(2,1)}, bf16[192,384]{1,0:T(8,128)(2,1)S(1)}, u32[]{:S(2)}, u32[]{:S(2)}) collective-permute-start(bf16[192,384]{1,0:T(8,128)(2,1)} %copy-done.14), channel_id=1, source_target_pairs={{0,32},{32,64},{64,96},{96,0},{1,33},{33,65},{65,97},{97,1},{2,34}... | collective-permute-start | bytes 442376 | tf_op jit(solution)/shard_map/ppermute | solution.py:27
  58.8 0.9 copy-start.4
  59.7 0.9 copy-start.6
  63.4 3.4 %copy-start.11 = (bf16[192,384]{1,0:T(8,128)(2,1)}, bf16[192,384]{1,0:T(8,128)(2,1)S(1)}, u32[]{:S(2)}) copy-start(bf16[192,384]{1,0:T(8,128)(2,1)S(1)} %get-tuple-element.64) | copy-start | bytes 442372
  63.4 3.4 %copy-start.12 = (bf16[192,384]{1,0:T(8,128)(2,1)}, bf16[192,384]{1,0:T(8,128)(2,1)S(1)}, u32[]{:S(2)}) copy-start(bf16[192,384]{1,0:T(8,128)(2,1)S(1)} %get-tuple-element.63) | copy-start | bytes 442372
  63.4 3.4 %copy-start.13 = (bf16[192,384]{1,0:T(8,128)(2,1)}, bf16[192,384]{1,0:T(8,128)(2,1)S(1)}, u32[]{:S(2)}) copy-start(bf16[192,384]{1,0:T(8,128)(2,1)S(1)} %get-tuple-element.62) | copy-start | bytes 442372
  63.4 3.4 %collective-permute-start.13 = (bf16[128,1152]{1,0:T(8,128)(2,1)S(1)}, bf16[128,1152]{1,0:T(8,128)(2,1)S(1)}, u32[]{:S(2)}, u32[]{:S(2)}) collective-permute-start(bf16[128,1152]{1,0:T(8,128)(2,1)S(1)} %get-tuple-element.57), channel_id=1, source_target_pairs={{0,1},{1,0},{2,3},{3,2},{4,5},{5,4},{6,7},{7,6},{8,9},{9,8},{10,11... | collective-permute-start | bytes 884744 | tf_op jit(solution)/shard_map/ppermute | solution.py:22
  63.4 16.1 %collective-permute-start.14 = (bf16[8,96,384]{2,1,0:T(8,128)(2,1)}, bf16[8,96,384]{2,1,0:T(8,128)(2,1)}, u32[]{:S(2)}, u32[]{:S(2)}) collective-permute-start(bf16[8,96,384]{2,1,0:T(8,128)(2,1)} %get-tuple-element.59.w), channel_id=1, source_target_pairs={{0,128},{128,0},{1,129},{129,1},{2,130},{130,2},{3,131},{131,3},{4... | collective-permute-start | bytes 1769480 | tf_op jit(solution)/shard_map/ppermute | solution.py:36
  65.3 15.6 %collective-permute-start.23 = (bf16[8,96,384]{2,1,0:T(8,128)(2,1)}, bf16[8,96,384]{2,1,0:T(8,128)(2,1)S(1)}, u32[]{:S(2)}, u32[]{:S(2)}) collective-permute-start(bf16[8,96,384]{2,1,0:T(8,128)(2,1)} %get-tuple-element.59.w), channel_id=1, source_target_pairs={{0,144},{128,16},{16,128},{144,0},{1,145},{129,17},{17,129},{145,1... | collective-permute-start | bytes 1769480 | tf_op jit(solution)/shard_map/ppermute | solution.py:32
  68.2 25.9 %all-to-all-start.1 = ((bf16[8,96,384]{2,1,0:T(8,128)(2,1)}), bf16[8,96,384]{2,1,0:T(8,128)(2,1)S(1)}, u32[]{:S(2)}, u32[]{:S(2)}) async-start(bf16[8,96,384]{2,1,0:T(8,128)(2,1)} %shard_map.115), calls=%async_computation.1 | async-start | bytes 1179648 | tf_op jit(solution)/shard_map/all_to_all | solution.py:44
  75.1 11.9 %collective-permute-start.15 = (bf16[8,96,384]{2,1,0:T(8,128)(2,1)}, bf16[8,96,384]{2,1,0:T(8,128)(2,1)S(1)}, u32[]{:S(2)}, u32[]{:S(2)}) collective-permute-start(bf16[8,96,384]{2,1,0:T(8,128)(2,1)} %get-tuple-element.59.w), channel_id=1, source_target_pairs={{0,1},{1,0},{2,3},{3,2},{4,5},{5,4},{6,7},{7,6},{8,9},{9,8},{10,11... | collective-permute-start | bytes 1769480 | tf_op jit(solution)/shard_map/ppermute | solution.py:22
  79.5 8.1 %collective-permute-start.16 = (bf16[8,96,384]{2,1,0:T(8,128)(2,1)}, bf16[8,96,384]{2,1,0:T(8,128)(2,1)S(1)}, u32[]{:S(2)}, u32[]{:S(2)}) collective-permute-start(bf16[8,96,384]{2,1,0:T(8,128)(2,1)} %collective-permute-done.14.w_pair), channel_id=1, source_target_pairs={{0,1},{1,0},{2,3},{3,2},{4,5},{5,4},{6,7},{7,6},{8,9},{9,8},{10,11... | collective-permute-start | bytes 1769480 | tf_op jit(solution)/shard_map/ppermute | solution.py:22
  80.9 17.0 %collective-permute-start.24 = (bf16[8,96,384]{2,1,0:T(8,128)(2,1)S(1)}, bf16[8,96,384]{2,1,0:T(8,128)(2,1)S(1)}, u32[]{:S(2)}, u32[]{:S(2)}) collective-permute-start(bf16[8,96,384]{2,1,0:T(8,128)(2,1)S(1)} %collective-permute-done.23.w_pair), channel_id=1, source_target_pairs={{0,128},{128,0},{1,129},{129,1},{2,130},{130,2},{3,131},{131,3},{4... | collective-permute-start | bytes 1769480 | tf_op jit(solution)/shard_map/ppermute | solution.py:36
  82.4 11.7 %collective-permute-start.17 = (bf16[192,384]{1,0:T(8,128)(2,1)}, bf16[192,384]{1,0:T(8,128)(2,1)S(1)}, u32[]{:S(2)}, u32[]{:S(2)}) collective-permute-start(bf16[192,384]{1,0:T(8,128)(2,1)} %copy-done.13), channel_id=1, source_target_pairs={{0,32},{32,64},{64,96},{96,0},{1,33},{33,65},{65,97},{97,1},{2,34}... | collective-permute-start | bytes 442376 | tf_op jit(solution)/shard_map/ppermute | solution.py:27
  83.9 10.2 %collective-permute-start.18 = (bf16[192,384]{1,0:T(8,128)(2,1)}, bf16[192,384]{1,0:T(8,128)(2,1)}, u32[]{:S(2)}, u32[]{:S(2)}) collective-permute-start(bf16[192,384]{1,0:T(8,128)(2,1)} %copy-done.12), channel_id=1, source_target_pairs={{0,64},{32,96},{64,0},{96,32},{1,65},{33,97},{65,1},{97,33},{2,66}... | collective-permute-start | bytes 442376 | tf_op jit(solution)/shard_map/ppermute | solution.py:27
  87.0 7.1 %copy-start.2 = (f32[16,1152]{1,0:T(8,128)S(1)}, f32[16,1152]{1,0:T(8,128)}, u32[]{:S(2)}) copy-start(f32[16,1152]{1,0:T(8,128)} %cap.3) | copy-start | bytes 221188
  87.0 7.1 %collective-permute-start.19 = (bf16[192,384]{1,0:T(8,128)(2,1)}, bf16[192,384]{1,0:T(8,128)(2,1)}, u32[]{:S(2)}, u32[]{:S(2)}) collective-permute-start(bf16[192,384]{1,0:T(8,128)(2,1)} %copy-done.11), channel_id=1, source_target_pairs={{0,96},{32,0},{64,32},{96,64},{1,97},{33,1},{65,33},{97,65},{2,98}... | collective-permute-start | bytes 442376 | tf_op jit(solution)/shard_map/ppermute | solution.py:27
  96.0 0.6 copy-start.15
  97.2 0.6 copy-start.17
  97.8 8.9 %collective-permute-start.26 = (bf16[8,96,384]{2,1,0:T(8,128)(2,1)S(1)}, bf16[8,96,384]{2,1,0:T(8,128)(2,1)S(1)}, u32[]{:S(2)}, u32[]{:S(2)}) collective-permute-start(bf16[8,96,384]{2,1,0:T(8,128)(2,1)S(1)} %collective-permute-done.23.w_pair), channel_id=1, source_target_pairs={{0,1},{1,0},{2,3},{3,2},{4,5},{5,4},{6,7},{7,6},{8,9},{9,8},{10,11... | collective-permute-start | bytes 1769480 | tf_op jit(solution)/shard_map/ppermute | solution.py:22
  97.9 8.9 %collective-permute-start.25 = (bf16[8,96,384]{2,1,0:T(8,128)(2,1)S(1)}, bf16[8,96,384]{2,1,0:T(8,128)(2,1)}, u32[]{:S(2)}, u32[]{:S(2)}) collective-permute-start(bf16[8,96,384]{2,1,0:T(8,128)(2,1)S(1)} %collective-permute-done.24.w), channel_id=1, source_target_pairs={{0,1},{1,0},{2,3},{3,2},{4,5},{5,4},{6,7},{7,6},{8,9},{9,8},{10,11... | collective-permute-start | bytes 1769480 | tf_op jit(solution)/shard_map/ppermute | solution.py:22
  98.4 12.4 %all-to-all-start.2 = ((bf16[8,48,384]{2,1,0:T(8,128)(2,1)}), bf16[8,48,384]{2,1,0:T(8,128)(2,1)S(1)}, u32[]{:S(2)}, u32[]{:S(2)}) async-start(bf16[8,48,384]{2,1,0:T(8,128)(2,1)} %get-tuple-element.69), calls=%async_computation.2 | async-start | bytes 589824 | tf_op jit(solution)/shard_map/all_to_all | solution.py:44
  103.3 7.5 %collective-permute-start.20 = (bf16[48,384]{1,0:T(8,128)(2,1)}, bf16[48,384]{1,0:T(8,128)(2,1)S(1)}, u32[]{:S(2)}, u32[]{:S(2)}) collective-permute-start(bf16[48,384]{1,0:T(8,128)(2,1)} %copy-done.17), channel_id=1, source_target_pairs={{0,144},{128,16},{16,128},{144,0},{1,145},{129,17},{17,129},{145,1... | collective-permute-start | bytes 110600 | tf_op jit(solution)/shard_map/ppermute | solution.py:32
  103.7 7.1 %collective-permute-start.21 = (bf16[48,384]{1,0:T(8,128)(2,1)}, bf16[48,384]{1,0:T(8,128)(2,1)S(1)}, u32[]{:S(2)}, u32[]{:S(2)}) collective-permute-start(bf16[48,384]{1,0:T(8,128)(2,1)} %copy-done.16), channel_id=1, source_target_pairs={{0,128},{128,0},{1,129},{129,1},{2,130},{130,2},{3,131},{131,3},{4... | collective-permute-start | bytes 110600 | tf_op jit(solution)/shard_map/ppermute | solution.py:36
  106.3 5.7 %copy-start.9 = (f32[16,1152]{1,0:T(8,128)S(1)}, f32[16,1152]{1,0:T(8,128)}, u32[]{:S(2)}) copy-start(f32[16,1152]{1,0:T(8,128)} %pic.3) | copy-start | bytes 221188
  106.3 5.7 %collective-permute-start.22 = (bf16[48,384]{1,0:T(8,128)(2,1)}, bf16[48,384]{1,0:T(8,128)(2,1)S(1)}, u32[]{:S(2)}, u32[]{:S(2)}) collective-permute-start(bf16[48,384]{1,0:T(8,128)(2,1)} %copy-done.15), channel_id=1, source_target_pairs={{0,16},{16,0},{1,17},{17,1},{2,18},{18,2},{3,19},{19,3},{4,20},{20... | collective-permute-start | bytes 110600 | tf_op jit(solution)/shard_map/ppermute | solution.py:40
  (1 other events, 0.6 us)

commit v6 on v5

--- a/solution.py
+++ b/solution.py
@@ -319,9 +319,10 @@
     )
     near_in = swap_halves(near)
     b = [b[0]] + [turn(b[k], COLUMN, -k) for k in (1, 2, 3)]
-    pair_in, far_in = swap_pairs(column), swap_far(column)
     along_z = after(along_z, near)
     other_text = swap_cores(along_z[:, :48])
+    sent = after(column, other_text)
+    pair_in, far_in = swap_pairs(sent), swap_far(sent)
     here, weight_plane, *g, t_own, t_out = call(
         tile_kernel,
         (

time: 114 us -> 111 us (0.974)
  waiting for transfers between devices: 33.3 us -> 36.4 us
  starting transfers between devices: 46.8 us -> 44 us
  local copies, waits for them, and re-layouts: 7.57 us -> 5.11 us
    ppermute x9, starting transfers between devices: 12.2 us -> 9.18 us  [turn(): return lax.ppermute(x, axes, [(at[i], at[(i + by) % 4]) for i in range(4)])]
    unnamed x38 -> x32, local copies, waits for them, and re-layouts: 7.46 us -> 5 us
    ppermute x4, waiting for transfers between devices: 4.38 us -> 5.83 us  [swap_pairs(): return lax.ppermute(x, 'xl', [(0, 1), (1, 0)])]
    ppermute x4, starting transfers between devices: 3.97 us -> 2.57 us  [swap_halves(): return lax.ppermute(x, axes, [(at[i], at[3 - i]) for i in range(4)])]
  transfers between devices with their start and end apart: 30 -> 30, of which waited for: 8 -> 11; matrix products, arithmetic and copies ran while one was open for 0% -> 0% of each run, Pallas kernels for 17% -> 17%
where the time goes in v6:
time: 111 us
  starting transfers between devices  44 us (40%)
  waiting for transfers between devices  36.4 us (33%)
  Pallas kernels  23 us (21%)
  local copies, waits for them, and re-layouts  5.11 us (5%)
  between operations  2.07 us (2%)
    ppermute x9, waiting for transfers between devices, turn(): return lax.ppermute(x, axes, [(at[i], at[(i + by) % 4]) for i in range(4)])  24.6 us
    all_to_all x3, starting transfers between devices, exchange(): return lax.all_to_all(x, axes, 0, 0, tiled=True)  20.3 us
    pallas_call x7, Pallas kernels, call(): pl.pallas_call(kernel, out_shape=tuple(outs), in_specs=[pl.BlockSpec(memo...  14.8 us
    ppermute x9, starting transfers between devices, turn(): return lax.ppermute(x, axes, [(at[i], at[(i + by) % 4]) for i in range(4)])  9.18 us
    ppermute x4, starting transfers between devices, swap_pairs(): return lax.ppermute(x, 'xl', [(0, 1), (1, 0)])  8.85 us
    pallas_call x2, Pallas kernels, project(): pl.pallas_call(project_kernel, grid_spec=pltpu.PrefetchScalarGridSpec(num...  8.22 us
    ppermute x4, waiting for transfers between devices, swap_pairs(): return lax.ppermute(x, 'xl', [(0, 1), (1, 0)])  5.83 us
    unnamed x32, local copies, waits for them, and re-layouts  5 us
  transfers between devices with their start and end apart: 30, of which 11 were waited for; matrix products, arithmetic and copies ran while one was open for 0% of the time, Pallas kernels for 17%

profile of v6, /device:TPU:2, one launch (start us, length us, event | category | flops | bytes accessed | tf_op | source)
XLA Modules:
  0.0 110.6 jit_solution(7846612512016378697)
XLA Ops:
  0.7 0.5 collective-permute-start.1
  1.3 0.9 copy-done.1
  2.2 0.9 copy-done.3
  3.1 1.6 %shard_map.113 = bf16[8,144,384]{2,1,0:T(8,128)(2,1)} custom-call(s32[5]{0:T(128)S(1)} %stack.23.place, f32[16,1152]{1,0:T(8,128)S(1)} %copy-done.1, bf16[48,1536]{1,0:T(8,128)(2,1)S(1)} %copy-done.3), custom_call_target="tpu_custom_call" | custom-call | bytes 1105920 | tf_op jit(solution)/shard_map/pallas_call | solution.py:73
  4.7 8.5 %all-to-all-start = ((bf16[8,144,384]{2,1,0:T(8,128)(2,1)}), bf16[8,144,384]{2,1,0:T(8,128)(2,1)S(1)}, u32[]{:S(2)}, u32[]{:S(2)}) async-start(bf16[8,144,384]{2,1,0:T(8,128)(2,1)} %shard_map.113), calls=%async_computation | async-start | bytes 1769472 | tf_op jit(solution)/shard_map/all_to_all | solution.py:44
  13.2 4.8 %shard_map.111 = (bf16[384,384]{1,0:T(8,128)(2,1)S(1)}, bf16[448,384]{1,0:T(8,128)(2,1)S(1)}, bf16[448,384]{1,0:T(8,128)(2,1)S(1)}, bf16[448,384]{1,0:T(8,128)(2...) custom-call(s32[5]{0:T(128)S(1)} %stack.23.place, ...), custom_call_target="tpu_custom_call" | custom-call | flops 1811939328 | bytes 7348288 | tf_op jit(solution)/shard_map/pallas_call | solution.py:73
  18.0 1.6 %collective-permute-start.5 = (bf16[192,1536]{1,0:T(8,128)(2,1)S(1)}, bf16[192,1536]{1,0:T(8,128)(2,1)S(1)}, u32[]{:S(2)}, u32[]{:S(2)}) collective-permute-start(bf16[192,1536]{1,0:T(8,128)(2,1)S(1)} %get-tuple-element.46), channel_id=1, source_target_pairs={{0,144},{128,16},{16,128},{144,0},{1,145},{129,17},{17,129},{145,1... | collective-permute-start | bytes 1769480 | tf_op jit(solution)/shard_map/ppermute | solution.py:32
  19.6 3.0 %collective-permute-start.2 = (bf16[448,384]{1,0:T(8,128)(2,1)S(1)}, bf16[448,384]{1,0:T(8,128)(2,1)S(1)}, u32[]{:S(2)}, u32[]{:S(2)}) collective-permute-start(bf16[448,384]{1,0:T(8,128)(2,1)S(1)} %get-tuple-element.42), channel_id=1, source_target_pairs={{0,96},{32,0},{64,32},{96,64},{1,97},{33,1},{65,33},{97,65},{2,98}... | collective-permute-start | bytes 1032200 | tf_op jit(solution)/shard_map/ppermute | solution.py:27
  22.6 0.6 collective-permute-start.3
  23.3 1.0 collective-permute-start.4
  24.3 12.8 %collective-permute-done.2.a1 = bf16[448,384]{1,0:T(8,128)(2,1)S(1)} collective-permute-done((bf16[448,384]{1,0:T(8,128)(2,1)S(1)}, bf16[448,384]{1,0:T(8,128)(2,1)S(1)}, u32[]{:S(2)}, u32[]{:S(2)}) %collective-permute-start.2) | collective-permute-done | bytes 344096 | tf_op jit(solution)/shard_map/ppermute | solution.py:27
  37.1 3.7 %collective-permute-done.4.a3 = bf16[448,384]{1,0:T(8,128)(2,1)S(1)} collective-permute-done((bf16[448,384]{1,0:T(8,128)(2,1)S(1)}, bf16[448,384]{1,0:T(8,128)(2,1)S(1)}, u32[]{:S(2)}, u32[]{:S(2)}) %collective-permute-start.4) | collective-permute-done | bytes 344096 | tf_op jit(solution)/shard_map/ppermute | solution.py:27
  40.8 0.8 shard_map.112
  41.6 0.7 copy-done.8
  42.5 0.6 collective-permute-start.6
  43.1 0.6 collective-permute-start.10
  43.7 0.3 collective-permute-done.7.other_text
  44.0 1.8 %collective-permute-start.8 = (bf16[256,384]{1,0:T(8,128)(2,1)S(1)}, bf16[256,384]{1,0:T(8,128)(2,1)S(1)}, u32[]{:S(2)}, u32[]{:S(2)}) collective-permute-start(bf16[256,384]{1,0:T(8,128)(2,1)S(1)} %get-tuple-element.52.i0), channel_id=1, source_target_pairs={{0,128},{128,0},{1,129},{129,1},{2,130},{130,2},{3,131},{131,3},{4... | collective-permute-start | bytes 589832 | tf_op jit(solution)/shard_map/ppermute | solution.py:36
  45.8 1.2 %collective-permute-start.9 = (bf16[256,384]{1,0:T(8,128)(2,1)S(1)}, bf16[256,384]{1,0:T(8,128)(2,1)S(1)}, u32[]{:S(2)}, u32[]{:S(2)}) collective-permute-start(bf16[256,384]{1,0:T(8,128)(2,1)S(1)} %get-tuple-element.52.i0), channel_id=1, source_target_pairs={{0,16},{16,0},{1,17},{17,1},{2,18},{18,2},{3,19},{19,3},{4,20},{20... | collective-permute-start | bytes 589832 | tf_op jit(solution)/shard_map/ppermute | solution.py:40
  47.0 0.6 collective-permute-start.11
  47.7 1.3 %collective-permute-done.10.rest_1_ = bf16[192,384]{1,0:T(8,128)(2,1)S(1)} collective-permute-done((bf16[192,384]{1,0:T(8,128)(2,1)S(1)}, bf16[192,384]{1,0:T(8,128)(2,1)S(1)}, u32[]{:S(2)}, u32[]{:S(2)}) %collective-permute-start.10) | collective-permute-done | bytes 147488 | tf_op jit(solution)/shard_map/ppermute | solution.py:27
  50.3 5.0 %collective-permute-done.11.rest_2_ = bf16[192,384]{1,0:T(8,128)(2,1)S(1)} collective-permute-done((bf16[192,384]{1,0:T(8,128)(2,1)S(1)}, bf16[192,384]{1,0:T(8,128)(2,1)S(1)}, u32[]{:S(2)}, u32[]{:S(2)}) %collective-permute-start.11) | collective-permute-done | bytes 147488 | tf_op jit(solution)/shard_map/ppermute | solution.py:27
  55.3 1.7 %collective-permute-done.12.rest_3_ = bf16[192,384]{1,0:T(8,128)(2,1)S(1)} collective-permute-done((bf16[192,384]{1,0:T(8,128)(2,1)S(1)}, bf16[192,384]{1,0:T(8,128)(2,1)S(1)}, u32[]{:S(2)}, u32[]{:S(2)}) %collective-permute-start.12) | collective-permute-done | bytes 147488 | tf_op jit(solution)/shard_map/ppermute | solution.py:27
  57.0 0.3 collective-permute-done.6.i1
  57.4 2.8 %shard_map.114 = (bf16[8,96,384]{2,1,0:T(8,128)(2,1)}, bf16[384,384]{1,0:T(8,128)(2,1)S(1)}, f32[192,384]{1,0:T(8,128)S(1)}, bf16[192,384]{1,0:T(8,128)(2,1)S(1)...) custom-call(s32[5]{0:T(128)S(1)} %stack.23.place, ...), custom_call_target="tpu_custom_call" | custom-call | flops 452984832 | bytes 5652488 | tf_op jit(solution)/shard_map/pallas_call | solution.py:73
  60.2 3.1 %collective-permute-start.14 = (bf16[8,96,384]{2,1,0:T(8,128)(2,1)}, bf16[8,96,384]{2,1,0:T(8,128)(2,1)}, u32[]{:S(2)}, u32[]{:S(2)}) collective-permute-start(bf16[8,96,384]{2,1,0:T(8,128)(2,1)} %get-tuple-element.61.w), channel_id=1, source_target_pairs={{0,128},{128,0},{1,129},{129,1},{2,130},{130,2},{3,131},{131,3},{4... | collective-permute-start | bytes 1769480 | tf_op jit(solution)/shard_map/ppermute | solution.py:36
  63.3 1.5 %shard_map.115 = bf16[8,96,384]{2,1,0:T(8,128)(2,1)} custom-call(s32[5]{0:T(128)S(1)} %stack.23.place, f32[128,1152]{1,0:T(8,128)S(1)} %get-tuple-element.58.t_own, bf16[128,1152]{1,0:T(8,128)(2,1)S(1)} %collective-permute-done.13.t_in, bf16[384,384]{1,0:T(8,128)(2,1)S(1)} %get-tuple-element.60.weight), custom_call_target="tpu_custom_call" | custom-call | bytes 1769472 | tf_op jit(solution)/shard_map/pallas_call | solution.py:73
  64.7 6.9 %all-to-all-start.1 = ((bf16[8,96,384]{2,1,0:T(8,128)(2,1)}), bf16[8,96,384]{2,1,0:T(8,128)(2,1)S(1)}, u32[]{:S(2)}, u32[]{:S(2)}) async-start(bf16[8,96,384]{2,1,0:T(8,128)(2,1)} %shard_map.115), calls=%async_computation.1 | async-start | bytes 1179648 | tf_op jit(solution)/shard_map/all_to_all | solution.py:44
  71.7 5.8 %collective-permute-done.14.w_pair = bf16[8,96,384]{2,1,0:T(8,128)(2,1)} collective-permute-done((bf16[8,96,384]{2,1,0:T(8,128)(2,1)}, bf16[8,96,384]{2,1,0:T(8,128)(2,1)}, u32[]{:S(2)}, u32[]{:S(2)}) %collective-permute-start.14) | collective-permute-done | bytes 589856 | tf_op jit(solution)/shard_map/ppermute | solution.py:36
  77.5 1.4 %collective-permute-done.23.w_pair = bf16[8,96,384]{2,1,0:T(8,128)(2,1)S(1)} collective-permute-done((bf16[8,96,384]{2,1,0:T(8,128)(2,1)}, bf16[8,96,384]{2,1,0:T(8,128)(2,1)S(1)}, u32[]{:S(2)}, u32[]{:S(2)}) %collective-permute-start.23) | collective-permute-done | bytes 589856 | tf_op jit(solution)/shard_map/ppermute | solution.py:32
  78.9 1.5 %collective-permute-start.24 = (bf16[8,96,384]{2,1,0:T(8,128)(2,1)S(1)}, bf16[8,96,384]{2,1,0:T(8,128)(2,1)S(1)}, u32[]{:S(2)}, u32[]{:S(2)}) collective-permute-start(bf16[8,96,384]{2,1,0:T(8,128)(2,1)S(1)} %collective-permute-done.23.w_pair), channel_id=1, source_target_pairs={{0,128},{128,0},{1,129},{129,1},{2,130},{130,2},{3,131},{131,3},{4... | collective-permute-start | bytes 1769480 | tf_op jit(solution)/shard_map/ppermute | solution.py:36
  80.3 2.1 %collective-permute-start.18 = (bf16[192,384]{1,0:T(8,128)(2,1)}, bf16[192,384]{1,0:T(8,128)(2,1)}, u32[]{:S(2)}, u32[]{:S(2)}) collective-permute-start(bf16[192,384]{1,0:T(8,128)(2,1)} %copy-done.10), channel_id=1, source_target_pairs={{0,64},{32,96},{64,0},{96,32},{1,65},{33,97},{65,1},{97,33},{2,66}... | collective-permute-start | bytes 442376 | tf_op jit(solution)/shard_map/ppermute | solution.py:27
  82.4 1.2 %collective-permute-start.19 = (bf16[192,384]{1,0:T(8,128)(2,1)}, bf16[192,384]{1,0:T(8,128)(2,1)}, u32[]{:S(2)}, u32[]{:S(2)}) collective-permute-start(bf16[192,384]{1,0:T(8,128)(2,1)} %copy-done.9), channel_id=1, source_target_pairs={{0,96},{32,0},{64,32},{96,64},{1,97},{33,1},{65,33},{97,65},{2,98}... | collective-permute-start | bytes 442376 | tf_op jit(solution)/shard_map/ppermute | solution.py:27
  83.7 4.2 %shard_map.116.rest_0_ = bf16[384,1536]{1,0:T(8,128)(2,1)} custom-call(s32[5]{0:T(128)S(1)} %stack.23.place, bf16[384,1536]{1,0:T(8,128)(2,1)S(1)} %copy-done, bf16[8,96,384]{2,1,0:T(8,128)(2,1)} %get-tuple-element.61.w, bf16[8,96,384]{2,1,0:T(8,128)(2,1)} %collective-permute-done.14.w_pair, bf16[8,96,384]{2,1,0:T(8,128)(2,1)S(1)} %collective-permute-done.15.other, ...), custom_call_target="tpu_custom_call" | custom-call | flops 905969664 | bytes 6291456 | tf_op jit(solution)/shard_map/pallas_call | solution.py:239
  87.9 3.0 %all-to-all-done.1.back = bf16[8,96,384]{2,1,0:T(8,128)(2,1)S(1)} async-done(((bf16[8,96,384]{2,1,0:T(8,128)(2,1)}), bf16[8,96,384]{2,1,0:T(8,128)(2,1)S(1)}, u32[]{:S(2)}, u32[]{:S(2)}) %all-to-all-start.1) | async-done | bytes 589856 | tf_op jit(solution)/shard_map/all_to_all | solution.py:44
  90.9 1.9 %shard_map.117 = (f32[16,1152]{1,0:T(8,128)}, bf16[8,48,384]{2,1,0:T(8,128)(2,1)}, f32[48,384]{1,0:T(8,128)S(1)}, bf16[48,384]{1,0:T(8,128)(2,1)S(1)}, bf16[48,3...) custom-call(s32[5]{0:T(128)S(1)} %stack.23.place, bf16[8,96,384]{2,1,0:T(8,128)(2,1)S(1)} %all-to-all-done.1.back, ...), custom_call_target="tpu_custom_call" | custom-call | bytes 1953792 | tf_op jit(solution)/shard_map/pallas_call | solution.py:73
  92.8 0.6 copy-done.5
  93.4 0.6 copy-done.12
  94.0 0.6 copy-done.13
  94.6 0.6 copy-done.14
  95.3 0.5 collective-permute-start.25
  95.8 4.9 %all-to-all-start.2 = ((bf16[8,48,384]{2,1,0:T(8,128)(2,1)}), bf16[8,48,384]{2,1,0:T(8,128)(2,1)S(1)}, u32[]{:S(2)}, u32[]{:S(2)}) async-start(bf16[8,48,384]{2,1,0:T(8,128)(2,1)} %get-tuple-element.71), calls=%async_computation.2 | async-start | bytes 589824 | tf_op jit(solution)/shard_map/all_to_all | solution.py:44
  100.7 0.4 collective-permute-start.20
  101.0 2.5 %collective-permute-start.21 = (bf16[48,384]{1,0:T(8,128)(2,1)}, bf16[48,384]{1,0:T(8,128)(2,1)S(1)}, u32[]{:S(2)}, u32[]{:S(2)}) collective-permute-start(bf16[48,384]{1,0:T(8,128)(2,1)} %copy-done.13), channel_id=1, source_target_pairs={{0,128},{128,0},{1,129},{129,1},{2,130},{130,2},{3,131},{131,3},{4... | collective-permute-start | bytes 110600 | tf_op jit(solution)/shard_map/ppermute | solution.py:36
  103.5 0.7 collective-permute-start.22
  104.2 4.0 %shard_map.118 = bf16[384,1536]{1,0:T(8,128)(2,1)} custom-call(s32[5]{0:T(128)S(1)} %stack.23.place, bf16[384,1536]{1,0:T(8,128)(2,1)S(1)} %copy-done, bf16[8,96,384]{2,1,0:T(8,128)(2,1)S(1)} %collective-permute-done.24.w, bf16[8,96,384]{2,1,0:T(8,128)(2,1)S(1)} %collective-permute-done.23.w_pair, ...), custom_call_target="tpu_custom_call", output_to_operand_aliasing={{}: (6, {})} | custom-call | flops 905969664 | bytes 6291456 | tf_op jit(solution)/shard_map/pallas_call | solution.py:239
  108.2 1.0 collective-permute-done.22.h3
  109.2 1.4 %shard_map.119 = (f32[16,1152]{1,0:T(8,128)}, f32[48,1536]{1,0:T(8,128)}) custom-call(s32[5]{0:T(128)S(1)} %stack.23.place, f32[48,384]{1,0:T(8,128)S(1)} %copy-done.6, bf16[48,384]{1,0:T(8,128)(2,1)S(1)} %collective-permute-done.20.h1, bf16[48,384]{1,0:T(8,128)(2,1)S(1)} %collective-permute-done.21.h2, bf16[48,384]{1,0:T(8,128)(2,1)S(1)} %collective-permute-done.22.h3, ...), custom_call_target="tpu_custom_call" | custom-call | bytes 921600 | tf_op jit(solution)/shard_map/pallas_call | solution.py:73
  (55 shorter events, 0.4 us)
Async XLA Ops:
  0.6 4.1 %collective-permute-start = (bf16[384,1536]{1,0:T(8,128)(2,1)}, bf16[384,1536]{1,0:T(8,128)(2,1)}, u32[]{:S(2)}, u32[]{:S(2)}) collective-permute-start(bf16[384,1536]{1,0:T(8,128)(2,1)} %tokens.1), channel_id=1, source_target_pairs={{0,1},{1,0},{2,3},{3,2},{4,5},{5,4},{6,7},{7,6},{8,9},{9,8},{10,11... | collective-permute-start | bytes 3538952 | tf_op jit(solution)/shard_map/ppermute | solution.py:22
  0.7 12.4 %collective-permute-start.1 = (bf16[384,1536]{1,0:T(8,128)(2,1)}, bf16[384,1536]{1,0:T(8,128)(2,1)}, u32[]{:S(2)}, u32[]{:S(2)}) collective-permute-start(bf16[384,1536]{1,0:T(8,128)(2,1)} %adj.5), channel_id=1, source_target_pairs={{0,1},{1,0},{2,3},{3,2},{4,5},{5,4},{6,7},{7,6},{8,9},{9,8},{10,11... | collective-permute-start | bytes 3538952 | tf_op jit(solution)/shard_map/ppermute | solution.py:22
  1.3 0.9 copy-start.1
  2.2 0.9 copy-start.3
  3.1 10.1 %copy-start = (bf16[384,1536]{1,0:T(8,128)(2,1)S(1)}, bf16[384,1536]{1,0:T(8,128)(2,1)}, u32[]{:S(2)}) copy-start(bf16[384,1536]{1,0:T(8,128)(2,1)} %adj.5) | copy-start | bytes 3538948
  3.1 10.1 %copy-start.4 = (f32[16,1152]{1,0:T(8,128)S(1)}, f32[16,1152]{1,0:T(8,128)}, u32[]{:S(2)}) copy-start(f32[16,1152]{1,0:T(8,128)} %pic.3) | copy-start | bytes 221188
  3.1 10.1 %copy-start.7 = (bf16[384,1536]{1,0:T(8,128)(2,1)S(1)}, bf16[384,1536]{1,0:T(8,128)(2,1)}, u32[]{:S(2)}) copy-start(bf16[384,1536]{1,0:T(8,128)(2,1)} %tokens.1) | copy-start | bytes 3538948
  3.1 10.1 %copy-start.15 = (s32[16]{0:T(128)S(1)}, s32[16]{0:T(128)}, u32[]{:S(2)}) copy-start(s32[16]{0:T(128)} %ids.1) | copy-start | bytes 196
  4.7 37.6 %all-to-all-start = ((bf16[8,144,384]{2,1,0:T(8,128)(2,1)}), bf16[8,144,384]{2,1,0:T(8,128)(2,1)S(1)}, u32[]{:S(2)}, u32[]{:S(2)}) async-start(bf16[8,144,384]{2,1,0:T(8,128)(2,1)} %shard_map.113), calls=%async_computation | async-start | bytes 1769472 | tf_op jit(solution)/shard_map/all_to_all | solution.py:44
  18.0 22.7 %collective-permute-start.5 = (bf16[192,1536]{1,0:T(8,128)(2,1)S(1)}, bf16[192,1536]{1,0:T(8,128)(2,1)S(1)}, u32[]{:S(2)}, u32[]{:S(2)}) collective-permute-start(bf16[192,1536]{1,0:T(8,128)(2,1)S(1)} %get-tuple-element.46), channel_id=1, source_target_pairs={{0,144},{128,16},{16,128},{144,0},{1,145},{129,17},{17,129},{145,1... | collective-permute-start | bytes 1769480 | tf_op jit(solution)/shard_map/ppermute | solution.py:32
  19.6 17.4 %collective-permute-start.2 = (bf16[448,384]{1,0:T(8,128)(2,1)S(1)}, bf16[448,384]{1,0:T(8,128)(2,1)S(1)}, u32[]{:S(2)}, u32[]{:S(2)}) collective-permute-start(bf16[448,384]{1,0:T(8,128)(2,1)S(1)} %get-tuple-element.42), channel_id=1, source_target_pairs={{0,96},{32,0},{64,32},{96,64},{1,97},{33,1},{65,33},{97,65},{2,98}... | collective-permute-start | bytes 1032200 | tf_op jit(solution)/shard_map/ppermute | solution.py:27
  22.6 14.4 %collective-permute-start.3 = (bf16[448,384]{1,0:T(8,128)(2,1)S(1)}, bf16[448,384]{1,0:T(8,128)(2,1)S(1)}, u32[]{:S(2)}, u32[]{:S(2)}) collective-permute-start(bf16[448,384]{1,0:T(8,128)(2,1)S(1)} %get-tuple-element.43), channel_id=1, source_target_pairs={{0,64},{32,96},{64,0},{96,32},{1,65},{33,97},{65,1},{97,33},{2,66}... | collective-permute-start | bytes 1032200 | tf_op jit(solution)/shard_map/ppermute | solution.py:27
  23.3 17.5 %collective-permute-start.4 = (bf16[448,384]{1,0:T(8,128)(2,1)S(1)}, bf16[448,384]{1,0:T(8,128)(2,1)S(1)}, u32[]{:S(2)}, u32[]{:S(2)}) collective-permute-start(bf16[448,384]{1,0:T(8,128)(2,1)S(1)} %get-tuple-element.44), channel_id=1, source_target_pairs={{0,32},{32,64},{64,96},{96,0},{1,33},{33,65},{65,97},{97,1},{2,34}... | collective-permute-start | bytes 1032200 | tf_op jit(solution)/shard_map/ppermute | solution.py:27
  41.6 0.7 copy-start.8
  42.4 1.7 %collective-permute-start.7 = (bf16[8,48,384]{2,1,0:T(8,128)(2,1)S(1)}, bf16[8,48,384]{2,1,0:T(8,128)(2,1)S(1)}, u32[]{:S(2)}, u32[]{:S(2)}) collective-permute-start(bf16[8,48,384]{2,1,0:T(8,128)(2,1)S(1)} %slice.3), channel_id=1, source_target_pairs={{0,1},{1,0},{2,3},{3,2},{4,5},{5,4},{6,7},{7,6},{8,9},{9,8},{10,11... | collective-permute-start | bytes 884744 | tf_op jit(solution)/shard_map/ppermute | solution.py:22
  42.5 14.9 %collective-permute-start.6 = (bf16[448,384]{1,0:T(8,128)(2,1)}, bf16[448,384]{1,0:T(8,128)(2,1)S(1)}, u32[]{:S(2)}, u32[]{:S(2)}) collective-permute-start(bf16[448,384]{1,0:T(8,128)(2,1)} %copy-done.8), channel_id=1, source_target_pairs={{0,144},{128,16},{16,128},{144,0},{1,145},{129,17},{17,129},{145,1... | collective-permute-start | bytes 1032200 | tf_op jit(solution)/shard_map/ppermute | solution.py:32
  43.1 5.9 %collective-permute-start.10 = (bf16[192,384]{1,0:T(8,128)(2,1)S(1)}, bf16[192,384]{1,0:T(8,128)(2,1)S(1)}, u32[]{:S(2)}, u32[]{:S(2)}) collective-permute-start(bf16[192,384]{1,0:T(8,128)(2,1)S(1)} %get-tuple-element.55), channel_id=1, source_target_pairs={{0,96},{32,0},{64,32},{96,64},{1,97},{33,1},{65,33},{97,65},{2,98}... | collective-permute-start | bytes 442376 | tf_op jit(solution)/shard_map/ppermute | solution.py:27
  44.0 13.3 %collective-permute-start.8 = (bf16[256,384]{1,0:T(8,128)(2,1)S(1)}, bf16[256,384]{1,0:T(8,128)(2,1)S(1)}, u32[]{:S(2)}, u32[]{:S(2)}) collective-permute-start(bf16[256,384]{1,0:T(8,128)(2,1)S(1)} %get-tuple-element.52.i0), channel_id=1, source_target_pairs={{0,128},{128,0},{1,129},{129,1},{2,130},{130,2},{3,131},{131,3},{4... | collective-permute-start | bytes 589832 | tf_op jit(solution)/shard_map/ppermute | solution.py:36
  45.8 11.5 %collective-permute-start.9 = (bf16[256,384]{1,0:T(8,128)(2,1)S(1)}, bf16[256,384]{1,0:T(8,128)(2,1)S(1)}, u32[]{:S(2)}, u32[]{:S(2)}) collective-permute-start(bf16[256,384]{1,0:T(8,128)(2,1)S(1)} %get-tuple-element.52.i0), channel_id=1, source_target_pairs={{0,16},{16,0},{1,17},{17,1},{2,18},{18,2},{3,19},{19,3},{4,20},{20... | collective-permute-start | bytes 589832 | tf_op jit(solution)/shard_map/ppermute | solution.py:40
  47.0 8.3 %collective-permute-start.11 = (bf16[192,384]{1,0:T(8,128)(2,1)S(1)}, bf16[192,384]{1,0:T(8,128)(2,1)S(1)}, u32[]{:S(2)}, u32[]{:S(2)}) collective-permute-start(bf16[192,384]{1,0:T(8,128)(2,1)S(1)} %get-tuple-element.56), channel_id=1, source_target_pairs={{0,64},{32,96},{64,0},{96,32},{1,65},{33,97},{65,1},{97,33},{2,66}... | collective-permute-start | bytes 442376 | tf_op jit(solution)/shard_map/ppermute | solution.py:27
  49.0 8.0 %collective-permute-start.12 = (bf16[192,384]{1,0:T(8,128)(2,1)S(1)}, bf16[192,384]{1,0:T(8,128)(2,1)S(1)}, u32[]{:S(2)}, u32[]{:S(2)}) collective-permute-start(bf16[192,384]{1,0:T(8,128)(2,1)S(1)} %get-tuple-element.57), channel_id=1, source_target_pairs={{0,32},{32,64},{64,96},{96,0},{1,33},{33,65},{65,97},{97,1},{2,34}... | collective-permute-start | bytes 442376 | tf_op jit(solution)/shard_map/ppermute | solution.py:27
  60.1 3.1 %copy-start.9 = (bf16[192,384]{1,0:T(8,128)(2,1)}, bf16[192,384]{1,0:T(8,128)(2,1)S(1)}, u32[]{:S(2)}) copy-start(bf16[192,384]{1,0:T(8,128)(2,1)S(1)} %get-tuple-element.66) | copy-start | bytes 442372
  60.1 4.6 %copy-start.10 = (bf16[192,384]{1,0:T(8,128)(2,1)}, bf16[192,384]{1,0:T(8,128)(2,1)S(1)}, u32[]{:S(2)}) copy-start(bf16[192,384]{1,0:T(8,128)(2,1)S(1)} %get-tuple-element.65) | copy-start | bytes 442372
  60.1 4.6 %copy-start.11 = (bf16[192,384]{1,0:T(8,128)(2,1)}, bf16[192,384]{1,0:T(8,128)(2,1)S(1)}, u32[]{:S(2)}) copy-start(bf16[192,384]{1,0:T(8,128)(2,1)S(1)} %get-tuple-element.64) | copy-start | bytes 442372
  60.2 3.1 %collective-permute-start.13 = (bf16[128,1152]{1,0:T(8,128)(2,1)S(1)}, bf16[128,1152]{1,0:T(8,128)(2,1)S(1)}, u32[]{:S(2)}, u32[]{:S(2)}) collective-permute-start(bf16[128,1152]{1,0:T(8,128)(2,1)S(1)} %get-tuple-element.59), channel_id=1, source_target_pairs={{0,1},{1,0},{2,3},{3,2},{4,5},{5,4},{6,7},{7,6},{8,9},{9,8},{10,11... | collective-permute-start | bytes 884744 | tf_op jit(solution)/shard_map/ppermute | solution.py:22
  60.2 17.3 %collective-permute-start.14 = (bf16[8,96,384]{2,1,0:T(8,128)(2,1)}, bf16[8,96,384]{2,1,0:T(8,128)(2,1)}, u32[]{:S(2)}, u32[]{:S(2)}) collective-permute-start(bf16[8,96,384]{2,1,0:T(8,128)(2,1)} %get-tuple-element.61.w), channel_id=1, source_target_pairs={{0,128},{128,0},{1,129},{129,1},{2,130},{130,2},{3,131},{131,3},{4... | collective-permute-start | bytes 1769480 | tf_op jit(solution)/shard_map/ppermute | solution.py:36
  63.3 15.6 %collective-permute-start.23 = (bf16[8,96,384]{2,1,0:T(8,128)(2,1)}, bf16[8,96,384]{2,1,0:T(8,128)(2,1)S(1)}, u32[]{:S(2)}, u32[]{:S(2)}) collective-permute-start(bf16[8,96,384]{2,1,0:T(8,128)(2,1)} %get-tuple-element.61.w), channel_id=1, source_target_pairs={{0,144},{128,16},{16,128},{144,0},{1,145},{129,17},{17,129},{145,1... | collective-permute-start | bytes 1769480 | tf_op jit(solution)/shard_map/ppermute | solution.py:32
  64.7 26.1 %all-to-all-start.1 = ((bf16[8,96,384]{2,1,0:T(8,128)(2,1)}), bf16[8,96,384]{2,1,0:T(8,128)(2,1)S(1)}, u32[]{:S(2)}, u32[]{:S(2)}) async-start(bf16[8,96,384]{2,1,0:T(8,128)(2,1)} %shard_map.115), calls=%async_computation.1 | async-start | bytes 1179648 | tf_op jit(solution)/shard_map/all_to_all | solution.py:44
  71.7 10.8 %collective-permute-start.15 = (bf16[8,96,384]{2,1,0:T(8,128)(2,1)}, bf16[8,96,384]{2,1,0:T(8,128)(2,1)S(1)}, u32[]{:S(2)}, u32[]{:S(2)}) collective-permute-start(bf16[8,96,384]{2,1,0:T(8,128)(2,1)} %get-tuple-element.61.w), channel_id=1, source_target_pairs={{0,1},{1,0},{2,3},{3,2},{4,5},{5,4},{6,7},{7,6},{8,9},{9,8},{10,11... | collective-permute-start | bytes 1769480 | tf_op jit(solution)/shard_map/ppermute | solution.py:22
  77.5 6.2 %collective-permute-start.16 = (bf16[8,96,384]{2,1,0:T(8,128)(2,1)}, bf16[8,96,384]{2,1,0:T(8,128)(2,1)S(1)}, u32[]{:S(2)}, u32[]{:S(2)}) collective-permute-start(bf16[8,96,384]{2,1,0:T(8,128)(2,1)} %collective-permute-done.14.w_pair), channel_id=1, source_target_pairs={{0,1},{1,0},{2,3},{3,2},{4,5},{5,4},{6,7},{7,6},{8,9},{9,8},{10,11... | collective-permute-start | bytes 1769480 | tf_op jit(solution)/shard_map/ppermute | solution.py:22
  78.9 16.4 %collective-permute-start.24 = (bf16[8,96,384]{2,1,0:T(8,128)(2,1)S(1)}, bf16[8,96,384]{2,1,0:T(8,128)(2,1)S(1)}, u32[]{:S(2)}, u32[]{:S(2)}) collective-permute-start(bf16[8,96,384]{2,1,0:T(8,128)(2,1)S(1)} %collective-permute-done.23.w_pair), channel_id=1, source_target_pairs={{0,128},{128,0},{1,129},{129,1},{2,130},{130,2},{3,131},{131,3},{4... | collective-permute-start | bytes 1769480 | tf_op jit(solution)/shard_map/ppermute | solution.py:36
  80.3 10.5 %collective-permute-start.17 = (bf16[192,384]{1,0:T(8,128)(2,1)}, bf16[192,384]{1,0:T(8,128)(2,1)S(1)}, u32[]{:S(2)}, u32[]{:S(2)}) collective-permute-start(bf16[192,384]{1,0:T(8,128)(2,1)} %copy-done.11), channel_id=1, source_target_pairs={{0,32},{32,64},{64,96},{96,0},{1,33},{33,65},{65,97},{97,1},{2,34}... | collective-permute-start | bytes 442376 | tf_op jit(solution)/shard_map/ppermute | solution.py:27
  80.3 10.5 %collective-permute-start.18 = (bf16[192,384]{1,0:T(8,128)(2,1)}, bf16[192,384]{1,0:T(8,128)(2,1)}, u32[]{:S(2)}, u32[]{:S(2)}) collective-permute-start(bf16[192,384]{1,0:T(8,128)(2,1)} %copy-done.10), channel_id=1, source_target_pairs={{0,64},{32,96},{64,0},{96,32},{1,65},{33,97},{65,1},{97,33},{2,66}... | collective-permute-start | bytes 442376 | tf_op jit(solution)/shard_map/ppermute | solution.py:27
  82.4 8.5 %copy-start.2 = (f32[16,1152]{1,0:T(8,128)S(1)}, f32[16,1152]{1,0:T(8,128)}, u32[]{:S(2)}) copy-start(f32[16,1152]{1,0:T(8,128)} %cap.3) | copy-start | bytes 221188
  82.4 8.5 %collective-permute-start.19 = (bf16[192,384]{1,0:T(8,128)(2,1)}, bf16[192,384]{1,0:T(8,128)(2,1)}, u32[]{:S(2)}, u32[]{:S(2)}) collective-permute-start(bf16[192,384]{1,0:T(8,128)(2,1)} %copy-done.9), channel_id=1, source_target_pairs={{0,96},{32,0},{64,32},{96,64},{1,97},{33,1},{65,33},{97,65},{2,98}... | collective-permute-start | bytes 442376 | tf_op jit(solution)/shard_map/ppermute | solution.py:27
  92.8 0.6 copy-start.5
  93.4 0.6 copy-start.12
  94.0 0.6 copy-start.13
  94.6 0.6 copy-start.14
  95.3 8.9 %collective-permute-start.26 = (bf16[8,96,384]{2,1,0:T(8,128)(2,1)S(1)}, bf16[8,96,384]{2,1,0:T(8,128)(2,1)S(1)}, u32[]{:S(2)}, u32[]{:S(2)}) collective-permute-start(bf16[8,96,384]{2,1,0:T(8,128)(2,1)S(1)} %collective-permute-done.23.w_pair), channel_id=1, source_target_pairs={{0,1},{1,0},{2,3},{3,2},{4,5},{5,4},{6,7},{7,6},{8,9},{9,8},{10,11... | collective-permute-start | bytes 1769480 | tf_op jit(solution)/shard_map/ppermute | solution.py:22
  95.3 8.9 %collective-permute-start.25 = (bf16[8,96,384]{2,1,0:T(8,128)(2,1)S(1)}, bf16[8,96,384]{2,1,0:T(8,128)(2,1)}, u32[]{:S(2)}, u32[]{:S(2)}) collective-permute-start(bf16[8,96,384]{2,1,0:T(8,128)(2,1)S(1)} %collective-permute-done.24.w), channel_id=1, source_target_pairs={{0,1},{1,0},{2,3},{3,2},{4,5},{5,4},{6,7},{7,6},{8,9},{9,8},{10,11... | collective-permute-start | bytes 1769480 | tf_op jit(solution)/shard_map/ppermute | solution.py:22
  95.8 12.4 %all-to-all-start.2 = ((bf16[8,48,384]{2,1,0:T(8,128)(2,1)}), bf16[8,48,384]{2,1,0:T(8,128)(2,1)S(1)}, u32[]{:S(2)}, u32[]{:S(2)}) async-start(bf16[8,48,384]{2,1,0:T(8,128)(2,1)} %get-tuple-element.71), calls=%async_computation.2 | async-start | bytes 589824 | tf_op jit(solution)/shard_map/all_to_all | solution.py:44
  100.7 7.5 %collective-permute-start.20 = (bf16[48,384]{1,0:T(8,128)(2,1)}, bf16[48,384]{1,0:T(8,128)(2,1)S(1)}, u32[]{:S(2)}, u32[]{:S(2)}) collective-permute-start(bf16[48,384]{1,0:T(8,128)(2,1)} %copy-done.14), channel_id=1, source_target_pairs={{0,144},{128,16},{16,128},{144,0},{1,145},{129,17},{17,129},{145,1... | collective-permute-start | bytes 110600 | tf_op jit(solution)/shard_map/ppermute | solution.py:32
  101.0 7.2 %collective-permute-start.21 = (bf16[48,384]{1,0:T(8,128)(2,1)}, bf16[48,384]{1,0:T(8,128)(2,1)S(1)}, u32[]{:S(2)}, u32[]{:S(2)}) collective-permute-start(bf16[48,384]{1,0:T(8,128)(2,1)} %copy-done.13), channel_id=1, source_target_pairs={{0,128},{128,0},{1,129},{129,1},{2,130},{130,2},{3,131},{131,3},{4... | collective-permute-start | bytes 110600 | tf_op jit(solution)/shard_map/ppermute | solution.py:36
  103.5 5.7 %copy-start.6 = (f32[48,384]{1,0:T(8,128)S(1)}, f32[48,384]{1,0:T(8,128)}, u32[]{:S(2)}) copy-start(f32[48,384]{1,0:T(8,128)} %copy-done.5) | copy-start | bytes 221188
  103.5 5.7 %collective-permute-start.22 = (bf16[48,384]{1,0:T(8,128)(2,1)}, bf16[48,384]{1,0:T(8,128)(2,1)S(1)}, u32[]{:S(2)}, u32[]{:S(2)}) collective-permute-start(bf16[48,384]{1,0:T(8,128)(2,1)} %copy-done.12), channel_id=1, source_target_pairs={{0,16},{16,0},{1,17},{17,1},{2,18},{18,2},{3,19},{19,3},{4,20},{20... | collective-permute-start | bytes 110600 | tf_op jit(solution)/shard_map/ppermute | solution.py:40

commit v7 on v6

--- a/solution.py
+++ b/solution.py
@@ -102,7 +102,7 @@
     for i in range(16):
         number = jnp.where(line == i, ids[i], number)
     lane = lax.broadcasted_iota(jnp.int32, (16, 384), 1)
-    split = jnp.where(lane == 0, number >> 6, jnp.where(lane == 1, number & 63, 0))
+    split = jnp.where(lane % 2 == 0, number >> 6, number & 63)
     image[48:, :] = split.astype(f32).astype(bf16)
     image[:48, :] = fold(unit_rows(pic[...])[0].astype(bf16))
     for source, first in ((tokens, 0), (other_tokens, 384)):
@@ -139,11 +139,16 @@
         at = pl.ds(pl.multiple_of(((y - k) & 3) * 384, 384), 384)
         both = b_own[:, at].astype(f32) + b_in[:, at].astype(f32)
         out[...] = both.astype(out.dtype)
+    lane = lax.broadcasted_iota(jnp.int32, (16, 384), 1)
+    ids = image[48:, :].astype(f32)
+    for k, part in enumerate((a1, a2, a3), 1):
+        ids = jnp.where(lane // 2 == k, part[2 * CUT + 48 :, :].astype(f32), ids)
     for target, first in ((near, CUT), (column, 0)):
-        target[first : first + 64, :] = image[...]
-        for k, part in enumerate((a1, a2, a3)):
-            at = first + 64 + 64 * k
-            target[at : at + 64, :] = part[2 * CUT :, :]
+        target[first : first + 48, :] = image[:48, :]
+        for k, part in enumerate((a1, a2, a3), 1):
+            at = first + 48 * k
+            target[at : at + 48, :] = part[2 * CUT : 2 * CUT + 48, :]
+        target[first + 192 :, :] = ids.astype(bf16)
 
 
 def tile_kernel(place, sharp, bias, i0, i1, i2, i3, other_text, along_z, a_own, *rest):
@@ -157,13 +162,14 @@
     weight[CUT:, :] = total.astype(bf16)
     y, xl, xh, c = place[0], place[1], place[2], place[3]
     for k, part in enumerate((i0, i1, i2, i3)):
-        first = part.shape[0] - 256
+        first = part.shape[0] - 208
+        split = part[first + 192 :, :128].astype(f32)
         for j in range(4):
             at = k * 64 + j * 16
-            here = first + j * 64
+            here = first + j * 48
             images[at : at + 16, :] = unfold(part[here : here + 48, :])
-            split = part[here + 48 : here + 64, :128].astype(f32)
-            ids[at : at + 16, :] = (split[:, 0:1] * 64.0 + split[:, 1:2]).astype(jnp.int32)
+            number = split[:, 2 * j : 2 * j + 1] * 64.0 + split[:, 2 * j + 1 : 2 * j + 2]
+            ids[at : at + 16, :] = number.astype(jnp.int32)
     for k in range(8):
         texts[k * 16 : k * 16 + 16, :] = unfold(along_z[k, :48, :])
         texts[128 + k * 16 : 144 + k * 16, :] = unfold(other_text[k, :, :])
@@ -304,8 +310,8 @@
         first_sum_kernel,
         (
             shape(CUT, 384, dtype=f32),
-            shape(CUT + 256, 384),
-            shape(256, 384),
+            shape(CUT + 208, 384),
+            shape(208, 384),
             shape(384 - CUT, 384, dtype=f32),
             *[shape(384 - CUT, 384)] * 3,
         ),

time: 111 us -> 110 us (level)
  transfers between devices with their start and end apart: 30 -> 30, of which waited for: 11 -> 10; matrix products, arithmetic and copies ran while one was open for 0% -> 0% of each run, Pallas kernels for 17% -> 17%
where the time goes in v7:
time: 110 us
  starting transfers between devices  43.5 us (40%)
  waiting for transfers between devices  35.9 us (33%)
  Pallas kernels  23.1 us (21%)
  local copies, waits for them, and re-layouts  5.06 us (5%)
  between operations  2.07 us (2%)
    ppermute x9, waiting for transfers between devices, turn(): return lax.ppermute(x, axes, [(at[i], at[(i + by) % 4]) for i in range(4)])  24.6 us
    all_to_all x3, starting transfers between devices, exchange(): return lax.all_to_all(x, axes, 0, 0, tiled=True)  19.7 us
    pallas_call x7, Pallas kernels, call(): pl.pallas_call(kernel, out_shape=tuple(outs), in_specs=[pl.BlockSpec(memo...  14.8 us
    ppermute x9, starting transfers between devices, turn(): return lax.ppermute(x, axes, [(at[i], at[(i + by) % 4]) for i in range(4)])  9.19 us
    pallas_call x2, Pallas kernels, project(): pl.pallas_call(project_kernel, grid_spec=pltpu.PrefetchScalarGridSpec(num...  8.21 us
    ppermute x4, starting transfers between devices, swap_pairs(): return lax.ppermute(x, 'xl', [(0, 1), (1, 0)])  8.17 us
    ppermute x4, waiting for transfers between devices, swap_pairs(): return lax.ppermute(x, 'xl', [(0, 1), (1, 0)])  4.96 us
    unnamed x32, local copies, waits for them, and re-layouts  4.94 us
  transfers between devices with their start and end apart: 30, of which 10 were waited for; matrix products, arithmetic and copies ran while one was open for 0% of the time, Pallas kernels for 17%

profile of v7, /device:TPU:2, one launch (start us, length us, event | category | flops | bytes accessed | tf_op | source)
XLA Modules:
  0.0 109.6 jit_solution(7783782007845515663)
XLA Ops:
  0.7 0.5 collective-permute-start.1
  1.3 0.9 copy-done.1
  2.2 0.9 copy-done.3
  3.1 1.6 %shard_map.113 = bf16[8,144,384]{2,1,0:T(8,128)(2,1)} custom-call(s32[5]{0:T(128)S(1)} %stack.23.place, f32[16,1152]{1,0:T(8,128)S(1)} %copy-done.1, bf16[48,1536]{1,0:T(8,128)(2,1)S(1)} %copy-done.3), custom_call_target="tpu_custom_call" | custom-call | bytes 1105920 | tf_op jit(solution)/shard_map/pallas_call | solution.py:73
  4.7 8.5 %all-to-all-start = ((bf16[8,144,384]{2,1,0:T(8,128)(2,1)}), bf16[8,144,384]{2,1,0:T(8,128)(2,1)S(1)}, u32[]{:S(2)}, u32[]{:S(2)}) async-start(bf16[8,144,384]{2,1,0:T(8,128)(2,1)} %shard_map.113), calls=%async_computation | async-start | bytes 1769472 | tf_op jit(solution)/shard_map/all_to_all | solution.py:44
  13.2 4.9 %shard_map.111 = (bf16[384,384]{1,0:T(8,128)(2,1)S(1)}, bf16[448,384]{1,0:T(8,128)(2,1)S(1)}, bf16[448,384]{1,0:T(8,128)(2,1)S(1)}, bf16[448,384]{1,0:T(8,128)(2...) custom-call(s32[5]{0:T(128)S(1)} %stack.23.place, ...), custom_call_target="tpu_custom_call" | custom-call | flops 1811939328 | bytes 7348288 | tf_op jit(solution)/shard_map/pallas_call | solution.py:73
  18.1 1.5 %collective-permute-start.5 = (bf16[192,1536]{1,0:T(8,128)(2,1)S(1)}, bf16[192,1536]{1,0:T(8,128)(2,1)S(1)}, u32[]{:S(2)}, u32[]{:S(2)}) collective-permute-start(bf16[192,1536]{1,0:T(8,128)(2,1)S(1)} %get-tuple-element.46), channel_id=1, source_target_pairs={{0,144},{128,16},{16,128},{144,0},{1,145},{129,17},{17,129},{145,1... | collective-permute-start | bytes 1769480 | tf_op jit(solution)/shard_map/ppermute | solution.py:32
  19.6 3.0 %collective-permute-start.2 = (bf16[448,384]{1,0:T(8,128)(2,1)S(1)}, bf16[448,384]{1,0:T(8,128)(2,1)S(1)}, u32[]{:S(2)}, u32[]{:S(2)}) collective-permute-start(bf16[448,384]{1,0:T(8,128)(2,1)S(1)} %get-tuple-element.42), channel_id=1, source_target_pairs={{0,96},{32,0},{64,32},{96,64},{1,97},{33,1},{65,33},{97,65},{2,98}... | collective-permute-start | bytes 1032200 | tf_op jit(solution)/shard_map/ppermute | solution.py:27
  22.6 0.6 collective-permute-start.3
  23.3 1.0 collective-permute-start.4
  24.3 12.8 %collective-permute-done.2.a1 = bf16[448,384]{1,0:T(8,128)(2,1)S(1)} collective-permute-done((bf16[448,384]{1,0:T(8,128)(2,1)S(1)}, bf16[448,384]{1,0:T(8,128)(2,1)S(1)}, u32[]{:S(2)}, u32[]{:S(2)}) %collective-permute-start.2) | collective-permute-done | bytes 344096 | tf_op jit(solution)/shard_map/ppermute | solution.py:27
  37.1 3.7 %collective-permute-done.4.a3 = bf16[448,384]{1,0:T(8,128)(2,1)S(1)} collective-permute-done((bf16[448,384]{1,0:T(8,128)(2,1)S(1)}, bf16[448,384]{1,0:T(8,128)(2,1)S(1)}, u32[]{:S(2)}, u32[]{:S(2)}) %collective-permute-start.4) | collective-permute-done | bytes 344096 | tf_op jit(solution)/shard_map/ppermute | solution.py:27
  40.8 0.8 shard_map.112
  41.6 0.7 copy-done.11
  42.4 0.6 collective-permute-start.6
  43.0 0.6 collective-permute-start.10
  43.6 0.3 collective-permute-done.7.other_text
  44.0 1.8 %collective-permute-start.8 = (bf16[208,384]{1,0:T(8,128)(2,1)S(1)}, bf16[208,384]{1,0:T(8,128)(2,1)S(1)}, u32[]{:S(2)}, u32[]{:S(2)}) collective-permute-start(bf16[208,384]{1,0:T(8,128)(2,1)S(1)} %get-tuple-element.52.i0), channel_id=1, source_target_pairs={{0,128},{128,0},{1,129},{129,1},{2,130},{130,2},{3,131},{131,3},{4... | collective-permute-start | bytes 479240 | tf_op jit(solution)/shard_map/ppermute | solution.py:36
  45.8 1.2 %collective-permute-start.9 = (bf16[208,384]{1,0:T(8,128)(2,1)S(1)}, bf16[208,384]{1,0:T(8,128)(2,1)S(1)}, u32[]{:S(2)}, u32[]{:S(2)}) collective-permute-start(bf16[208,384]{1,0:T(8,128)(2,1)S(1)} %get-tuple-element.52.i0), channel_id=1, source_target_pairs={{0,16},{16,0},{1,17},{17,1},{2,18},{18,2},{3,19},{19,3},{4,20},{20... | collective-permute-start | bytes 479240 | tf_op jit(solution)/shard_map/ppermute | solution.py:40
  47.0 0.6 collective-permute-start.11
  47.6 1.8 %collective-permute-done.10.rest_1_ = bf16[192,384]{1,0:T(8,128)(2,1)S(1)} collective-permute-done((bf16[192,384]{1,0:T(8,128)(2,1)}, bf16[192,384]{1,0:T(8,128)(2,1)S(1)}, u32[]{:S(2)}, u32[]{:S(2)}) %collective-permute-start.10) | collective-permute-done | bytes 147488 | tf_op jit(solution)/shard_map/ppermute | solution.py:27
  50.7 4.5 %collective-permute-done.11.rest_2_ = bf16[192,384]{1,0:T(8,128)(2,1)S(1)} collective-permute-done((bf16[192,384]{1,0:T(8,128)(2,1)S(1)}, bf16[192,384]{1,0:T(8,128)(2,1)S(1)}, u32[]{:S(2)}, u32[]{:S(2)}) %collective-permute-start.11) | collective-permute-done | bytes 147488 | tf_op jit(solution)/shard_map/ppermute | solution.py:27
  55.2 1.7 %collective-permute-done.12.rest_3_ = bf16[192,384]{1,0:T(8,128)(2,1)S(1)} collective-permute-done((bf16[192,384]{1,0:T(8,128)(2,1)S(1)}, bf16[192,384]{1,0:T(8,128)(2,1)S(1)}, u32[]{:S(2)}, u32[]{:S(2)}) %collective-permute-start.12) | collective-permute-done | bytes 147488 | tf_op jit(solution)/shard_map/ppermute | solution.py:27
  57.0 2.8 %shard_map.114 = (bf16[8,96,384]{2,1,0:T(8,128)(2,1)}, bf16[384,384]{1,0:T(8,128)(2,1)S(1)}, f32[192,384]{1,0:T(8,128)S(1)}, bf16[192,384]{1,0:T(8,128)(2,1)S(1)...) custom-call(s32[5]{0:T(128)S(1)} %stack.23.place, ...), custom_call_target="tpu_custom_call" | custom-call | flops 452984832 | bytes 5505032 | tf_op jit(solution)/shard_map/pallas_call | solution.py:73
  59.8 2.4 %collective-permute-start.14 = (bf16[8,96,384]{2,1,0:T(8,128)(2,1)}, bf16[8,96,384]{2,1,0:T(8,128)(2,1)}, u32[]{:S(2)}, u32[]{:S(2)}) collective-permute-start(bf16[8,96,384]{2,1,0:T(8,128)(2,1)} %get-tuple-element.61.w), channel_id=1, source_target_pairs={{0,128},{128,0},{1,129},{129,1},{2,130},{130,2},{3,131},{131,3},{4... | collective-permute-start | bytes 1769480 | tf_op jit(solution)/shard_map/ppermute | solution.py:36
  62.2 0.9 collective-permute-start.23
  63.1 1.5 %shard_map.115 = bf16[8,96,384]{2,1,0:T(8,128)(2,1)} custom-call(s32[5]{0:T(128)S(1)} %stack.23.place, f32[128,1152]{1,0:T(8,128)S(1)} %get-tuple-element.58.t_own, bf16[128,1152]{1,0:T(8,128)(2,1)S(1)} %collective-permute-done.13.t_in, bf16[384,384]{1,0:T(8,128)(2,1)S(1)} %get-tuple-element.60.weight), custom_call_target="tpu_custom_call" | custom-call | bytes 1769472 | tf_op jit(solution)/shard_map/pallas_call | solution.py:73
  64.6 6.9 %all-to-all-start.1 = ((bf16[8,96,384]{2,1,0:T(8,128)(2,1)}), bf16[8,96,384]{2,1,0:T(8,128)(2,1)S(1)}, u32[]{:S(2)}, u32[]{:S(2)}) async-start(bf16[8,96,384]{2,1,0:T(8,128)(2,1)} %shard_map.115), calls=%async_computation.1 | async-start | bytes 1179648 | tf_op jit(solution)/shard_map/all_to_all | solution.py:44
  71.5 5.0 %collective-permute-done.14.w_pair = bf16[8,96,384]{2,1,0:T(8,128)(2,1)} collective-permute-done((bf16[8,96,384]{2,1,0:T(8,128)(2,1)}, bf16[8,96,384]{2,1,0:T(8,128)(2,1)}, u32[]{:S(2)}, u32[]{:S(2)}) %collective-permute-start.14) | collective-permute-done | bytes 589856 | tf_op jit(solution)/shard_map/ppermute | solution.py:36
  76.5 1.4 %collective-permute-done.23.w_pair = bf16[8,96,384]{2,1,0:T(8,128)(2,1)S(1)} collective-permute-done((bf16[8,96,384]{2,1,0:T(8,128)(2,1)}, bf16[8,96,384]{2,1,0:T(8,128)(2,1)S(1)}, u32[]{:S(2)}, u32[]{:S(2)}) %collective-permute-start.23) | collective-permute-done | bytes 589856 | tf_op jit(solution)/shard_map/ppermute | solution.py:32
  77.8 1.5 %collective-permute-start.24 = (bf16[8,96,384]{2,1,0:T(8,128)(2,1)S(1)}, bf16[8,96,384]{2,1,0:T(8,128)(2,1)S(1)}, u32[]{:S(2)}, u32[]{:S(2)}) collective-permute-start(bf16[8,96,384]{2,1,0:T(8,128)(2,1)S(1)} %collective-permute-done.23.w_pair), channel_id=1, source_target_pairs={{0,128},{128,0},{1,129},{129,1},{2,130},{130,2},{3,131},{131,3},{4... | collective-permute-start | bytes 1769480 | tf_op jit(solution)/shard_map/ppermute | solution.py:36
  79.3 2.1 %collective-permute-start.18 = (bf16[192,384]{1,0:T(8,128)(2,1)}, bf16[192,384]{1,0:T(8,128)(2,1)}, u32[]{:S(2)}, u32[]{:S(2)}) collective-permute-start(bf16[192,384]{1,0:T(8,128)(2,1)} %copy-done.9), channel_id=1, source_target_pairs={{0,64},{32,96},{64,0},{96,32},{1,65},{33,97},{65,1},{97,33},{2,66}... | collective-permute-start | bytes 442376 | tf_op jit(solution)/shard_map/ppermute | solution.py:27
  81.4 1.2 %collective-permute-start.19 = (bf16[192,384]{1,0:T(8,128)(2,1)}, bf16[192,384]{1,0:T(8,128)(2,1)}, u32[]{:S(2)}, u32[]{:S(2)}) collective-permute-start(bf16[192,384]{1,0:T(8,128)(2,1)} %copy-done.8), channel_id=1, source_target_pairs={{0,96},{32,0},{64,32},{96,64},{1,97},{33,1},{65,33},{97,65},{2,98}... | collective-permute-start | bytes 442376 | tf_op jit(solution)/shard_map/ppermute | solution.py:27
  82.6 4.2 %shard_map.116.rest_0_ = bf16[384,1536]{1,0:T(8,128)(2,1)} custom-call(s32[5]{0:T(128)S(1)} %stack.23.place, bf16[384,1536]{1,0:T(8,128)(2,1)S(1)} %copy-done, bf16[8,96,384]{2,1,0:T(8,128)(2,1)} %get-tuple-element.61.w, bf16[8,96,384]{2,1,0:T(8,128)(2,1)} %collective-permute-done.14.w_pair, bf16[8,96,384]{2,1,0:T(8,128)(2,1)S(1)} %collective-permute-done.15.other, ...), custom_call_target="tpu_custom_call" | custom-call | flops 905969664 | bytes 6291456 | tf_op jit(solution)/shard_map/pallas_call | solution.py:245
  86.8 3.6 %all-to-all-done.1.back = bf16[8,96,384]{2,1,0:T(8,128)(2,1)S(1)} async-done(((bf16[8,96,384]{2,1,0:T(8,128)(2,1)}), bf16[8,96,384]{2,1,0:T(8,128)(2,1)S(1)}, u32[]{:S(2)}, u32[]{:S(2)}) %all-to-all-start.1) | async-done | bytes 589856 | tf_op jit(solution)/shard_map/all_to_all | solution.py:44
  90.4 1.9 %shard_map.117 = (f32[16,1152]{1,0:T(8,128)}, bf16[8,48,384]{2,1,0:T(8,128)(2,1)}, f32[48,384]{1,0:T(8,128)S(1)}, bf16[48,384]{1,0:T(8,128)(2,1)S(1)}, bf16[48,3...) custom-call(s32[5]{0:T(128)S(1)} %stack.23.place, bf16[8,96,384]{2,1,0:T(8,128)(2,1)S(1)} %all-to-all-done.1.back, ...), custom_call_target="tpu_custom_call" | custom-call | bytes 1953792 | tf_op jit(solution)/shard_map/pallas_call | solution.py:73
  92.3 0.6 copy-done.5
  93.0 0.6 copy-done.12
  93.6 0.6 copy-done.13
  94.2 0.6 copy-done.14
  94.8 0.5 collective-permute-start.25
  95.3 4.3 %all-to-all-start.2 = ((bf16[8,48,384]{2,1,0:T(8,128)(2,1)}), bf16[8,48,384]{2,1,0:T(8,128)(2,1)S(1)}, u32[]{:S(2)}, u32[]{:S(2)}) async-start(bf16[8,48,384]{2,1,0:T(8,128)(2,1)} %get-tuple-element.71), calls=%async_computation.2 | async-start | bytes 589824 | tf_op jit(solution)/shard_map/all_to_all | solution.py:44
  99.6 0.4 collective-permute-start.20
  100.0 2.5 %collective-permute-start.21 = (bf16[48,384]{1,0:T(8,128)(2,1)}, bf16[48,384]{1,0:T(8,128)(2,1)S(1)}, u32[]{:S(2)}, u32[]{:S(2)}) collective-permute-start(bf16[48,384]{1,0:T(8,128)(2,1)} %copy-done.13), channel_id=1, source_target_pairs={{0,128},{128,0},{1,129},{129,1},{2,130},{130,2},{3,131},{131,3},{4... | collective-permute-start | bytes 110600 | tf_op jit(solution)/shard_map/ppermute | solution.py:36
  102.5 0.6 collective-permute-start.22
  103.1 4.0 %shard_map.118 = bf16[384,1536]{1,0:T(8,128)(2,1)} custom-call(s32[5]{0:T(128)S(1)} %stack.23.place, bf16[384,1536]{1,0:T(8,128)(2,1)S(1)} %copy-done, bf16[8,96,384]{2,1,0:T(8,128)(2,1)S(1)} %collective-permute-done.24.w, bf16[8,96,384]{2,1,0:T(8,128)(2,1)S(1)} %collective-permute-done.23.w_pair, ...), custom_call_target="tpu_custom_call", output_to_operand_aliasing={{}: (6, {})} | custom-call | flops 905969664 | bytes 6291456 | tf_op jit(solution)/shard_map/pallas_call | solution.py:245
  107.2 1.0 collective-permute-done.22.h3
  108.1 1.4 %shard_map.119 = (f32[16,1152]{1,0:T(8,128)}, f32[48,1536]{1,0:T(8,128)}) custom-call(s32[5]{0:T(128)S(1)} %stack.23.place, f32[48,384]{1,0:T(8,128)S(1)} %copy-done.6, bf16[48,384]{1,0:T(8,128)(2,1)S(1)} %collective-permute-done.20.h1, bf16[48,384]{1,0:T(8,128)(2,1)S(1)} %collective-permute-done.21.h2, bf16[48,384]{1,0:T(8,128)(2,1)S(1)} %collective-permute-done.22.h3, ...), custom_call_target="tpu_custom_call" | custom-call | bytes 921600 | tf_op jit(solution)/shard_map/pallas_call | solution.py:73
  (55 shorter events, 0.4 us)
Async XLA Ops:
  0.6 4.1 %collective-permute-start = (bf16[384,1536]{1,0:T(8,128)(2,1)}, bf16[384,1536]{1,0:T(8,128)(2,1)}, u32[]{:S(2)}, u32[]{:S(2)}) collective-permute-start(bf16[384,1536]{1,0:T(8,128)(2,1)} %tokens.1), channel_id=1, source_target_pairs={{0,1},{1,0},{2,3},{3,2},{4,5},{5,4},{6,7},{7,6},{8,9},{9,8},{10,11... | collective-permute-start | bytes 3538952 | tf_op jit(solution)/shard_map/ppermute | solution.py:22
  0.7 12.4 %collective-permute-start.1 = (bf16[384,1536]{1,0:T(8,128)(2,1)}, bf16[384,1536]{1,0:T(8,128)(2,1)}, u32[]{:S(2)}, u32[]{:S(2)}) collective-permute-start(bf16[384,1536]{1,0:T(8,128)(2,1)} %adj.5), channel_id=1, source_target_pairs={{0,1},{1,0},{2,3},{3,2},{4,5},{5,4},{6,7},{7,6},{8,9},{9,8},{10,11... | collective-permute-start | bytes 3538952 | tf_op jit(solution)/shard_map/ppermute | solution.py:22
  1.3 0.9 copy-start.1
  2.2 0.9 copy-start.3
  3.1 10.1 %copy-start = (bf16[384,1536]{1,0:T(8,128)(2,1)S(1)}, bf16[384,1536]{1,0:T(8,128)(2,1)}, u32[]{:S(2)}) copy-start(bf16[384,1536]{1,0:T(8,128)(2,1)} %adj.5) | copy-start | bytes 3538948
  3.1 10.1 %copy-start.4 = (f32[16,1152]{1,0:T(8,128)S(1)}, f32[16,1152]{1,0:T(8,128)}, u32[]{:S(2)}) copy-start(f32[16,1152]{1,0:T(8,128)} %pic.3) | copy-start | bytes 221188
  3.1 10.1 %copy-start.7 = (bf16[384,1536]{1,0:T(8,128)(2,1)S(1)}, bf16[384,1536]{1,0:T(8,128)(2,1)}, u32[]{:S(2)}) copy-start(bf16[384,1536]{1,0:T(8,128)(2,1)} %tokens.1) | copy-start | bytes 3538948
  3.1 10.1 %copy-start.15 = (s32[16]{0:T(128)S(1)}, s32[16]{0:T(128)}, u32[]{:S(2)}) copy-start(s32[16]{0:T(128)} %ids.1) | copy-start | bytes 196
  4.7 37.6 %all-to-all-start = ((bf16[8,144,384]{2,1,0:T(8,128)(2,1)}), bf16[8,144,384]{2,1,0:T(8,128)(2,1)S(1)}, u32[]{:S(2)}, u32[]{:S(2)}) async-start(bf16[8,144,384]{2,1,0:T(8,128)(2,1)} %shard_map.113), calls=%async_computation | async-start | bytes 1769472 | tf_op jit(solution)/shard_map/all_to_all | solution.py:44
  18.1 22.7 %collective-permute-start.5 = (bf16[192,1536]{1,0:T(8,128)(2,1)S(1)}, bf16[192,1536]{1,0:T(8,128)(2,1)S(1)}, u32[]{:S(2)}, u32[]{:S(2)}) collective-permute-start(bf16[192,1536]{1,0:T(8,128)(2,1)S(1)} %get-tuple-element.46), channel_id=1, source_target_pairs={{0,144},{128,16},{16,128},{144,0},{1,145},{129,17},{17,129},{145,1... | collective-permute-start | bytes 1769480 | tf_op jit(solution)/shard_map/ppermute | solution.py:32
  19.6 17.4 %collective-permute-start.2 = (bf16[448,384]{1,0:T(8,128)(2,1)S(1)}, bf16[448,384]{1,0:T(8,128)(2,1)S(1)}, u32[]{:S(2)}, u32[]{:S(2)}) collective-permute-start(bf16[448,384]{1,0:T(8,128)(2,1)S(1)} %get-tuple-element.42), channel_id=1, source_target_pairs={{0,96},{32,0},{64,32},{96,64},{1,97},{33,1},{65,33},{97,65},{2,98}... | collective-permute-start | bytes 1032200 | tf_op jit(solution)/shard_map/ppermute | solution.py:27
  22.6 14.4 %collective-permute-start.3 = (bf16[448,384]{1,0:T(8,128)(2,1)S(1)}, bf16[448,384]{1,0:T(8,128)(2,1)S(1)}, u32[]{:S(2)}, u32[]{:S(2)}) collective-permute-start(bf16[448,384]{1,0:T(8,128)(2,1)S(1)} %get-tuple-element.43), channel_id=1, source_target_pairs={{0,64},{32,96},{64,0},{96,32},{1,65},{33,97},{65,1},{97,33},{2,66}... | collective-permute-start | bytes 1032200 | tf_op jit(solution)/shard_map/ppermute | solution.py:27
  23.3 17.5 %collective-permute-start.4 = (bf16[448,384]{1,0:T(8,128)(2,1)S(1)}, bf16[448,384]{1,0:T(8,128)(2,1)S(1)}, u32[]{:S(2)}, u32[]{:S(2)}) collective-permute-start(bf16[448,384]{1,0:T(8,128)(2,1)S(1)} %get-tuple-element.44), channel_id=1, source_target_pairs={{0,32},{32,64},{64,96},{96,0},{1,33},{33,65},{65,97},{97,1},{2,34}... | collective-permute-start | bytes 1032200 | tf_op jit(solution)/shard_map/ppermute | solution.py:27
  41.6 0.7 copy-start.11
  42.3 1.7 %collective-permute-start.7 = (bf16[8,48,384]{2,1,0:T(8,128)(2,1)S(1)}, bf16[8,48,384]{2,1,0:T(8,128)(2,1)S(1)}, u32[]{:S(2)}, u32[]{:S(2)}) collective-permute-start(bf16[8,48,384]{2,1,0:T(8,128)(2,1)S(1)} %slice.3), channel_id=1, source_target_pairs={{0,1},{1,0},{2,3},{3,2},{4,5},{5,4},{6,7},{7,6},{8,9},{9,8},{10,11... | collective-permute-start | bytes 884744 | tf_op jit(solution)/shard_map/ppermute | solution.py:22
  42.4 14.6 %collective-permute-start.6 = (bf16[400,384]{1,0:T(8,128)(2,1)S(1)}, bf16[400,384]{1,0:T(8,128)(2,1)S(1)}, u32[]{:S(2)}, u32[]{:S(2)}) collective-permute-start(bf16[400,384]{1,0:T(8,128)(2,1)S(1)} %get-tuple-element.49), channel_id=1, source_target_pairs={{0,144},{128,16},{16,128},{144,0},{1,145},{129,17},{17,129},{145,1... | collective-permute-start | bytes 921608 | tf_op jit(solution)/shard_map/ppermute | solution.py:32
  43.0 6.4 %collective-permute-start.10 = (bf16[192,384]{1,0:T(8,128)(2,1)}, bf16[192,384]{1,0:T(8,128)(2,1)S(1)}, u32[]{:S(2)}, u32[]{:S(2)}) collective-permute-start(bf16[192,384]{1,0:T(8,128)(2,1)} %copy-done.11), channel_id=1, source_target_pairs={{0,96},{32,0},{64,32},{96,64},{1,97},{33,1},{65,33},{97,65},{2,98}... | collective-permute-start | bytes 442376 | tf_op jit(solution)/shard_map/ppermute | solution.py:27
  44.0 13.0 %collective-permute-start.8 = (bf16[208,384]{1,0:T(8,128)(2,1)S(1)}, bf16[208,384]{1,0:T(8,128)(2,1)S(1)}, u32[]{:S(2)}, u32[]{:S(2)}) collective-permute-start(bf16[208,384]{1,0:T(8,128)(2,1)S(1)} %get-tuple-element.52.i0), channel_id=1, source_target_pairs={{0,128},{128,0},{1,129},{129,1},{2,130},{130,2},{3,131},{131,3},{4... | collective-permute-start | bytes 479240 | tf_op jit(solution)/shard_map/ppermute | solution.py:36
  45.8 11.2 %collective-permute-start.9 = (bf16[208,384]{1,0:T(8,128)(2,1)S(1)}, bf16[208,384]{1,0:T(8,128)(2,1)S(1)}, u32[]{:S(2)}, u32[]{:S(2)}) collective-permute-start(bf16[208,384]{1,0:T(8,128)(2,1)S(1)} %get-tuple-element.52.i0), channel_id=1, source_target_pairs={{0,16},{16,0},{1,17},{17,1},{2,18},{18,2},{3,19},{19,3},{4,20},{20... | collective-permute-start | bytes 479240 | tf_op jit(solution)/shard_map/ppermute | solution.py:40
  47.0 8.3 %collective-permute-start.11 = (bf16[192,384]{1,0:T(8,128)(2,1)S(1)}, bf16[192,384]{1,0:T(8,128)(2,1)S(1)}, u32[]{:S(2)}, u32[]{:S(2)}) collective-permute-start(bf16[192,384]{1,0:T(8,128)(2,1)S(1)} %get-tuple-element.56), channel_id=1, source_target_pairs={{0,64},{32,96},{64,0},{96,32},{1,65},{33,97},{65,1},{97,33},{2,66}... | collective-permute-start | bytes 442376 | tf_op jit(solution)/shard_map/ppermute | solution.py:27
  49.4 7.6 %collective-permute-start.12 = (bf16[192,384]{1,0:T(8,128)(2,1)S(1)}, bf16[192,384]{1,0:T(8,128)(2,1)S(1)}, u32[]{:S(2)}, u32[]{:S(2)}) collective-permute-start(bf16[192,384]{1,0:T(8,128)(2,1)S(1)} %get-tuple-element.57), channel_id=1, source_target_pairs={{0,32},{32,64},{64,96},{96,0},{1,33},{33,65},{65,97},{97,1},{2,34}... | collective-permute-start | bytes 442376 | tf_op jit(solution)/shard_map/ppermute | solution.py:27
  59.8 3.3 %copy-start.8 = (bf16[192,384]{1,0:T(8,128)(2,1)}, bf16[192,384]{1,0:T(8,128)(2,1)S(1)}, u32[]{:S(2)}) copy-start(bf16[192,384]{1,0:T(8,128)(2,1)S(1)} %get-tuple-element.66) | copy-start | bytes 442372
  59.8 4.8 %copy-start.9 = (bf16[192,384]{1,0:T(8,128)(2,1)}, bf16[192,384]{1,0:T(8,128)(2,1)S(1)}, u32[]{:S(2)}) copy-start(bf16[192,384]{1,0:T(8,128)(2,1)S(1)} %get-tuple-element.65) | copy-start | bytes 442372
  59.8 19.5 %copy-start.10 = (bf16[192,384]{1,0:T(8,128)(2,1)}, bf16[192,384]{1,0:T(8,128)(2,1)S(1)}, u32[]{:S(2)}) copy-start(bf16[192,384]{1,0:T(8,128)(2,1)S(1)} %get-tuple-element.64) | copy-start | bytes 442372
  59.8 3.3 %collective-permute-start.13 = (bf16[128,1152]{1,0:T(8,128)(2,1)S(1)}, bf16[128,1152]{1,0:T(8,128)(2,1)S(1)}, u32[]{:S(2)}, u32[]{:S(2)}) collective-permute-start(bf16[128,1152]{1,0:T(8,128)(2,1)S(1)} %get-tuple-element.59), channel_id=1, source_target_pairs={{0,1},{1,0},{2,3},{3,2},{4,5},{5,4},{6,7},{7,6},{8,9},{9,8},{10,11... | collective-permute-start | bytes 884744 | tf_op jit(solution)/shard_map/ppermute | solution.py:22
  59.8 16.7 %collective-permute-start.14 = (bf16[8,96,384]{2,1,0:T(8,128)(2,1)}, bf16[8,96,384]{2,1,0:T(8,128)(2,1)}, u32[]{:S(2)}, u32[]{:S(2)}) collective-permute-start(bf16[8,96,384]{2,1,0:T(8,128)(2,1)} %get-tuple-element.61.w), channel_id=1, source_target_pairs={{0,128},{128,0},{1,129},{129,1},{2,130},{130,2},{3,131},{131,3},{4... | collective-permute-start | bytes 1769480 | tf_op jit(solution)/shard_map/ppermute | solution.py:36
  62.2 15.6 %collective-permute-start.23 = (bf16[8,96,384]{2,1,0:T(8,128)(2,1)}, bf16[8,96,384]{2,1,0:T(8,128)(2,1)S(1)}, u32[]{:S(2)}, u32[]{:S(2)}) collective-permute-start(bf16[8,96,384]{2,1,0:T(8,128)(2,1)} %get-tuple-element.61.w), channel_id=1, source_target_pairs={{0,144},{128,16},{16,128},{144,0},{1,145},{129,17},{17,129},{145,1... | collective-permute-start | bytes 1769480 | tf_op jit(solution)/shard_map/ppermute | solution.py:32
  64.6 25.9 %all-to-all-start.1 = ((bf16[8,96,384]{2,1,0:T(8,128)(2,1)}), bf16[8,96,384]{2,1,0:T(8,128)(2,1)S(1)}, u32[]{:S(2)}, u32[]{:S(2)}) async-start(bf16[8,96,384]{2,1,0:T(8,128)(2,1)} %shard_map.115), calls=%async_computation.1 | async-start | bytes 1179648 | tf_op jit(solution)/shard_map/all_to_all | solution.py:44
  71.5 9.9 %collective-permute-start.15 = (bf16[8,96,384]{2,1,0:T(8,128)(2,1)}, bf16[8,96,384]{2,1,0:T(8,128)(2,1)S(1)}, u32[]{:S(2)}, u32[]{:S(2)}) collective-permute-start(bf16[8,96,384]{2,1,0:T(8,128)(2,1)} %get-tuple-element.61.w), channel_id=1, source_target_pairs={{0,1},{1,0},{2,3},{3,2},{4,5},{5,4},{6,7},{7,6},{8,9},{9,8},{10,11... | collective-permute-start | bytes 1769480 | tf_op jit(solution)/shard_map/ppermute | solution.py:22
  76.5 6.2 %collective-permute-start.16 = (bf16[8,96,384]{2,1,0:T(8,128)(2,1)}, bf16[8,96,384]{2,1,0:T(8,128)(2,1)S(1)}, u32[]{:S(2)}, u32[]{:S(2)}) collective-permute-start(bf16[8,96,384]{2,1,0:T(8,128)(2,1)} %collective-permute-done.14.w_pair), channel_id=1, source_target_pairs={{0,1},{1,0},{2,3},{3,2},{4,5},{5,4},{6,7},{7,6},{8,9},{9,8},{10,11... | collective-permute-start | bytes 1769480 | tf_op jit(solution)/shard_map/ppermute | solution.py:22
  77.8 17.0 %collective-permute-start.24 = (bf16[8,96,384]{2,1,0:T(8,128)(2,1)S(1)}, bf16[8,96,384]{2,1,0:T(8,128)(2,1)S(1)}, u32[]{:S(2)}, u32[]{:S(2)}) collective-permute-start(bf16[8,96,384]{2,1,0:T(8,128)(2,1)S(1)} %collective-permute-done.23.w_pair), channel_id=1, source_target_pairs={{0,128},{128,0},{1,129},{129,1},{2,130},{130,2},{3,131},{131,3},{4... | collective-permute-start | bytes 1769480 | tf_op jit(solution)/shard_map/ppermute | solution.py:36
  79.3 11.1 %collective-permute-start.17 = (bf16[192,384]{1,0:T(8,128)(2,1)}, bf16[192,384]{1,0:T(8,128)(2,1)S(1)}, u32[]{:S(2)}, u32[]{:S(2)}) collective-permute-start(bf16[192,384]{1,0:T(8,128)(2,1)} %copy-done.10), channel_id=1, source_target_pairs={{0,32},{32,64},{64,96},{96,0},{1,33},{33,65},{65,97},{97,1},{2,34}... | collective-permute-start | bytes 442376 | tf_op jit(solution)/shard_map/ppermute | solution.py:27
  79.3 11.1 %collective-permute-start.18 = (bf16[192,384]{1,0:T(8,128)(2,1)}, bf16[192,384]{1,0:T(8,128)(2,1)}, u32[]{:S(2)}, u32[]{:S(2)}) collective-permute-start(bf16[192,384]{1,0:T(8,128)(2,1)} %copy-done.9), channel_id=1, source_target_pairs={{0,64},{32,96},{64,0},{96,32},{1,65},{33,97},{65,1},{97,33},{2,66}... | collective-permute-start | bytes 442376 | tf_op jit(solution)/shard_map/ppermute | solution.py:27
  81.4 9.0 %copy-start.2 = (f32[16,1152]{1,0:T(8,128)S(1)}, f32[16,1152]{1,0:T(8,128)}, u32[]{:S(2)}) copy-start(f32[16,1152]{1,0:T(8,128)} %cap.3) | copy-start | bytes 221188
  81.4 9.0 %collective-permute-start.19 = (bf16[192,384]{1,0:T(8,128)(2,1)}, bf16[192,384]{1,0:T(8,128)(2,1)}, u32[]{:S(2)}, u32[]{:S(2)}) collective-permute-start(bf16[192,384]{1,0:T(8,128)(2,1)} %copy-done.8), channel_id=1, source_target_pairs={{0,96},{32,0},{64,32},{96,64},{1,97},{33,1},{65,33},{97,65},{2,98}... | collective-permute-start | bytes 442376 | tf_op jit(solution)/shard_map/ppermute | solution.py:27
  92.3 0.6 copy-start.5
  93.0 0.6 copy-start.12
  93.6 0.6 copy-start.13
  94.2 0.6 copy-start.14
  94.8 8.3 %collective-permute-start.26 = (bf16[8,96,384]{2,1,0:T(8,128)(2,1)S(1)}, bf16[8,96,384]{2,1,0:T(8,128)(2,1)S(1)}, u32[]{:S(2)}, u32[]{:S(2)}) collective-permute-start(bf16[8,96,384]{2,1,0:T(8,128)(2,1)S(1)} %collective-permute-done.23.w_pair), channel_id=1, source_target_pairs={{0,1},{1,0},{2,3},{3,2},{4,5},{5,4},{6,7},{7,6},{8,9},{9,8},{10,11... | collective-permute-start | bytes 1769480 | tf_op jit(solution)/shard_map/ppermute | solution.py:22
  94.8 8.3 %collective-permute-start.25 = (bf16[8,96,384]{2,1,0:T(8,128)(2,1)S(1)}, bf16[8,96,384]{2,1,0:T(8,128)(2,1)}, u32[]{:S(2)}, u32[]{:S(2)}) collective-permute-start(bf16[8,96,384]{2,1,0:T(8,128)(2,1)S(1)} %collective-permute-done.24.w), channel_id=1, source_target_pairs={{0,1},{1,0},{2,3},{3,2},{4,5},{5,4},{6,7},{7,6},{8,9},{9,8},{10,11... | collective-permute-start | bytes 1769480 | tf_op jit(solution)/shard_map/ppermute | solution.py:22
  95.3 11.8 %all-to-all-start.2 = ((bf16[8,48,384]{2,1,0:T(8,128)(2,1)}), bf16[8,48,384]{2,1,0:T(8,128)(2,1)S(1)}, u32[]{:S(2)}, u32[]{:S(2)}) async-start(bf16[8,48,384]{2,1,0:T(8,128)(2,1)} %get-tuple-element.71), calls=%async_computation.2 | async-start | bytes 589824 | tf_op jit(solution)/shard_map/all_to_all | solution.py:44
  99.6 7.5 %collective-permute-start.20 = (bf16[48,384]{1,0:T(8,128)(2,1)}, bf16[48,384]{1,0:T(8,128)(2,1)S(1)}, u32[]{:S(2)}, u32[]{:S(2)}) collective-permute-start(bf16[48,384]{1,0:T(8,128)(2,1)} %copy-done.14), channel_id=1, source_target_pairs={{0,144},{128,16},{16,128},{144,0},{1,145},{129,17},{17,129},{145,1... | collective-permute-start | bytes 110600 | tf_op jit(solution)/shard_map/ppermute | solution.py:32
  100.0 7.1 %collective-permute-start.21 = (bf16[48,384]{1,0:T(8,128)(2,1)}, bf16[48,384]{1,0:T(8,128)(2,1)S(1)}, u32[]{:S(2)}, u32[]{:S(2)}) collective-permute-start(bf16[48,384]{1,0:T(8,128)(2,1)} %copy-done.13), channel_id=1, source_target_pairs={{0,128},{128,0},{1,129},{129,1},{2,130},{130,2},{3,131},{131,3},{4... | collective-permute-start | bytes 110600 | tf_op jit(solution)/shard_map/ppermute | solution.py:36
  102.5 5.7 %copy-start.6 = (f32[48,384]{1,0:T(8,128)S(1)}, f32[48,384]{1,0:T(8,128)}, u32[]{:S(2)}) copy-start(f32[48,384]{1,0:T(8,128)} %copy-done.5) | copy-start | bytes 221188
  102.5 5.7 %collective-permute-start.22 = (bf16[48,384]{1,0:T(8,128)(2,1)}, bf16[48,384]{1,0:T(8,128)(2,1)S(1)}, u32[]{:S(2)}, u32[]{:S(2)}) collective-permute-start(bf16[48,384]{1,0:T(8,128)(2,1)} %copy-done.12), channel_id=1, source_target_pairs={{0,16},{16,0},{1,17},{17,1},{2,18},{18,2},{3,19},{19,3},{4,20},{20... | collective-permute-start | bytes 110600 | tf_op jit(solution)/shard_map/ppermute | solution.py:40

commit v8 on v7

--- a/solution.py
+++ b/solution.py
@@ -182,13 +182,15 @@
     labels = (ids[...] == index).astype(f32)
     weights = sharpness * (jax.nn.sigmoid(sharpness * dots + offset) - labels)
     half = weights.astype(bf16)
+    part = jnp.dot(half, texts[...], preferred_element_type=f32)
     for k in range(4):
-        part = jnp.dot(half[k * 64 : k * 64 + 64], texts[...], preferred_element_type=f32)
         for j, out in enumerate((g0, g1, g2, g3)):
-            out[k * 48 : k * 48 + 48, :] = fold(part[j * 16 : j * 16 + 16]).astype(out.dtype)
+            at = k * 64 + j * 16
+            out[k * 48 : k * 48 + 48, :] = fold(part[at : at + 16]).astype(out.dtype)
     half = weights.T.astype(bf16)
-    t_own[...] = jnp.dot(half[:128], images[...], preferred_element_type=f32)
-    t_out[...] = jnp.dot(half[128:], images[...], preferred_element_type=f32).astype(bf16)
+    part = jnp.dot(half, images[...], preferred_element_type=f32)
+    t_own[...] = part[:128]
+    t_out[...] = part[128:].astype(bf16)
 
 
 def send_back_kernel(place, t_own, t_in, weight, out):
@@ -231,11 +233,9 @@
             at = pl.ds(pl.multiple_of(side * 768 + k * 384, 384), 384)
             for z in range(8):
                 rows[z * 2 + core, :, at] = part[z, k * 48 : k * 48 + 48, :]
-    for k in range(2):
-        part = rows[k * 8 : k * 8 + 8].reshape(384, 1536)
-        out[:, k * 384 : k * 384 + 384] = lax.dot_general(
-            adj[...], part, BACK, preferred_element_type=f32
-        ).astype(bf16)
+    part = rows[...].reshape(768, 1536)
+    part = lax.dot_general(adj[...], part, BACK, preferred_element_type=f32)
+    out[...] = part.astype(bf16)
 
 
 def project(place, half, adj, parts, before=None):

time: 110 us -> 110 us (level)
  no operation moved by 1% of the time
where the time goes in v8:
time: 110 us; the launch traced here: 109 us
  starting transfers between devices  43.5 us (40%)
  waiting for transfers between devices  36.4 us (33%)
  Pallas kernels  22.3 us (20%)
  local copies, waits for them, and re-layouts  5.06 us (5%)
  between operations  2.07 us (2%)
    ppermute x9, waiting for transfers between devices, turn(): return lax.ppermute(x, axes, [(at[i], at[(i + by) % 4]) for i in range(4)])  24.6 us
    all_to_all x3, starting transfers between devices, exchange(): return lax.all_to_all(x, axes, 0, 0, tiled=True)  19.7 us
    pallas_call x7, Pallas kernels, call(): pl.pallas_call(kernel, out_shape=tuple(outs), in_specs=[pl.BlockSpec(memo...  14.7 us
    ppermute x9, starting transfers between devices, turn(): return lax.ppermute(x, axes, [(at[i], at[(i + by) % 4]) for i in range(4)])  9.19 us
    ppermute x4, starting transfers between devices, swap_pairs(): return lax.ppermute(x, 'xl', [(0, 1), (1, 0)])  8.17 us
    pallas_call x2, Pallas kernels, project(): pl.pallas_call(project_kernel, grid_spec=pltpu.PrefetchScalarGridSpec(num...  7.66 us
    ppermute x4, waiting for transfers between devices, swap_pairs(): return lax.ppermute(x, 'xl', [(0, 1), (1, 0)])  4.96 us
    unnamed x32, local copies, waits for them, and re-layouts  4.94 us
  transfers between devices with their start and end apart: 30, of which 10 were waited for; matrix products, arithmetic and copies ran while one was open for 0% of the time, Pallas kernels for 17%

profile of v8, /device:TPU:2, one launch (start us, length us, event | category | flops | bytes accessed | tf_op | source)
XLA Modules:
  0.0 109.4 jit_solution(15401058390021834234)
XLA Ops:
  0.7 0.5 collective-permute-start.1
  1.3 0.9 copy-done.1
  2.2 0.9 copy-done.3
  3.1 1.6 %shard_map.113 = bf16[8,144,384]{2,1,0:T(8,128)(2,1)} custom-call(s32[5]{0:T(128)S(1)} %stack.23.place, f32[16,1152]{1,0:T(8,128)S(1)} %copy-done.1, bf16[48,1536]{1,0:T(8,128)(2,1)S(1)} %copy-done.3), custom_call_target="tpu_custom_call" | custom-call | bytes 1105920 | tf_op jit(solution)/shard_map/pallas_call | solution.py:73
  4.7 8.5 %all-to-all-start = ((bf16[8,144,384]{2,1,0:T(8,128)(2,1)}), bf16[8,144,384]{2,1,0:T(8,128)(2,1)S(1)}, u32[]{:S(2)}, u32[]{:S(2)}) async-start(bf16[8,144,384]{2,1,0:T(8,128)(2,1)} %shard_map.113), calls=%async_computation | async-start | bytes 1769472 | tf_op jit(solution)/shard_map/all_to_all | solution.py:44
  13.2 4.9 %shard_map.111 = (bf16[384,384]{1,0:T(8,128)(2,1)S(1)}, bf16[448,384]{1,0:T(8,128)(2,1)S(1)}, bf16[448,384]{1,0:T(8,128)(2,1)S(1)}, bf16[448,384]{1,0:T(8,128)(2...) custom-call(s32[5]{0:T(128)S(1)} %stack.23.place, ...), custom_call_target="tpu_custom_call" | custom-call | flops 1811939328 | bytes 7348288 | tf_op jit(solution)/shard_map/pallas_call | solution.py:73
  18.1 1.5 %collective-permute-start.5 = (bf16[192,1536]{1,0:T(8,128)(2,1)S(1)}, bf16[192,1536]{1,0:T(8,128)(2,1)S(1)}, u32[]{:S(2)}, u32[]{:S(2)}) collective-permute-start(bf16[192,1536]{1,0:T(8,128)(2,1)S(1)} %get-tuple-element.46), channel_id=1, source_target_pairs={{0,144},{128,16},{16,128},{144,0},{1,145},{129,17},{17,129},{145,1... | collective-permute-start | bytes 1769480 | tf_op jit(solution)/shard_map/ppermute | solution.py:32
  19.6 3.0 %collective-permute-start.2 = (bf16[448,384]{1,0:T(8,128)(2,1)S(1)}, bf16[448,384]{1,0:T(8,128)(2,1)S(1)}, u32[]{:S(2)}, u32[]{:S(2)}) collective-permute-start(bf16[448,384]{1,0:T(8,128)(2,1)S(1)} %get-tuple-element.42), channel_id=1, source_target_pairs={{0,96},{32,0},{64,32},{96,64},{1,97},{33,1},{65,33},{97,65},{2,98}... | collective-permute-start | bytes 1032200 | tf_op jit(solution)/shard_map/ppermute | solution.py:27
  22.6 0.6 collective-permute-start.3
  23.3 1.0 collective-permute-start.4
  24.3 12.8 %collective-permute-done.2.a1 = bf16[448,384]{1,0:T(8,128)(2,1)S(1)} collective-permute-done((bf16[448,384]{1,0:T(8,128)(2,1)S(1)}, bf16[448,384]{1,0:T(8,128)(2,1)S(1)}, u32[]{:S(2)}, u32[]{:S(2)}) %collective-permute-start.2) | collective-permute-done | bytes 344096 | tf_op jit(solution)/shard_map/ppermute | solution.py:27
  37.1 3.7 %collective-permute-done.4.a3 = bf16[448,384]{1,0:T(8,128)(2,1)S(1)} collective-permute-done((bf16[448,384]{1,0:T(8,128)(2,1)S(1)}, bf16[448,384]{1,0:T(8,128)(2,1)S(1)}, u32[]{:S(2)}, u32[]{:S(2)}) %collective-permute-start.4) | collective-permute-done | bytes 344096 | tf_op jit(solution)/shard_map/ppermute | solution.py:27
  40.8 0.8 shard_map.112
  41.6 0.7 copy-done.11
  42.4 0.6 collective-permute-start.6
  43.0 0.6 collective-permute-start.10
  43.6 0.3 collective-permute-done.7.other_text
  44.0 1.8 %collective-permute-start.8 = (bf16[208,384]{1,0:T(8,128)(2,1)S(1)}, bf16[208,384]{1,0:T(8,128)(2,1)S(1)}, u32[]{:S(2)}, u32[]{:S(2)}) collective-permute-start(bf16[208,384]{1,0:T(8,128)(2,1)S(1)} %get-tuple-element.52.i0), channel_id=1, source_target_pairs={{0,128},{128,0},{1,129},{129,1},{2,130},{130,2},{3,131},{131,3},{4... | collective-permute-start | bytes 479240 | tf_op jit(solution)/shard_map/ppermute | solution.py:36
  45.8 1.2 %collective-permute-start.9 = (bf16[208,384]{1,0:T(8,128)(2,1)S(1)}, bf16[208,384]{1,0:T(8,128)(2,1)S(1)}, u32[]{:S(2)}, u32[]{:S(2)}) collective-permute-start(bf16[208,384]{1,0:T(8,128)(2,1)S(1)} %get-tuple-element.52.i0), channel_id=1, source_target_pairs={{0,16},{16,0},{1,17},{17,1},{2,18},{18,2},{3,19},{19,3},{4,20},{20... | collective-permute-start | bytes 479240 | tf_op jit(solution)/shard_map/ppermute | solution.py:40
  47.0 0.6 collective-permute-start.11
  47.6 1.8 %collective-permute-done.10.rest_1_ = bf16[192,384]{1,0:T(8,128)(2,1)S(1)} collective-permute-done((bf16[192,384]{1,0:T(8,128)(2,1)}, bf16[192,384]{1,0:T(8,128)(2,1)S(1)}, u32[]{:S(2)}, u32[]{:S(2)}) %collective-permute-start.10) | collective-permute-done | bytes 147488 | tf_op jit(solution)/shard_map/ppermute | solution.py:27
  50.7 4.5 %collective-permute-done.11.rest_2_ = bf16[192,384]{1,0:T(8,128)(2,1)S(1)} collective-permute-done((bf16[192,384]{1,0:T(8,128)(2,1)S(1)}, bf16[192,384]{1,0:T(8,128)(2,1)S(1)}, u32[]{:S(2)}, u32[]{:S(2)}) %collective-permute-start.11) | collective-permute-done | bytes 147488 | tf_op jit(solution)/shard_map/ppermute | solution.py:27
  55.2 1.7 %collective-permute-done.12.rest_3_ = bf16[192,384]{1,0:T(8,128)(2,1)S(1)} collective-permute-done((bf16[192,384]{1,0:T(8,128)(2,1)S(1)}, bf16[192,384]{1,0:T(8,128)(2,1)S(1)}, u32[]{:S(2)}, u32[]{:S(2)}) %collective-permute-start.12) | collective-permute-done | bytes 147488 | tf_op jit(solution)/shard_map/ppermute | solution.py:27
  57.0 2.6 %shard_map.114 = (bf16[8,96,384]{2,1,0:T(8,128)(2,1)}, bf16[384,384]{1,0:T(8,128)(2,1)S(1)}, f32[192,384]{1,0:T(8,128)S(1)}, bf16[192,384]{1,0:T(8,128)(2,1)S(1)...) custom-call(s32[5]{0:T(128)S(1)} %stack.23.place, ...), custom_call_target="tpu_custom_call" | custom-call | flops 452984832 | bytes 5505032 | tf_op jit(solution)/shard_map/pallas_call | solution.py:73
  59.6 2.4 %collective-permute-start.14 = (bf16[8,96,384]{2,1,0:T(8,128)(2,1)}, bf16[8,96,384]{2,1,0:T(8,128)(2,1)}, u32[]{:S(2)}, u32[]{:S(2)}) collective-permute-start(bf16[8,96,384]{2,1,0:T(8,128)(2,1)} %get-tuple-element.61.w), channel_id=1, source_target_pairs={{0,128},{128,0},{1,129},{129,1},{2,130},{130,2},{3,131},{131,3},{4... | collective-permute-start | bytes 1769480 | tf_op jit(solution)/shard_map/ppermute | solution.py:36
  62.0 0.9 collective-permute-start.23
  62.9 1.5 %shard_map.115 = bf16[8,96,384]{2,1,0:T(8,128)(2,1)} custom-call(s32[5]{0:T(128)S(1)} %stack.23.place, f32[128,1152]{1,0:T(8,128)S(1)} %get-tuple-element.58.t_own, bf16[128,1152]{1,0:T(8,128)(2,1)S(1)} %collective-permute-done.13.t_in, bf16[384,384]{1,0:T(8,128)(2,1)S(1)} %get-tuple-element.60.weight), custom_call_target="tpu_custom_call" | custom-call | bytes 1769472 | tf_op jit(solution)/shard_map/pallas_call | solution.py:73
  64.4 6.9 %all-to-all-start.1 = ((bf16[8,96,384]{2,1,0:T(8,128)(2,1)}), bf16[8,96,384]{2,1,0:T(8,128)(2,1)S(1)}, u32[]{:S(2)}, u32[]{:S(2)}) async-start(bf16[8,96,384]{2,1,0:T(8,128)(2,1)} %shard_map.115), calls=%async_computation.1 | async-start | bytes 1179648 | tf_op jit(solution)/shard_map/all_to_all | solution.py:44
  71.3 5.0 %collective-permute-done.14.w_pair = bf16[8,96,384]{2,1,0:T(8,128)(2,1)} collective-permute-done((bf16[8,96,384]{2,1,0:T(8,128)(2,1)}, bf16[8,96,384]{2,1,0:T(8,128)(2,1)}, u32[]{:S(2)}, u32[]{:S(2)}) %collective-permute-start.14) | collective-permute-done | bytes 589856 | tf_op jit(solution)/shard_map/ppermute | solution.py:36
  76.3 1.4 %collective-permute-done.23.w_pair = bf16[8,96,384]{2,1,0:T(8,128)(2,1)S(1)} collective-permute-done((bf16[8,96,384]{2,1,0:T(8,128)(2,1)}, bf16[8,96,384]{2,1,0:T(8,128)(2,1)S(1)}, u32[]{:S(2)}, u32[]{:S(2)}) %collective-permute-start.23) | collective-permute-done | bytes 589856 | tf_op jit(solution)/shard_map/ppermute | solution.py:32
  77.6 1.5 %collective-permute-start.24 = (bf16[8,96,384]{2,1,0:T(8,128)(2,1)S(1)}, bf16[8,96,384]{2,1,0:T(8,128)(2,1)S(1)}, u32[]{:S(2)}, u32[]{:S(2)}) collective-permute-start(bf16[8,96,384]{2,1,0:T(8,128)(2,1)S(1)} %collective-permute-done.23.w_pair), channel_id=1, source_target_pairs={{0,128},{128,0},{1,129},{129,1},{2,130},{130,2},{3,131},{131,3},{4... | collective-permute-start | bytes 1769480 | tf_op jit(solution)/shard_map/ppermute | solution.py:36
  79.1 2.1 %collective-permute-start.18 = (bf16[192,384]{1,0:T(8,128)(2,1)}, bf16[192,384]{1,0:T(8,128)(2,1)}, u32[]{:S(2)}, u32[]{:S(2)}) collective-permute-start(bf16[192,384]{1,0:T(8,128)(2,1)} %copy-done.9), channel_id=1, source_target_pairs={{0,64},{32,96},{64,0},{96,32},{1,65},{33,97},{65,1},{97,33},{2,66}... | collective-permute-start | bytes 442376 | tf_op jit(solution)/shard_map/ppermute | solution.py:27
  81.2 1.2 %collective-permute-start.19 = (bf16[192,384]{1,0:T(8,128)(2,1)}, bf16[192,384]{1,0:T(8,128)(2,1)}, u32[]{:S(2)}, u32[]{:S(2)}) collective-permute-start(bf16[192,384]{1,0:T(8,128)(2,1)} %copy-done.8), channel_id=1, source_target_pairs={{0,96},{32,0},{64,32},{96,64},{1,97},{33,1},{65,33},{97,65},{2,98}... | collective-permute-start | bytes 442376 | tf_op jit(solution)/shard_map/ppermute | solution.py:27
  82.5 3.9 %shard_map.116.rest_0_ = bf16[384,1536]{1,0:T(8,128)(2,1)} custom-call(s32[5]{0:T(128)S(1)} %stack.23.place, bf16[384,1536]{1,0:T(8,128)(2,1)S(1)} %copy-done, bf16[8,96,384]{2,1,0:T(8,128)(2,1)} %get-tuple-element.61.w, bf16[8,96,384]{2,1,0:T(8,128)(2,1)} %collective-permute-done.14.w_pair, bf16[8,96,384]{2,1,0:T(8,128)(2,1)S(1)} %collective-permute-done.15.other, ...), custom_call_target="tpu_custom_call" | custom-call | flops 905969664 | bytes 6291456 | tf_op jit(solution)/shard_map/pallas_call | solution.py:245
  86.4 3.9 %all-to-all-done.1.back = bf16[8,96,384]{2,1,0:T(8,128)(2,1)S(1)} async-done(((bf16[8,96,384]{2,1,0:T(8,128)(2,1)}), bf16[8,96,384]{2,1,0:T(8,128)(2,1)S(1)}, u32[]{:S(2)}, u32[]{:S(2)}) %all-to-all-start.1) | async-done | bytes 589856 | tf_op jit(solution)/shard_map/all_to_all | solution.py:44
  90.3 1.9 %shard_map.117 = (f32[16,1152]{1,0:T(8,128)}, bf16[8,48,384]{2,1,0:T(8,128)(2,1)}, f32[48,384]{1,0:T(8,128)S(1)}, bf16[48,384]{1,0:T(8,128)(2,1)S(1)}, bf16[48,3...) custom-call(s32[5]{0:T(128)S(1)} %stack.23.place, bf16[8,96,384]{2,1,0:T(8,128)(2,1)S(1)} %all-to-all-done.1.back, ...), custom_call_target="tpu_custom_call" | custom-call | bytes 1953792 | tf_op jit(solution)/shard_map/pallas_call | solution.py:73
  92.2 0.6 copy-done.5
  92.8 0.6 copy-done.12
  93.4 0.6 copy-done.13
  94.0 0.6 copy-done.14
  94.6 0.5 collective-permute-start.25
  95.1 4.3 %all-to-all-start.2 = ((bf16[8,48,384]{2,1,0:T(8,128)(2,1)}), bf16[8,48,384]{2,1,0:T(8,128)(2,1)S(1)}, u32[]{:S(2)}, u32[]{:S(2)}) async-start(bf16[8,48,384]{2,1,0:T(8,128)(2,1)} %get-tuple-element.71), calls=%async_computation.2 | async-start | bytes 589824 | tf_op jit(solution)/shard_map/all_to_all | solution.py:44
  99.4 0.4 collective-permute-start.20
  99.8 2.5 %collective-permute-start.21 = (bf16[48,384]{1,0:T(8,128)(2,1)}, bf16[48,384]{1,0:T(8,128)(2,1)S(1)}, u32[]{:S(2)}, u32[]{:S(2)}) collective-permute-start(bf16[48,384]{1,0:T(8,128)(2,1)} %copy-done.13), channel_id=1, source_target_pairs={{0,128},{128,0},{1,129},{129,1},{2,130},{130,2},{3,131},{131,3},{4... | collective-permute-start | bytes 110600 | tf_op jit(solution)/shard_map/ppermute | solution.py:36
  102.3 0.6 collective-permute-start.22
  102.9 3.7 %shard_map.118 = bf16[384,1536]{1,0:T(8,128)(2,1)} custom-call(s32[5]{0:T(128)S(1)} %stack.23.place, bf16[384,1536]{1,0:T(8,128)(2,1)S(1)} %copy-done, bf16[8,96,384]{2,1,0:T(8,128)(2,1)S(1)} %collective-permute-done.24.w, bf16[8,96,384]{2,1,0:T(8,128)(2,1)S(1)} %collective-permute-done.23.w_pair, ...), custom_call_target="tpu_custom_call", output_to_operand_aliasing={{}: (6, {})} | custom-call | flops 905969664 | bytes 6291456 | tf_op jit(solution)/shard_map/pallas_call | solution.py:245
  106.7 1.3 %collective-permute-done.22.h3 = bf16[48,384]{1,0:T(8,128)(2,1)S(1)} collective-permute-done((bf16[48,384]{1,0:T(8,128)(2,1)}, bf16[48,384]{1,0:T(8,128)(2,1)S(1)}, u32[]{:S(2)}, u32[]{:S(2)}) %collective-permute-start.22) | collective-permute-done | bytes 36896 | tf_op jit(solution)/shard_map/ppermute | solution.py:40
  108.0 1.4 %shard_map.119 = (f32[16,1152]{1,0:T(8,128)}, f32[48,1536]{1,0:T(8,128)}) custom-call(s32[5]{0:T(128)S(1)} %stack.23.place, f32[48,384]{1,0:T(8,128)S(1)} %copy-done.6, bf16[48,384]{1,0:T(8,128)(2,1)S(1)} %collective-permute-done.20.h1, bf16[48,384]{1,0:T(8,128)(2,1)S(1)} %collective-permute-done.21.h2, bf16[48,384]{1,0:T(8,128)(2,1)S(1)} %collective-permute-done.22.h3, ...), custom_call_target="tpu_custom_call" | custom-call | bytes 921600 | tf_op jit(solution)/shard_map/pallas_call | solution.py:73
  (55 shorter events, 0.4 us)
Async XLA Ops:
  0.6 4.1 %collective-permute-start = (bf16[384,1536]{1,0:T(8,128)(2,1)}, bf16[384,1536]{1,0:T(8,128)(2,1)}, u32[]{:S(2)}, u32[]{:S(2)}) collective-permute-start(bf16[384,1536]{1,0:T(8,128)(2,1)} %tokens.1), channel_id=1, source_target_pairs={{0,1},{1,0},{2,3},{3,2},{4,5},{5,4},{6,7},{7,6},{8,9},{9,8},{10,11... | collective-permute-start | bytes 3538952 | tf_op jit(solution)/shard_map/ppermute | solution.py:22
  0.7 12.4 %collective-permute-start.1 = (bf16[384,1536]{1,0:T(8,128)(2,1)}, bf16[384,1536]{1,0:T(8,128)(2,1)}, u32[]{:S(2)}, u32[]{:S(2)}) collective-permute-start(bf16[384,1536]{1,0:T(8,128)(2,1)} %adj.5), channel_id=1, source_target_pairs={{0,1},{1,0},{2,3},{3,2},{4,5},{5,4},{6,7},{7,6},{8,9},{9,8},{10,11... | collective-permute-start | bytes 3538952 | tf_op jit(solution)/shard_map/ppermute | solution.py:22
  1.3 0.9 copy-start.1
  2.2 0.9 copy-start.3
  3.1 10.1 %copy-start = (bf16[384,1536]{1,0:T(8,128)(2,1)S(1)}, bf16[384,1536]{1,0:T(8,128)(2,1)}, u32[]{:S(2)}) copy-start(bf16[384,1536]{1,0:T(8,128)(2,1)} %adj.5) | copy-start | bytes 3538948
  3.1 10.1 %copy-start.4 = (f32[16,1152]{1,0:T(8,128)S(1)}, f32[16,1152]{1,0:T(8,128)}, u32[]{:S(2)}) copy-start(f32[16,1152]{1,0:T(8,128)} %pic.3) | copy-start | bytes 221188
  3.1 10.1 %copy-start.7 = (bf16[384,1536]{1,0:T(8,128)(2,1)S(1)}, bf16[384,1536]{1,0:T(8,128)(2,1)}, u32[]{:S(2)}) copy-start(bf16[384,1536]{1,0:T(8,128)(2,1)} %tokens.1) | copy-start | bytes 3538948
  3.1 10.1 %copy-start.15 = (s32[16]{0:T(128)S(1)}, s32[16]{0:T(128)}, u32[]{:S(2)}) copy-start(s32[16]{0:T(128)} %ids.1) | copy-start | bytes 196
  4.7 37.6 %all-to-all-start = ((bf16[8,144,384]{2,1,0:T(8,128)(2,1)}), bf16[8,144,384]{2,1,0:T(8,128)(2,1)S(1)}, u32[]{:S(2)}, u32[]{:S(2)}) async-start(bf16[8,144,384]{2,1,0:T(8,128)(2,1)} %shard_map.113), calls=%async_computation | async-start | bytes 1769472 | tf_op jit(solution)/shard_map/all_to_all | solution.py:44
  18.1 22.7 %collective-permute-start.5 = (bf16[192,1536]{1,0:T(8,128)(2,1)S(1)}, bf16[192,1536]{1,0:T(8,128)(2,1)S(1)}, u32[]{:S(2)}, u32[]{:S(2)}) collective-permute-start(bf16[192,1536]{1,0:T(8,128)(2,1)S(1)} %get-tuple-element.46), channel_id=1, source_target_pairs={{0,144},{128,16},{16,128},{144,0},{1,145},{129,17},{17,129},{145,1... | collective-permute-start | bytes 1769480 | tf_op jit(solution)/shard_map/ppermute | solution.py:32
  19.6 17.4 %collective-permute-start.2 = (bf16[448,384]{1,0:T(8,128)(2,1)S(1)}, bf16[448,384]{1,0:T(8,128)(2,1)S(1)}, u32[]{:S(2)}, u32[]{:S(2)}) collective-permute-start(bf16[448,384]{1,0:T(8,128)(2,1)S(1)} %get-tuple-element.42), channel_id=1, source_target_pairs={{0,96},{32,0},{64,32},{96,64},{1,97},{33,1},{65,33},{97,65},{2,98}... | collective-permute-start | bytes 1032200 | tf_op jit(solution)/shard_map/ppermute | solution.py:27
  22.6 14.4 %collective-permute-start.3 = (bf16[448,384]{1,0:T(8,128)(2,1)S(1)}, bf16[448,384]{1,0:T(8,128)(2,1)S(1)}, u32[]{:S(2)}, u32[]{:S(2)}) collective-permute-start(bf16[448,384]{1,0:T(8,128)(2,1)S(1)} %get-tuple-element.43), channel_id=1, source_target_pairs={{0,64},{32,96},{64,0},{96,32},{1,65},{33,97},{65,1},{97,33},{2,66}... | collective-permute-start | bytes 1032200 | tf_op jit(solution)/shard_map/ppermute | solution.py:27
  23.3 17.5 %collective-permute-start.4 = (bf16[448,384]{1,0:T(8,128)(2,1)S(1)}, bf16[448,384]{1,0:T(8,128)(2,1)S(1)}, u32[]{:S(2)}, u32[]{:S(2)}) collective-permute-start(bf16[448,384]{1,0:T(8,128)(2,1)S(1)} %get-tuple-element.44), channel_id=1, source_target_pairs={{0,32},{32,64},{64,96},{96,0},{1,33},{33,65},{65,97},{97,1},{2,34}... | collective-permute-start | bytes 1032200 | tf_op jit(solution)/shard_map/ppermute | solution.py:27
  41.6 0.7 copy-start.11
  42.3 1.7 %collective-permute-start.7 = (bf16[8,48,384]{2,1,0:T(8,128)(2,1)S(1)}, bf16[8,48,384]{2,1,0:T(8,128)(2,1)S(1)}, u32[]{:S(2)}, u32[]{:S(2)}) collective-permute-start(bf16[8,48,384]{2,1,0:T(8,128)(2,1)S(1)} %slice.3), channel_id=1, source_target_pairs={{0,1},{1,0},{2,3},{3,2},{4,5},{5,4},{6,7},{7,6},{8,9},{9,8},{10,11... | collective-permute-start | bytes 884744 | tf_op jit(solution)/shard_map/ppermute | solution.py:22
  42.4 14.6 %collective-permute-start.6 = (bf16[400,384]{1,0:T(8,128)(2,1)S(1)}, bf16[400,384]{1,0:T(8,128)(2,1)S(1)}, u32[]{:S(2)}, u32[]{:S(2)}) collective-permute-start(bf16[400,384]{1,0:T(8,128)(2,1)S(1)} %get-tuple-element.49), channel_id=1, source_target_pairs={{0,144},{128,16},{16,128},{144,0},{1,145},{129,17},{17,129},{145,1... | collective-permute-start | bytes 921608 | tf_op jit(solution)/shard_map/ppermute | solution.py:32
  43.0 6.4 %collective-permute-start.10 = (bf16[192,384]{1,0:T(8,128)(2,1)}, bf16[192,384]{1,0:T(8,128)(2,1)S(1)}, u32[]{:S(2)}, u32[]{:S(2)}) collective-permute-start(bf16[192,384]{1,0:T(8,128)(2,1)} %copy-done.11), channel_id=1, source_target_pairs={{0,96},{32,0},{64,32},{96,64},{1,97},{33,1},{65,33},{97,65},{2,98}... | collective-permute-start | bytes 442376 | tf_op jit(solution)/shard_map/ppermute | solution.py:27
  44.0 13.0 %collective-permute-start.8 = (bf16[208,384]{1,0:T(8,128)(2,1)S(1)}, bf16[208,384]{1,0:T(8,128)(2,1)S(1)}, u32[]{:S(2)}, u32[]{:S(2)}) collective-permute-start(bf16[208,384]{1,0:T(8,128)(2,1)S(1)} %get-tuple-element.52.i0), channel_id=1, source_target_pairs={{0,128},{128,0},{1,129},{129,1},{2,130},{130,2},{3,131},{131,3},{4... | collective-permute-start | bytes 479240 | tf_op jit(solution)/shard_map/ppermute | solution.py:36
  45.8 11.2 %collective-permute-start.9 = (bf16[208,384]{1,0:T(8,128)(2,1)S(1)}, bf16[208,384]{1,0:T(8,128)(2,1)S(1)}, u32[]{:S(2)}, u32[]{:S(2)}) collective-permute-start(bf16[208,384]{1,0:T(8,128)(2,1)S(1)} %get-tuple-element.52.i0), channel_id=1, source_target_pairs={{0,16},{16,0},{1,17},{17,1},{2,18},{18,2},{3,19},{19,3},{4,20},{20... | collective-permute-start | bytes 479240 | tf_op jit(solution)/shard_map/ppermute | solution.py:40
  47.0 8.3 %collective-permute-start.11 = (bf16[192,384]{1,0:T(8,128)(2,1)S(1)}, bf16[192,384]{1,0:T(8,128)(2,1)S(1)}, u32[]{:S(2)}, u32[]{:S(2)}) collective-permute-start(bf16[192,384]{1,0:T(8,128)(2,1)S(1)} %get-tuple-element.56), channel_id=1, source_target_pairs={{0,64},{32,96},{64,0},{96,32},{1,65},{33,97},{65,1},{97,33},{2,66}... | collective-permute-start | bytes 442376 | tf_op jit(solution)/shard_map/ppermute | solution.py:27
  49.4 7.6 %collective-permute-start.12 = (bf16[192,384]{1,0:T(8,128)(2,1)S(1)}, bf16[192,384]{1,0:T(8,128)(2,1)S(1)}, u32[]{:S(2)}, u32[]{:S(2)}) collective-permute-start(bf16[192,384]{1,0:T(8,128)(2,1)S(1)} %get-tuple-element.57), channel_id=1, source_target_pairs={{0,32},{32,64},{64,96},{96,0},{1,33},{33,65},{65,97},{97,1},{2,34}... | collective-permute-start | bytes 442376 | tf_op jit(solution)/shard_map/ppermute | solution.py:27
  59.6 3.3 %copy-start.8 = (bf16[192,384]{1,0:T(8,128)(2,1)}, bf16[192,384]{1,0:T(8,128)(2,1)S(1)}, u32[]{:S(2)}) copy-start(bf16[192,384]{1,0:T(8,128)(2,1)S(1)} %get-tuple-element.66) | copy-start | bytes 442372
  59.6 4.8 %copy-start.9 = (bf16[192,384]{1,0:T(8,128)(2,1)}, bf16[192,384]{1,0:T(8,128)(2,1)S(1)}, u32[]{:S(2)}) copy-start(bf16[192,384]{1,0:T(8,128)(2,1)S(1)} %get-tuple-element.65) | copy-start | bytes 442372
  59.6 19.5 %copy-start.10 = (bf16[192,384]{1,0:T(8,128)(2,1)}, bf16[192,384]{1,0:T(8,128)(2,1)S(1)}, u32[]{:S(2)}) copy-start(bf16[192,384]{1,0:T(8,128)(2,1)S(1)} %get-tuple-element.64) | copy-start | bytes 442372
  59.6 3.3 %collective-permute-start.13 = (bf16[128,1152]{1,0:T(8,128)(2,1)S(1)}, bf16[128,1152]{1,0:T(8,128)(2,1)S(1)}, u32[]{:S(2)}, u32[]{:S(2)}) collective-permute-start(bf16[128,1152]{1,0:T(8,128)(2,1)S(1)} %get-tuple-element.59), channel_id=1, source_target_pairs={{0,1},{1,0},{2,3},{3,2},{4,5},{5,4},{6,7},{7,6},{8,9},{9,8},{10,11... | collective-permute-start | bytes 884744 | tf_op jit(solution)/shard_map/ppermute | solution.py:22
  59.6 16.7 %collective-permute-start.14 = (bf16[8,96,384]{2,1,0:T(8,128)(2,1)}, bf16[8,96,384]{2,1,0:T(8,128)(2,1)}, u32[]{:S(2)}, u32[]{:S(2)}) collective-permute-start(bf16[8,96,384]{2,1,0:T(8,128)(2,1)} %get-tuple-element.61.w), channel_id=1, source_target_pairs={{0,128},{128,0},{1,129},{129,1},{2,130},{130,2},{3,131},{131,3},{4... | collective-permute-start | bytes 1769480 | tf_op jit(solution)/shard_map/ppermute | solution.py:36
  62.0 15.6 %collective-permute-start.23 = (bf16[8,96,384]{2,1,0:T(8,128)(2,1)}, bf16[8,96,384]{2,1,0:T(8,128)(2,1)S(1)}, u32[]{:S(2)}, u32[]{:S(2)}) collective-permute-start(bf16[8,96,384]{2,1,0:T(8,128)(2,1)} %get-tuple-element.61.w), channel_id=1, source_target_pairs={{0,144},{128,16},{16,128},{144,0},{1,145},{129,17},{17,129},{145,1... | collective-permute-start | bytes 1769480 | tf_op jit(solution)/shard_map/ppermute | solution.py:32
  64.4 25.9 %all-to-all-start.1 = ((bf16[8,96,384]{2,1,0:T(8,128)(2,1)}), bf16[8,96,384]{2,1,0:T(8,128)(2,1)S(1)}, u32[]{:S(2)}, u32[]{:S(2)}) async-start(bf16[8,96,384]{2,1,0:T(8,128)(2,1)} %shard_map.115), calls=%async_computation.1 | async-start | bytes 1179648 | tf_op jit(solution)/shard_map/all_to_all | solution.py:44
  71.3 9.9 %collective-permute-start.15 = (bf16[8,96,384]{2,1,0:T(8,128)(2,1)}, bf16[8,96,384]{2,1,0:T(8,128)(2,1)S(1)}, u32[]{:S(2)}, u32[]{:S(2)}) collective-permute-start(bf16[8,96,384]{2,1,0:T(8,128)(2,1)} %get-tuple-element.61.w), channel_id=1, source_target_pairs={{0,1},{1,0},{2,3},{3,2},{4,5},{5,4},{6,7},{7,6},{8,9},{9,8},{10,11... | collective-permute-start | bytes 1769480 | tf_op jit(solution)/shard_map/ppermute | solution.py:22
  76.3 6.2 %collective-permute-start.16 = (bf16[8,96,384]{2,1,0:T(8,128)(2,1)}, bf16[8,96,384]{2,1,0:T(8,128)(2,1)S(1)}, u32[]{:S(2)}, u32[]{:S(2)}) collective-permute-start(bf16[8,96,384]{2,1,0:T(8,128)(2,1)} %collective-permute-done.14.w_pair), channel_id=1, source_target_pairs={{0,1},{1,0},{2,3},{3,2},{4,5},{5,4},{6,7},{7,6},{8,9},{9,8},{10,11... | collective-permute-start | bytes 1769480 | tf_op jit(solution)/shard_map/ppermute | solution.py:22
  77.6 17.0 %collective-permute-start.24 = (bf16[8,96,384]{2,1,0:T(8,128)(2,1)S(1)}, bf16[8,96,384]{2,1,0:T(8,128)(2,1)S(1)}, u32[]{:S(2)}, u32[]{:S(2)}) collective-permute-start(bf16[8,96,384]{2,1,0:T(8,128)(2,1)S(1)} %collective-permute-done.23.w_pair), channel_id=1, source_target_pairs={{0,128},{128,0},{1,129},{129,1},{2,130},{130,2},{3,131},{131,3},{4... | collective-permute-start | bytes 1769480 | tf_op jit(solution)/shard_map/ppermute | solution.py:36
  79.1 11.1 %collective-permute-start.17 = (bf16[192,384]{1,0:T(8,128)(2,1)}, bf16[192,384]{1,0:T(8,128)(2,1)S(1)}, u32[]{:S(2)}, u32[]{:S(2)}) collective-permute-start(bf16[192,384]{1,0:T(8,128)(2,1)} %copy-done.10), channel_id=1, source_target_pairs={{0,32},{32,64},{64,96},{96,0},{1,33},{33,65},{65,97},{97,1},{2,34}... | collective-permute-start | bytes 442376 | tf_op jit(solution)/shard_map/ppermute | solution.py:27
  79.1 11.1 %collective-permute-start.18 = (bf16[192,384]{1,0:T(8,128)(2,1)}, bf16[192,384]{1,0:T(8,128)(2,1)}, u32[]{:S(2)}, u32[]{:S(2)}) collective-permute-start(bf16[192,384]{1,0:T(8,128)(2,1)} %copy-done.9), channel_id=1, source_target_pairs={{0,64},{32,96},{64,0},{96,32},{1,65},{33,97},{65,1},{97,33},{2,66}... | collective-permute-start | bytes 442376 | tf_op jit(solution)/shard_map/ppermute | solution.py:27
  81.2 9.0 %copy-start.2 = (f32[16,1152]{1,0:T(8,128)S(1)}, f32[16,1152]{1,0:T(8,128)}, u32[]{:S(2)}) copy-start(f32[16,1152]{1,0:T(8,128)} %cap.3) | copy-start | bytes 221188
  81.2 9.0 %collective-permute-start.19 = (bf16[192,384]{1,0:T(8,128)(2,1)}, bf16[192,384]{1,0:T(8,128)(2,1)}, u32[]{:S(2)}, u32[]{:S(2)}) collective-permute-start(bf16[192,384]{1,0:T(8,128)(2,1)} %copy-done.8), channel_id=1, source_target_pairs={{0,96},{32,0},{64,32},{96,64},{1,97},{33,1},{65,33},{97,65},{2,98}... | collective-permute-start | bytes 442376 | tf_op jit(solution)/shard_map/ppermute | solution.py:27
  92.2 0.6 copy-start.5
  92.8 0.6 copy-start.12
  93.4 0.6 copy-start.13
  94.0 0.6 copy-start.14
  94.6 8.3 %collective-permute-start.26 = (bf16[8,96,384]{2,1,0:T(8,128)(2,1)S(1)}, bf16[8,96,384]{2,1,0:T(8,128)(2,1)S(1)}, u32[]{:S(2)}, u32[]{:S(2)}) collective-permute-start(bf16[8,96,384]{2,1,0:T(8,128)(2,1)S(1)} %collective-permute-done.23.w_pair), channel_id=1, source_target_pairs={{0,1},{1,0},{2,3},{3,2},{4,5},{5,4},{6,7},{7,6},{8,9},{9,8},{10,11... | collective-permute-start | bytes 1769480 | tf_op jit(solution)/shard_map/ppermute | solution.py:22
  94.6 8.3 %collective-permute-start.25 = (bf16[8,96,384]{2,1,0:T(8,128)(2,1)S(1)}, bf16[8,96,384]{2,1,0:T(8,128)(2,1)}, u32[]{:S(2)}, u32[]{:S(2)}) collective-permute-start(bf16[8,96,384]{2,1,0:T(8,128)(2,1)S(1)} %collective-permute-done.24.w), channel_id=1, source_target_pairs={{0,1},{1,0},{2,3},{3,2},{4,5},{5,4},{6,7},{7,6},{8,9},{9,8},{10,11... | collective-permute-start | bytes 1769480 | tf_op jit(solution)/shard_map/ppermute | solution.py:22
  95.1 11.5 %all-to-all-start.2 = ((bf16[8,48,384]{2,1,0:T(8,128)(2,1)}), bf16[8,48,384]{2,1,0:T(8,128)(2,1)S(1)}, u32[]{:S(2)}, u32[]{:S(2)}) async-start(bf16[8,48,384]{2,1,0:T(8,128)(2,1)} %get-tuple-element.71), calls=%async_computation.2 | async-start | bytes 589824 | tf_op jit(solution)/shard_map/all_to_all | solution.py:44
  99.4 7.2 %collective-permute-start.20 = (bf16[48,384]{1,0:T(8,128)(2,1)}, bf16[48,384]{1,0:T(8,128)(2,1)S(1)}, u32[]{:S(2)}, u32[]{:S(2)}) collective-permute-start(bf16[48,384]{1,0:T(8,128)(2,1)} %copy-done.14), channel_id=1, source_target_pairs={{0,144},{128,16},{16,128},{144,0},{1,145},{129,17},{17,129},{145,1... | collective-permute-start | bytes 110600 | tf_op jit(solution)/shard_map/ppermute | solution.py:32
  99.8 6.9 %collective-permute-start.21 = (bf16[48,384]{1,0:T(8,128)(2,1)}, bf16[48,384]{1,0:T(8,128)(2,1)S(1)}, u32[]{:S(2)}, u32[]{:S(2)}) collective-permute-start(bf16[48,384]{1,0:T(8,128)(2,1)} %copy-done.13), channel_id=1, source_target_pairs={{0,128},{128,0},{1,129},{129,1},{2,130},{130,2},{3,131},{131,3},{4... | collective-permute-start | bytes 110600 | tf_op jit(solution)/shard_map/ppermute | solution.py:36
  102.3 5.7 %copy-start.6 = (f32[48,384]{1,0:T(8,128)S(1)}, f32[48,384]{1,0:T(8,128)}, u32[]{:S(2)}) copy-start(f32[48,384]{1,0:T(8,128)} %copy-done.5) | copy-start | bytes 221188
  102.3 5.7 %collective-permute-start.22 = (bf16[48,384]{1,0:T(8,128)(2,1)}, bf16[48,384]{1,0:T(8,128)(2,1)S(1)}, u32[]{:S(2)}, u32[]{:S(2)}) collective-permute-start(bf16[48,384]{1,0:T(8,128)(2,1)} %copy-done.12), channel_id=1, source_target_pairs={{0,16},{16,0},{1,17},{17,1},{2,18},{18,2},{3,19},{19,3},{4,20},{20... | collective-permute-start | bytes 110600 | tf_op jit(solution)/shard_map/ppermute | solution.py:40
